TPU v7x, 256 devices: a whole 4x4x8 slice. The times are simulated.
256 devices in a mesh: role: 2 (over y_hi), dp: 8 (over z), tensor: 16 (over x, y_lo, core).
Axes of the slice: x: 4, y: 4 (y_hi: 2, y_lo: 2; y = y_hi * 2 + y_lo), z: 8, core: 2. Of those that a mesh axis runs over, the one named last changes fastest.
Arguments:
- learner_inputs: bfloat16 [16384, 8192], P(('role', 'dp'), 'tensor'), may hold values from -6 to 6
- learner_cotangent: bfloat16 [16384, 5120], P(('role', 'dp'), 'tensor'), may hold values from -0.0625 to 0.0625
- master_weight: float32 [8192, 5120], P('tensor', ('role', 'dp')), may hold values from -5 to 5
- first_moment: float32 [8192, 5120], P('tensor', ('role', 'dp')), may hold values from -3 to 3
- second_moment: float32 [8192, 5120], P('tensor', ('role', 'dp')), may hold values from 0.02 to 1
- query_weight: bfloat16 [5120, 8192], P(None, 'tensor'), may hold values from -0.078125 to 0.078125
- keyval_weight: bfloat16 [5120, 2048], P(None, 'tensor'), may hold values from -0.078125 to 0.078125
- prefix_cache: bfloat16 [64, 512, 2048], P(('role', 'dp'), None, 'tensor'), may hold values from -4000 to 4000
- block_states: bfloat16 [64, 32, 5120], P(('role', 'dp'), None, 'tensor'), may hold values from -50 to 50
- norm_gain: float32 [5120], replicated, may hold values from 0.1 to 1.9
- mask_vector: bfloat16 [5120], replicated, may hold values from -5 to 5
- prefix_lengths: int32 [64], P(('role', 'dp')), may hold values from 128 to 512, as said below
- position_picks: int32 [2, 64, 32], P(None, ('role', 'dp')), may hold values from 0 to 2
Outputs:
- next_states: bfloat16 [64, 32, 5120], P(('role', 'dp'), None, 'tensor')
- new_weight: float32 [8192, 5120], P('tensor', ('role', 'dp'))
- new_first: float32 [8192, 5120], P('tensor', ('role', 'dp'))
- new_second: float32 [8192, 5120], P('tensor', ('role', 'dp'))
Inputs may be any that keep to these rules, and one draw needn't show every extreme that they name: `prefix_lengths`: every row has 128 or more valid positions; some row has all 512 and some row exactly 128.
All inputs are finite; a program needn't handle non-finite values.
Results may differ from a plain program's by a relative error of at most 0.025.
Values may be sent and summed in bfloat16 or wider, within the bound.
No kernel may reach another device: no remote copies, remote signals or barrier semaphores. Data moves between devices by JAX's collectives and lax.ppermute only.
A program may use at most 128 MiB of HBM per device.

v0:
```python
import jax
import jax.numpy as jnp
from jax import lax
from jax.sharding import PartitionSpec as P

HEADS = 64
HEAD = 128
STEPS = 2


BETA_ONE = 0.9
BETA_TWO = 0.95
ADAM_EPS = 1e-08
LEARN_RATE = 0.5
DECAY_RATE = 0.1
STEP_COUNT = 50
NORM_EPS = 1e-06


def partner(block, axis, stride):
    count = lax.axis_size(axis)
    route = []
    for low in range(count):
        high = low | 1 << stride
        if high != low and high < count:
            route += [(low, high), (high, low)]
    return lax.ppermute(block, axis, route)


def contract_tokens(left_side, right_side):
    return lax.dot_general(
        left_side, right_side, (((0,), (0,)), ((), ())), preferred_element_type=jnp.float32
    )


def adam_update(gradient, master_weight, first_moment, second_moment):
    first_new = BETA_ONE * first_moment + (1.0 - BETA_ONE) * gradient
    second_new = BETA_TWO * second_moment + (1.0 - BETA_TWO) * gradient * gradient
    first_hat = first_new / (1.0 - BETA_ONE**STEP_COUNT)
    second_hat = second_new / (1.0 - BETA_TWO**STEP_COUNT)
    weight_new = master_weight - LEARN_RATE * (
        first_hat / (jnp.sqrt(second_hat) + ADAM_EPS) + DECAY_RATE * master_weight
    )
    return (weight_new, first_new, second_new)


def normalize(current_state, norm_gain):
    values = current_state.astype(jnp.float32)
    mean_square = jnp.mean(values * values, axis=-1, keepdims=True)
    return (values * lax.rsqrt(mean_square + NORM_EPS) * norm_gain).astype(jnp.bfloat16)


def revise(current_state, update, pick_codes, mask_values):
    values = current_state.astype(jnp.float32)
    pick_cols = pick_codes[..., None]
    masked = jnp.broadcast_to(mask_values.astype(jnp.float32), values.shape)
    return jnp.where(
        pick_cols == 1, values + update, jnp.where(pick_cols == 2, masked, values)
    ).astype(jnp.bfloat16)


def attend(queries, cache_keys, cache_values, block_keys, block_values, prefix_lengths):
    score_scale = HEAD ** (-0.5)
    prefix_len = cache_keys.shape[1]
    prefix_scores = (
        jnp.einsum("rbkgh,rpkh->rkgbp", queries, cache_keys, preferred_element_type=jnp.float32)
        * score_scale
    )
    valid_keys = jnp.arange(prefix_len, dtype=jnp.int32)[None, :] < prefix_lengths[:, None]
    prefix_scores = jnp.where(valid_keys[:, None, None, None, :], prefix_scores, -jnp.inf)
    block_scores = (
        jnp.einsum("rbkgh,rckh->rkgbc", queries, block_keys, preferred_element_type=jnp.float32)
        * score_scale
    )
    score_top = jnp.maximum(jnp.max(prefix_scores, axis=-1), jnp.max(block_scores, axis=-1))[
        ..., None
    ]
    prefix_exp = jnp.exp(prefix_scores - score_top)
    block_exp = jnp.exp(block_scores - score_top)
    denom_sum = (jnp.sum(prefix_exp, axis=-1) + jnp.sum(block_exp, axis=-1))[..., None]
    prefix_probs = (prefix_exp / denom_sum).astype(jnp.bfloat16)
    block_probs = (block_exp / denom_sum).astype(jnp.bfloat16)
    attended = jnp.einsum(
        "rkgbp,rpkh->rbkgh", prefix_probs, cache_values, preferred_element_type=jnp.float32
    )
    attended = attended + jnp.einsum(
        "rkgbc,rckh->rbkgh", block_probs, block_values, preferred_element_type=jnp.float32
    )
    row_count = attended.shape[0]
    block_len = attended.shape[1]
    return attended.astype(jnp.bfloat16).reshape(row_count, block_len, -1)


def on_device(
    learner_inputs,
    learner_cotangent,
    master_weight,
    first_moment,
    second_moment,
    query_weight,
    keyval_weight,
    prefix_cache,
    block_states,
    norm_gain,
    mask_vector,
    prefix_lengths,
    position_picks,
):
    width = query_weight.shape[0]
    grad_term = contract_tokens(
        learner_inputs, lax.all_gather(learner_cotangent, "tensor", axis=1, tiled=True)
    )
    gradient = lax.psum_scatter(grad_term, ("role", "dp"), scatter_dimension=1, tiled=True)
    new_weight, new_first, new_second = adam_update(
        gradient, master_weight, first_moment, second_moment
    )
    layer_rows = lax.all_gather(new_weight.astype(jnp.bfloat16), ("role", "dp"), axis=1, tiled=True)
    row_count, block_len, part_width = block_states.shape
    prefix_len = prefix_cache.shape[1]
    out_scale = (HEADS * HEAD) ** (-0.5)
    pair_cols = keyval_weight.shape[1]
    local_heads = max(pair_cols // (2 * HEAD), 1)
    query_heads = query_weight.shape[1] // HEAD
    group_size = query_heads // local_heads
    even_side = lax.axis_index("tensor") % 2 == 0
    feature_start = lax.axis_index("tensor") * part_width
    mask_part = lax.dynamic_slice_in_dim(mask_vector, feature_start, part_width, 0)
    cache_other = partner(prefix_cache, "tensor", 0)
    cache_pair = jnp.where(
        even_side,
        jnp.stack([prefix_cache, cache_other], 2),
        jnp.stack([cache_other, prefix_cache], 2),
    )
    cache_pair = cache_pair.reshape(row_count, prefix_len, 1, 2, HEAD)
    cache_keys = cache_pair[:, :, :, 0]
    cache_values = cache_pair[:, :, :, 1]
    current_state = block_states
    for step_index in range(STEPS):
        full_state = lax.all_gather(current_state, "tensor", axis=2, tiled=True)
        normed = normalize(full_state, norm_gain)
        layer_flat_normed = normed.reshape(row_count * block_len, width)
        queries = jnp.dot(
            layer_flat_normed, query_weight, preferred_element_type=jnp.float32
        ).astype(jnp.bfloat16)
        queries = queries.reshape(row_count, block_len, local_heads, group_size, HEAD)
        own_half = jnp.dot(
            layer_flat_normed, keyval_weight, preferred_element_type=jnp.float32
        ).astype(jnp.bfloat16)
        own_half = own_half.reshape(row_count, block_len, 1, 1, HEAD)
        other_half = partner(own_half, "tensor", 0)
        block_pairs = jnp.where(
            even_side,
            jnp.concatenate([own_half, other_half], 3),
            jnp.concatenate([other_half, own_half], 3),
        )
        attended = attend(
            queries,
            cache_keys,
            cache_values,
            block_pairs[:, :, :, 0],
            block_pairs[:, :, :, 1],
            prefix_lengths,
        )
        partial_terms = jnp.dot(
            attended.reshape(row_count * block_len, -1),
            layer_rows,
            preferred_element_type=jnp.float32,
        )
        state_shard = lax.psum_scatter(
            partial_terms.reshape(row_count, block_len, width) * out_scale,
            "tensor",
            scatter_dimension=2,
            tiled=True,
        )
        current_state = revise(current_state, state_shard, position_picks[step_index], mask_part)
    return (current_state, new_weight, new_first, new_second)


def solution(mesh):
    placed = (
        P(("role", "dp"), "tensor"),
        P(("role", "dp"), "tensor"),
        P("tensor", ("role", "dp")),
        P("tensor", ("role", "dp")),
        P("tensor", ("role", "dp")),
        P(None, "tensor"),
        P(None, "tensor"),
        P(("role", "dp"), None, "tensor"),
        P(("role", "dp"), None, "tensor"),
        P(),
        P(),
        P(("role", "dp")),
        P(None, ("role", "dp"), None),
    )
    return jax.shard_map(
        on_device,
        mesh=mesh,
        in_specs=placed,
        out_specs=(
            P(("role", "dp"), None, "tensor"),
            P("tensor", ("role", "dp")),
            P("tensor", ("role", "dp")),
            P("tensor", ("role", "dp")),
        ),
        check_vma=False,
    )
```

profile of v0, /device:TPU:16, one launch (start us, length us, event | category | flops | bytes accessed | tf_op | source)
XLA Modules:
  0.0 723.7 jit_solution(7629123382683742764)
XLA Ops:
  8.0 69.1 %all-gather.7.cloned.1.call-done = bf16[1024,5120]{0,1:T(8,128)(2,1)} async-done(((bf16[1024,320]{0,1:T(8,128)(2,1)}), bf16[1024,5120]{0,1:T(8,128)(2,1)}) %all-gather.7.cloned.1.call-update) | async-done | bytes 10485776 | tf_op jit(solution)/shard_map/all_gather | solution.py:111
  77.1 10.9 %fusion.47 = f32[512,5120]{0,1:T(8,128)} fusion(bf16[1024,5120]{0,1:T(8,128)(2,1)} %all-gather.7.cloned.1.call-done, bf16[1024,512]{1,0:T(8,128)(2,1)} %param.13), kind=kOutput, calls=%fused_computation.94 | convolution fusion | flops 5368709120 | bytes 22020096 | tf_op jit(solution)/shard_map/dot_general | solution.py:31
  89.9 235.4 %reduce-scatter.8.cloned.1.call-done = f32[512,320]{0,1:T(8,128)} async-done(((f32[512,5120]{0,1:T(8,128)}), f32[512,320]{0,1:T(8,128)}) %reduce-scatter.8.cloned.1.call-update) | async-done | bytes 655376 | tf_op jit(solution)/shard_map/reduce_scatter | solution.py:113
  325.4 2.8 fusion.41
  328.5 2.0 collective-permute-done
  330.5 2.4 maximum_select_fusion
  332.9 36.3 %all-gather.5.cloned.1.call-done = bf16[4,32,5120]{1,0,2:T(4,128)(2,1)} async-done(((bf16[4,32,320]{1,0,2:T(4,128)(2,1)}), bf16[4,32,5120]{1,0,2:T(4,128)(2,1)}) %all-gather.5.cloned.1.call-update) | async-done | bytes 1310736 | tf_op jit(solution)/shard_map/all_gather | solution.py:139
  369.2 6.0 copy.42
  376.3 1.7 fusion.4
  378.0 3.3 convolution_convert_fusion.1
  384.8 92.8 %all-gather.9.cloned.1.call-done = bf16[512,5120]{0,1:T(8,128)(2,1)} async-done(((bf16[512,320]{0,1:T(8,128)(2,1)}), bf16[512,5120]{0,1:T(8,128)(2,1)}) %all-gather.9.cloned.1.call-update) | async-done | bytes 5242896 | tf_op jit(solution)/shard_map/all_gather | solution.py:117
  477.6 5.8 convolution_multiply_fusion.1
  483.4 8.4 %copy.61 = f32[4,32,5120]{1,0,2:T(4,128)} copy(f32[4,32,5120]{2,1,0:T(8,128)} %convolution_multiply_fusion.1) | data formatting | bytes 5242880
  491.8 8.9 %reshape.433 = f32[5120,128]{1,0:T(8,128)} reshape(f32[5120,4,32]{2,1,0:T(4,128)} %bitcast.135) | data formatting | bytes 5242880
  501.6 65.4 %reduce-scatter.10.cloned.1.call-done = f32[320,128]{1,0:T(8,128)} async-done(((f32[5120,128]{1,0:T(8,128)}), f32[320,128]{1,0:T(8,128)}) %reduce-scatter.10.cloned.1.call-update) | async-done | bytes 163856
  567.0 1.2 reshape.434
  569.8 40.5 %all-gather.11.cloned.1.call-done = bf16[4,32,5120]{1,0,2:T(4,128)(2,1)} async-done(((bf16[4,32,320]{1,0,2:T(4,128)(2,1)}), bf16[4,32,5120]{1,0,2:T(4,128)(2,1)}) %all-gather.11.cloned.1.call-update) | async-done | bytes 1310736 | tf_op jit(solution)/shard_map/all_gather | solution.py:139
  610.3 6.0 copy.48
  617.6 3.5 convolution_convert_fusion
  624.0 5.8 convolution_multiply_fusion
  629.8 8.4 %copy.63 = f32[4,32,5120]{1,0,2:T(4,128)} copy(f32[4,32,5120]{2,1,0:T(8,128)} %convolution_multiply_fusion) | data formatting | bytes 5242880
  638.2 8.9 %reshape.435 = f32[5120,128]{1,0:T(8,128)} reshape(f32[5120,4,32]{2,1,0:T(4,128)} %bitcast.136) | data formatting | bytes 5242880
  647.2 67.5 %reduce-scatter.12.cloned.1.call-done = f32[320,128]{1,0:T(8,128)} async-done(((f32[5120,128]{1,0:T(8,128)}), f32[320,128]{1,0:T(8,128)}) %reduce-scatter.12.cloned.1.call-update) | async-done | bytes 163856
  714.6 1.2 reshape.436
  (81 shorter events, 14.8 us)
Async XLA Ops:
  7.2 374.2 %copy-start = (bf16[5120,128]{1,0:T(8,128)(2,1)S(1)}, bf16[5120,128]{1,0:T(8,128)(2,1)}, u32[]{:S(2)}) copy-start(bf16[5120,128]{1,0:T(8,128)(2,1)} %param.19) | copy-start | bytes 3932164
  7.2 69.9 %all-gather.7.cloned.1.call-start = ((), (), s32[]{:S(2)}) async-start(), calls=%async_computation.4 | async-start | bytes 11141120 | tf_op jit(solution)/shard_map/all_gather | solution.py:111
  7.9 317.5 %reduce-scatter.8.cloned.1.call-start = ((), (), s32[]{:S(2)}) async-start(), calls=%async_computation.5 | async-start | bytes 11141120 | tf_op jit(solution)/shard_map/reduce_scatter | solution.py:113
  88.0 0.9 copy-start.7
  88.0 237.4 %copy-start.4 = (f32[512,320]{0,1:T(8,128)S(1)}, f32[512,320]{0,1:T(8,128)}, u32[]{:S(2)}) copy-start(f32[512,320]{0,1:T(8,128)} %param.15) | copy-start | bytes 1966084
  88.0 237.4 %copy-start.5 = (f32[512,320]{0,1:T(8,128)S(1)}, f32[512,320]{0,1:T(8,128)}, u32[]{:S(2)}) copy-start(f32[512,320]{0,1:T(8,128)} %param.16) | copy-start | bytes 1966084
  88.0 237.4 %copy-start.6 = (f32[512,320]{0,1:T(8,128)S(1)}, f32[512,320]{0,1:T(8,128)}, u32[]{:S(2)}) copy-start(f32[512,320]{0,1:T(8,128)} %param.17) | copy-start | bytes 1966084
  88.1 281.1 %all-gather.5.cloned.1.call-start = ((), (), s32[]{:S(2)}) async-start(), calls=%async_computation.3 | async-start | bytes 5570560 | tf_op jit(solution)/shard_map/all_gather | solution.py:139
  89.9 238.5 %copy-start.10 = (s32[4]{0:T(128)S(1)}, s32[4]{0:T(128)}, u32[]{:S(2)}) copy-start(s32[4]{0:T(128)} %param.24) | copy-start | bytes 52
  89.9 387.7 %all-gather.9.cloned.1.call-start = ((), (), s32[]{:S(2)}) async-start(), calls=%async_computation.6 | async-start | bytes 5570560 | tf_op jit(solution)/shard_map/all_gather | solution.py:117
  328.2 238.7 %reduce-scatter.10.cloned.1.call-start = ((), (), s32[]{:S(2)}) async-start(), calls=%async_computation.8 | async-start | bytes 2785280
  328.3 2.2 collective-permute-start
  332.9 43.4 %copy-start.8 = (f32[5120]{0:T(1024)S(1)}, f32[5120]{0:T(1024)}, u32[]{:S(2)}) copy-start(f32[5120]{0:T(1024)} %param.22) | copy-start | bytes 61444
  375.2 1.1 copy-start.1
  381.4 1.2 copy-start.2
  381.9 1.3 collective-permute-start.1
  500.7 0.9 copy-start.9
  500.7 109.5 %all-gather.11.cloned.1.call-start = ((), (), s32[]{:S(2)}) async-start(), calls=%async_computation.7 | async-start | bytes 5570560 | tf_op jit(solution)/shard_map/all_gather | solution.py:139
  569.5 145.1 %reduce-scatter.12.cloned.1.call-start = ((), (), s32[]{:S(2)}) async-start(), calls=%async_computation.9 | async-start | bytes 2785280
  617.6 3.9 copy-start.3
  621.1 1.3 collective-permute-start.2
Sparse Core Ops, SparseCore 0:
  9.9 67.1 all-gather.6
  88.2 237.1 reduce-scatter.7
  327.4 41.7 all-gather.4
  372.0 105.5 all-gather.8
  500.8 66.0 reduce-scatter.9
  569.7 40.5 all-gather.10
  647.3 67.3 reduce-scatter.11
where the time goes:
time: 725 us; the launch traced here: 724 us
  waiting for transfers between devices  611 us (84%)
  local copies, waits for them, and re-layouts  54.6 us (8%)
  matrix products  33.1 us (5%)
  between operations  14.4 us (2%)
  other arithmetic  9.83 us (1%)
    reduce_scatter x1, waiting for transfers between devices, on_device(): lax.psum_scatter(grad_term, ('role', 'dp'), scatter_dimension=1, tiled=True)  235 us
    unnamed x9, waiting for transfers between devices  134 us
    all_gather x1, waiting for transfers between devices, on_device(): lax.all_gather(new_weight.astype(jnp.bfloat16), ('role', 'dp'), axis=1, t...  92.8 us
    all_gather x2, waiting for transfers between devices, on_device(): full_state = lax.all_gather(current_state, 'tensor', axis=2, tiled=True)  76.8 us
    all_gather x1, waiting for transfers between devices, on_device(): lax.all_gather(learner_cotangent, 'tensor', axis=1, tiled=True)  69.1 us
    unnamed x31, local copies, waits for them, and re-layouts  40.5 us
  transfers between devices with their start and end apart: 10, of which 10 were waited for; matrix products, arithmetic and copies ran while one was open for 3% of the time, Pallas kernels for 0%

commit v1 on v0

v1 whole, which is shorter than its diff:
```python
import jax
import jax.numpy as jnp
from jax import lax
from jax.sharding import Mesh, PartitionSpec as P

HEADS = 64
HEAD = 128
STEPS = 2

BETA_ONE = 0.9
BETA_TWO = 0.95
ADAM_EPS = 1e-08
LEARN_RATE = 0.5
DECAY_RATE = 0.1
STEP_COUNT = 50
NORM_EPS = 1e-06

RD = ("role", "dp")
TENSOR = ("x", "y", "core")
EVERY = RD + TENSOR


def rotate(block, axis, shift):
    count = lax.axis_size(axis)
    return lax.ppermute(block, axis, [(low, (low + shift) % count) for low in range(count)])


def pick(blocks, index):
    return lax.dynamic_index_in_dim(blocks, index, 0, keepdims=False)


def pair_order(own, other, index, axis):
    return jnp.where(index == 0, jnp.stack([own, other], axis), jnp.stack([other, own], axis))


def adam_update(gradient, master_weight, first_moment, second_moment):
    first_new = BETA_ONE * first_moment + (1.0 - BETA_ONE) * gradient
    second_new = BETA_TWO * second_moment + (1.0 - BETA_TWO) * gradient * gradient
    first_hat = first_new / (1.0 - BETA_ONE**STEP_COUNT)
    second_hat = second_new / (1.0 - BETA_TWO**STEP_COUNT)
    weight_new = master_weight - LEARN_RATE * (
        first_hat / (jnp.sqrt(second_hat) + ADAM_EPS) + DECAY_RATE * master_weight
    )
    return (weight_new, first_new, second_new)


def gather_features(part):
    iy, ix, ic = lax.axis_index("y"), lax.axis_index("x"), lax.axis_index("core")
    rows = pair_order(part, rotate(part, "y", 1), iy, 0)
    ahead, back, across = rotate(rows, "x", 1), rotate(rows, "x", -1), rotate(rows, "x", 2)
    square = jnp.zeros((4,) + rows.shape, rows.dtype)
    square = lax.dynamic_update_index_in_dim(square, rows, ix, 0)
    square = lax.dynamic_update_index_in_dim(square, ahead, (ix + 3) % 4, 0)
    square = lax.dynamic_update_index_in_dim(square, back, (ix + 1) % 4, 0)
    square = lax.dynamic_update_index_in_dim(square, across, (ix + 2) % 4, 0)
    whole = pair_order(square, rotate(square, "core", 1), ic, 2)
    return whole.reshape(-1, part.shape[-1])


def scatter_sum(parts):
    iy, ix, ic = lax.axis_index("y"), lax.axis_index("x"), lax.axis_index("core")
    bf16, f32 = jnp.bfloat16, jnp.float32
    away = lax.dynamic_index_in_dim(parts, 1 - ic, 2, keepdims=False).astype(bf16)
    near = lax.dynamic_index_in_dim(parts, ic, 2, keepdims=False)
    sums = near + rotate(away, "core", 1).astype(f32)
    sent = sums.astype(bf16)
    ahead = rotate(pick(sent, (ix + 1) % 4), "x", 1)
    back = rotate(pick(sent, (ix + 3) % 4), "x", -1)
    across = rotate(pick(sent, (ix + 2) % 4), "x", 2)
    sums = pick(sums, ix) + ahead.astype(f32) + back.astype(f32) + across.astype(f32)
    return pick(sums, iy) + rotate(pick(sums, 1 - iy).astype(bf16), "y", 1).astype(f32)


def normalize(state, norm_gain):
    values = state.astype(jnp.float32)
    mean_square = jnp.mean(values * values, axis=0, keepdims=True)
    return (values * lax.rsqrt(mean_square + NORM_EPS) * norm_gain[:, None]).astype(jnp.bfloat16)


def revise(current_state, update, pick_codes, mask_values):
    values = current_state.astype(jnp.float32)
    masked = jnp.broadcast_to(mask_values.astype(jnp.float32)[:, None], values.shape)
    return jnp.where(
        pick_codes == 1, values + update, jnp.where(pick_codes == 2, masked, values)
    ).astype(jnp.bfloat16)


def attend(queries, cache_keys, cache_values, block_keys, block_values, prefix_lengths):
    score_scale = HEAD ** (-0.5)
    prefix_len = cache_keys.shape[1]
    prefix_scores = (
        jnp.einsum("rbgh,rph->rgbp", queries, cache_keys, preferred_element_type=jnp.float32)
        * score_scale
    )
    valid_keys = jnp.arange(prefix_len, dtype=jnp.int32)[None, :] < prefix_lengths[:, None]
    prefix_scores = jnp.where(valid_keys[:, None, None, :], prefix_scores, -jnp.inf)
    block_scores = (
        jnp.einsum("rbgh,rch->rgbc", queries, block_keys, preferred_element_type=jnp.float32)
        * score_scale
    )
    score_top = jnp.maximum(jnp.max(prefix_scores, axis=-1), jnp.max(block_scores, axis=-1))[
        ..., None
    ]
    prefix_exp = jnp.exp(prefix_scores - score_top)
    block_exp = jnp.exp(block_scores - score_top)
    denom_sum = (jnp.sum(prefix_exp, axis=-1) + jnp.sum(block_exp, axis=-1))[..., None]
    prefix_probs = (prefix_exp / denom_sum).astype(jnp.bfloat16)
    block_probs = (block_exp / denom_sum).astype(jnp.bfloat16)
    attended = jnp.einsum(
        "rgbp,rph->rbgh", prefix_probs, cache_values, preferred_element_type=jnp.float32
    )
    attended = attended + jnp.einsum(
        "rgbc,rch->rbgh", block_probs, block_values, preferred_element_type=jnp.float32
    )
    return attended.astype(jnp.bfloat16).reshape(queries.shape[0] * queries.shape[1], -1)


def on_device(
    learner_inputs,
    learner_cotangent,
    master_weight,
    first_moment,
    second_moment,
    query_weight,
    keyval_weight,
    prefix_cache,
    block_states,
    norm_gain,
    mask_vector,
    prefix_lengths,
    position_picks,
):
    bf16, f32 = jnp.bfloat16, jnp.float32
    role, core = lax.axis_index("role"), lax.axis_index("core")
    rows, block_len, part = block_states.shape
    tokens = rows * block_len
    depth = learner_inputs.shape[1]
    out_scale = (HEADS * HEAD) ** (-0.5)

    cache_other = rotate(prefix_cache, "core", 1)
    cache_keys = jnp.where(core == 0, prefix_cache, cache_other)
    cache_values = jnp.where(core == 0, cache_other, prefix_cache)
    mask_part = lax.dynamic_slice_in_dim(mask_vector, lax.axis_index(TENSOR) * part, part, 0)

    def attended_of(state):
        normed = normalize(gather_features(state), norm_gain)
        own_half = lax.dot_general(
            normed, keyval_weight, (((0,), (0,)), ((), ())), preferred_element_type=f32
        ).astype(bf16)
        other_half = rotate(own_half, "core", 1)
        queries = lax.dot_general(
            normed, query_weight, (((0,), (0,)), ((), ())), preferred_element_type=f32
        ).astype(bf16)
        block_keys = jnp.where(core == 0, own_half, other_half).reshape(rows, block_len, HEAD)
        block_values = jnp.where(core == 0, other_half, own_half).reshape(rows, block_len, HEAD)
        return attend(
            queries.reshape(rows, block_len, -1, HEAD),
            cache_keys,
            cache_values,
            block_keys,
            block_values,
            prefix_lengths,
        )

    state = block_states.reshape(tokens, part).T
    attended = attended_of(state)
    both = pair_order(attended, rotate(attended, "role", 1), role, 0)
    attended_all = lax.all_gather(both, "dp", axis=0)

    cotangent = lax.all_gather(learner_cotangent, TENSOR, axis=1, tiled=True)
    terms = lax.dot_general(
        cotangent, learner_inputs, (((0,), (0,)), ((), ())), preferred_element_type=f32
    ).astype(bf16)
    terms = terms.reshape(2, 8, part, depth).transpose(1, 0, 2, 3)
    halves = lax.psum_scatter(terms, "dp", scatter_dimension=0, tiled=False)
    gradient = pick(halves, role).astype(f32) + rotate(pick(halves, 1 - role), "role", 1).astype(f32)
    new_weight, new_first, new_second = adam_update(
        gradient, master_weight.T, first_moment.T, second_moment.T
    )
    weight_part = new_weight.astype(bf16)

    weight_both = pair_order(weight_part, rotate(weight_part, "role", 1), role, 0)
    weight_all = lax.all_gather(weight_both, "dp", axis=0)

    partial = jnp.einsum("ck,drtk->rdct", weight_part, attended_all, preferred_element_type=f32)
    update = scatter_sum(partial.reshape(4, 2, 2, part, tokens))
    swap = [(a * 16 + b, b * 16 + a) for a in range(16) for b in range(16)]
    update = lax.ppermute(update.astype(bf16), EVERY, swap).astype(f32) * out_scale
    picks = position_picks.reshape(STEPS, 1, tokens)
    state = revise(state, update, picks[0], mask_part)

    attended = attended_of(state)
    partial = jnp.einsum("drck,tk->rdct", weight_all, attended, preferred_element_type=f32)
    update = scatter_sum(partial.reshape(4, 2, 2, part, tokens)) * out_scale
    state = revise(state, update, picks[1], mask_part)
    return (state.T.reshape(rows, block_len, part), new_weight.T, new_first.T, new_second.T)


def solution(mesh):
    fine = Mesh(mesh.devices.reshape(2, 8, 4, 2, 2), EVERY)
    weights = P(TENSOR, RD)
    return jax.shard_map(
        on_device,
        mesh=fine,
        in_specs=(
            P(RD, TENSOR),
            P(RD, TENSOR),
            weights,
            weights,
            weights,
            P(None, TENSOR),
            P(None, TENSOR),
            P(RD, None, TENSOR),
            P(RD, None, TENSOR),
            P(),
            P(),
            P(RD),
            P(None, RD, None),
        ),
        out_specs=(P(RD, None, TENSOR), weights, weights, weights),
        check_vma=False,
    )
```

time: 725 us -> 321 us (0.44)
  waiting for transfers between devices: 611 us -> 198 us
  starting transfers between devices: 1.2 us -> 42.6 us
  local copies, waits for them, and re-layouts: 54.6 us -> 15.9 us
  other arithmetic: 9.83 us -> 20 us
  matrix products: 33.1 us -> 24.3 us
    reduce_scatter x1, waiting for transfers between devices: 235 us -> 23.8 us  [on_device(): halves = lax.psum_scatter(terms, 'dp', scatter_dimension=0, tiled=False)]
    all_gather x4 -> x3, waiting for transfers between devices: 239 us -> 84.6 us  [the longest x1 69.1 us: on_device(): cotangent = lax.all_gather(learner_cotangent, TENSOR, axis=1, tiled=True)]
    unnamed x9 -> x4, waiting for transfers between devices: 134 us -> 0.73 us
    ppermute x3 -> x27, waiting for transfers between devices: 2.79 us -> 88.9 us  [the longest x26 81.2 us: rotate(): lax.ppermute(block, axis, [(low, (low + shift) % count) for low in range(...]
    ppermute x3 -> x27, starting transfers between devices: 0.73 us -> 42.4 us  [the longest x26 39.7 us: rotate(): lax.ppermute(block, axis, [(low, (low + shift) % count) for low in range(...]
    unnamed x31, local copies, waits for them, and re-layouts: 40.5 us -> 3.74 us
    all_gather x2 -> x0, local copies, waits for them, and re-layouts: 12.1 us -> none  [on_device(): full_state = lax.all_gather(current_state, 'tensor', axis=2, tiled=True)]
    dot_general x15, matrix products: 33.1 us -> 24.3 us  [the longest x1 8.58 us: on_device(): lax.dot_general(cotangent, learner_inputs, (((0,), (0,)), ((), ())), pref...]
  transfers between devices with their start and end apart: 10 -> 31, of which waited for: 10 -> 27; matrix products, arithmetic and copies ran while one was open for 3% -> 12% of each run, Pallas kernels for 0% -> 0%
where the time goes in v1:
time: 321 us; the launch traced here: 315 us
  waiting for transfers between devices  198 us (62%)
  starting transfers between devices  42.6 us (13%)
  matrix products  24.3 us (8%)
  other arithmetic  20 us (6%)
  local copies, waits for them, and re-layouts  15.9 us (5%)
  between operations  14.7 us (5%)
    ppermute x26, waiting for transfers between devices, rotate(): lax.ppermute(block, axis, [(low, (low + shift) % count) for low in range(...  81.2 us
    all_gather x1, waiting for transfers between devices, on_device(): cotangent = lax.all_gather(learner_cotangent, TENSOR, axis=1, tiled=True)  69.1 us
    ppermute x26, starting transfers between devices, rotate(): lax.ppermute(block, axis, [(low, (low + shift) % count) for low in range(...  39.7 us
    reduce_scatter x1, waiting for transfers between devices, on_device(): halves = lax.psum_scatter(terms, 'dp', scatter_dimension=0, tiled=False)  23.8 us
    all_gather x1, waiting for transfers between devices, on_device(): attended_all = lax.all_gather(both, 'dp', axis=0)  15.4 us
    dot_general x1, matrix products, on_device(): lax.dot_general(cotangent, learner_inputs, (((0,), (0,)), ((), ())), pref...  8.58 us
    ppermute x1, waiting for transfers between devices, on_device(): lax.ppermute(update.astype(bf16), EVERY, swap).astype(f32) * out_scale  7.69 us
  transfers between devices with their start and end apart: 31, of which 27 were waited for; matrix products, arithmetic and copies ran while one was open for 12% of the time, Pallas kernels for 0%

profile of v1, /device:TPU:16, one launch (start us, length us, event | category | flops | bytes accessed | tf_op | source)
XLA Modules:
  0.0 315.4 jit_solution(9293559067528451726)
XLA Ops:
  8.0 69.1 %all-gather.6.cloned.1.call-done = bf16[1024,5120]{0,1:T(8,128)(2,1)} async-done(((bf16[1024,320]{0,1:T(8,128)(2,1)}), bf16[1024,5120]{0,1:T(8,128)(2,1)}) %all-gather.6.cloned.1.call-update) | async-done | bytes 10485776 | tf_op jit(solution)/shard_map/all_gather | solution.py:170
  77.1 8.6 %convolution_convert_fusion = bf16[5120,512]{1,0:T(8,128)(2,1)S(1)} fusion(bf16[1024,5120]{0,1:T(8,128)(2,1)} %all-gather.6.cloned.1.call-done, bf16[1024,512]{1,0:T(8,128)(2,1)} %param.13), kind=kOutput, calls=%fused_computation | convolution fusion | flops 5371330560 | bytes 16777216 | tf_op jit(solution)/shard_map/dot_general | solution.py:171
  85.7 2.9 copy.129
  90.7 3.6 %collective-permute-done.1 = bf16[320,128]{0,1:T(8,128)(2,1)S(1)} collective-permute-done((bf16[320,128]{0,1:T(8,128)(2,1)S(1)}, bf16[320,128]{0,1:T(8,128)(2,1)S(1)}, u32[]{:S(2)}, u32[]{:S(2)}) %collective-permute-start.1) | collective-permute-done | bytes 81952 | tf_op jit(solution)/shard_map/ppermute | solution.py:25
  94.5 2.8 collective-permute-start.4
  99.6 4.2 %collective-permute-done.4 = bf16[2,320,128]{1,2,0:T(8,128)(2,1)S(1)} collective-permute-done((bf16[2,320,128]{1,2,0:T(8,128)(2,1)S(1)}, bf16[2,320,128]{1,2,0:T(8,128)(2,1)S(1)}, u32[]{:S(2)}, u32[]{:S(2)}) %collective-permute-start.4) | collective-permute-done | bytes 163872 | tf_op jit(solution)/shard_map/ppermute | solution.py:25
  124.3 6.0 %collective-permute-done.7 = bf16[128,512]{1,0:T(8,128)(2,1)S(1)} collective-permute-done((bf16[128,512]{1,0:T(8,128)(2,1)S(1)}, bf16[128,512]{1,0:T(8,128)(2,1)S(1)}, u32[]{:S(2)}, u32[]{:S(2)}) %collective-permute-start.7) | collective-permute-done | bytes 131104 | tf_op jit(solution)/shard_map/ppermute | solution.py:25
  131.1 23.8 %reduce-scatter.2.cloned.1.call-done = bf16[1,2,320,512]{3,2,1,0:T(8,128)(2,1)} async-done(((bf16[8,2,320,512]{3,2,1,0:T(8,128)(2,1)}), bf16[1,2,320,512]{3,2,1,0:T(8,128)(2,1)}) %reduce-scatter.2.cloned.1.call-update) | async-done | bytes 655376 | tf_op jit(solution)/shard_map/reduce_scatter | solution.py:175
  156.5 10.5 %collective-permute-done.8 = bf16[320,512]{1,0:T(8,128)(2,1)S(1)} collective-permute-done((bf16[320,512]{1,0:T(8,128)(2,1)S(1)}, bf16[320,512]{1,0:T(8,128)(2,1)S(1)}, u32[]{:S(2)}, u32[]{:S(2)}) %collective-permute-start.8) | collective-permute-done | bytes 327712 | tf_op jit(solution)/shard_map/ppermute | solution.py:25
  167.0 2.8 fusion.53
  170.4 9.7 %collective-permute-done.21 = bf16[320,512]{1,0:T(8,128)(2,1)S(1)} collective-permute-done((bf16[320,512]{1,0:T(8,128)(2,1)S(1)}, bf16[320,512]{1,0:T(8,128)(2,1)S(1)}, u32[]{:S(2)}, u32[]{:S(2)}) %collective-permute-start.21) | collective-permute-done | bytes 327712 | tf_op jit(solution)/shard_map/ppermute | solution.py:25
  181.1 15.4 %all-gather.4.cloned.1.call-done = bf16[8,2,128,512]{3,2,1,0:T(8,128)(2,1)} async-done(((bf16[1,2,128,512]{3,2,1,0:T(8,128)(2,1)}), bf16[8,2,128,512]{3,2,1,0:T(8,128)(2,1)}) %all-gather.4.cloned.1.call-update) | async-done | bytes 2097168 | tf_op jit(solution)/shard_map/all_gather | solution.py:168
  206.8 2.7 collective-permute-start.11
  211.4 7.1 %collective-permute-done.11 = bf16[2,320,128]{1,2,0:T(8,128)(2,1)} collective-permute-done((bf16[2,320,128]{1,2,0:T(8,128)(2,1)}, bf16[2,320,128]{1,2,0:T(8,128)(2,1)}, u32[]{:S(2)}, u32[]{:S(2)}) %collective-permute-start.11) | collective-permute-done | bytes 163872 | tf_op jit(solution)/shard_map/ppermute | solution.py:25
  219.2 3.0 collective-permute-done.10
  224.7 3.5 %collective-permute-done.13 = bf16[320,128]{0,1:T(8,128)(2,1)S(1)} collective-permute-done((bf16[320,128]{0,1:T(8,128)(2,1)S(1)}, bf16[320,128]{0,1:T(8,128)(2,1)S(1)}, u32[]{:S(2)}, u32[]{:S(2)}) %collective-permute-start.13) | collective-permute-done | bytes 81952 | tf_op jit(solution)/shard_map/ppermute | solution.py:25
  228.3 2.7 collective-permute-start.14
  231.9 7.7 %collective-permute-done.14 = bf16[320,128]{0,1:T(8,128)(2,1)S(1)} collective-permute-done((bf16[320,128]{0,1:T(8,128)(2,1)S(1)}, bf16[320,128]{0,1:T(8,128)(2,1)S(1)}, u32[]{:S(2)}, u32[]{:S(2)}) %collective-permute-start.14) | collective-permute-done | bytes 81952 | tf_op jit(solution)/shard_map/ppermute | solution.py:188
  239.7 8.5 %collective-permute-start.15 = (bf16[320,128]{0,1:T(8,128)(2,1)S(1)}, bf16[320,128]{0,1:T(8,128)(2,1)S(1)}, u32[]{:S(2)}, u32[]{:S(2)}) collective-permute-start(bf16[320,128]{0,1:T(8,128)(2,1)S(1)} %fusion.35), channel_id=1, source_target_pairs={{0,2},{2,0},{1,3},{3,1},{4,6},{6,4},{5,7},{7,5},{8,10},{10,8},{9,1... | collective-permute-start | bytes 245768 | tf_op jit(solution)/shard_map/ppermute | solution.py:25
  248.2 2.6 collective-permute-done.15
  251.1 11.0 %collective-permute-start.16 = (bf16[2,320,128]{1,2,0:T(8,128)(2,1)S(1)}, bf16[2,320,128]{1,2,0:T(8,128)(2,1)S(1)}, u32[]{:S(2)}, u32[]{:S(2)}) collective-permute-start(bf16[2,320,128]{1,2,0:T(8,128)(2,1)S(1)} %maximum_select_fusion.7), channel_id=1, source_target_pairs={{0,4},{4,8},{8,12},{12,0},{1,5},{5,9},{9,13},{13,1},{2,6},{6,10},{... | collective-permute-start | bytes 491528 | tf_op jit(solution)/shard_map/ppermute | solution.py:25
  262.8 4.9 %collective-permute-done.16 = bf16[2,320,128]{1,2,0:T(8,128)(2,1)S(1)} collective-permute-done((bf16[2,320,128]{1,2,0:T(8,128)(2,1)S(1)}, bf16[2,320,128]{1,2,0:T(8,128)(2,1)S(1)}, u32[]{:S(2)}, u32[]{:S(2)}) %collective-permute-start.16) | collective-permute-done | bytes 163872 | tf_op jit(solution)/shard_map/ppermute | solution.py:25
  279.1 4.0 %convolution_bitcast_fusion = f32[2,8,320,128]{3,2,0,1:T(8,128)S(1)} fusion(bf16[8,2,320,512]{3,2,1,0:T(8,128)(2,1)} %all-gather.8.cloned.1.call-done, bf16[128,512,1,1]{1,0,2,3:T(8,128)(2,1)S(1)} %reshape.426), kind=kOutput, calls=%fused_computation.10 | convolution fusion | flops 671088640 | bytes 7995392 | tf_op jit(solution)/shard_map/drck,tk->rdct/dot_general | solution.py:193
  290.8 8.0 %collective-permute-done.24 = bf16[2,320,128]{1,2,0:T(8,128)(2,1)} collective-permute-done((bf16[2,320,128]{1,2,0:T(8,128)(2,1)}, bf16[2,320,128]{1,2,0:T(8,128)(2,1)}, u32[]{:S(2)}, u32[]{:S(2)}) %collective-permute-start.24) | collective-permute-done | bytes 163872 | tf_op jit(solution)/shard_map/ppermute | solution.py:25
  (174 shorter events, 75.5 us)
Async XLA Ops:
  7.2 69.9 %all-gather.6.cloned.1.call-start = ((), (), s32[]{:S(2)}) async-start(), calls=%async_computation.2 | async-start | bytes 11141120 | tf_op jit(solution)/shard_map/all_gather | solution.py:170
  7.9 147.0 %reduce-scatter.2.cloned.1.call-start = ((), (), s32[]{:S(2)}) async-start(), calls=%async_computation.3 | async-start | bytes 5898240 | tf_op jit(solution)/shard_map/reduce_scatter | solution.py:175
  88.6 107.9 %all-gather.4.cloned.1.call-start = ((), (), s32[]{:S(2)}) async-start(), calls=%async_computation.1 | async-start | bytes 2359296 | tf_op jit(solution)/shard_map/all_gather | solution.py:168
  89.4 4.9 %collective-permute-start.1 = (bf16[320,128]{0,1:T(8,128)(2,1)S(1)}, bf16[320,128]{0,1:T(8,128)(2,1)S(1)}, u32[]{:S(2)}, u32[]{:S(2)}) collective-permute-start(bf16[320,128]{0,1:T(8,128)(2,1)S(1)} %bitcast.237), channel_id=1, source_target_pairs={{0,2},{2,0},{1,3},{3,1},{4,6},{6,4},{5,7},{7,5},{8,10},{10,8},{9,1... | collective-permute-start | bytes 245768 | tf_op jit(solution)/shard_map/ppermute | solution.py:25
  94.5 9.4 %collective-permute-start.4 = (bf16[2,320,128]{1,2,0:T(8,128)(2,1)S(1)}, bf16[2,320,128]{1,2,0:T(8,128)(2,1)S(1)}, u32[]{:S(2)}, u32[]{:S(2)}) collective-permute-start(bf16[2,320,128]{1,2,0:T(8,128)(2,1)S(1)} %maximum_select_fusion.5), channel_id=1, source_target_pairs={{0,8},{4,12},{8,0},{12,4},{1,9},{5,13},{9,1},{13,5},{2,10},{6,14},... | collective-permute-start | bytes 491528 | tf_op jit(solution)/shard_map/ppermute | solution.py:25
  97.2 9.0 %collective-permute-start.3 = (bf16[2,320,128]{1,2,0:T(8,128)(2,1)S(1)}, bf16[2,320,128]{1,2,0:T(8,128)(2,1)S(1)}, u32[]{:S(2)}, u32[]{:S(2)}) collective-permute-start(bf16[2,320,128]{1,2,0:T(8,128)(2,1)S(1)} %maximum_select_fusion.5), channel_id=1, source_target_pairs={{0,12},{4,0},{8,4},{12,8},{1,13},{5,1},{9,5},{13,9},{2,14},{6,2},{... | collective-permute-start | bytes 491528 | tf_op jit(solution)/shard_map/ppermute | solution.py:25
  98.7 8.1 %collective-permute-start.2 = (bf16[2,320,128]{1,2,0:T(8,128)(2,1)S(1)}, bf16[2,320,128]{1,2,0:T(8,128)(2,1)S(1)}, u32[]{:S(2)}, u32[]{:S(2)}) collective-permute-start(bf16[2,320,128]{1,2,0:T(8,128)(2,1)S(1)} %maximum_select_fusion.5), channel_id=1, source_target_pairs={{0,4},{4,8},{8,12},{12,0},{1,5},{5,9},{9,13},{13,1},{2,6},{6,10},{... | collective-permute-start | bytes 491528 | tf_op jit(solution)/shard_map/ppermute | solution.py:25
  107.2 12.6 %collective-permute-start = (bf16[4,512,128]{2,1,0:T(8,128)(2,1)}, bf16[4,512,128]{2,1,0:T(8,128)(2,1)}, u32[]{:S(2)}, u32[]{:S(2)}) collective-permute-start(bf16[4,512,128]{2,1,0:T(8,128)(2,1)} %param.20), channel_id=1, source_target_pairs={{0,1},{1,0},{2,3},{3,2},{4,5},{5,4},{6,7},{7,6},{8,9},{9,8},{10,11... | collective-permute-start | bytes 1572872 | tf_op jit(solution)/shard_map/ppermute | solution.py:25
  123.6 6.7 %collective-permute-start.7 = (bf16[128,512]{1,0:T(8,128)(2,1)S(1)}, bf16[128,512]{1,0:T(8,128)(2,1)S(1)}, u32[]{:S(2)}, u32[]{:S(2)}) collective-permute-start(bf16[128,512]{1,0:T(8,128)(2,1)S(1)} %bitcast.257), channel_id=1, source_target_pairs={{0,128},{128,0},{1,129},{129,1},{2,130},{130,2},{3,131},{131,3},{4... | collective-permute-start | bytes 393224 | tf_op jit(solution)/shard_map/ppermute | solution.py:25
  131.1 148.0 %all-gather.8.cloned.1.call-start = ((), (), s32[]{:S(2)}) async-start(), calls=%async_computation.4 | async-start | bytes 5898240 | tf_op jit(solution)/shard_map/all_gather | solution.py:183
  155.9 11.1 %collective-permute-start.8 = (bf16[320,512]{1,0:T(8,128)(2,1)S(1)}, bf16[320,512]{1,0:T(8,128)(2,1)S(1)}, u32[]{:S(2)}, u32[]{:S(2)}) collective-permute-start(bf16[320,512]{1,0:T(8,128)(2,1)S(1)} %dynamic-slice_bitcast_fusion), channel_id=1, source_target_pairs={{0,128},{128,0},{1,129},{129,1},{2,130},{130,2},{3,131},{131,3},{4... | collective-permute-start | bytes 983048 | tf_op jit(solution)/shard_map/ppermute | solution.py:25
  169.9 10.2 %collective-permute-start.21 = (bf16[320,512]{1,0:T(8,128)(2,1)S(1)}, bf16[320,512]{1,0:T(8,128)(2,1)S(1)}, u32[]{:S(2)}, u32[]{:S(2)}) collective-permute-start(bf16[320,512]{1,0:T(8,128)(2,1)S(1)} %get-tuple-element.12), channel_id=1, source_target_pairs={{0,128},{128,0},{1,129},{129,1},{2,130},{130,2},{3,131},{131,3},{4... | collective-permute-start | bytes 983048 | tf_op jit(solution)/shard_map/ppermute | solution.py:25
  206.8 11.7 %collective-permute-start.11 = (bf16[2,320,128]{1,2,0:T(8,128)(2,1)}, bf16[2,320,128]{1,2,0:T(8,128)(2,1)}, u32[]{:S(2)}, u32[]{:S(2)}) collective-permute-start(bf16[2,320,128]{1,2,0:T(8,128)(2,1)} %bitcast.44), channel_id=1, source_target_pairs={{0,12},{4,0},{8,4},{12,8},{1,13},{5,1},{9,5},{13,9},{2,14},{6,2},{... | collective-permute-start | bytes 491528 | tf_op jit(solution)/shard_map/ppermute | solution.py:25
  209.5 9.7 %collective-permute-start.12 = (bf16[2,320,128]{1,2,0:T(8,128)(2,1)}, bf16[2,320,128]{1,2,0:T(8,128)(2,1)}, u32[]{:S(2)}, u32[]{:S(2)}) collective-permute-start(bf16[2,320,128]{1,2,0:T(8,128)(2,1)} %bitcast.247), channel_id=1, source_target_pairs={{0,8},{4,12},{8,0},{12,4},{1,9},{5,13},{9,1},{13,5},{2,10},{6,14},... | collective-permute-start | bytes 491528 | tf_op jit(solution)/shard_map/ppermute | solution.py:25
  210.4 11.9 %collective-permute-start.10 = (bf16[2,320,128]{1,2,0:T(8,128)(2,1)S(1)}, bf16[2,320,128]{1,2,0:T(8,128)(2,1)}, u32[]{:S(2)}, u32[]{:S(2)}) collective-permute-start(bf16[2,320,128]{1,2,0:T(8,128)(2,1)S(1)} %bitcast.246), channel_id=1, source_target_pairs={{0,4},{4,8},{8,12},{12,0},{1,5},{5,9},{9,13},{13,1},{2,6},{6,10},{... | collective-permute-start | bytes 491528 | tf_op jit(solution)/shard_map/ppermute | solution.py:25
  223.4 4.8 %collective-permute-start.13 = (bf16[320,128]{0,1:T(8,128)(2,1)S(1)}, bf16[320,128]{0,1:T(8,128)(2,1)S(1)}, u32[]{:S(2)}, u32[]{:S(2)}) collective-permute-start(bf16[320,128]{0,1:T(8,128)(2,1)S(1)} %fusion.48), channel_id=1, source_target_pairs={{0,2},{2,0},{1,3},{3,1},{4,6},{6,4},{5,7},{7,5},{8,10},{10,8},{9,1... | collective-permute-start | bytes 245768 | tf_op jit(solution)/shard_map/ppermute | solution.py:25
  228.3 11.4 %collective-permute-start.14 = (bf16[320,128]{0,1:T(8,128)(2,1)S(1)}, bf16[320,128]{0,1:T(8,128)(2,1)S(1)}, u32[]{:S(2)}, u32[]{:S(2)}) collective-permute-start(bf16[320,128]{0,1:T(8,128)(2,1)S(1)} %fusion.39), channel_id=1, source_target_pairs={{0,0},{1,16},{2,32},{3,48},{4,64},{5,80},{6,96},{7,112},{8,128},{9... | collective-permute-start | bytes 245768 | tf_op jit(solution)/shard_map/ppermute | solution.py:188
  239.7 11.1 %collective-permute-start.15 = (bf16[320,128]{0,1:T(8,128)(2,1)S(1)}, bf16[320,128]{0,1:T(8,128)(2,1)S(1)}, u32[]{:S(2)}, u32[]{:S(2)}) collective-permute-start(bf16[320,128]{0,1:T(8,128)(2,1)S(1)} %fusion.35), channel_id=1, source_target_pairs={{0,2},{2,0},{1,3},{3,1},{4,6},{6,4},{5,7},{7,5},{8,10},{10,8},{9,1... | collective-permute-start | bytes 245768 | tf_op jit(solution)/shard_map/ppermute | solution.py:25
  250.9 11.6 %collective-permute-start.18 = (bf16[2,320,128]{1,2,0:T(8,128)(2,1)S(1)}, bf16[2,320,128]{1,2,0:T(8,128)(2,1)S(1)}, u32[]{:S(2)}, u32[]{:S(2)}) collective-permute-start(bf16[2,320,128]{1,2,0:T(8,128)(2,1)S(1)} %maximum_select_fusion.7), channel_id=1, source_target_pairs={{0,8},{4,12},{8,0},{12,4},{1,9},{5,13},{9,1},{13,5},{2,10},{6,14},... | collective-permute-start | bytes 491528 | tf_op jit(solution)/shard_map/ppermute | solution.py:25
  251.0 11.6 %collective-permute-start.17 = (bf16[2,320,128]{1,2,0:T(8,128)(2,1)S(1)}, bf16[2,320,128]{1,2,0:T(8,128)(2,1)S(1)}, u32[]{:S(2)}, u32[]{:S(2)}) collective-permute-start(bf16[2,320,128]{1,2,0:T(8,128)(2,1)S(1)} %maximum_select_fusion.7), channel_id=1, source_target_pairs={{0,12},{4,0},{8,4},{12,8},{1,13},{5,1},{9,5},{13,9},{2,14},{6,2},{... | collective-permute-start | bytes 491528 | tf_op jit(solution)/shard_map/ppermute | solution.py:25
  251.1 16.6 %collective-permute-start.16 = (bf16[2,320,128]{1,2,0:T(8,128)(2,1)S(1)}, bf16[2,320,128]{1,2,0:T(8,128)(2,1)S(1)}, u32[]{:S(2)}, u32[]{:S(2)}) collective-permute-start(bf16[2,320,128]{1,2,0:T(8,128)(2,1)S(1)} %maximum_select_fusion.7), channel_id=1, source_target_pairs={{0,4},{4,8},{8,12},{12,0},{1,5},{5,9},{9,13},{13,1},{2,6},{6,10},{... | collective-permute-start | bytes 491528 | tf_op jit(solution)/shard_map/ppermute | solution.py:25
  287.7 11.0 %collective-permute-start.24 = (bf16[2,320,128]{1,2,0:T(8,128)(2,1)}, bf16[2,320,128]{1,2,0:T(8,128)(2,1)}, u32[]{:S(2)}, u32[]{:S(2)}) collective-permute-start(bf16[2,320,128]{1,2,0:T(8,128)(2,1)} %bitcast.78), channel_id=1, source_target_pairs={{0,12},{4,0},{8,4},{12,8},{1,13},{5,1},{9,5},{13,9},{2,14},{6,2},{... | collective-permute-start | bytes 491528 | tf_op jit(solution)/shard_map/ppermute | solution.py:25
  289.8 9.6 %collective-permute-start.25 = (bf16[2,320,128]{1,2,0:T(8,128)(2,1)}, bf16[2,320,128]{1,2,0:T(8,128)(2,1)}, u32[]{:S(2)}, u32[]{:S(2)}) collective-permute-start(bf16[2,320,128]{1,2,0:T(8,128)(2,1)} %bitcast.249), channel_id=1, source_target_pairs={{0,8},{4,12},{8,0},{12,4},{1,9},{5,13},{9,1},{13,5},{2,10},{6,14},... | collective-permute-start | bytes 491528 | tf_op jit(solution)/shard_map/ppermute | solution.py:25
  289.9 12.1 %collective-permute-start.23 = (bf16[2,320,128]{1,2,0:T(8,128)(2,1)S(1)}, bf16[2,320,128]{1,2,0:T(8,128)(2,1)}, u32[]{:S(2)}, u32[]{:S(2)}) collective-permute-start(bf16[2,320,128]{1,2,0:T(8,128)(2,1)S(1)} %bitcast.248), channel_id=1, source_target_pairs={{0,4},{4,8},{8,12},{12,0},{1,5},{5,9},{9,13},{13,1},{2,6},{6,10},{... | collective-permute-start | bytes 491528 | tf_op jit(solution)/shard_map/ppermute | solution.py:25
  (22 other events, 273.4 us)
Sparse Core Ops, SparseCore 0:
  9.9 67.1 all-gather.5
  88.7 66.1 reduce-scatter.1
  156.7 39.7 all-gather.3
  198.2 69.4 all-gather.7

commit v2 on v1

--- a/solution.py
+++ b/solution.py
@@ -1,6 +1,8 @@
 import jax
 import jax.numpy as jnp
 from jax import lax
+from jax.experimental import pallas as pl
+from jax.experimental.pallas import tpu as pltpu
 from jax.sharding import Mesh, PartitionSpec as P
 
 HEADS = 64
@@ -57,18 +59,97 @@
     return whole.reshape(-1, part.shape[-1])
 
 
+def swap_cores(block, flip_role):
+    route = []
+    for role in range(2):
+        for dp in range(8):
+            for core in range(2):
+                low = dp % 2
+                source = (role * 8 + dp) * 2 + core
+                target_role = 1 - role if flip_role else role
+                target = (target_role * 8 + dp - low + core) * 2 + low
+                route.append((source, target))
+    return lax.ppermute(block, ("role", "dp", "core"), route)
+
+
+def gather_ring(block):
+    me = lax.axis_index("dp")
+    whole = jnp.zeros((8,) + block.shape, block.dtype)
+    whole = lax.dynamic_update_index_in_dim(whole, block, me, 0)
+    up = down = block
+    for step in range(1, 5):
+        up = rotate(up, "dp", 1)
+        whole = lax.dynamic_update_index_in_dim(whole, up, (me + 8 - step) % 8, 0)
+        if step < 4:
+            down = rotate(down, "dp", -1)
+            whole = lax.dynamic_update_index_in_dim(whole, down, (me + step) % 8, 0)
+    return whole
+
+
 def scatter_sum(parts):
-    iy, ix, ic = lax.axis_index("y"), lax.axis_index("x"), lax.axis_index("core")
-    bf16, f32 = jnp.bfloat16, jnp.float32
-    away = lax.dynamic_index_in_dim(parts, 1 - ic, 2, keepdims=False).astype(bf16)
-    near = lax.dynamic_index_in_dim(parts, ic, 2, keepdims=False)
-    sums = near + rotate(away, "core", 1).astype(f32)
-    sent = sums.astype(bf16)
-    ahead = rotate(pick(sent, (ix + 1) % 4), "x", 1)
-    back = rotate(pick(sent, (ix + 3) % 4), "x", -1)
-    across = rotate(pick(sent, (ix + 2) % 4), "x", 2)
-    sums = pick(sums, ix) + ahead.astype(f32) + back.astype(f32) + across.astype(f32)
-    return pick(sums, iy) + rotate(pick(sums, 1 - iy).astype(bf16), "y", 1).astype(f32)
+    blocks = lax.all_to_all(parts, ("x", "y"), 0, 0, tiled=True)
+    return jnp.sum(blocks.astype(jnp.float32), axis=0)
+
+
+def gradient_kernel(cotangent_ref, inputs_ref, out_ref):
+    out_ref[0, 0] = jnp.dot(
+        cotangent_ref[...], inputs_ref[...], preferred_element_type=jnp.float32
+    ).astype(out_ref.dtype)
+
+
+def gradient_terms(cotangent, inputs):
+    tokens, depth = inputs.shape
+    part = cotangent.shape[0] // 16
+    return pl.pallas_call(
+        gradient_kernel,
+        grid=(16,),
+        in_specs=[
+            pl.BlockSpec((part, tokens), lambda j: (j, 0)),
+            pl.BlockSpec((tokens, depth), lambda j: (0, 0)),
+        ],
+        out_specs=pl.BlockSpec((1, 1, part, depth), lambda j: (j % 8, j // 8, 0, 0)),
+        out_shape=jax.ShapeDtypeStruct((8, 2, part, depth), jnp.bfloat16),
+        compiler_params=pltpu.CompilerParams(vmem_limit_bytes=32 * 1024 * 1024),
+        cost_estimate=pl.CostEstimate(
+            flops=2 * 16 * part * tokens * depth, bytes_accessed=17_000_000, transcendentals=0
+        ),
+    )(cotangent, inputs)
+
+
+def project_kernel(weight_ref, tokens_ref, out_ref):
+    dims = (((1,), (1,)), ((), ()))
+    total = lax.dot_general(
+        weight_ref[0, 0, 0], tokens_ref[0, 0, 0], dims, preferred_element_type=jnp.float32
+    )
+    total += lax.dot_general(
+        weight_ref[0, 1, 0], tokens_ref[0, 1, 0], dims, preferred_element_type=jnp.float32
+    )
+    out_ref[0, 0] = total.astype(out_ref.dtype)
+
+
+def project(weight, attended):
+    part, depth = weight.shape[3:]
+    tokens = attended.shape[3]
+
+    def spec(array):
+        several = array.shape[0] > 1
+        return pl.BlockSpec(
+            (1, 2, 1) + array.shape[3:],
+            (lambda r, k: (k, 0, r, 0, 0)) if several else (lambda r, k: (0, 0, 0, 0, 0)),
+        )
+
+    out = pl.pallas_call(
+        project_kernel,
+        grid=(2, 4),
+        in_specs=[spec(weight), spec(attended)],
+        out_specs=pl.BlockSpec((1, 1, part, tokens), lambda r, k: (r, k, 0, 0)),
+        out_shape=jax.ShapeDtypeStruct((2, 4, part, tokens), jnp.bfloat16),
+        compiler_params=pltpu.CompilerParams(vmem_limit_bytes=32 * 1024 * 1024),
+        cost_estimate=pl.CostEstimate(
+            flops=32 * part * depth * tokens, bytes_accessed=6_000_000, transcendentals=0
+        ),
+    )(weight, attended)
+    return out.reshape(8, part, tokens)
 
 
 def normalize(state, norm_gain):
@@ -162,36 +243,40 @@
             prefix_lengths,
         )
 
+    cotangent = lax.all_gather(learner_cotangent, TENSOR, axis=1, tiled=True)
     state = block_states.reshape(tokens, part).T
     attended = attended_of(state)
-    both = pair_order(attended, rotate(attended, "role", 1), role, 0)
-    attended_all = lax.all_gather(both, "dp", axis=0)
-
-    cotangent = lax.all_gather(learner_cotangent, TENSOR, axis=1, tiled=True)
-    terms = lax.dot_general(
-        cotangent, learner_inputs, (((0,), (0,)), ((), ())), preferred_element_type=f32
-    ).astype(bf16)
-    terms = terms.reshape(2, 8, part, depth).transpose(1, 0, 2, 3)
+    both = pair_order(swap_cores(attended, False), swap_cores(attended, True), role, 0)
+    attended_all = gather_ring(both)
+    cotangent, attended_all = lax.optimization_barrier((cotangent, attended_all))
+
+    terms = gradient_terms(cotangent.T, learner_inputs)
     halves = lax.psum_scatter(terms, "dp", scatter_dimension=0, tiled=False)
     gradient = pick(halves, role).astype(f32) + rotate(pick(halves, 1 - role), "role", 1).astype(f32)
     new_weight, new_first, new_second = adam_update(
         gradient, master_weight.T, first_moment.T, second_moment.T
     )
     weight_part = new_weight.astype(bf16)
-
-    weight_both = pair_order(weight_part, rotate(weight_part, "role", 1), role, 0)
+    weight_pair = pair_order(weight_part, rotate(weight_part, "core", 1), core, 0)
+
+    weight_both = pair_order(swap_cores(weight_part, False), swap_cores(weight_part, True), role, 0)
     weight_all = lax.all_gather(weight_both, "dp", axis=0)
 
-    partial = jnp.einsum("ck,drtk->rdct", weight_part, attended_all, preferred_element_type=f32)
-    update = scatter_sum(partial.reshape(4, 2, 2, part, tokens))
+    partial = project(
+        weight_pair.reshape(1, 2, 1, part, depth), attended_all.reshape(4, 2, 2, tokens, depth)
+    )
+    update = scatter_sum(partial)
     swap = [(a * 16 + b, b * 16 + a) for a in range(16) for b in range(16)]
     update = lax.ppermute(update.astype(bf16), EVERY, swap).astype(f32) * out_scale
     picks = position_picks.reshape(STEPS, 1, tokens)
     state = revise(state, update, picks[0], mask_part)
 
     attended = attended_of(state)
-    partial = jnp.einsum("drck,tk->rdct", weight_all, attended, preferred_element_type=f32)
-    update = scatter_sum(partial.reshape(4, 2, 2, part, tokens)) * out_scale
+    attended_pair = pair_order(attended, rotate(attended, "core", 1), core, 0)
+    partial = project(
+        weight_all.reshape(4, 2, 2, part, depth), attended_pair.reshape(1, 2, 1, tokens, depth)
+    )
+    update = scatter_sum(partial) * out_scale
     state = revise(state, update, picks[1], mask_part)
     return (state.T.reshape(rows, block_len, part), new_weight.T, new_first.T, new_second.T)
 

time: 321 us -> 300 us (0.935); the launches traced: 315 us -> 300 us
  waiting for transfers between devices: 198 us -> 168 us
  blocking collectives: 0 us -> 16.3 us
  Pallas kernels: 0 us -> 15.5 us
  matrix products: 24.3 us -> 9.23 us
  local copies, waits for them, and re-layouts: 15.9 us -> 19.8 us
  starting transfers between devices: 42.6 us -> 39.1 us
    all_gather x1, waiting for transfers between devices: 69.1 us -> 0.02 us  [on_device(): cotangent = lax.all_gather(learner_cotangent, TENSOR, axis=1, tiled=True)]
    reduce_scatter x1, waiting for transfers between devices: 23.8 us -> 64 us  [on_device(): halves = lax.psum_scatter(terms, 'dp', scatter_dimension=0, tiled=False)]
    ppermute x0 -> x4, waiting for transfers between devices: none -> 21.7 us  [swap_cores(): return lax.ppermute(block, ('role', 'dp', 'core'), route)]
    ppermute x26 -> x23, waiting for transfers between devices: 81.2 us -> 60.4 us  [rotate(): lax.ppermute(block, axis, [(low, (low + shift) % count) for low in range(...]
    all_to_all x0 -> x1, blocking collectives: none -> 16.3 us  [scatter_sum(): blocks = lax.all_to_all(parts, ('x', 'y'), 0, 0, tiled=True)]
    pallas_call x0 -> x3, Pallas kernels: none -> 15.5 us  [the longest x1 8.09 us: gradient_terms(): pl.pallas_call(gradient_kernel, grid=(16,), in_specs=[pl.BlockSpec((part,...]
    all_gather x1 -> x0, waiting for transfers between devices: 15.4 us -> none  [on_device(): attended_all = lax.all_gather(both, 'dp', axis=0)]
    dot_general x3 -> x0, matrix products: 15 us -> none  [the longest x1 8.58 us: on_device(): lax.dot_general(cotangent, learner_inputs, (((0,), (0,)), ((), ())), pref...]
  transfers between devices with their start and end apart: 31 -> 32, of which waited for: 27 -> 23; matrix products, arithmetic and copies ran while one was open for 12% -> 9% of each run, Pallas kernels for 0% -> 1%
where the time goes in v2:
time: 300 us
  waiting for transfers between devices  168 us (56%)
  starting transfers between devices  39.1 us (13%)
  local copies, waits for them, and re-layouts  19.8 us (7%)
  other arithmetic  17 us (6%)
  blocking collectives  16.3 us (5%)
  Pallas kernels  15.5 us (5%)
  between operations  14.3 us (5%)
  matrix products  9.23 us (3%)
    reduce_scatter x1, waiting for transfers between devices, on_device(): halves = lax.psum_scatter(terms, 'dp', scatter_dimension=0, tiled=False)  64 us
    ppermute x23, waiting for transfers between devices, rotate(): lax.ppermute(block, axis, [(low, (low + shift) % count) for low in range(...  60.4 us
    ppermute x23, starting transfers between devices, rotate(): lax.ppermute(block, axis, [(low, (low + shift) % count) for low in range(...  27.4 us
    ppermute x4, waiting for transfers between devices, swap_cores(): return lax.ppermute(block, ('role', 'dp', 'core'), route)  21.7 us
    all_to_all x1, blocking collectives, scatter_sum(): blocks = lax.all_to_all(parts, ('x', 'y'), 0, 0, tiled=True)  16.3 us
    unnamed x40, local copies, waits for them, and re-layouts  12.1 us
    all_to_all x1, waiting for transfers between devices, scatter_sum(): blocks = lax.all_to_all(parts, ('x', 'y'), 0, 0, tiled=True)  10.7 us
    pallas_call x1, Pallas kernels, gradient_terms(): pl.pallas_call(gradient_kernel, grid=(16,), in_specs=[pl.BlockSpec((part,...  8.09 us
  transfers between devices with their start and end apart: 32, of which 23 were waited for; matrix products, arithmetic and copies ran while one was open for 9% of the time, Pallas kernels for 1%

profile of v2, /device:TPU:16, one launch (start us, length us, event | category | flops | bytes accessed | tf_op | source)
XLA Modules:
  0.0 299.5 jit_solution(6456814751430768808)
XLA Ops:
  10.3 3.2 %collective-permute-done.1 = bf16[320,128]{1,0:T(8,128)(2,1)S(1)} collective-permute-done((bf16[320,128]{1,0:T(8,128)(2,1)S(1)}, bf16[320,128]{1,0:T(8,128)(2,1)S(1)}, u32[]{:S(2)}, u32[]{:S(2)}) %collective-permute-start.1) | collective-permute-done | bytes 81952 | tf_op jit(solution)/shard_map/ppermute | solution.py:27
  42.7 9.9 %collective-permute-done.8 = bf16[128,512]{1,0:T(8,128)(2,1)S(1)} collective-permute-done((bf16[128,512]{1,0:T(8,128)(2,1)S(1)}, bf16[128,512]{1,0:T(8,128)(2,1)S(1)}, u32[]{:S(2)}, u32[]{:S(2)}) %collective-permute-start.8) | collective-permute-done | bytes 131104 | tf_op jit(solution)/shard_map/ppermute | solution.py:72
  53.4 3.2 %collective-permute-start.10 = (bf16[2,128,512]{2,1,0:T(8,128)(2,1)}, bf16[2,128,512]{2,1,0:T(8,128)(2,1)}, u32[]{:S(2)}, u32[]{:S(2)}) collective-permute-start(bf16[2,128,512]{2,1,0:T(8,128)(2,1)} %maximum_select_fusion.5), channel_id=1, source_target_pairs={{0,112},{16,0},{32,16},{48,32},{64,48},{80,64},{96,80},{112,96},{1... | collective-permute-start | bytes 786440 | tf_op jit(solution)/shard_map/ppermute | solution.py:27
  57.6 6.4 %collective-permute-done.9 = bf16[2,128,512]{2,1,0:T(8,128)(2,1)} collective-permute-done((bf16[2,128,512]{2,1,0:T(8,128)(2,1)}, bf16[2,128,512]{2,1,0:T(8,128)(2,1)}, u32[]{:S(2)}, u32[]{:S(2)}) %collective-permute-start.9) | collective-permute-done | bytes 262176 | tf_op jit(solution)/shard_map/ppermute | solution.py:27
  64.0 3.2 %collective-permute-start.12 = (bf16[2,128,512]{2,1,0:T(8,128)(2,1)}, bf16[2,128,512]{2,1,0:T(8,128)(2,1)S(1)}, u32[]{:S(2)}, u32[]{:S(2)}) collective-permute-start(bf16[2,128,512]{2,1,0:T(8,128)(2,1)} %collective-permute-done.10), channel_id=1, source_target_pairs={{0,112},{16,0},{32,16},{48,32},{64,48},{80,64},{96,80},{112,96},{1... | collective-permute-start | bytes 786440 | tf_op jit(solution)/shard_map/ppermute | solution.py:27
  69.2 4.4 %collective-permute-done.11 = bf16[2,128,512]{2,1,0:T(8,128)(2,1)S(1)} collective-permute-done((bf16[2,128,512]{2,1,0:T(8,128)(2,1)}, bf16[2,128,512]{2,1,0:T(8,128)(2,1)S(1)}, u32[]{:S(2)}, u32[]{:S(2)}) %collective-permute-start.11) | collective-permute-done | bytes 262176 | tf_op jit(solution)/shard_map/ppermute | solution.py:27
  73.7 3.2 %collective-permute-start.14 = (bf16[2,128,512]{2,1,0:T(8,128)(2,1)S(1)}, bf16[2,128,512]{2,1,0:T(8,128)(2,1)S(1)}, u32[]{:S(2)}, u32[]{:S(2)}) collective-permute-start(bf16[2,128,512]{2,1,0:T(8,128)(2,1)S(1)} %collective-permute-done.12), channel_id=1, source_target_pairs={{0,112},{16,0},{32,16},{48,32},{64,48},{80,64},{96,80},{112,96},{1... | collective-permute-start | bytes 786440 | tf_op jit(solution)/shard_map/ppermute | solution.py:27
  76.9 5.3 %collective-permute-done.13 = bf16[2,128,512]{2,1,0:T(8,128)(2,1)S(1)} collective-permute-done((bf16[2,128,512]{2,1,0:T(8,128)(2,1)S(1)}, bf16[2,128,512]{2,1,0:T(8,128)(2,1)S(1)}, u32[]{:S(2)}, u32[]{:S(2)}) %collective-permute-start.13) | collective-permute-done | bytes 262176 | tf_op jit(solution)/shard_map/ppermute | solution.py:27
  82.3 7.6 %collective-permute-done.15 = bf16[2,128,512]{2,1,0:T(8,128)(2,1)S(1)} collective-permute-done((bf16[2,128,512]{2,1,0:T(8,128)(2,1)S(1)}, bf16[2,128,512]{2,1,0:T(8,128)(2,1)S(1)}, u32[]{:S(2)}, u32[]{:S(2)}) %collective-permute-start.15) | collective-permute-done | bytes 262176 | tf_op jit(solution)/shard_map/ppermute | solution.py:27
  90.0 4.0 %copy-done.3 = bf16[1024,5120]{0,1:T(8,128)(2,1)S(1)} copy-done((bf16[1024,5120]{0,1:T(8,128)(2,1)S(1)}, bf16[1024,5120]{0,1:T(8,128)(2,1)}, u32[]{:S(2)}) %copy-start.3) | copy-done | bytes 10485784
  95.2 8.1 %shard_map.156 = bf16[8,2,320,512]{3,2,1,0:T(8,128)(2,1)S(1)} custom-call(bf16[5120,1024]{1,0:T(8,128)(2,1)S(1)} %bitcast.191, bf16[1024,512]{1,0:T(8,128)(2,1)S(1)} %copy-done.4), custom_call_target="tpu_custom_call" | custom-call | flops 5368709120 | bytes 17000000 | tf_op jit(solution)/shard_map/pallas_call | solution.py:103
  105.7 64.0 %reduce-scatter.2.cloned.1.call-done = bf16[1,2,320,512]{3,2,1,0:T(8,128)(2,1)} async-done(((bf16[8,2,320,512]{3,2,1,0:T(8,128)(2,1)}), bf16[1,2,320,512]{3,2,1,0:T(8,128)(2,1)}) %reduce-scatter.2.cloned.1.call-update) | async-done | bytes 655376 | tf_op jit(solution)/shard_map/reduce_scatter | solution.py:254
  172.0 10.8 %collective-permute-done.16 = bf16[320,512]{1,0:T(8,128)(2,1)} collective-permute-done((bf16[320,512]{1,0:T(8,128)(2,1)}, bf16[320,512]{1,0:T(8,128)(2,1)}, u32[]{:S(2)}, u32[]{:S(2)}) %collective-permute-start.16) | collective-permute-done | bytes 327712 | tf_op jit(solution)/shard_map/ppermute | solution.py:27
  182.8 3.6 %fusion.43 = (bf16[320,512]{1,0:T(8,128)(2,1)}, f32[320,512]{1,0:T(8,128)}, f32[512,320]{0,1:T(8,128)}, f32[512,320]{0,1:T(8,128)}) fusion(f32[512,320]{0,1:T(8,128)} %param.17, bf16[320,512]{1,0:T(8,128)(2,1)} %collective-permute-done.16, bf16[1,2,320,512]{3,2,1,0:T(8,128)(2,1)} %reduce-scatter.2.cloned.1.call-done, s32[]{:T(128)S(6)} %select_n.310, ...), kind=kLoop, calls=%fused_computation.116 | loop fusion | flops 3112960 | bytes 4915204 | tf_op jit(solution)/shard_map/convert_element_type | solution.py:259
  188.5 11.8 %collective-permute-done.20 = bf16[320,512]{1,0:T(8,128)(2,1)S(1)} collective-permute-done((bf16[320,512]{1,0:T(8,128)(2,1)}, bf16[320,512]{1,0:T(8,128)(2,1)S(1)}, u32[]{:S(2)}, u32[]{:S(2)}) %collective-permute-start.20) | collective-permute-done | bytes 327712 | tf_op jit(solution)/shard_map/ppermute | solution.py:72
  207.3 16.3 %all_to_all.10 = bf16[8,320,128]{2,1,0:T(8,128)(2,1)S(1)} all-to-all(bf16[8,320,128]{2,1,0:T(8,128)(2,1)S(1)} %bitcast.190), channel_id=1, replica_groups=mesh['role'=2,'dp'=8,'x'=4,'y'=2,'core'=2] {'x','y'}, dimensions={0} | all-to-all | bytes 1310720 | tf_op jit(solution)/shard_map/all_to_all | solution.py:90
  223.7 3.6 %collective-permute-start.18 = (bf16[320,128]{1,0:T(8,128)(2,1)S(1)}, bf16[320,128]{1,0:T(8,128)(2,1)S(1)}, u32[]{:S(2)}, u32[]{:S(2)}) collective-permute-start(bf16[320,128]{1,0:T(8,128)(2,1)S(1)} %reduce_sum.78), channel_id=1, source_target_pairs={{0,0},{1,16},{2,32},{3,48},{4,64},{5,80},{6,96},{7,112},{8,128},{9... | collective-permute-start | bytes 245768 | tf_op jit(solution)/shard_map/ppermute | solution.py:270
  228.3 6.6 %collective-permute-done.18 = bf16[320,128]{1,0:T(8,128)(2,1)S(1)} collective-permute-done((bf16[320,128]{1,0:T(8,128)(2,1)S(1)}, bf16[320,128]{1,0:T(8,128)(2,1)S(1)}, u32[]{:S(2)}, u32[]{:S(2)}) %collective-permute-start.18) | collective-permute-done | bytes 81952 | tf_op jit(solution)/shard_map/ppermute | solution.py:270
  235.1 5.5 %collective-permute-start.21 = (bf16[320,128]{1,0:T(8,128)(2,1)S(1)}, bf16[320,128]{1,0:T(8,128)(2,1)S(1)}, u32[]{:S(2)}, u32[]{:S(2)}) collective-permute-start(bf16[320,128]{1,0:T(8,128)(2,1)S(1)} %fusion.29), channel_id=1, source_target_pairs={{0,2},{2,0},{1,3},{3,1},{4,6},{6,4},{5,7},{7,5},{8,10},{10,8},{9,1... | collective-permute-start | bytes 245768 | tf_op jit(solution)/shard_map/ppermute | solution.py:27
  246.6 4.8 %collective-permute-done.22 = bf16[2,320,128]{2,1,0:T(8,128)(2,1)S(1)} collective-permute-done((bf16[2,320,128]{2,1,0:T(8,128)(2,1)S(1)}, bf16[2,320,128]{2,1,0:T(8,128)(2,1)S(1)}, u32[]{:S(2)}, u32[]{:S(2)}) %collective-permute-start.22) | collective-permute-done | bytes 163872 | tf_op jit(solution)/shard_map/ppermute | solution.py:27
  265.9 4.1 %all-gather.5.cloned.1.call-done = bf16[8,2,320,512]{3,2,1,0:T(8,128)(2,1)} async-done(((bf16[1,2,320,512]{3,2,1,0:T(8,128)(2,1)}), bf16[8,2,320,512]{3,2,1,0:T(8,128)(2,1)}) %all-gather.5.cloned.1.call-update) | async-done | bytes 5242896 | tf_op jit(solution)/shard_map/all_gather | solution.py:263
  272.5 4.4 %shard_map.158 = bf16[2,4,320,128]{3,2,1,0:T(8,128)(2,1)} custom-call(bf16[4,2,2,320,512]{4,3,2,1,0:T(8,128)(2,1)S(1)} %bitcast.189, bf16[1,2,1,128,512]{4,3,2,1,0:T(8,128)(2,1)S(1)} %maximum_select_fusion.6.tokens_ref), custom_call_target="tpu_custom_call" | custom-call | flops 671088640 | bytes 6000000 | tf_op jit(solution)/shard_map/pallas_call | solution.py:141
  276.9 4.3 %all-to-all-start.1 = ((bf16[8,320,128]{2,1,0:T(8,128)(2,1)}), bf16[8,320,128]{2,1,0:T(8,128)(2,1)S(1)}, u32[]{:S(2)}, u32[]{:S(2)}) async-start(bf16[8,320,128]{2,1,0:T(8,128)(2,1)} %bitcast.73), calls=%async_computation.2 | async-start | bytes 1310720 | tf_op jit(solution)/shard_map/all_to_all | solution.py:90
  281.3 10.7 %all-to-all-done.1 = bf16[8,320,128]{2,1,0:T(8,128)(2,1)S(1)} async-done(((bf16[8,320,128]{2,1,0:T(8,128)(2,1)}), bf16[8,320,128]{2,1,0:T(8,128)(2,1)S(1)}, u32[]{:S(2)}, u32[]{:S(2)}) %all-to-all-start.1) | async-done | bytes 655392 | tf_op jit(solution)/shard_map/all_to_all | solution.py:90
  (165 shorter events, 76.1 us)
Async XLA Ops:
  7.2 82.8 %all-gather.3.cloned.1.call-start = ((), (), s32[]{:S(2)}) async-start(), calls=%async_computation.3 | async-start | bytes 11141120 | tf_op jit(solution)/shard_map/all_gather | solution.py:246
  7.9 161.8 %reduce-scatter.2.cloned.1.call-start = ((), (), s32[]{:S(2)}) async-start(), calls=%async_computation.4 | async-start | bytes 5898240 | tf_op jit(solution)/shard_map/reduce_scatter | solution.py:254
  9.0 4.5 %collective-permute-start.1 = (bf16[320,128]{1,0:T(8,128)(2,1)S(1)}, bf16[320,128]{1,0:T(8,128)(2,1)S(1)}, u32[]{:S(2)}, u32[]{:S(2)}) collective-permute-start(bf16[320,128]{1,0:T(8,128)(2,1)S(1)} %bitcast.204), channel_id=1, source_target_pairs={{0,2},{2,0},{1,3},{3,1},{4,6},{6,4},{5,7},{7,5},{8,10},{10,8},{9,1... | collective-permute-start | bytes 245768 | tf_op jit(solution)/shard_map/ppermute | solution.py:27
  13.5 8.0 %collective-permute-start.2 = (bf16[2,320,128]{2,1,0:T(8,128)(2,1)S(1)}, bf16[2,320,128]{2,1,0:T(8,128)(2,1)S(1)}, u32[]{:S(2)}, u32[]{:S(2)}) collective-permute-start(bf16[2,320,128]{2,1,0:T(8,128)(2,1)S(1)} %maximum_select_fusion.8), channel_id=1, source_target_pairs={{0,4},{4,8},{8,12},{12,0},{1,5},{5,9},{9,13},{13,1},{2,6},{6,10},{... | collective-permute-start | bytes 491528 | tf_op jit(solution)/shard_map/ppermute | solution.py:27
  15.1 6.4 %collective-permute-start.3 = (bf16[2,320,128]{2,1,0:T(8,128)(2,1)S(1)}, bf16[2,320,128]{2,1,0:T(8,128)(2,1)S(1)}, u32[]{:S(2)}, u32[]{:S(2)}) collective-permute-start(bf16[2,320,128]{2,1,0:T(8,128)(2,1)S(1)} %maximum_select_fusion.8), channel_id=1, source_target_pairs={{0,12},{4,0},{8,4},{12,8},{1,13},{5,1},{9,5},{13,9},{2,14},{6,2},{... | collective-permute-start | bytes 491528 | tf_op jit(solution)/shard_map/ppermute | solution.py:27
  16.8 7.5 %collective-permute-start.4 = (bf16[2,320,128]{2,1,0:T(8,128)(2,1)S(1)}, bf16[2,320,128]{2,1,0:T(8,128)(2,1)S(1)}, u32[]{:S(2)}, u32[]{:S(2)}) collective-permute-start(bf16[2,320,128]{2,1,0:T(8,128)(2,1)S(1)} %maximum_select_fusion.8), channel_id=1, source_target_pairs={{0,8},{4,12},{8,0},{12,4},{1,9},{5,13},{9,1},{13,5},{2,10},{6,14},... | collective-permute-start | bytes 491528 | tf_op jit(solution)/shard_map/ppermute | solution.py:27
  24.5 13.2 %collective-permute-start = (bf16[4,512,128]{2,1,0:T(8,128)(2,1)}, bf16[4,512,128]{2,1,0:T(8,128)(2,1)}, u32[]{:S(2)}, u32[]{:S(2)}) collective-permute-start(bf16[4,512,128]{2,1,0:T(8,128)(2,1)} %param.20), channel_id=1, source_target_pairs={{0,1},{1,0},{2,3},{3,2},{4,5},{5,4},{6,7},{7,6},{8,9},{9,8},{10,11... | collective-permute-start | bytes 1572872 | tf_op jit(solution)/shard_map/ppermute | solution.py:27
  41.9 10.7 %collective-permute-start.8 = (bf16[128,512]{1,0:T(8,128)(2,1)S(1)}, bf16[128,512]{1,0:T(8,128)(2,1)S(1)}, u32[]{:S(2)}, u32[]{:S(2)}) collective-permute-start(bf16[128,512]{1,0:T(8,128)(2,1)S(1)} %bitcast.223), channel_id=1, source_target_pairs={{0,128},{1,144},{16,129},{17,145},{32,160},{33,176},{48,161},{49,1... | collective-permute-start | bytes 393224 | tf_op jit(solution)/shard_map/ppermute | solution.py:72
  53.4 10.6 %collective-permute-start.9 = (bf16[2,128,512]{2,1,0:T(8,128)(2,1)}, bf16[2,128,512]{2,1,0:T(8,128)(2,1)}, u32[]{:S(2)}, u32[]{:S(2)}) collective-permute-start(bf16[2,128,512]{2,1,0:T(8,128)(2,1)} %maximum_select_fusion.5), channel_id=1, source_target_pairs={{0,16},{16,32},{32,48},{48,64},{64,80},{80,96},{96,112},{112,0},{1... | collective-permute-start | bytes 786440 | tf_op jit(solution)/shard_map/ppermute | solution.py:27
  53.4 10.6 %collective-permute-start.10 = (bf16[2,128,512]{2,1,0:T(8,128)(2,1)}, bf16[2,128,512]{2,1,0:T(8,128)(2,1)}, u32[]{:S(2)}, u32[]{:S(2)}) collective-permute-start(bf16[2,128,512]{2,1,0:T(8,128)(2,1)} %maximum_select_fusion.5), channel_id=1, source_target_pairs={{0,112},{16,0},{32,16},{48,32},{64,48},{80,64},{96,80},{112,96},{1... | collective-permute-start | bytes 786440 | tf_op jit(solution)/shard_map/ppermute | solution.py:27
  64.0 9.7 %collective-permute-start.11 = (bf16[2,128,512]{2,1,0:T(8,128)(2,1)}, bf16[2,128,512]{2,1,0:T(8,128)(2,1)S(1)}, u32[]{:S(2)}, u32[]{:S(2)}) collective-permute-start(bf16[2,128,512]{2,1,0:T(8,128)(2,1)} %collective-permute-done.9), channel_id=1, source_target_pairs={{0,16},{16,32},{32,48},{48,64},{64,80},{80,96},{96,112},{112,0},{1... | collective-permute-start | bytes 786440 | tf_op jit(solution)/shard_map/ppermute | solution.py:27
  64.0 9.7 %collective-permute-start.12 = (bf16[2,128,512]{2,1,0:T(8,128)(2,1)}, bf16[2,128,512]{2,1,0:T(8,128)(2,1)S(1)}, u32[]{:S(2)}, u32[]{:S(2)}) collective-permute-start(bf16[2,128,512]{2,1,0:T(8,128)(2,1)} %collective-permute-done.10), channel_id=1, source_target_pairs={{0,112},{16,0},{32,16},{48,32},{64,48},{80,64},{96,80},{112,96},{1... | collective-permute-start | bytes 786440 | tf_op jit(solution)/shard_map/ppermute | solution.py:27
  73.6 8.6 %collective-permute-start.13 = (bf16[2,128,512]{2,1,0:T(8,128)(2,1)S(1)}, bf16[2,128,512]{2,1,0:T(8,128)(2,1)S(1)}, u32[]{:S(2)}, u32[]{:S(2)}) collective-permute-start(bf16[2,128,512]{2,1,0:T(8,128)(2,1)S(1)} %collective-permute-done.11), channel_id=1, source_target_pairs={{0,16},{16,32},{32,48},{48,64},{64,80},{80,96},{96,112},{112,0},{1... | collective-permute-start | bytes 786440 | tf_op jit(solution)/shard_map/ppermute | solution.py:27
  73.7 8.6 %collective-permute-start.14 = (bf16[2,128,512]{2,1,0:T(8,128)(2,1)S(1)}, bf16[2,128,512]{2,1,0:T(8,128)(2,1)S(1)}, u32[]{:S(2)}, u32[]{:S(2)}) collective-permute-start(bf16[2,128,512]{2,1,0:T(8,128)(2,1)S(1)} %collective-permute-done.12), channel_id=1, source_target_pairs={{0,112},{16,0},{32,16},{48,32},{64,48},{80,64},{96,80},{112,96},{1... | collective-permute-start | bytes 786440 | tf_op jit(solution)/shard_map/ppermute | solution.py:27
  82.2 7.7 %collective-permute-start.15 = (bf16[2,128,512]{2,1,0:T(8,128)(2,1)S(1)}, bf16[2,128,512]{2,1,0:T(8,128)(2,1)S(1)}, u32[]{:S(2)}, u32[]{:S(2)}) collective-permute-start(bf16[2,128,512]{2,1,0:T(8,128)(2,1)S(1)} %collective-permute-done.13), channel_id=1, source_target_pairs={{0,16},{16,32},{32,48},{48,64},{64,80},{80,96},{96,112},{112,0},{1... | collective-permute-start | bytes 786440 | tf_op jit(solution)/shard_map/ppermute | solution.py:27
  105.6 164.3 %all-gather.5.cloned.1.call-start = ((), (), s32[]{:S(2)}) async-start(), calls=%async_computation.5 | async-start | bytes 5898240 | tf_op jit(solution)/shard_map/all_gather | solution.py:263
  171.4 11.3 %collective-permute-start.16 = (bf16[320,512]{1,0:T(8,128)(2,1)}, bf16[320,512]{1,0:T(8,128)(2,1)}, u32[]{:S(2)}, u32[]{:S(2)}) collective-permute-start(bf16[320,512]{1,0:T(8,128)(2,1)} %dynamic-slice_bitcast_fusion), channel_id=1, source_target_pairs={{0,128},{128,0},{1,129},{129,1},{2,130},{130,2},{3,131},{131,3},{4... | collective-permute-start | bytes 983048 | tf_op jit(solution)/shard_map/ppermute | solution.py:27
  188.0 12.3 %collective-permute-start.20 = (bf16[320,512]{1,0:T(8,128)(2,1)}, bf16[320,512]{1,0:T(8,128)(2,1)S(1)}, u32[]{:S(2)}, u32[]{:S(2)}) collective-permute-start(bf16[320,512]{1,0:T(8,128)(2,1)} %get-tuple-element.12), channel_id=1, source_target_pairs={{0,128},{1,144},{16,129},{17,145},{32,160},{33,176},{48,161},{49,1... | collective-permute-start | bytes 983048 | tf_op jit(solution)/shard_map/ppermute | solution.py:72
  223.7 11.2 %collective-permute-start.18 = (bf16[320,128]{1,0:T(8,128)(2,1)S(1)}, bf16[320,128]{1,0:T(8,128)(2,1)S(1)}, u32[]{:S(2)}, u32[]{:S(2)}) collective-permute-start(bf16[320,128]{1,0:T(8,128)(2,1)S(1)} %reduce_sum.78), channel_id=1, source_target_pairs={{0,0},{1,16},{2,32},{3,48},{4,64},{5,80},{6,96},{7,112},{8,128},{9... | collective-permute-start | bytes 245768 | tf_op jit(solution)/shard_map/ppermute | solution.py:270
  235.1 7.9 %collective-permute-start.21 = (bf16[320,128]{1,0:T(8,128)(2,1)S(1)}, bf16[320,128]{1,0:T(8,128)(2,1)S(1)}, u32[]{:S(2)}, u32[]{:S(2)}) collective-permute-start(bf16[320,128]{1,0:T(8,128)(2,1)S(1)} %fusion.29), channel_id=1, source_target_pairs={{0,2},{2,0},{1,3},{3,1},{4,6},{6,4},{5,7},{7,5},{8,10},{10,8},{9,1... | collective-permute-start | bytes 245768 | tf_op jit(solution)/shard_map/ppermute | solution.py:27
  243.0 8.4 %collective-permute-start.22 = (bf16[2,320,128]{2,1,0:T(8,128)(2,1)S(1)}, bf16[2,320,128]{2,1,0:T(8,128)(2,1)S(1)}, u32[]{:S(2)}, u32[]{:S(2)}) collective-permute-start(bf16[2,320,128]{2,1,0:T(8,128)(2,1)S(1)} %maximum_select_fusion.10), channel_id=1, source_target_pairs={{0,4},{4,8},{8,12},{12,0},{1,5},{5,9},{9,13},{13,1},{2,6},{6,10},{... | collective-permute-start | bytes 491528 | tf_op jit(solution)/shard_map/ppermute | solution.py:27
  244.3 7.1 %collective-permute-start.23 = (bf16[2,320,128]{2,1,0:T(8,128)(2,1)S(1)}, bf16[2,320,128]{2,1,0:T(8,128)(2,1)S(1)}, u32[]{:S(2)}, u32[]{:S(2)}) collective-permute-start(bf16[2,320,128]{2,1,0:T(8,128)(2,1)S(1)} %maximum_select_fusion.10), channel_id=1, source_target_pairs={{0,12},{4,0},{8,4},{12,8},{1,13},{5,1},{9,5},{13,9},{2,14},{6,2},{... | collective-permute-start | bytes 491528 | tf_op jit(solution)/shard_map/ppermute | solution.py:27
  246.3 6.8 %collective-permute-start.24 = (bf16[2,320,128]{2,1,0:T(8,128)(2,1)S(1)}, bf16[2,320,128]{2,1,0:T(8,128)(2,1)S(1)}, u32[]{:S(2)}, u32[]{:S(2)}) collective-permute-start(bf16[2,320,128]{2,1,0:T(8,128)(2,1)S(1)} %maximum_select_fusion.10), channel_id=1, source_target_pairs={{0,8},{4,12},{8,0},{12,4},{1,9},{5,13},{9,1},{13,5},{2,10},{6,14},... | collective-permute-start | bytes 491528 | tf_op jit(solution)/shard_map/ppermute | solution.py:27
  276.9 15.1 %all-to-all-start.1 = ((bf16[8,320,128]{2,1,0:T(8,128)(2,1)}), bf16[8,320,128]{2,1,0:T(8,128)(2,1)S(1)}, u32[]{:S(2)}, u32[]{:S(2)}) async-start(bf16[8,320,128]{2,1,0:T(8,128)(2,1)} %bitcast.73), calls=%async_computation.2 | async-start | bytes 1310720 | tf_op jit(solution)/shard_map/all_to_all | solution.py:90
  (27 other events, 143.3 us)
Sparse Core Ops, SparseCore 0:
  9.9 69.8 all-gather.2
  105.8 63.9 reduce-scatter.1
  201.4 68.5 all-gather.4

commit v3 on v2

--- a/solution.py
+++ b/solution.py
@@ -46,7 +46,7 @@
     return (weight_new, first_new, second_new)
 
 
-def gather_features(part):
+def gather_features(part, beside=None):
     iy, ix, ic = lax.axis_index("y"), lax.axis_index("x"), lax.axis_index("core")
     rows = pair_order(part, rotate(part, "y", 1), iy, 0)
     ahead, back, across = rotate(rows, "x", 1), rotate(rows, "x", -1), rotate(rows, "x", 2)
@@ -55,11 +55,12 @@
     square = lax.dynamic_update_index_in_dim(square, ahead, (ix + 3) % 4, 0)
     square = lax.dynamic_update_index_in_dim(square, back, (ix + 1) % 4, 0)
     square = lax.dynamic_update_index_in_dim(square, across, (ix + 2) % 4, 0)
+    square, beside = lax.optimization_barrier((square, beside))
     whole = pair_order(square, rotate(square, "core", 1), ic, 2)
-    return whole.reshape(-1, part.shape[-1])
-
-
-def swap_cores(block, flip_role):
+    return whole.reshape(-1, part.shape[-1]), beside
+
+
+def swap_cores(block, flip_role=False):
     route = []
     for role in range(2):
         for dp in range(8):
@@ -72,18 +73,20 @@
     return lax.ppermute(block, ("role", "dp", "core"), route)
 
 
-def gather_ring(block):
+def gather_ring(block, before):
     me = lax.axis_index("dp")
+    up, down = [block], [block]
+    for step in range(3):
+        up.append(rotate(up[-1], "dp", 1))
+        down.append(rotate(down[-1], "dp", -1))
+    before, up, down = lax.optimization_barrier((before, up, down))
+    up.append(rotate(up[-1], "dp", 1))
     whole = jnp.zeros((8,) + block.shape, block.dtype)
-    whole = lax.dynamic_update_index_in_dim(whole, block, me, 0)
-    up = down = block
-    for step in range(1, 5):
-        up = rotate(up, "dp", 1)
-        whole = lax.dynamic_update_index_in_dim(whole, up, (me + 8 - step) % 8, 0)
-        if step < 4:
-            down = rotate(down, "dp", -1)
-            whole = lax.dynamic_update_index_in_dim(whole, down, (me + step) % 8, 0)
-    return whole
+    for step in range(5):
+        whole = lax.dynamic_update_index_in_dim(whole, up[step], (me + 8 - step) % 8, 0)
+    for step in range(1, 4):
+        whole = lax.dynamic_update_index_in_dim(whole, down[step], (me + step) % 8, 0)
+    return whole, before
 
 
 def scatter_sum(parts):
@@ -109,7 +112,7 @@
         ],
         out_specs=pl.BlockSpec((1, 1, part, depth), lambda j: (j % 8, j // 8, 0, 0)),
         out_shape=jax.ShapeDtypeStruct((8, 2, part, depth), jnp.bfloat16),
-        compiler_params=pltpu.CompilerParams(vmem_limit_bytes=32 * 1024 * 1024),
+        compiler_params=pltpu.CompilerParams(vmem_limit_bytes=60 * 1024 * 1024),
         cost_estimate=pl.CostEstimate(
             flops=2 * 16 * part * tokens * depth, bytes_accessed=17_000_000, transcendentals=0
         ),
@@ -132,10 +135,10 @@
     tokens = attended.shape[3]
 
     def spec(array):
-        several = array.shape[0] > 1
+        pairs, _, roles = array.shape[:3]
         return pl.BlockSpec(
             (1, 2, 1) + array.shape[3:],
-            (lambda r, k: (k, 0, r, 0, 0)) if several else (lambda r, k: (0, 0, 0, 0, 0)),
+            lambda r, k: (k if pairs > 1 else 0, 0, r if roles > 1 else 0, 0, 0),
         )
 
     out = pl.pallas_call(
@@ -223,8 +226,9 @@
     cache_values = jnp.where(core == 0, cache_other, prefix_cache)
     mask_part = lax.dynamic_slice_in_dim(mask_vector, lax.axis_index(TENSOR) * part, part, 0)
 
-    def attended_of(state):
-        normed = normalize(gather_features(state), norm_gain)
+    def attended_of(state, beside=None):
+        whole, beside = gather_features(state, beside)
+        normed = normalize(whole, norm_gain)
         own_half = lax.dot_general(
             normed, keyval_weight, (((0,), (0,)), ((), ())), preferred_element_type=f32
         ).astype(bf16)
@@ -234,7 +238,7 @@
         ).astype(bf16)
         block_keys = jnp.where(core == 0, own_half, other_half).reshape(rows, block_len, HEAD)
         block_values = jnp.where(core == 0, other_half, own_half).reshape(rows, block_len, HEAD)
-        return attend(
+        attended = attend(
             queries.reshape(rows, block_len, -1, HEAD),
             cache_keys,
             cache_values,
@@ -242,13 +246,13 @@
             block_values,
             prefix_lengths,
         )
+        return attended, beside
 
     cotangent = lax.all_gather(learner_cotangent, TENSOR, axis=1, tiled=True)
     state = block_states.reshape(tokens, part).T
-    attended = attended_of(state)
+    attended, _ = attended_of(state)
     both = pair_order(swap_cores(attended, False), swap_cores(attended, True), role, 0)
-    attended_all = gather_ring(both)
-    cotangent, attended_all = lax.optimization_barrier((cotangent, attended_all))
+    attended_all, cotangent = gather_ring(both, cotangent)
 
     terms = gradient_terms(cotangent.T, learner_inputs)
     halves = lax.psum_scatter(terms, "dp", scatter_dimension=0, tiled=False)
@@ -259,24 +263,27 @@
     weight_part = new_weight.astype(bf16)
     weight_pair = pair_order(weight_part, rotate(weight_part, "core", 1), core, 0)
 
-    weight_both = pair_order(swap_cores(weight_part, False), swap_cores(weight_part, True), role, 0)
-    weight_all = lax.all_gather(weight_both, "dp", axis=0)
-
     partial = project(
         weight_pair.reshape(1, 2, 1, part, depth), attended_all.reshape(4, 2, 2, tokens, depth)
     )
+    weight_half, partial = lax.optimization_barrier((swap_cores(weight_part), partial))
+    weight_all = lax.all_gather(weight_half, "dp", axis=0)
     update = scatter_sum(partial)
     swap = [(a * 16 + b, b * 16 + a) for a in range(16) for b in range(16)]
     update = lax.ppermute(update.astype(bf16), EVERY, swap).astype(f32) * out_scale
     picks = position_picks.reshape(STEPS, 1, tokens)
     state = revise(state, update, picks[0], mask_part)
 
-    attended = attended_of(state)
+    attended, weight_all = attended_of(state, weight_all)
     attended_pair = pair_order(attended, rotate(attended, "core", 1), core, 0)
-    partial = project(
-        weight_all.reshape(4, 2, 2, part, depth), attended_pair.reshape(1, 2, 1, tokens, depth)
-    )
-    update = scatter_sum(partial) * out_scale
+    route = [(r * 2 + c, (1 - r) * 2 + 1 - c) for r in range(2) for c in range(2)]
+    far = lax.ppermute(attended, ("role", "core"), route)
+    far_pair = pair_order(rotate(attended, "role", 1), far, core, 0)
+    attended_four = pair_order(attended_pair, far_pair, role, 1)
+    partial = project(weight_all.reshape(4, 2, 1, part, depth), attended_four[None])
+    update = scatter_sum(partial).astype(bf16)
+    route = [(r * 4 + x, (x // 2) * 4 + r * 2 + x % 2) for r in range(2) for x in range(4)]
+    update = lax.ppermute(update, ("role", "x"), route).astype(f32) * out_scale
     state = revise(state, update, picks[1], mask_part)
     return (state.T.reshape(rows, block_len, part), new_weight.T, new_first.T, new_second.T)
 

time: 300 us -> 293 us (0.977)
  waiting for transfers between devices: 168 us -> 141 us
  blocking collectives: 16.3 us -> 33 us
  Pallas kernels: 15.5 us -> 21.5 us
  local copies, waits for them, and re-layouts: 19.8 us -> 16.5 us
    all_to_all x1 -> x2, blocking collectives: 16.3 us -> 33 us  [scatter_sum(): blocks = lax.all_to_all(parts, ('x', 'y'), 0, 0, tiled=True)]
    ppermute x4 -> x3, waiting for transfers between devices: 21.7 us -> 9.9 us  [swap_cores(): return lax.ppermute(block, ('role', 'dp', 'core'), route)]
    all_to_all x1 -> x0, waiting for transfers between devices: 10.7 us -> none  [scatter_sum(): blocks = lax.all_to_all(parts, ('x', 'y'), 0, 0, tiled=True)]
    ppermute x0 -> x2, waiting for transfers between devices: none -> 9.03 us  [the longest x1 7.17 us: on_device(): update = lax.ppermute(update, ('role', 'x'), route).astype(f32) * out_scale]
    pallas_call x1, Pallas kernels: 8.09 us -> 15.7 us  [gradient_terms(): pl.pallas_call(gradient_kernel, grid=(16,), in_specs=[pl.BlockSpec((part,...]
    unnamed x40 -> x42, local copies, waits for them, and re-layouts: 12.1 us -> 4.68 us
    ppermute x23 -> x24, waiting for transfers between devices: 60.4 us -> 54.4 us  [rotate(): lax.ppermute(block, axis, [(low, (low + shift) % count) for low in range(...]
    dynamic_update_slice x7 -> x8, local copies, waits for them, and re-layouts: 2.08 us -> 6.83 us  [the longest x5 4.87 us: gather_ring(): lax.dynamic_update_index_in_dim(whole, up[step], (me + 8 - step) % 8, 0)]
  transfers between devices with their start and end apart: 32 -> 33, of which waited for: 23 -> 20; matrix products, arithmetic and copies ran while one was open for 9% -> 8% of each run, Pallas kernels for 1% -> 1%
where the time goes in v3:
time: 293 us; the launch traced here: 292 us
  waiting for transfers between devices  141 us (48%)
  starting transfers between devices  41.7 us (14%)
  blocking collectives  33 us (11%)
  Pallas kernels  21.5 us (7%)
  local copies, waits for them, and re-layouts  16.5 us (6%)
  between operations  14.5 us (5%)
  other arithmetic  14.3 us (5%)
  matrix products  9.31 us (3%)
    reduce_scatter x1, waiting for transfers between devices, on_device(): halves = lax.psum_scatter(terms, 'dp', scatter_dimension=0, tiled=False)  60 us
    ppermute x24, waiting for transfers between devices, rotate(): lax.ppermute(block, axis, [(low, (low + shift) % count) for low in range(...  54.4 us
    all_to_all x2, blocking collectives, scatter_sum(): blocks = lax.all_to_all(parts, ('x', 'y'), 0, 0, tiled=True)  33 us
    ppermute x24, starting transfers between devices, rotate(): lax.ppermute(block, axis, [(low, (low + shift) % count) for low in range(...  30.2 us
    pallas_call x1, Pallas kernels, gradient_terms(): pl.pallas_call(gradient_kernel, grid=(16,), in_specs=[pl.BlockSpec((part,...  15.7 us
    ppermute x3, waiting for transfers between devices, swap_cores(): return lax.ppermute(block, ('role', 'dp', 'core'), route)  9.9 us
    ppermute x1, waiting for transfers between devices, on_device(): update = lax.ppermute(update, ('role', 'x'), route).astype(f32) * out_scale  7.17 us
  transfers between devices with their start and end apart: 33, of which 20 were waited for; matrix products, arithmetic and copies ran while one was open for 8% of the time, Pallas kernels for 1%

profile of v3, /device:TPU:16, one launch (start us, length us, event | category | flops | bytes accessed | tf_op | source)
XLA Modules:
  0.0 291.9 jit_solution(10959629910842389600)
XLA Ops:
  10.3 3.2 %collective-permute-done.1 = bf16[320,128]{1,0:T(8,128)(2,1)S(1)} collective-permute-done((bf16[320,128]{1,0:T(8,128)(2,1)S(1)}, bf16[320,128]{1,0:T(8,128)(2,1)S(1)}, u32[]{:S(2)}, u32[]{:S(2)}) %collective-permute-start.1) | collective-permute-done | bytes 81952 | tf_op jit(solution)/shard_map/ppermute | solution.py:27
  21.6 2.8 collective-permute-done.4
  42.7 9.9 %collective-permute-done.8 = bf16[128,512]{1,0:T(8,128)(2,1)S(1)} collective-permute-done((bf16[128,512]{1,0:T(8,128)(2,1)S(1)}, bf16[128,512]{1,0:T(8,128)(2,1)S(1)}, u32[]{:S(2)}, u32[]{:S(2)}) %collective-permute-start.8) | collective-permute-done | bytes 131104 | tf_op jit(solution)/shard_map/ppermute | solution.py:73
  53.3 3.2 %collective-permute-start.12 = (bf16[2,128,512]{2,1,0:T(8,128)(2,1)}, bf16[2,128,512]{2,1,0:T(8,128)(2,1)S(1)}, u32[]{:S(2)}, u32[]{:S(2)}) collective-permute-start(bf16[2,128,512]{2,1,0:T(8,128)(2,1)} %maximum_select_fusion.4), channel_id=1, source_target_pairs={{0,112},{16,0},{32,16},{48,32},{64,48},{80,64},{96,80},{112,96},{1... | collective-permute-start | bytes 786440 | tf_op jit(solution)/shard_map/ppermute | solution.py:27
  56.6 7.3 %collective-permute-done.9 = bf16[2,128,512]{2,1,0:T(8,128)(2,1)S(1)} collective-permute-done((bf16[2,128,512]{2,1,0:T(8,128)(2,1)}, bf16[2,128,512]{2,1,0:T(8,128)(2,1)S(1)}, u32[]{:S(2)}, u32[]{:S(2)}) %collective-permute-start.9) | collective-permute-done | bytes 262176 | tf_op jit(solution)/shard_map/ppermute | solution.py:27
  63.9 3.2 %collective-permute-start.13 = (bf16[2,128,512]{2,1,0:T(8,128)(2,1)S(1)}, bf16[2,128,512]{2,1,0:T(8,128)(2,1)S(1)}, u32[]{:S(2)}, u32[]{:S(2)}) collective-permute-start(bf16[2,128,512]{2,1,0:T(8,128)(2,1)S(1)} %collective-permute-done.12), channel_id=1, source_target_pairs={{0,112},{16,0},{32,16},{48,32},{64,48},{80,64},{96,80},{112,96},{1... | collective-permute-start | bytes 786440 | tf_op jit(solution)/shard_map/ppermute | solution.py:27
  67.1 6.2 %collective-permute-done.10 = bf16[2,128,512]{2,1,0:T(8,128)(2,1)S(1)} collective-permute-done((bf16[2,128,512]{2,1,0:T(8,128)(2,1)S(1)}, bf16[2,128,512]{2,1,0:T(8,128)(2,1)S(1)}, u32[]{:S(2)}, u32[]{:S(2)}) %collective-permute-start.10) | collective-permute-done | bytes 262176 | tf_op jit(solution)/shard_map/ppermute | solution.py:27
  74.1 3.2 %collective-permute-start.14 = (bf16[2,128,512]{2,1,0:T(8,128)(2,1)S(1)}, bf16[2,128,512]{2,1,0:T(8,128)(2,1)}, u32[]{:S(2)}, u32[]{:S(2)}) collective-permute-start(bf16[2,128,512]{2,1,0:T(8,128)(2,1)S(1)} %collective-permute-done.13), channel_id=1, source_target_pairs={{0,112},{16,0},{32,16},{48,32},{64,48},{80,64},{96,80},{112,96},{1... | collective-permute-start | bytes 786440 | tf_op jit(solution)/shard_map/ppermute | solution.py:27
  77.3 4.8 %collective-permute-done.11 = bf16[2,128,512]{2,1,0:T(8,128)(2,1)} collective-permute-done((bf16[2,128,512]{2,1,0:T(8,128)(2,1)S(1)}, bf16[2,128,512]{2,1,0:T(8,128)(2,1)}, u32[]{:S(2)}, u32[]{:S(2)}) %collective-permute-start.11) | collective-permute-done | bytes 262176 | tf_op jit(solution)/shard_map/ppermute | solution.py:27
  82.1 15.7 %shard_map.156 = bf16[8,2,320,512]{3,2,1,0:T(8,128)(2,1)} custom-call(bf16[5120,1024]{1,0:T(8,128)(2,1)} %bitcast.241, bf16[1024,512]{1,0:T(8,128)(2,1)} %inputs_ref.1), custom_call_target="tpu_custom_call" | custom-call | flops 5368709120 | bytes 17000000 | tf_op jit(solution)/shard_map/pallas_call | solution.py:106
  102.2 60.0 %reduce-scatter.2.cloned.1.call-done = bf16[1,2,320,512]{3,2,1,0:T(8,128)(2,1)} async-done(((bf16[8,2,320,512]{3,2,1,0:T(8,128)(2,1)}), bf16[1,2,320,512]{3,2,1,0:T(8,128)(2,1)}) %reduce-scatter.2.cloned.1.call-update) | async-done | bytes 655376 | tf_op jit(solution)/shard_map/reduce_scatter | solution.py:258
  165.8 8.5 %collective-permute-done.15 = bf16[320,512]{1,0:T(8,128)(2,1)S(1)} collective-permute-done((bf16[320,512]{1,0:T(8,128)(2,1)S(1)}, bf16[320,512]{1,0:T(8,128)(2,1)S(1)}, u32[]{:S(2)}, u32[]{:S(2)}) %collective-permute-start.15) | collective-permute-done | bytes 327712 | tf_op jit(solution)/shard_map/ppermute | solution.py:27
  174.4 2.8 fusion.44
  179.8 2.9 %shard_map.157 = bf16[2,4,320,128]{3,2,1,0:T(8,128)(2,1)S(1)} custom-call(bf16[1,2,1,320,512]{4,3,2,1,0:T(8,128)(2,1)S(1)} %maximum_select_fusion.2.weight_ref, bf16[4,2,2,128,512]{4,3,2,1,0:T(8,128)(2,1)S(1)} %bitcast.197), custom_call_target="tpu_custom_call" | custom-call | flops 671088640 | bytes 6000000 | tf_op jit(solution)/shard_map/pallas_call | solution.py:144
  183.6 15.8 %all_to_all.10 = bf16[8,320,128]{2,1,0:T(8,128)(2,1)S(1)} all-to-all(bf16[8,320,128]{2,1,0:T(8,128)(2,1)} %bitcast.199), channel_id=1, replica_groups=mesh['role'=2,'dp'=8,'x'=4,'y'=2,'core'=2] {'x','y'}, dimensions={0} | all-to-all | bytes 1310720 | tf_op jit(solution)/shard_map/all_to_all | solution.py:93
  199.4 3.9 %collective-permute-start.19 = (bf16[320,128]{1,0:T(8,128)(2,1)S(1)}, bf16[320,128]{1,0:T(8,128)(2,1)S(1)}, u32[]{:S(2)}, u32[]{:S(2)}) collective-permute-start(bf16[320,128]{1,0:T(8,128)(2,1)S(1)} %reduce_sum.81), channel_id=1, source_target_pairs={{0,0},{1,16},{2,32},{3,48},{4,64},{5,80},{6,96},{7,112},{8,128},{9... | collective-permute-start | bytes 245768 | tf_op jit(solution)/shard_map/ppermute | solution.py:273
  204.3 5.7 %collective-permute-done.19 = bf16[320,128]{1,0:T(8,128)(2,1)S(1)} collective-permute-done((bf16[320,128]{1,0:T(8,128)(2,1)S(1)}, bf16[320,128]{1,0:T(8,128)(2,1)S(1)}, u32[]{:S(2)}, u32[]{:S(2)}) %collective-permute-start.19) | collective-permute-done | bytes 81952 | tf_op jit(solution)/shard_map/ppermute | solution.py:273
  210.1 6.8 %collective-permute-start.20 = (bf16[320,128]{1,0:T(8,128)(2,1)S(1)}, bf16[320,128]{1,0:T(8,128)(2,1)S(1)}, u32[]{:S(2)}, u32[]{:S(2)}) collective-permute-start(bf16[320,128]{1,0:T(8,128)(2,1)S(1)} %fusion.30), channel_id=1, source_target_pairs={{0,2},{2,0},{1,3},{3,1},{4,6},{6,4},{5,7},{7,5},{8,10},{10,8},{9,1... | collective-permute-start | bytes 245768 | tf_op jit(solution)/shard_map/ppermute | solution.py:27
  223.0 6.8 %collective-permute-done.21 = bf16[2,320,128]{2,1,0:T(8,128)(2,1)S(1)} collective-permute-done((bf16[2,320,128]{2,1,0:T(8,128)(2,1)S(1)}, bf16[2,320,128]{2,1,0:T(8,128)(2,1)S(1)}, u32[]{:S(2)}, u32[]{:S(2)}) %collective-permute-start.21) | collective-permute-done | bytes 163872 | tf_op jit(solution)/shard_map/ppermute | solution.py:27
  245.9 4.4 %collective-permute-done.27 = bf16[128,512]{1,0:T(8,128)(2,1)S(1)} collective-permute-done((bf16[128,512]{1,0:T(8,128)(2,1)S(1)}, bf16[128,512]{1,0:T(8,128)(2,1)S(1)}, u32[]{:S(2)}, u32[]{:S(2)}) %collective-permute-start.27) | collective-permute-done | bytes 131104 | tf_op jit(solution)/shard_map/ppermute | solution.py:27
  254.1 2.8 shard_map.158
  256.9 17.3 %all_to_all.11 = bf16[8,320,128]{2,1,0:T(8,128)(2,1)S(1)} all-to-all(bf16[8,320,128]{2,1,0:T(8,128)(2,1)S(1)} %bitcast.200), channel_id=1, replica_groups=mesh['role'=2,'dp'=8,'x'=4,'y'=2,'core'=2] {'x','y'}, dimensions={0} | all-to-all | bytes 1310720 | tf_op jit(solution)/shard_map/all_to_all | solution.py:93
  274.3 2.9 collective-permute-start.29
  277.3 7.2 %collective-permute-done.29 = bf16[320,128]{1,0:T(8,128)(2,1)S(1)} collective-permute-done((bf16[320,128]{1,0:T(8,128)(2,1)S(1)}, bf16[320,128]{1,0:T(8,128)(2,1)S(1)}, u32[]{:S(2)}, u32[]{:S(2)}) %collective-permute-start.29) | collective-permute-done | bytes 81952 | tf_op jit(solution)/shard_map/ppermute | solution.py:286
  (171 shorter events, 70.3 us)
Async XLA Ops:
  7.2 74.9 %all-gather.4.cloned.1.call-start = ((), (), s32[]{:S(2)}) async-start(), calls=%async_computation.3 | async-start | bytes 11141120 | tf_op jit(solution)/shard_map/all_gather | solution.py:251
  7.9 154.2 %reduce-scatter.2.cloned.1.call-start = ((), (), s32[]{:S(2)}) async-start(), calls=%async_computation.4 | async-start | bytes 5898240 | tf_op jit(solution)/shard_map/reduce_scatter | solution.py:258
  13.5 8.0 %collective-permute-start.2 = (bf16[2,320,128]{2,1,0:T(8,128)(2,1)S(1)}, bf16[2,320,128]{2,1,0:T(8,128)(2,1)S(1)}, u32[]{:S(2)}, u32[]{:S(2)}) collective-permute-start(bf16[2,320,128]{2,1,0:T(8,128)(2,1)S(1)} %maximum_select_fusion.7), channel_id=1, source_target_pairs={{0,4},{4,8},{8,12},{12,0},{1,5},{5,9},{9,13},{13,1},{2,6},{6,10},{... | collective-permute-start | bytes 491528 | tf_op jit(solution)/shard_map/ppermute | solution.py:27
  15.1 6.4 %collective-permute-start.3 = (bf16[2,320,128]{2,1,0:T(8,128)(2,1)S(1)}, bf16[2,320,128]{2,1,0:T(8,128)(2,1)S(1)}, u32[]{:S(2)}, u32[]{:S(2)}) collective-permute-start(bf16[2,320,128]{2,1,0:T(8,128)(2,1)S(1)} %maximum_select_fusion.7), channel_id=1, source_target_pairs={{0,12},{4,0},{8,4},{12,8},{1,13},{5,1},{9,5},{13,9},{2,14},{6,2},{... | collective-permute-start | bytes 491528 | tf_op jit(solution)/shard_map/ppermute | solution.py:27
  16.8 7.5 %collective-permute-start.4 = (bf16[2,320,128]{2,1,0:T(8,128)(2,1)S(1)}, bf16[2,320,128]{2,1,0:T(8,128)(2,1)S(1)}, u32[]{:S(2)}, u32[]{:S(2)}) collective-permute-start(bf16[2,320,128]{2,1,0:T(8,128)(2,1)S(1)} %maximum_select_fusion.7), channel_id=1, source_target_pairs={{0,8},{4,12},{8,0},{12,4},{1,9},{5,13},{9,1},{13,5},{2,10},{6,14},... | collective-permute-start | bytes 491528 | tf_op jit(solution)/shard_map/ppermute | solution.py:27
  24.5 13.2 %collective-permute-start = (bf16[4,512,128]{2,1,0:T(8,128)(2,1)}, bf16[4,512,128]{2,1,0:T(8,128)(2,1)}, u32[]{:S(2)}, u32[]{:S(2)}) collective-permute-start(bf16[4,512,128]{2,1,0:T(8,128)(2,1)} %param.20), channel_id=1, source_target_pairs={{0,1},{1,0},{2,3},{3,2},{4,5},{5,4},{6,7},{7,6},{8,9},{9,8},{10,11... | collective-permute-start | bytes 1572872 | tf_op jit(solution)/shard_map/ppermute | solution.py:27
  41.9 10.7 %collective-permute-start.8 = (bf16[128,512]{1,0:T(8,128)(2,1)S(1)}, bf16[128,512]{1,0:T(8,128)(2,1)S(1)}, u32[]{:S(2)}, u32[]{:S(2)}) collective-permute-start(bf16[128,512]{1,0:T(8,128)(2,1)S(1)} %bitcast.234), channel_id=1, source_target_pairs={{0,128},{1,144},{16,129},{17,145},{32,160},{33,176},{48,161},{49,1... | collective-permute-start | bytes 393224 | tf_op jit(solution)/shard_map/ppermute | solution.py:73
  53.3 10.5 %collective-permute-start.9 = (bf16[2,128,512]{2,1,0:T(8,128)(2,1)}, bf16[2,128,512]{2,1,0:T(8,128)(2,1)S(1)}, u32[]{:S(2)}, u32[]{:S(2)}) collective-permute-start(bf16[2,128,512]{2,1,0:T(8,128)(2,1)} %maximum_select_fusion.4), channel_id=1, source_target_pairs={{0,16},{16,32},{32,48},{48,64},{64,80},{80,96},{96,112},{112,0},{1... | collective-permute-start | bytes 786440 | tf_op jit(solution)/shard_map/ppermute | solution.py:27
  53.3 10.5 %collective-permute-start.12 = (bf16[2,128,512]{2,1,0:T(8,128)(2,1)}, bf16[2,128,512]{2,1,0:T(8,128)(2,1)S(1)}, u32[]{:S(2)}, u32[]{:S(2)}) collective-permute-start(bf16[2,128,512]{2,1,0:T(8,128)(2,1)} %maximum_select_fusion.4), channel_id=1, source_target_pairs={{0,112},{16,0},{32,16},{48,32},{64,48},{80,64},{96,80},{112,96},{1... | collective-permute-start | bytes 786440 | tf_op jit(solution)/shard_map/ppermute | solution.py:27
  63.9 9.4 %collective-permute-start.10 = (bf16[2,128,512]{2,1,0:T(8,128)(2,1)S(1)}, bf16[2,128,512]{2,1,0:T(8,128)(2,1)S(1)}, u32[]{:S(2)}, u32[]{:S(2)}) collective-permute-start(bf16[2,128,512]{2,1,0:T(8,128)(2,1)S(1)} %collective-permute-done.9), channel_id=1, source_target_pairs={{0,16},{16,32},{32,48},{48,64},{64,80},{80,96},{96,112},{112,0},{1... | collective-permute-start | bytes 786440 | tf_op jit(solution)/shard_map/ppermute | solution.py:27
  63.9 9.4 %collective-permute-start.13 = (bf16[2,128,512]{2,1,0:T(8,128)(2,1)S(1)}, bf16[2,128,512]{2,1,0:T(8,128)(2,1)S(1)}, u32[]{:S(2)}, u32[]{:S(2)}) collective-permute-start(bf16[2,128,512]{2,1,0:T(8,128)(2,1)S(1)} %collective-permute-done.12), channel_id=1, source_target_pairs={{0,112},{16,0},{32,16},{48,32},{64,48},{80,64},{96,80},{112,96},{1... | collective-permute-start | bytes 786440 | tf_op jit(solution)/shard_map/ppermute | solution.py:27
  73.3 8.7 %collective-permute-start.11 = (bf16[2,128,512]{2,1,0:T(8,128)(2,1)S(1)}, bf16[2,128,512]{2,1,0:T(8,128)(2,1)}, u32[]{:S(2)}, u32[]{:S(2)}) collective-permute-start(bf16[2,128,512]{2,1,0:T(8,128)(2,1)S(1)} %collective-permute-done.10), channel_id=1, source_target_pairs={{0,16},{16,32},{32,48},{48,64},{64,80},{80,96},{96,112},{112,0},{1... | collective-permute-start | bytes 786440 | tf_op jit(solution)/shard_map/ppermute | solution.py:27
  74.1 8.0 %collective-permute-start.14 = (bf16[2,128,512]{2,1,0:T(8,128)(2,1)S(1)}, bf16[2,128,512]{2,1,0:T(8,128)(2,1)}, u32[]{:S(2)}, u32[]{:S(2)}) collective-permute-start(bf16[2,128,512]{2,1,0:T(8,128)(2,1)S(1)} %collective-permute-done.13), channel_id=1, source_target_pairs={{0,112},{16,0},{32,16},{48,32},{64,48},{80,64},{96,80},{112,96},{1... | collective-permute-start | bytes 786440 | tf_op jit(solution)/shard_map/ppermute | solution.py:27
  97.8 133.5 %all-gather.6.cloned.1.call-start = ((), (), s32[]{:S(2)}) async-start(), calls=%async_computation.5 | async-start | bytes 2949120 | tf_op jit(solution)/shard_map/all_gather | solution.py:270
  98.0 65.9 %collective-permute-start.18 = (bf16[2,128,512]{2,1,0:T(8,128)(2,1)}, bf16[2,128,512]{2,1,0:T(8,128)(2,1)}, u32[]{:S(2)}, u32[]{:S(2)}) collective-permute-start(bf16[2,128,512]{2,1,0:T(8,128)(2,1)} %collective-permute-done.11), channel_id=1, source_target_pairs={{0,16},{16,32},{32,48},{48,64},{64,80},{80,96},{96,112},{112,0},{1... | collective-permute-start | bytes 786440 | tf_op jit(solution)/shard_map/ppermute | solution.py:27
  163.3 11.1 %collective-permute-start.15 = (bf16[320,512]{1,0:T(8,128)(2,1)S(1)}, bf16[320,512]{1,0:T(8,128)(2,1)S(1)}, u32[]{:S(2)}, u32[]{:S(2)}) collective-permute-start(bf16[320,512]{1,0:T(8,128)(2,1)S(1)} %dynamic-slice_bitcast_fusion), channel_id=1, source_target_pairs={{0,128},{128,0},{1,129},{129,1},{2,130},{130,2},{3,131},{131,3},{4... | collective-permute-start | bytes 983048 | tf_op jit(solution)/shard_map/ppermute | solution.py:27
  199.4 10.5 %collective-permute-start.19 = (bf16[320,128]{1,0:T(8,128)(2,1)S(1)}, bf16[320,128]{1,0:T(8,128)(2,1)S(1)}, u32[]{:S(2)}, u32[]{:S(2)}) collective-permute-start(bf16[320,128]{1,0:T(8,128)(2,1)S(1)} %reduce_sum.81), channel_id=1, source_target_pairs={{0,0},{1,16},{2,32},{3,48},{4,64},{5,80},{6,96},{7,112},{8,128},{9... | collective-permute-start | bytes 245768 | tf_op jit(solution)/shard_map/ppermute | solution.py:273
  210.1 9.3 %collective-permute-start.20 = (bf16[320,128]{1,0:T(8,128)(2,1)S(1)}, bf16[320,128]{1,0:T(8,128)(2,1)S(1)}, u32[]{:S(2)}, u32[]{:S(2)}) collective-permute-start(bf16[320,128]{1,0:T(8,128)(2,1)S(1)} %fusion.30), channel_id=1, source_target_pairs={{0,2},{2,0},{1,3},{3,1},{4,6},{6,4},{5,7},{7,5},{8,10},{10,8},{9,1... | collective-permute-start | bytes 245768 | tf_op jit(solution)/shard_map/ppermute | solution.py:27
  219.4 10.4 %collective-permute-start.21 = (bf16[2,320,128]{2,1,0:T(8,128)(2,1)S(1)}, bf16[2,320,128]{2,1,0:T(8,128)(2,1)S(1)}, u32[]{:S(2)}, u32[]{:S(2)}) collective-permute-start(bf16[2,320,128]{2,1,0:T(8,128)(2,1)S(1)} %maximum_select_fusion.9), channel_id=1, source_target_pairs={{0,4},{4,8},{8,12},{12,0},{1,5},{5,9},{9,13},{13,1},{2,6},{6,10},{... | collective-permute-start | bytes 491528 | tf_op jit(solution)/shard_map/ppermute | solution.py:27
  220.7 9.1 %collective-permute-start.22 = (bf16[2,320,128]{2,1,0:T(8,128)(2,1)S(1)}, bf16[2,320,128]{2,1,0:T(8,128)(2,1)S(1)}, u32[]{:S(2)}, u32[]{:S(2)}) collective-permute-start(bf16[2,320,128]{2,1,0:T(8,128)(2,1)S(1)} %maximum_select_fusion.9), channel_id=1, source_target_pairs={{0,12},{4,0},{8,4},{12,8},{1,13},{5,1},{9,5},{13,9},{2,14},{6,2},{... | collective-permute-start | bytes 491528 | tf_op jit(solution)/shard_map/ppermute | solution.py:27
  222.7 7.1 %collective-permute-start.23 = (bf16[2,320,128]{2,1,0:T(8,128)(2,1)S(1)}, bf16[2,320,128]{2,1,0:T(8,128)(2,1)S(1)}, u32[]{:S(2)}, u32[]{:S(2)}) collective-permute-start(bf16[2,320,128]{2,1,0:T(8,128)(2,1)S(1)} %maximum_select_fusion.9), channel_id=1, source_target_pairs={{0,8},{4,12},{8,0},{12,4},{1,9},{5,13},{9,1},{13,5},{2,10},{6,14},... | collective-permute-start | bytes 491528 | tf_op jit(solution)/shard_map/ppermute | solution.py:27
  242.5 7.9 %collective-permute-start.27 = (bf16[128,512]{1,0:T(8,128)(2,1)S(1)}, bf16[128,512]{1,0:T(8,128)(2,1)S(1)}, u32[]{:S(2)}, u32[]{:S(2)}) collective-permute-start(bf16[128,512]{1,0:T(8,128)(2,1)S(1)} %bitcast.231), channel_id=1, source_target_pairs={{0,128},{128,0},{1,129},{129,1},{2,130},{130,2},{3,131},{131,3},{4... | collective-permute-start | bytes 393224 | tf_op jit(solution)/shard_map/ppermute | solution.py:27
  244.2 8.0 %collective-permute-start.28 = (bf16[128,512]{1,0:T(8,128)(2,1)S(1)}, bf16[128,512]{1,0:T(8,128)(2,1)S(1)}, u32[]{:S(2)}, u32[]{:S(2)}) collective-permute-start(bf16[128,512]{1,0:T(8,128)(2,1)S(1)} %bitcast.232), channel_id=1, source_target_pairs={{0,129},{1,128},{128,1},{129,0},{2,131},{3,130},{130,3},{131,2},{4... | collective-permute-start | bytes 393224 | tf_op jit(solution)/shard_map/ppermute | solution.py:280
  274.3 10.2 %collective-permute-start.29 = (bf16[320,128]{1,0:T(8,128)(2,1)S(1)}, bf16[320,128]{1,0:T(8,128)(2,1)S(1)}, u32[]{:S(2)}, u32[]{:S(2)}) collective-permute-start(bf16[320,128]{1,0:T(8,128)(2,1)S(1)} %reduce_sum.85), channel_id=1, source_target_pairs={{0,0},{4,4},{8,128},{12,132},{128,8},{132,12},{136,136},{140,140},... | collective-permute-start | bytes 245768 | tf_op jit(solution)/shard_map/ppermute | solution.py:286
  (29 other events, 203.2 us)
Sparse Core Ops, SparseCore 0:
  9.9 69.8 all-gather.3
  97.9 64.1 reduce-scatter.1
  183.7 47.5 all-gather.5

commit v4 on v3

--- a/solution.py
+++ b/solution.py
@@ -18,12 +18,13 @@
 NORM_EPS = 1e-06
 
 RD = ("role", "dp")
-TENSOR = ("x", "y", "core")
+X = ("x1", "x0")
+TENSOR = X + ("y", "core")
 EVERY = RD + TENSOR
 
 
 def rotate(block, axis, shift):
-    count = lax.axis_size(axis)
+    count = 4 if axis == X else lax.axis_size(axis)
     return lax.ppermute(block, axis, [(low, (low + shift) % count) for low in range(count)])
 
 
@@ -46,18 +47,18 @@
     return (weight_new, first_new, second_new)
 
 
-def gather_features(part, beside=None):
-    iy, ix, ic = lax.axis_index("y"), lax.axis_index("x"), lax.axis_index("core")
-    rows = pair_order(part, rotate(part, "y", 1), iy, 0)
-    ahead, back, across = rotate(rows, "x", 1), rotate(rows, "x", -1), rotate(rows, "x", 2)
+def gather_features(part, shift_x, shift_y, beside=None):
+    iy, ix, ic = lax.axis_index("y"), lax.axis_index(X), lax.axis_index("core")
+    rows = pair_order(part, rotate(part, "y", 1), iy ^ shift_y, 0)
+    ahead, back, across = rotate(rows, X, 1), rotate(rows, X, -1), rotate(rows, X, 2)
     square = jnp.zeros((4,) + rows.shape, rows.dtype)
-    square = lax.dynamic_update_index_in_dim(square, rows, ix, 0)
-    square = lax.dynamic_update_index_in_dim(square, ahead, (ix + 3) % 4, 0)
-    square = lax.dynamic_update_index_in_dim(square, back, (ix + 1) % 4, 0)
-    square = lax.dynamic_update_index_in_dim(square, across, (ix + 2) % 4, 0)
+    square = lax.dynamic_update_index_in_dim(square, rows, ix ^ shift_x, 0)
+    square = lax.dynamic_update_index_in_dim(square, ahead, ((ix + 3) % 4) ^ shift_x, 0)
+    square = lax.dynamic_update_index_in_dim(square, back, ((ix + 1) % 4) ^ shift_x, 0)
+    square = lax.dynamic_update_index_in_dim(square, across, ((ix + 2) % 4) ^ shift_x, 0)
     square, beside = lax.optimization_barrier((square, beside))
     whole = pair_order(square, rotate(square, "core", 1), ic, 2)
-    return whole.reshape(-1, part.shape[-1]), beside
+    return whole.reshape((16,) + part.shape), beside
 
 
 def swap_cores(block, flip_role=False):
@@ -75,6 +76,7 @@
 
 def gather_ring(block, before):
     me = lax.axis_index("dp")
+    high = me - me % 2
     up, down = [block], [block]
     for step in range(3):
         up.append(rotate(up[-1], "dp", 1))
@@ -83,40 +85,15 @@
     up.append(rotate(up[-1], "dp", 1))
     whole = jnp.zeros((8,) + block.shape, block.dtype)
     for step in range(5):
-        whole = lax.dynamic_update_index_in_dim(whole, up[step], (me + 8 - step) % 8, 0)
+        whole = lax.dynamic_update_index_in_dim(whole, up[step], ((me + 8 - step) % 8) ^ high, 0)
     for step in range(1, 4):
-        whole = lax.dynamic_update_index_in_dim(whole, down[step], (me + step) % 8, 0)
+        whole = lax.dynamic_update_index_in_dim(whole, down[step], ((me + step) % 8) ^ high, 0)
     return whole, before
 
 
 def scatter_sum(parts):
-    blocks = lax.all_to_all(parts, ("x", "y"), 0, 0, tiled=True)
+    blocks = lax.all_to_all(parts, X + ("y",), 0, 0, tiled=True)
     return jnp.sum(blocks.astype(jnp.float32), axis=0)
-
-
-def gradient_kernel(cotangent_ref, inputs_ref, out_ref):
-    out_ref[0, 0] = jnp.dot(
-        cotangent_ref[...], inputs_ref[...], preferred_element_type=jnp.float32
-    ).astype(out_ref.dtype)
-
-
-def gradient_terms(cotangent, inputs):
-    tokens, depth = inputs.shape
-    part = cotangent.shape[0] // 16
-    return pl.pallas_call(
-        gradient_kernel,
-        grid=(16,),
-        in_specs=[
-            pl.BlockSpec((part, tokens), lambda j: (j, 0)),
-            pl.BlockSpec((tokens, depth), lambda j: (0, 0)),
-        ],
-        out_specs=pl.BlockSpec((1, 1, part, depth), lambda j: (j % 8, j // 8, 0, 0)),
-        out_shape=jax.ShapeDtypeStruct((8, 2, part, depth), jnp.bfloat16),
-        compiler_params=pltpu.CompilerParams(vmem_limit_bytes=60 * 1024 * 1024),
-        cost_estimate=pl.CostEstimate(
-            flops=2 * 16 * part * tokens * depth, bytes_accessed=17_000_000, transcendentals=0
-        ),
-    )(cotangent, inputs)
 
 
 def project_kernel(weight_ref, tokens_ref, out_ref):
@@ -215,7 +192,7 @@
     position_picks,
 ):
     bf16, f32 = jnp.bfloat16, jnp.float32
-    role, core = lax.axis_index("role"), lax.axis_index("core")
+    role, core, dp = lax.axis_index("role"), lax.axis_index("core"), lax.axis_index("dp")
     rows, block_len, part = block_states.shape
     tokens = rows * block_len
     depth = learner_inputs.shape[1]
@@ -224,11 +201,12 @@
     cache_other = rotate(prefix_cache, "core", 1)
     cache_keys = jnp.where(core == 0, prefix_cache, cache_other)
     cache_values = jnp.where(core == 0, cache_other, prefix_cache)
-    mask_part = lax.dynamic_slice_in_dim(mask_vector, lax.axis_index(TENSOR) * part, part, 0)
-
-    def attended_of(state, beside=None):
-        whole, beside = gather_features(state, beside)
-        normed = normalize(whole, norm_gain)
+
+    def mask_of(block):
+        return lax.dynamic_slice_in_dim(mask_vector, block * part, part, 0)
+
+    def attended_of(whole):
+        normed = normalize(whole.reshape(-1, tokens), norm_gain)
         own_half = lax.dot_general(
             normed, keyval_weight, (((0,), (0,)), ((), ())), preferred_element_type=f32
         ).astype(bf16)
@@ -238,7 +216,7 @@
         ).astype(bf16)
         block_keys = jnp.where(core == 0, own_half, other_half).reshape(rows, block_len, HEAD)
         block_values = jnp.where(core == 0, other_half, own_half).reshape(rows, block_len, HEAD)
-        attended = attend(
+        return attend(
             queries.reshape(rows, block_len, -1, HEAD),
             cache_keys,
             cache_values,
@@ -246,15 +224,16 @@
             block_values,
             prefix_lengths,
         )
-        return attended, beside
-
-    cotangent = lax.all_gather(learner_cotangent, TENSOR, axis=1, tiled=True)
-    state = block_states.reshape(tokens, part).T
-    attended, _ = attended_of(state)
-    both = pair_order(swap_cores(attended, False), swap_cores(attended, True), role, 0)
+    cotangent = lax.all_gather(learner_cotangent, ("x0", "y", "core", "x1"), axis=1, tiled=True)
+    whole, _ = gather_features(block_states.reshape(tokens, part).T, 0, 0)
+    attended = attended_of(whole)
+    both = jnp.stack([swap_cores(attended), swap_cores(attended, True)])
     attended_all, cotangent = gather_ring(both, cotangent)
 
-    terms = gradient_terms(cotangent.T, learner_inputs)
+    terms = lax.dot_general(
+        cotangent, learner_inputs, (((0,), (0,)), ((), ())), preferred_element_type=f32
+    ).astype(bf16)
+    terms = terms.reshape(8, 2, part, depth)
     halves = lax.psum_scatter(terms, "dp", scatter_dimension=0, tiled=False)
     gradient = pick(halves, role).astype(f32) + rotate(pick(halves, 1 - role), "role", 1).astype(f32)
     new_weight, new_first, new_second = adam_update(
@@ -268,13 +247,20 @@
     )
     weight_half, partial = lax.optimization_barrier((swap_cores(weight_part), partial))
     weight_all = lax.all_gather(weight_half, "dp", axis=0)
-    update = scatter_sum(partial)
-    swap = [(a * 16 + b, b * 16 + a) for a in range(16) for b in range(16)]
-    update = lax.ppermute(update.astype(bf16), EVERY, swap).astype(f32) * out_scale
+    update = scatter_sum(partial).astype(bf16)
+    route = []
+    for source in range(256):
+        r, d2, d1, d0, x1, x0, y, c = [source >> k & 1 for k in range(7, -1, -1)]
+        target = [r ^ x1, d2 ^ x0, d1 ^ y, c, x1, x0, y, d0]
+        route.append((source, sum(bit << 7 - k for k, bit in enumerate(target))))
+    update = lax.ppermute(update, EVERY, route).astype(f32) * out_scale
     picks = position_picks.reshape(STEPS, 1, tokens)
-    state = revise(state, update, picks[0], mask_part)
-
-    attended, weight_all = attended_of(state, weight_all)
+    shift_x, shift_y = role * 2 + dp // 4, dp // 2 % 2
+    block = ((lax.axis_index(X) ^ shift_x) * 2 + (lax.axis_index("y") ^ shift_y)) * 2 + core
+    state = revise(pick(whole, block), update, picks[0], mask_of(block))
+
+    whole, weight_all = gather_features(state, shift_x, shift_y, weight_all)
+    attended = attended_of(whole)
     attended_pair = pair_order(attended, rotate(attended, "core", 1), core, 0)
     route = [(r * 2 + c, (1 - r) * 2 + 1 - c) for r in range(2) for c in range(2)]
     far = lax.ppermute(attended, ("role", "core"), route)
@@ -282,14 +268,14 @@
     attended_four = pair_order(attended_pair, far_pair, role, 1)
     partial = project(weight_all.reshape(4, 2, 1, part, depth), attended_four[None])
     update = scatter_sum(partial).astype(bf16)
-    route = [(r * 4 + x, (x // 2) * 4 + r * 2 + x % 2) for r in range(2) for x in range(4)]
-    update = lax.ppermute(update, ("role", "x"), route).astype(f32) * out_scale
-    state = revise(state, update, picks[1], mask_part)
+    update = lax.ppermute(update, ("role", "x1"), [(0, 0), (1, 2), (2, 1), (3, 3)])
+    block = lax.axis_index(TENSOR)
+    state = revise(pick(whole, block), update.astype(f32) * out_scale, picks[1], mask_of(block))
     return (state.T.reshape(rows, block_len, part), new_weight.T, new_first.T, new_second.T)
 
 
 def solution(mesh):
-    fine = Mesh(mesh.devices.reshape(2, 8, 4, 2, 2), EVERY)
+    fine = Mesh(mesh.devices.reshape(2, 8, 2, 2, 2, 2), EVERY)
     weights = P(TENSOR, RD)
     return jax.shard_map(
         on_device,

time: 293 us -> 289 us (0.986)
  blocking collectives: 33 us -> 14.8 us
  starting transfers between devices: 41.7 us -> 58.2 us
  Pallas kernels: 21.5 us -> 5.75 us
  matrix products: 9.31 us -> 20.2 us
  waiting for transfers between devices: 141 us -> 145 us
    all_to_all x2 -> x1, blocking collectives: 33 us -> 14.8 us  [scatter_sum(): blocks = lax.all_to_all(parts, X + ('y',), 0, 0, tiled=True)]
    pallas_call x1 -> x0, Pallas kernels: 15.7 us -> none  [gradient_terms(): pl.pallas_call(gradient_kernel, grid=(16,), in_specs=[pl.BlockSpec((part,...]
    ppermute x24, starting transfers between devices: 30.2 us -> 43.2 us  [rotate(): lax.ppermute(block, axis, [(low, (low + shift) % count) for low in range(...]
    dot_general x0 -> x1, matrix products: none -> 11.3 us  [on_device(): lax.dot_general(cotangent, learner_inputs, (((0,), (0,)), ((), ())), pref...]
    all_to_all x0 -> x1, waiting for transfers between devices: none -> 11.1 us  [scatter_sum(): blocks = lax.all_to_all(parts, X + ('y',), 0, 0, tiled=True)]
    ppermute x2, waiting for transfers between devices: 12.8 us -> 6.13 us  [the longest x1 6.13 us: on_device(): lax.ppermute(update, ('role', 'x1'), [(0, 0), (1, 2), (2, 1), (3, 3)])]
    all_gather x1, waiting for transfers between devices: 0.02 us -> 5.44 us  [on_device(): lax.all_gather(learner_cotangent, ('x0', 'y', 'core', 'x1'), axis=1, tile...]
    all_to_all x0 -> x1, starting transfers between devices: none -> 4.9 us  [scatter_sum(): blocks = lax.all_to_all(parts, X + ('y',), 0, 0, tiled=True)]
  transfers between devices with their start and end apart: 33 -> 34, of which waited for: 20 -> 22; matrix products, arithmetic and copies ran while one was open for 8% -> 8% of each run, Pallas kernels for 1% -> 1%
where the time goes in v4:
time: 289 us; the launch traced here: 288 us
  waiting for transfers between devices  145 us (50%)
  starting transfers between devices  58.2 us (20%)
  matrix products  20.2 us (7%)
  local copies, waits for them, and re-layouts  16.4 us (6%)
  blocking collectives  14.8 us (5%)
  between operations  14.5 us (5%)
  other arithmetic  13.2 us (5%)
  Pallas kernels  5.75 us (2%)
    reduce_scatter x1, waiting for transfers between devices, on_device(): halves = lax.psum_scatter(terms, 'dp', scatter_dimension=0, tiled=False)  60.3 us
    ppermute x24, waiting for transfers between devices, rotate(): lax.ppermute(block, axis, [(low, (low + shift) % count) for low in range(...  51.8 us
    ppermute x24, starting transfers between devices, rotate(): lax.ppermute(block, axis, [(low, (low + shift) % count) for low in range(...  43.2 us
    all_to_all x1, blocking collectives, scatter_sum(): blocks = lax.all_to_all(parts, X + ('y',), 0, 0, tiled=True)  14.8 us
    dot_general x1, matrix products, on_device(): lax.dot_general(cotangent, learner_inputs, (((0,), (0,)), ((), ())), pref...  11.3 us
    all_to_all x1, waiting for transfers between devices, scatter_sum(): blocks = lax.all_to_all(parts, X + ('y',), 0, 0, tiled=True)  11.1 us
    ppermute x3, waiting for transfers between devices, swap_cores(): return lax.ppermute(block, ('role', 'dp', 'core'), route)  7.18 us
    ppermute x1, waiting for transfers between devices, on_device(): lax.ppermute(update, ('role', 'x1'), [(0, 0), (1, 2), (2, 1), (3, 3)])  6.13 us
  transfers between devices with their start and end apart: 34, of which 22 were waited for; matrix products, arithmetic and copies ran while one was open for 8% of the time, Pallas kernels for 1%

profile of v4, /device:TPU:16, one launch (start us, length us, event | category | flops | bytes accessed | tf_op | source)
XLA Modules:
  0.0 287.7 jit_solution(10810333817026671769)
XLA Ops:
  9.3 3.5 %collective-permute-done = bf16[320,128]{0,1:T(8,128)(2,1)S(1)} collective-permute-done((bf16[320,128]{0,1:T(8,128)(2,1)}, bf16[320,128]{0,1:T(8,128)(2,1)S(1)}, u32[]{:S(2)}, u32[]{:S(2)}) %collective-permute-start) | collective-permute-done | bytes 81952 | tf_op jit(solution)/shard_map/ppermute | solution.py:28
  39.3 7.2 %collective-permute-done.8 = bf16[128,512]{1,0:T(8,128)(2,1)S(1)} collective-permute-done((bf16[128,512]{1,0:T(8,128)(2,1)S(1)}, bf16[128,512]{1,0:T(8,128)(2,1)S(1)}, u32[]{:S(2)}, u32[]{:S(2)}) %collective-permute-start.8) | collective-permute-done | bytes 131104 | tf_op jit(solution)/shard_map/ppermute | solution.py:74
  48.8 5.2 %collective-permute-start.12 = (bf16[2,128,512]{2,1,0:T(8,128)(2,1)S(1)}, bf16[2,128,512]{2,1,0:T(8,128)(2,1)S(1)}, u32[]{:S(2)}, u32[]{:S(2)}) collective-permute-start(bf16[2,128,512]{2,1,0:T(8,128)(2,1)S(1)} %pad_maximum_fusion), channel_id=1, source_target_pairs={{0,112},{16,0},{32,16},{48,32},{64,48},{80,64},{96,80},{112,96},{1... | collective-permute-start | bytes 786440 | tf_op jit(solution)/shard_map/ppermute | solution.py:28
  54.0 4.3 %collective-permute-done.9 = bf16[2,128,512]{2,1,0:T(8,128)(2,1)S(1)} collective-permute-done((bf16[2,128,512]{2,1,0:T(8,128)(2,1)S(1)}, bf16[2,128,512]{2,1,0:T(8,128)(2,1)S(1)}, u32[]{:S(2)}, u32[]{:S(2)}) %collective-permute-start.9) | collective-permute-done | bytes 262176 | tf_op jit(solution)/shard_map/ppermute | solution.py:28
  58.3 3.8 %collective-permute-start.13 = (bf16[2,128,512]{2,1,0:T(8,128)(2,1)S(1)}, bf16[2,128,512]{2,1,0:T(8,128)(2,1)S(1)}, u32[]{:S(2)}, u32[]{:S(2)}) collective-permute-start(bf16[2,128,512]{2,1,0:T(8,128)(2,1)S(1)} %collective-permute-done.12), channel_id=1, source_target_pairs={{0,112},{16,0},{32,16},{48,32},{64,48},{80,64},{96,80},{112,96},{1... | collective-permute-start | bytes 786440 | tf_op jit(solution)/shard_map/ppermute | solution.py:28
  62.1 6.1 %collective-permute-done.10 = bf16[2,128,512]{2,1,0:T(8,128)(2,1)S(1)} collective-permute-done((bf16[2,128,512]{2,1,0:T(8,128)(2,1)S(1)}, bf16[2,128,512]{2,1,0:T(8,128)(2,1)S(1)}, u32[]{:S(2)}, u32[]{:S(2)}) %collective-permute-start.10) | collective-permute-done | bytes 262176 | tf_op jit(solution)/shard_map/ppermute | solution.py:28
  68.9 3.2 %collective-permute-start.14 = (bf16[2,128,512]{2,1,0:T(8,128)(2,1)S(1)}, bf16[2,128,512]{2,1,0:T(8,128)(2,1)}, u32[]{:S(2)}, u32[]{:S(2)}) collective-permute-start(bf16[2,128,512]{2,1,0:T(8,128)(2,1)S(1)} %collective-permute-done.13), channel_id=1, source_target_pairs={{0,112},{16,0},{32,16},{48,32},{64,48},{80,64},{96,80},{112,96},{1... | collective-permute-start | bytes 786440 | tf_op jit(solution)/shard_map/ppermute | solution.py:28
  72.1 4.7 %collective-permute-done.11 = bf16[2,128,512]{2,1,0:T(8,128)(2,1)} collective-permute-done((bf16[2,128,512]{2,1,0:T(8,128)(2,1)S(1)}, bf16[2,128,512]{2,1,0:T(8,128)(2,1)}, u32[]{:S(2)}, u32[]{:S(2)}) %collective-permute-start.11) | collective-permute-done | bytes 262176 | tf_op jit(solution)/shard_map/ppermute | solution.py:28
  76.9 5.4 %all-gather.4.cloned.1.call-done = bf16[1024,5120]{0,1:T(8,128)(2,1)} async-done(((bf16[1024,320]{0,1:T(8,128)(2,1)}), bf16[1024,5120]{0,1:T(8,128)(2,1)}) %all-gather.4.cloned.1.call-update) | async-done | bytes 10485776 | tf_op jit(solution)/shard_map/all_gather | solution.py:227
  82.3 11.3 %convolution_convert_fusion = bf16[5120,512]{1,0:T(8,128)(2,1)} fusion(bf16[1024,5120]{0,1:T(8,128)(2,1)} %all-gather.4.cloned.1.call-done, bf16[1024,512]{1,0:T(8,128)(2,1)S(1)} %copy-done.16), kind=kOutput, calls=%fused_computation | convolution fusion | flops 5371330560 | bytes 16777216 | tf_op jit(solution)/shard_map/dot_general | solution.py:233
  99.6 60.3 %reduce-scatter.2.cloned.1.call-done = bf16[1,2,320,512]{3,2,1,0:T(8,128)(2,1)} async-done(((bf16[8,2,320,512]{3,2,1,0:T(8,128)(2,1)}), bf16[1,2,320,512]{3,2,1,0:T(8,128)(2,1)}) %reduce-scatter.2.cloned.1.call-update) | async-done | bytes 655376 | tf_op jit(solution)/shard_map/reduce_scatter | solution.py:237
  163.6 8.5 %collective-permute-done.15 = bf16[320,512]{1,0:T(8,128)(2,1)S(1)} collective-permute-done((bf16[320,512]{1,0:T(8,128)(2,1)S(1)}, bf16[320,512]{1,0:T(8,128)(2,1)S(1)}, u32[]{:S(2)}, u32[]{:S(2)}) %collective-permute-start.15) | collective-permute-done | bytes 327712 | tf_op jit(solution)/shard_map/ppermute | solution.py:28
  177.5 2.9 %shard_map.156 = bf16[2,4,320,128]{3,2,1,0:T(8,128)(2,1)S(1)} custom-call(bf16[1,2,1,320,512]{4,3,2,1,0:T(8,128)(2,1)S(1)} %maximum_select_fusion.2.weight_ref, bf16[4,2,2,128,512]{4,3,2,1,0:T(8,128)(2,1)S(1)} %bitcast.204), custom_call_target="tpu_custom_call" | custom-call | flops 671088640 | bytes 6000000 | tf_op jit(solution)/shard_map/pallas_call | solution.py:121
  181.3 4.9 %all-to-all-start = ((bf16[8,320,128]{2,1,0:T(8,128)(2,1)}), bf16[8,320,128]{2,1,0:T(8,128)(2,1)S(1)}, u32[]{:S(2)}, u32[]{:S(2)}) async-start(bf16[8,320,128]{2,1,0:T(8,128)(2,1)} %bitcast.206), calls=%async_computation.1 | async-start | bytes 1310720 | tf_op jit(solution)/shard_map/all_to_all | solution.py:95
  186.4 11.1 %all-to-all-done = bf16[8,320,128]{2,1,0:T(8,128)(2,1)S(1)} async-done(((bf16[8,320,128]{2,1,0:T(8,128)(2,1)}), bf16[8,320,128]{2,1,0:T(8,128)(2,1)S(1)}, u32[]{:S(2)}, u32[]{:S(2)}) %all-to-all-start) | async-done | bytes 655392 | tf_op jit(solution)/shard_map/all_to_all | solution.py:95
  200.0 9.7 %collective-permute-start.20 = (bf16[320,128]{1,0:T(8,128)(2,1)S(1)}, bf16[320,128]{1,0:T(8,128)(2,1)S(1)}, u32[]{:S(2)}, u32[]{:S(2)}) collective-permute-start(bf16[320,128]{1,0:T(8,128)(2,1)S(1)} %fusion.28), channel_id=1, source_target_pairs={{0,2},{2,0},{1,3},{3,1},{4,6},{6,4},{5,7},{7,5},{8,10},{10,8},{9,1... | collective-permute-start | bytes 245768 | tf_op jit(solution)/shard_map/ppermute | solution.py:28
  209.7 3.0 %collective-permute-done.20 = bf16[320,128]{1,0:T(8,128)(2,1)S(1)} collective-permute-done((bf16[320,128]{1,0:T(8,128)(2,1)S(1)}, bf16[320,128]{1,0:T(8,128)(2,1)S(1)}, u32[]{:S(2)}, u32[]{:S(2)}) %collective-permute-start.20) | collective-permute-done | bytes 81952 | tf_op jit(solution)/shard_map/ppermute | solution.py:28
  212.8 4.5 %collective-permute-start.21 = (bf16[2,320,128]{2,1,0:T(8,128)(2,1)S(1)}, bf16[2,320,128]{2,1,0:T(8,128)(2,1)S(1)}, u32[]{:S(2)}, u32[]{:S(2)}) collective-permute-start(bf16[2,320,128]{2,1,0:T(8,128)(2,1)S(1)} %maximum_select_fusion.8), channel_id=1, source_target_pairs={{0,4},{4,8},{8,12},{12,0},{1,5},{5,9},{9,13},{13,1},{2,6},{6,10},{... | collective-permute-start | bytes 491528 | tf_op jit(solution)/shard_map/ppermute | solution.py:28
  221.3 3.4 %collective-permute-done.21 = bf16[2,320,128]{2,1,0:T(8,128)(2,1)S(1)} collective-permute-done((bf16[2,320,128]{2,1,0:T(8,128)(2,1)S(1)}, bf16[2,320,128]{2,1,0:T(8,128)(2,1)S(1)}, u32[]{:S(2)}, u32[]{:S(2)}) %collective-permute-start.21) | collective-permute-done | bytes 163872 | tf_op jit(solution)/shard_map/ppermute | solution.py:28
  224.7 2.9 collective-permute-done.22
  244.2 4.4 %collective-permute-done.27 = bf16[128,512]{1,0:T(8,128)(2,1)S(1)} collective-permute-done((bf16[128,512]{1,0:T(8,128)(2,1)S(1)}, bf16[128,512]{1,0:T(8,128)(2,1)S(1)}, u32[]{:S(2)}, u32[]{:S(2)}) %collective-permute-start.27) | collective-permute-done | bytes 131104 | tf_op jit(solution)/shard_map/ppermute | solution.py:28
  255.1 14.8 %all_to_all.10 = bf16[8,320,128]{2,1,0:T(8,128)(2,1)S(1)} all-to-all(bf16[8,320,128]{2,1,0:T(8,128)(2,1)S(1)} %bitcast.207), channel_id=1, replica_groups=mesh['role'=2,'dp'=8,'x1'=2,'x0'=2,'y'=2,'core'=2] {'x1','x0','y'}, dimensions={0} | all-to-all | bytes 1310720 | tf_op jit(solution)/shard_map/all_to_all | solution.py:95
  270.0 3.8 %collective-permute-start.29 = (bf16[320,128]{1,0:T(8,128)(2,1)S(1)}, bf16[320,128]{1,0:T(8,128)(2,1)S(1)}, u32[]{:S(2)}, u32[]{:S(2)}) collective-permute-start(bf16[320,128]{1,0:T(8,128)(2,1)S(1)} %reduce_sum.85), channel_id=1, source_target_pairs={{0,0},{8,128},{128,8},{136,136},{1,1},{9,129},{129,9},{137,137},{2... | collective-permute-start | bytes 245768 | tf_op jit(solution)/shard_map/ppermute | solution.py:271
  274.2 6.1 %collective-permute-done.29 = bf16[320,128]{1,0:T(8,128)(2,1)S(1)} collective-permute-done((bf16[320,128]{1,0:T(8,128)(2,1)S(1)}, bf16[320,128]{1,0:T(8,128)(2,1)S(1)}, u32[]{:S(2)}, u32[]{:S(2)}) %collective-permute-start.29) | collective-permute-done | bytes 81952 | tf_op jit(solution)/shard_map/ppermute | solution.py:271
  (176 shorter events, 78.0 us)
Async XLA Ops:
  7.2 75.1 %all-gather.4.cloned.1.call-start = ((), (), s32[]{:S(2)}) async-start(), calls=%async_computation.3 | async-start | bytes 11141120 | tf_op jit(solution)/shard_map/all_gather | solution.py:227
  7.9 152.0 %reduce-scatter.2.cloned.1.call-start = ((), (), s32[]{:S(2)}) async-start(), calls=%async_computation.4 | async-start | bytes 5898240 | tf_op jit(solution)/shard_map/reduce_scatter | solution.py:237
  13.9 8.5 %collective-permute-start.1 = (bf16[2,320,128]{1,2,0:T(8,128)(2,1)S(1)}, bf16[2,320,128]{1,2,0:T(8,128)(2,1)S(1)}, u32[]{:S(2)}, u32[]{:S(2)}) collective-permute-start(bf16[2,320,128]{1,2,0:T(8,128)(2,1)S(1)} %maximum_select_fusion.6), channel_id=1, source_target_pairs={{0,4},{4,8},{8,12},{12,0},{1,5},{5,9},{9,13},{13,1},{2,6},{6,10},{... | collective-permute-start | bytes 491528 | tf_op jit(solution)/shard_map/ppermute | solution.py:28
  15.5 8.7 %collective-permute-start.2 = (bf16[2,320,128]{1,2,0:T(8,128)(2,1)S(1)}, bf16[2,320,128]{1,2,0:T(8,128)(2,1)S(1)}, u32[]{:S(2)}, u32[]{:S(2)}) collective-permute-start(bf16[2,320,128]{1,2,0:T(8,128)(2,1)S(1)} %maximum_select_fusion.6), channel_id=1, source_target_pairs={{0,12},{4,0},{8,4},{12,8},{1,13},{5,1},{9,5},{13,9},{2,14},{6,2},{... | collective-permute-start | bytes 491528 | tf_op jit(solution)/shard_map/ppermute | solution.py:28
  17.2 8.7 %collective-permute-start.3 = (bf16[2,320,128]{1,2,0:T(8,128)(2,1)S(1)}, bf16[2,320,128]{1,2,0:T(8,128)(2,1)S(1)}, u32[]{:S(2)}, u32[]{:S(2)}) collective-permute-start(bf16[2,320,128]{1,2,0:T(8,128)(2,1)S(1)} %maximum_select_fusion.6), channel_id=1, source_target_pairs={{0,8},{4,12},{8,0},{12,4},{1,9},{5,13},{9,1},{13,5},{2,10},{6,14},... | collective-permute-start | bytes 491528 | tf_op jit(solution)/shard_map/ppermute | solution.py:28
  26.3 7.8 %collective-permute-start.5 = (bf16[4,512,128]{2,1,0:T(8,128)(2,1)}, bf16[4,512,128]{2,1,0:T(8,128)(2,1)}, u32[]{:S(2)}, u32[]{:S(2)}) collective-permute-start(bf16[4,512,128]{2,1,0:T(8,128)(2,1)} %param.20), channel_id=1, source_target_pairs={{0,1},{1,0},{2,3},{3,2},{4,5},{5,4},{6,7},{7,6},{8,9},{9,8},{10,11... | collective-permute-start | bytes 1572872 | tf_op jit(solution)/shard_map/ppermute | solution.py:28
  38.5 7.9 %collective-permute-start.8 = (bf16[128,512]{1,0:T(8,128)(2,1)S(1)}, bf16[128,512]{1,0:T(8,128)(2,1)S(1)}, u32[]{:S(2)}, u32[]{:S(2)}) collective-permute-start(bf16[128,512]{1,0:T(8,128)(2,1)S(1)} %bitcast.241), channel_id=1, source_target_pairs={{0,128},{1,144},{16,129},{17,145},{32,160},{33,176},{48,161},{49,1... | collective-permute-start | bytes 393224 | tf_op jit(solution)/shard_map/ppermute | solution.py:74
  46.5 11.8 %collective-permute-start.9 = (bf16[2,128,512]{2,1,0:T(8,128)(2,1)S(1)}, bf16[2,128,512]{2,1,0:T(8,128)(2,1)S(1)}, u32[]{:S(2)}, u32[]{:S(2)}) collective-permute-start(bf16[2,128,512]{2,1,0:T(8,128)(2,1)S(1)} %pad_maximum_fusion), channel_id=1, source_target_pairs={{0,16},{16,32},{32,48},{48,64},{64,80},{80,96},{96,112},{112,0},{1... | collective-permute-start | bytes 786440 | tf_op jit(solution)/shard_map/ppermute | solution.py:28
  48.8 9.5 %collective-permute-start.12 = (bf16[2,128,512]{2,1,0:T(8,128)(2,1)S(1)}, bf16[2,128,512]{2,1,0:T(8,128)(2,1)S(1)}, u32[]{:S(2)}, u32[]{:S(2)}) collective-permute-start(bf16[2,128,512]{2,1,0:T(8,128)(2,1)S(1)} %pad_maximum_fusion), channel_id=1, source_target_pairs={{0,112},{16,0},{32,16},{48,32},{64,48},{80,64},{96,80},{112,96},{1... | collective-permute-start | bytes 786440 | tf_op jit(solution)/shard_map/ppermute | solution.py:28
  58.3 9.9 %collective-permute-start.10 = (bf16[2,128,512]{2,1,0:T(8,128)(2,1)S(1)}, bf16[2,128,512]{2,1,0:T(8,128)(2,1)S(1)}, u32[]{:S(2)}, u32[]{:S(2)}) collective-permute-start(bf16[2,128,512]{2,1,0:T(8,128)(2,1)S(1)} %collective-permute-done.9), channel_id=1, source_target_pairs={{0,16},{16,32},{32,48},{48,64},{64,80},{80,96},{96,112},{112,0},{1... | collective-permute-start | bytes 786440 | tf_op jit(solution)/shard_map/ppermute | solution.py:28
  58.3 9.9 %collective-permute-start.13 = (bf16[2,128,512]{2,1,0:T(8,128)(2,1)S(1)}, bf16[2,128,512]{2,1,0:T(8,128)(2,1)S(1)}, u32[]{:S(2)}, u32[]{:S(2)}) collective-permute-start(bf16[2,128,512]{2,1,0:T(8,128)(2,1)S(1)} %collective-permute-done.12), channel_id=1, source_target_pairs={{0,112},{16,0},{32,16},{48,32},{64,48},{80,64},{96,80},{112,96},{1... | collective-permute-start | bytes 786440 | tf_op jit(solution)/shard_map/ppermute | solution.py:28
  68.2 8.7 %collective-permute-start.11 = (bf16[2,128,512]{2,1,0:T(8,128)(2,1)S(1)}, bf16[2,128,512]{2,1,0:T(8,128)(2,1)}, u32[]{:S(2)}, u32[]{:S(2)}) collective-permute-start(bf16[2,128,512]{2,1,0:T(8,128)(2,1)S(1)} %collective-permute-done.10), channel_id=1, source_target_pairs={{0,16},{16,32},{32,48},{48,64},{64,80},{80,96},{96,112},{112,0},{1... | collective-permute-start | bytes 786440 | tf_op jit(solution)/shard_map/ppermute | solution.py:28
  68.9 7.9 %collective-permute-start.14 = (bf16[2,128,512]{2,1,0:T(8,128)(2,1)S(1)}, bf16[2,128,512]{2,1,0:T(8,128)(2,1)}, u32[]{:S(2)}, u32[]{:S(2)}) collective-permute-start(bf16[2,128,512]{2,1,0:T(8,128)(2,1)S(1)} %collective-permute-done.13), channel_id=1, source_target_pairs={{0,112},{16,0},{32,16},{48,32},{64,48},{80,64},{96,80},{112,96},{1... | collective-permute-start | bytes 786440 | tf_op jit(solution)/shard_map/ppermute | solution.py:28
  93.6 135.7 %all-gather.6.cloned.1.call-start = ((), (), s32[]{:S(2)}) async-start(), calls=%async_computation.5 | async-start | bytes 2949120 | tf_op jit(solution)/shard_map/all_gather | solution.py:249
  93.8 67.8 %collective-permute-start.18 = (bf16[2,128,512]{2,1,0:T(8,128)(2,1)}, bf16[2,128,512]{2,1,0:T(8,128)(2,1)}, u32[]{:S(2)}, u32[]{:S(2)}) collective-permute-start(bf16[2,128,512]{2,1,0:T(8,128)(2,1)} %collective-permute-done.11), channel_id=1, source_target_pairs={{0,16},{16,32},{32,48},{48,64},{64,80},{80,96},{96,112},{112,0},{1... | collective-permute-start | bytes 786440 | tf_op jit(solution)/shard_map/ppermute | solution.py:28
  161.0 11.1 %collective-permute-start.15 = (bf16[320,512]{1,0:T(8,128)(2,1)S(1)}, bf16[320,512]{1,0:T(8,128)(2,1)S(1)}, u32[]{:S(2)}, u32[]{:S(2)}) collective-permute-start(bf16[320,512]{1,0:T(8,128)(2,1)S(1)} %dynamic-slice_bitcast_fusion), channel_id=1, source_target_pairs={{0,128},{128,0},{1,129},{129,1},{2,130},{130,2},{3,131},{131,3},{4... | collective-permute-start | bytes 983048 | tf_op jit(solution)/shard_map/ppermute | solution.py:28
  181.3 16.2 %all-to-all-start = ((bf16[8,320,128]{2,1,0:T(8,128)(2,1)}), bf16[8,320,128]{2,1,0:T(8,128)(2,1)S(1)}, u32[]{:S(2)}, u32[]{:S(2)}) async-start(bf16[8,320,128]{2,1,0:T(8,128)(2,1)} %bitcast.206), calls=%async_computation.1 | async-start | bytes 1310720 | tf_op jit(solution)/shard_map/all_to_all | solution.py:95
  200.0 12.7 %collective-permute-start.20 = (bf16[320,128]{1,0:T(8,128)(2,1)S(1)}, bf16[320,128]{1,0:T(8,128)(2,1)S(1)}, u32[]{:S(2)}, u32[]{:S(2)}) collective-permute-start(bf16[320,128]{1,0:T(8,128)(2,1)S(1)} %fusion.28), channel_id=1, source_target_pairs={{0,2},{2,0},{1,3},{3,1},{4,6},{6,4},{5,7},{7,5},{8,10},{10,8},{9,1... | collective-permute-start | bytes 245768 | tf_op jit(solution)/shard_map/ppermute | solution.py:28
  212.8 11.9 %collective-permute-start.21 = (bf16[2,320,128]{2,1,0:T(8,128)(2,1)S(1)}, bf16[2,320,128]{2,1,0:T(8,128)(2,1)S(1)}, u32[]{:S(2)}, u32[]{:S(2)}) collective-permute-start(bf16[2,320,128]{2,1,0:T(8,128)(2,1)S(1)} %maximum_select_fusion.8), channel_id=1, source_target_pairs={{0,4},{4,8},{8,12},{12,0},{1,5},{5,9},{9,13},{13,1},{2,6},{6,10},{... | collective-permute-start | bytes 491528 | tf_op jit(solution)/shard_map/ppermute | solution.py:28
  217.2 10.3 %collective-permute-start.22 = (bf16[2,320,128]{2,1,0:T(8,128)(2,1)S(1)}, bf16[2,320,128]{2,1,0:T(8,128)(2,1)S(1)}, u32[]{:S(2)}, u32[]{:S(2)}) collective-permute-start(bf16[2,320,128]{2,1,0:T(8,128)(2,1)S(1)} %maximum_select_fusion.8), channel_id=1, source_target_pairs={{0,12},{4,0},{8,4},{12,8},{1,13},{5,1},{9,5},{13,9},{2,14},{6,2},{... | collective-permute-start | bytes 491528 | tf_op jit(solution)/shard_map/ppermute | solution.py:28
  219.8 9.6 %collective-permute-start.23 = (bf16[2,320,128]{2,1,0:T(8,128)(2,1)S(1)}, bf16[2,320,128]{2,1,0:T(8,128)(2,1)S(1)}, u32[]{:S(2)}, u32[]{:S(2)}) collective-permute-start(bf16[2,320,128]{2,1,0:T(8,128)(2,1)S(1)} %maximum_select_fusion.8), channel_id=1, source_target_pairs={{0,8},{4,12},{8,0},{12,4},{1,9},{5,13},{9,1},{13,5},{2,10},{6,14},... | collective-permute-start | bytes 491528 | tf_op jit(solution)/shard_map/ppermute | solution.py:28
  240.7 7.9 %collective-permute-start.27 = (bf16[128,512]{1,0:T(8,128)(2,1)S(1)}, bf16[128,512]{1,0:T(8,128)(2,1)S(1)}, u32[]{:S(2)}, u32[]{:S(2)}) collective-permute-start(bf16[128,512]{1,0:T(8,128)(2,1)S(1)} %bitcast.238), channel_id=1, source_target_pairs={{0,128},{128,0},{1,129},{129,1},{2,130},{130,2},{3,131},{131,3},{4... | collective-permute-start | bytes 393224 | tf_op jit(solution)/shard_map/ppermute | solution.py:28
  241.5 8.9 %collective-permute-start.28 = (bf16[128,512]{1,0:T(8,128)(2,1)S(1)}, bf16[128,512]{1,0:T(8,128)(2,1)S(1)}, u32[]{:S(2)}, u32[]{:S(2)}) collective-permute-start(bf16[128,512]{1,0:T(8,128)(2,1)S(1)} %bitcast.239), channel_id=1, source_target_pairs={{0,129},{1,128},{128,1},{129,0},{2,131},{3,130},{130,3},{131,2},{4... | collective-permute-start | bytes 393224 | tf_op jit(solution)/shard_map/ppermute | solution.py:266
  270.0 10.2 %collective-permute-start.29 = (bf16[320,128]{1,0:T(8,128)(2,1)S(1)}, bf16[320,128]{1,0:T(8,128)(2,1)S(1)}, u32[]{:S(2)}, u32[]{:S(2)}) collective-permute-start(bf16[320,128]{1,0:T(8,128)(2,1)S(1)} %reduce_sum.85), channel_id=1, source_target_pairs={{0,0},{8,128},{128,8},{136,136},{1,1},{9,129},{129,9},{137,137},{2... | collective-permute-start | bytes 245768 | tf_op jit(solution)/shard_map/ppermute | solution.py:271
  (31 other events, 225.1 us)
Sparse Core Ops, SparseCore 0:
  9.8 72.4 all-gather.3
  93.8 66.1 reduce-scatter.1
  181.4 43.9 all-gather.5

commit v5 on v4

--- a/solution.py
+++ b/solution.py
@@ -47,9 +47,8 @@
     return (weight_new, first_new, second_new)
 
 
-def gather_features(part, shift_x, shift_y, beside=None):
-    iy, ix, ic = lax.axis_index("y"), lax.axis_index(X), lax.axis_index("core")
-    rows = pair_order(part, rotate(part, "y", 1), iy ^ shift_y, 0)
+def gather_rows(rows, shift_x, beside=None):
+    ix, ic = lax.axis_index(X), lax.axis_index("core")
     ahead, back, across = rotate(rows, X, 1), rotate(rows, X, -1), rotate(rows, X, 2)
     square = jnp.zeros((4,) + rows.shape, rows.dtype)
     square = lax.dynamic_update_index_in_dim(square, rows, ix ^ shift_x, 0)
@@ -57,8 +56,7 @@
     square = lax.dynamic_update_index_in_dim(square, back, ((ix + 1) % 4) ^ shift_x, 0)
     square = lax.dynamic_update_index_in_dim(square, across, ((ix + 2) % 4) ^ shift_x, 0)
     square, beside = lax.optimization_barrier((square, beside))
-    whole = pair_order(square, rotate(square, "core", 1), ic, 2)
-    return whole.reshape((16,) + part.shape), beside
+    return pair_order(square, rotate(square, "core", 1), ic, 2), beside
 
 
 def swap_cores(block, flip_role=False):
@@ -96,40 +94,120 @@
     return jnp.sum(blocks.astype(jnp.float32), axis=0)
 
 
-def project_kernel(weight_ref, tokens_ref, out_ref):
+def gradient_kernel(
+    cotangent_ref, inputs_ref, out_ref, cotangents, inputs, outs, inputs_sem, cotangent_sems, out_sems
+):
+    steps, block = cotangents.shape[:2]
+
+    def inputs_copy():
+        return pltpu.make_async_copy(inputs_ref, inputs, inputs_sem)
+
+    def cotangent_copy(i):
+        return pltpu.make_async_copy(
+            cotangent_ref.at[pl.ds(i * block, block)], cotangents.at[i], cotangent_sems.at[i]
+        )
+
+    def out_copy(i):
+        place = out_ref.at[pl.ds(2 * (i % (steps // 2)), 2), i // (steps // 2)]
+        return pltpu.make_async_copy(outs.at[i], place, out_sems.at[i])
+
+    cotangent_copy(0).start()
+    inputs_copy().start()
+    for i in range(1, steps):
+        cotangent_copy(i).start()
+    inputs_copy().wait()
+
+    def step(i, carry):
+        cotangent_copy(i).wait()
+        terms = jnp.dot(cotangents[i], inputs[...], preferred_element_type=jnp.float32)
+        outs[i] = terms.astype(outs.dtype).reshape(outs.shape[1:])
+        out_copy(i).start()
+        return carry
+
+    lax.fori_loop(0, steps, step, 0)
+    for i in range(steps):
+        out_copy(i).wait()
+
+
+def gradient_terms(cotangent, inputs):
+    tokens, depth = inputs.shape
+    part = cotangent.shape[0] // 16
+    steps = 8
+    return pl.pallas_call(
+        gradient_kernel,
+        in_specs=[pl.BlockSpec(memory_space=pl.ANY)] * 2,
+        out_specs=pl.BlockSpec(memory_space=pl.ANY),
+        out_shape=jax.ShapeDtypeStruct((8, 2, part, depth), jnp.bfloat16),
+        scratch_shapes=[
+            pltpu.VMEM((steps, 2 * part, tokens), jnp.bfloat16),
+            pltpu.VMEM((tokens, depth), jnp.bfloat16),
+            pltpu.VMEM((steps, 2, part, depth), jnp.bfloat16),
+            pltpu.SemaphoreType.DMA,
+            pltpu.SemaphoreType.DMA((steps,)),
+            pltpu.SemaphoreType.DMA((steps,)),
+        ],
+        compiler_params=pltpu.CompilerParams(vmem_limit_bytes=60 * 1024 * 1024),
+        cost_estimate=pl.CostEstimate(
+            flops=2 * 16 * part * tokens * depth, bytes_accessed=17_000_000, transcendentals=0
+        ),
+    )(cotangent, inputs)
+
+
+def project_block(weight, attended, out_ref, n):
     dims = (((1,), (1,)), ((), ()))
-    total = lax.dot_general(
-        weight_ref[0, 0, 0], tokens_ref[0, 0, 0], dims, preferred_element_type=jnp.float32
-    )
-    total += lax.dot_general(
-        weight_ref[0, 1, 0], tokens_ref[0, 1, 0], dims, preferred_element_type=jnp.float32
-    )
-    out_ref[0, 0] = total.astype(out_ref.dtype)
-
-
-def project(weight, attended):
-    part, depth = weight.shape[3:]
+    total = lax.dot_general(weight[0], attended[0], dims, preferred_element_type=jnp.float32)
+    total += lax.dot_general(weight[1], attended[1], dims, preferred_element_type=jnp.float32)
+    out_ref[n] = total.astype(out_ref.dtype)
+
+
+def project_all_kernel(weight_ref, tokens_ref, out_ref):
+    for n in range(8):
+        project_block(weight_ref, tokens_ref.at[n % 4, :, n // 4], out_ref, n)
+
+
+def project_all(weight, attended):
+    part, depth = weight.shape[1:]
     tokens = attended.shape[3]
-
-    def spec(array):
-        pairs, _, roles = array.shape[:3]
-        return pl.BlockSpec(
-            (1, 2, 1) + array.shape[3:],
-            lambda r, k: (k if pairs > 1 else 0, 0, r if roles > 1 else 0, 0, 0),
-        )
-
-    out = pl.pallas_call(
-        project_kernel,
-        grid=(2, 4),
-        in_specs=[spec(weight), spec(attended)],
-        out_specs=pl.BlockSpec((1, 1, part, tokens), lambda r, k: (r, k, 0, 0)),
-        out_shape=jax.ShapeDtypeStruct((2, 4, part, tokens), jnp.bfloat16),
+    return pl.pallas_call(
+        project_all_kernel,
+        out_shape=jax.ShapeDtypeStruct((8, part, tokens), jnp.bfloat16),
         compiler_params=pltpu.CompilerParams(vmem_limit_bytes=32 * 1024 * 1024),
         cost_estimate=pl.CostEstimate(
-            flops=32 * part * depth * tokens, bytes_accessed=6_000_000, transcendentals=0
+            flops=32 * part * depth * tokens, bytes_accessed=3_000_000, transcendentals=0
         ),
     )(weight, attended)
-    return out.reshape(8, part, tokens)
+
+
+def project_own_kernel(weight_ref, tokens_ref, out_ref, weights, sems):
+    copies = [
+        pltpu.make_async_copy(weight_ref.at[k], weights.at[k], sems.at[k]) for k in range(4)
+    ]
+    for copy in copies:
+        copy.start()
+    for k in range(4):
+        copies[k].wait()
+        for r in range(2):
+            project_block(weights.at[k], tokens_ref.at[:, r], out_ref, r * 4 + k)
+
+
+def project_own(weight, attended):
+    part, depth = weight.shape[2:]
+    tokens = attended.shape[2]
+    vmem = pl.BlockSpec(memory_space=pltpu.VMEM)
+    return pl.pallas_call(
+        project_own_kernel,
+        in_specs=[pl.BlockSpec(memory_space=pl.ANY), vmem],
+        out_specs=vmem,
+        out_shape=jax.ShapeDtypeStruct((8, part, tokens), jnp.bfloat16),
+        scratch_shapes=[
+            pltpu.VMEM(weight.shape, weight.dtype),
+            pltpu.SemaphoreType.DMA((4,)),
+        ],
+        compiler_params=pltpu.CompilerParams(vmem_limit_bytes=60 * 1024 * 1024),
+        cost_estimate=pl.CostEstimate(
+            flops=32 * part * depth * tokens, bytes_accessed=4_000_000, transcendentals=0
+        ),
+    )(weight, attended)
 
 
 def normalize(state, norm_gain):
@@ -140,7 +218,7 @@
 
 def revise(current_state, update, pick_codes, mask_values):
     values = current_state.astype(jnp.float32)
-    masked = jnp.broadcast_to(mask_values.astype(jnp.float32)[:, None], values.shape)
+    masked = jnp.broadcast_to(mask_values.astype(jnp.float32)[..., None], values.shape)
     return jnp.where(
         pick_codes == 1, values + update, jnp.where(pick_codes == 2, masked, values)
     ).astype(jnp.bfloat16)
@@ -193,8 +271,8 @@
 ):
     bf16, f32 = jnp.bfloat16, jnp.float32
     role, core, dp = lax.axis_index("role"), lax.axis_index("core"), lax.axis_index("dp")
-    rows, block_len, part = block_states.shape
-    tokens = rows * block_len
+    row_count, block_len, part = block_states.shape
+    tokens = row_count * block_len
     depth = learner_inputs.shape[1]
     out_scale = (HEADS * HEAD) ** (-0.5)
 
@@ -202,8 +280,11 @@
     cache_keys = jnp.where(core == 0, prefix_cache, cache_other)
     cache_values = jnp.where(core == 0, cache_other, prefix_cache)
 
-    def mask_of(block):
-        return lax.dynamic_slice_in_dim(mask_vector, block * part, part, 0)
+    masks = mask_vector.reshape(4, 2, 2, part)
+    ix, iy = lax.axis_index(X), lax.axis_index("y")
+
+    def rows_of(blocks, index):
+        return lax.dynamic_index_in_dim(pick(blocks, index), core, 1, keepdims=False)
 
     def attended_of(whole):
         normed = normalize(whole.reshape(-1, tokens), norm_gain)
@@ -214,26 +295,25 @@
         queries = lax.dot_general(
             normed, query_weight, (((0,), (0,)), ((), ())), preferred_element_type=f32
         ).astype(bf16)
-        block_keys = jnp.where(core == 0, own_half, other_half).reshape(rows, block_len, HEAD)
-        block_values = jnp.where(core == 0, other_half, own_half).reshape(rows, block_len, HEAD)
+        block_keys = jnp.where(core == 0, own_half, other_half).reshape(row_count, block_len, HEAD)
+        block_values = jnp.where(core == 0, other_half, own_half).reshape(row_count, block_len, HEAD)
         return attend(
-            queries.reshape(rows, block_len, -1, HEAD),
+            queries.reshape(row_count, block_len, -1, HEAD),
             cache_keys,
             cache_values,
             block_keys,
             block_values,
             prefix_lengths,
         )
-    cotangent = lax.all_gather(learner_cotangent, ("x0", "y", "core", "x1"), axis=1, tiled=True)
-    whole, _ = gather_features(block_states.reshape(tokens, part).T, 0, 0)
+
+    cotangent = lax.all_gather(learner_cotangent, TENSOR, axis=1, tiled=True)
+    state = block_states.reshape(tokens, part).T
+    whole, _ = gather_rows(pair_order(state, rotate(state, "y", 1), iy, 0), 0)
     attended = attended_of(whole)
     both = jnp.stack([swap_cores(attended), swap_cores(attended, True)])
     attended_all, cotangent = gather_ring(both, cotangent)
 
-    terms = lax.dot_general(
-        cotangent, learner_inputs, (((0,), (0,)), ((), ())), preferred_element_type=f32
-    ).astype(bf16)
-    terms = terms.reshape(8, 2, part, depth)
+    terms = gradient_terms(cotangent.T, learner_inputs)
     halves = lax.psum_scatter(terms, "dp", scatter_dimension=0, tiled=False)
     gradient = pick(halves, role).astype(f32) + rotate(pick(halves, 1 - role), "role", 1).astype(f32)
     new_weight, new_first, new_second = adam_update(
@@ -242,36 +322,37 @@
     weight_part = new_weight.astype(bf16)
     weight_pair = pair_order(weight_part, rotate(weight_part, "core", 1), core, 0)
 
-    partial = project(
-        weight_pair.reshape(1, 2, 1, part, depth), attended_all.reshape(4, 2, 2, tokens, depth)
-    )
+    partial = project_all(weight_pair, attended_all.reshape(4, 2, 2, tokens, depth))
     weight_half, partial = lax.optimization_barrier((swap_cores(weight_part), partial))
     weight_all = lax.all_gather(weight_half, "dp", axis=0)
     update = scatter_sum(partial).astype(bf16)
-    route = []
-    for source in range(256):
-        r, d2, d1, d0, x1, x0, y, c = [source >> k & 1 for k in range(7, -1, -1)]
-        target = [r ^ x1, d2 ^ x0, d1 ^ y, c, x1, x0, y, d0]
-        route.append((source, sum(bit << 7 - k for k, bit in enumerate(target))))
-    update = lax.ppermute(update, EVERY, route).astype(f32) * out_scale
+
+    def deal(flip):
+        route = []
+        for source in range(256):
+            r, d2, d1, d0, x1, x0, y, c = [source >> k & 1 for k in range(7, -1, -1)]
+            target = [r ^ x1, d2 ^ x0, d1 ^ y, c, x1, x0, y ^ flip, d0]
+            route.append((source, sum(bit << 7 - k for k, bit in enumerate(target))))
+        return lax.ppermute(update, EVERY, route)
+
+    shift_x, shift_y = role * 2 + dp // 4, dp // 2 % 2
+    update = pair_order(deal(0), deal(1), iy ^ shift_y, 0).astype(f32) * out_scale
     picks = position_picks.reshape(STEPS, 1, tokens)
-    shift_x, shift_y = role * 2 + dp // 4, dp // 2 % 2
-    block = ((lax.axis_index(X) ^ shift_x) * 2 + (lax.axis_index("y") ^ shift_y)) * 2 + core
-    state = revise(pick(whole, block), update, picks[0], mask_of(block))
-
-    whole, weight_all = gather_features(state, shift_x, shift_y, weight_all)
+    rows = revise(rows_of(whole, ix ^ shift_x), update, picks[0], rows_of(masks, ix ^ shift_x))
+
+    whole, weight_all = gather_rows(rows, shift_x, weight_all)
     attended = attended_of(whole)
     attended_pair = pair_order(attended, rotate(attended, "core", 1), core, 0)
     route = [(r * 2 + c, (1 - r) * 2 + 1 - c) for r in range(2) for c in range(2)]
     far = lax.ppermute(attended, ("role", "core"), route)
     far_pair = pair_order(rotate(attended, "role", 1), far, core, 0)
     attended_four = pair_order(attended_pair, far_pair, role, 1)
-    partial = project(weight_all.reshape(4, 2, 1, part, depth), attended_four[None])
+    partial = project_own(weight_all.reshape(4, 2, part, depth), attended_four)
     update = scatter_sum(partial).astype(bf16)
     update = lax.ppermute(update, ("role", "x1"), [(0, 0), (1, 2), (2, 1), (3, 3)])
-    block = lax.axis_index(TENSOR)
-    state = revise(pick(whole, block), update.astype(f32) * out_scale, picks[1], mask_of(block))
-    return (state.T.reshape(rows, block_len, part), new_weight.T, new_first.T, new_second.T)
+    state = pick(rows_of(whole, ix), iy)
+    state = revise(state, update.astype(f32) * out_scale, picks[1], pick(rows_of(masks, ix), iy))
+    return (state.T.reshape(row_count, block_len, part), new_weight.T, new_first.T, new_second.T)
 
 
 def solution(mesh):

time: 289 us -> 291 us (level)
  starting transfers between devices: 58.2 us -> 45.6 us
  Pallas kernels: 5.75 us -> 18.2 us
  matrix products: 20.2 us -> 8.85 us
  waiting for transfers between devices: 145 us -> 152 us
  blocking collectives: 14.8 us -> 21.3 us
    ppermute x24 -> x23, starting transfers between devices: 43.2 us -> 27.7 us  [rotate(): lax.ppermute(block, axis, [(low, (low + shift) % count) for low in range(...]
    ppermute x1 -> x2, waiting for transfers between devices: 0.01 us -> 12.8 us  [deal(): return lax.ppermute(update, EVERY, route)]
    pallas_call x2 -> x3, Pallas kernels: 5.75 us -> 18.2 us  [the longest x1 11.7 us: gradient_terms(): pl.pallas_call(gradient_kernel, in_specs=[pl.BlockSpec(memory_space=pl.AN...]
    dot_general x1 -> x0, matrix products: 11.3 us -> none  [on_device(): lax.dot_general(cotangent, learner_inputs, (((0,), (0,)), ((), ())), pref...]
    all_to_all x1, blocking collectives: 14.8 us -> 21.3 us  [scatter_sum(): blocks = lax.all_to_all(parts, X + ('y',), 0, 0, tiled=True)]
    all_gather x1, waiting for transfers between devices: 5.44 us -> 0.36 us  [on_device(): cotangent = lax.all_gather(learner_cotangent, TENSOR, axis=1, tiled=True)]
    ppermute x24 -> x23, waiting for transfers between devices: 51.8 us -> 47.7 us  [rotate(): lax.ppermute(block, axis, [(low, (low + shift) % count) for low in range(...]
    ppermute x1 -> x2, starting transfers between devices: 0.67 us -> 3.7 us  [deal(): return lax.ppermute(update, EVERY, route)]
  transfers between devices with their start and end apart: 34 -> 34, of which waited for: 22 -> 23; matrix products, arithmetic and copies ran while one was open for 8% -> 8% of each run, Pallas kernels for 1% -> 1%
where the time goes in v5:
time: 291 us; the launch traced here: 290 us
  waiting for transfers between devices  152 us (52%)
  starting transfers between devices  45.6 us (16%)
  blocking collectives  21.3 us (7%)
  Pallas kernels  18.2 us (6%)
  other arithmetic  15.2 us (5%)
  between operations  14.5 us (5%)
  local copies, waits for them, and re-layouts  14.4 us (5%)
  matrix products  8.85 us (3%)
    reduce_scatter x1, waiting for transfers between devices, on_device(): halves = lax.psum_scatter(terms, 'dp', scatter_dimension=0, tiled=False)  60.3 us
    ppermute x23, waiting for transfers between devices, rotate(): lax.ppermute(block, axis, [(low, (low + shift) % count) for low in range(...  47.7 us
    ppermute x23, starting transfers between devices, rotate(): lax.ppermute(block, axis, [(low, (low + shift) % count) for low in range(...  27.7 us
    all_to_all x1, blocking collectives, scatter_sum(): blocks = lax.all_to_all(parts, X + ('y',), 0, 0, tiled=True)  21.3 us
    ppermute x2, waiting for transfers between devices, deal(): return lax.ppermute(update, EVERY, route)  12.8 us
    pallas_call x1, Pallas kernels, gradient_terms(): pl.pallas_call(gradient_kernel, in_specs=[pl.BlockSpec(memory_space=pl.AN...  11.7 us
    ppermute x3, waiting for transfers between devices, swap_cores(): return lax.ppermute(block, ('role', 'dp', 'core'), route)  9.98 us
    all_to_all x1, waiting for transfers between devices, scatter_sum(): blocks = lax.all_to_all(parts, X + ('y',), 0, 0, tiled=True)  9.22 us
  transfers between devices with their start and end apart: 34, of which 23 were waited for; matrix products, arithmetic and copies ran while one was open for 8% of the time, Pallas kernels for 1%

profile of v5, /device:TPU:16, one launch (start us, length us, event | category | flops | bytes accessed | tf_op | source)
XLA Modules:
  0.0 290.1 jit_solution(2095628989618255473)
XLA Ops:
  9.3 3.5 %collective-permute-done = bf16[320,128]{0,1:T(8,128)(2,1)S(1)} collective-permute-done((bf16[320,128]{0,1:T(8,128)(2,1)}, bf16[320,128]{0,1:T(8,128)(2,1)S(1)}, u32[]{:S(2)}, u32[]{:S(2)}) %collective-permute-start) | collective-permute-done | bytes 81952 | tf_op jit(solution)/shard_map/ppermute | solution.py:28
  39.2 10.0 %collective-permute-done.8 = bf16[128,512]{1,0:T(8,128)(2,1)S(1)} collective-permute-done((bf16[128,512]{1,0:T(8,128)(2,1)S(1)}, bf16[128,512]{1,0:T(8,128)(2,1)S(1)}, u32[]{:S(2)}, u32[]{:S(2)}) %collective-permute-start.8) | collective-permute-done | bytes 131104 | tf_op jit(solution)/shard_map/ppermute | solution.py:72
  49.9 5.1 %collective-permute-start.12 = (bf16[2,128,512]{2,1,0:T(8,128)(2,1)S(1)}, bf16[2,128,512]{2,1,0:T(8,128)(2,1)S(1)}, u32[]{:S(2)}, u32[]{:S(2)}) collective-permute-start(bf16[2,128,512]{2,1,0:T(8,128)(2,1)S(1)} %pad_maximum_fusion), channel_id=1, source_target_pairs={{0,112},{16,0},{32,16},{48,32},{64,48},{80,64},{96,80},{112,96},{1... | collective-permute-start | bytes 786440 | tf_op jit(solution)/shard_map/ppermute | solution.py:28
  55.0 6.4 %collective-permute-done.9 = bf16[2,128,512]{2,1,0:T(8,128)(2,1)S(1)} collective-permute-done((bf16[2,128,512]{2,1,0:T(8,128)(2,1)S(1)}, bf16[2,128,512]{2,1,0:T(8,128)(2,1)S(1)}, u32[]{:S(2)}, u32[]{:S(2)}) %collective-permute-start.9) | collective-permute-done | bytes 262176 | tf_op jit(solution)/shard_map/ppermute | solution.py:28
  61.4 3.5 %collective-permute-start.13 = (bf16[2,128,512]{2,1,0:T(8,128)(2,1)S(1)}, bf16[2,128,512]{2,1,0:T(8,128)(2,1)S(1)}, u32[]{:S(2)}, u32[]{:S(2)}) collective-permute-start(bf16[2,128,512]{2,1,0:T(8,128)(2,1)S(1)} %collective-permute-done.12), channel_id=1, source_target_pairs={{0,112},{16,0},{32,16},{48,32},{64,48},{80,64},{96,80},{112,96},{1... | collective-permute-start | bytes 786440 | tf_op jit(solution)/shard_map/ppermute | solution.py:28
  64.9 5.8 %collective-permute-done.10 = bf16[2,128,512]{2,1,0:T(8,128)(2,1)S(1)} collective-permute-done((bf16[2,128,512]{2,1,0:T(8,128)(2,1)S(1)}, bf16[2,128,512]{2,1,0:T(8,128)(2,1)S(1)}, u32[]{:S(2)}, u32[]{:S(2)}) %collective-permute-start.10) | collective-permute-done | bytes 262176 | tf_op jit(solution)/shard_map/ppermute | solution.py:28
  71.5 3.3 %collective-permute-start.14 = (bf16[2,128,512]{2,1,0:T(8,128)(2,1)S(1)}, bf16[2,128,512]{2,1,0:T(8,128)(2,1)}, u32[]{:S(2)}, u32[]{:S(2)}) collective-permute-start(bf16[2,128,512]{2,1,0:T(8,128)(2,1)S(1)} %collective-permute-done.13), channel_id=1, source_target_pairs={{0,112},{16,0},{32,16},{48,32},{64,48},{80,64},{96,80},{112,96},{1... | collective-permute-start | bytes 786440 | tf_op jit(solution)/shard_map/ppermute | solution.py:28
  74.8 4.5 %collective-permute-done.11 = bf16[2,128,512]{2,1,0:T(8,128)(2,1)} collective-permute-done((bf16[2,128,512]{2,1,0:T(8,128)(2,1)S(1)}, bf16[2,128,512]{2,1,0:T(8,128)(2,1)}, u32[]{:S(2)}, u32[]{:S(2)}) %collective-permute-start.11) | collective-permute-done | bytes 262176 | tf_op jit(solution)/shard_map/ppermute | solution.py:28
  79.7 11.7 %shard_map.156 = bf16[8,2,320,512]{3,2,1,0:T(8,128)(2,1)} custom-call(bf16[5120,1024]{1,0:T(8,128)(2,1)} %bitcast.258, bf16[1024,512]{1,0:T(8,128)(2,1)} %inputs_ref.1), custom_call_target="tpu_custom_call" | custom-call | flops 5368709120 | bytes 17000000 | tf_op jit(solution)/shard_map/pallas_call | solution.py:136
  97.4 60.3 %reduce-scatter.2.cloned.1.call-done = bf16[1,2,320,512]{3,2,1,0:T(8,128)(2,1)} async-done(((bf16[8,2,320,512]{3,2,1,0:T(8,128)(2,1)}), bf16[1,2,320,512]{3,2,1,0:T(8,128)(2,1)}) %reduce-scatter.2.cloned.1.call-update) | async-done | bytes 655376 | tf_op jit(solution)/shard_map/reduce_scatter | solution.py:317
  161.4 8.5 %collective-permute-done.15 = bf16[320,512]{1,0:T(8,128)(2,1)S(1)} collective-permute-done((bf16[320,512]{1,0:T(8,128)(2,1)S(1)}, bf16[320,512]{1,0:T(8,128)(2,1)S(1)}, u32[]{:S(2)}, u32[]{:S(2)}) %collective-permute-start.15) | collective-permute-done | bytes 327712 | tf_op jit(solution)/shard_map/ppermute | solution.py:28
  169.9 2.8 fusion.48
  177.7 4.9 %all-to-all-start = ((bf16[8,320,128]{2,1,0:T(8,128)(2,1)}), bf16[8,320,128]{2,1,0:T(8,128)(2,1)S(1)}, u32[]{:S(2)}, u32[]{:S(2)}) async-start(bf16[8,320,128]{2,1,0:T(8,128)(2,1)} %copy-done.1), calls=%async_computation.1 | async-start | bytes 1310720 | tf_op jit(solution)/shard_map/all_to_all | solution.py:93
  182.7 9.2 %all-to-all-done = bf16[8,320,128]{2,1,0:T(8,128)(2,1)S(1)} async-done(((bf16[8,320,128]{2,1,0:T(8,128)(2,1)}), bf16[8,320,128]{2,1,0:T(8,128)(2,1)S(1)}, u32[]{:S(2)}, u32[]{:S(2)}) %all-to-all-start) | async-done | bytes 655392 | tf_op jit(solution)/shard_map/all_to_all | solution.py:93
  192.7 3.0 %collective-permute-start.20 = (bf16[320,128]{1,0:T(8,128)(2,1)S(1)}, bf16[320,128]{1,0:T(8,128)(2,1)S(1)}, u32[]{:S(2)}, u32[]{:S(2)}) collective-permute-start(bf16[320,128]{1,0:T(8,128)(2,1)S(1)} %reduce_sum.81), channel_id=1, source_target_pairs={{0,2},{1,18},{2,32},{3,48},{4,70},{5,86},{6,100},{7,116},{8,138},{... | collective-permute-start | bytes 245768 | tf_op jit(solution)/shard_map/ppermute | solution.py:336
  195.9 12.8 %collective-permute-done.20 = bf16[320,128]{1,0:T(8,128)(2,1)S(1)} collective-permute-done((bf16[320,128]{1,0:T(8,128)(2,1)S(1)}, bf16[320,128]{1,0:T(8,128)(2,1)S(1)}, u32[]{:S(2)}, u32[]{:S(2)}) %collective-permute-start.20) | collective-permute-done | bytes 81952 | tf_op jit(solution)/shard_map/ppermute | solution.py:336
  209.9 3.2 %collective-permute-start.22 = (bf16[2,320,128]{2,1,0:T(8,128)(2,1)S(1)}, bf16[2,320,128]{2,1,0:T(8,128)(2,1)S(1)}, u32[]{:S(2)}, u32[]{:S(2)}) collective-permute-start(bf16[2,320,128]{2,1,0:T(8,128)(2,1)S(1)} %fusion.28), channel_id=1, source_target_pairs={{0,12},{4,0},{8,4},{12,8},{1,13},{5,1},{9,5},{13,9},{2,14},{6,2},{... | collective-permute-start | bytes 491528 | tf_op jit(solution)/shard_map/ppermute | solution.py:28
  218.1 2.9 collective-permute-done.22
  236.0 2.8 collective-permute-start.28
  238.9 4.4 %collective-permute-done.27 = bf16[128,512]{1,0:T(8,128)(2,1)S(1)} collective-permute-done((bf16[128,512]{1,0:T(8,128)(2,1)S(1)}, bf16[128,512]{1,0:T(8,128)(2,1)S(1)}, u32[]{:S(2)}, u32[]{:S(2)}) %collective-permute-start.27) | collective-permute-done | bytes 131104 | tf_op jit(solution)/shard_map/ppermute | solution.py:28
  246.1 5.0 %shard_map.158 = bf16[8,320,128]{2,1,0:T(8,128)(2,1)} custom-call(bf16[4,2,320,512]{3,2,1,0:T(8,128)(2,1)} %bitcast.219, bf16[2,2,128,512]{3,2,1,0:T(8,128)(2,1)} %maximum_select_fusion.3.tokens_ref), custom_call_target="tpu_custom_call" | custom-call | flops 671088640 | bytes 4000000 | tf_op jit(solution)/shard_map/pallas_call | solution.py:197
  251.1 21.3 %all_to_all.10 = bf16[8,320,128]{2,1,0:T(8,128)(2,1)S(1)} all-to-all(bf16[8,320,128]{2,1,0:T(8,128)(2,1)} %shard_map.158), channel_id=1, replica_groups=mesh['role'=2,'dp'=8,'x1'=2,'x0'=2,'y'=2,'core'=2] {'x1','x0','y'}, dimensions={0} | all-to-all | bytes 1310720 | tf_op jit(solution)/shard_map/all_to_all | solution.py:93
  272.5 3.6 %collective-permute-start.29 = (bf16[320,128]{1,0:T(8,128)(2,1)S(1)}, bf16[320,128]{1,0:T(8,128)(2,1)S(1)}, u32[]{:S(2)}, u32[]{:S(2)}) collective-permute-start(bf16[320,128]{1,0:T(8,128)(2,1)S(1)} %reduce_sum.85), channel_id=1, source_target_pairs={{0,0},{8,128},{128,8},{136,136},{1,1},{9,129},{129,9},{137,137},{2... | collective-permute-start | bytes 245768 | tf_op jit(solution)/shard_map/ppermute | solution.py:352
  276.3 6.4 %collective-permute-done.29 = bf16[320,128]{1,0:T(8,128)(2,1)S(1)} collective-permute-done((bf16[320,128]{1,0:T(8,128)(2,1)S(1)}, bf16[320,128]{1,0:T(8,128)(2,1)S(1)}, u32[]{:S(2)}, u32[]{:S(2)}) %collective-permute-start.29) | collective-permute-done | bytes 81952 | tf_op jit(solution)/shard_map/ppermute | solution.py:352
  (175 shorter events, 70.5 us)
Async XLA Ops:
  7.2 72.6 %all-gather.4.cloned.1.call-start = ((), (), s32[]{:S(2)}) async-start(), calls=%async_computation.3 | async-start | bytes 11141120 | tf_op jit(solution)/shard_map/all_gather | solution.py:309
  7.9 149.8 %reduce-scatter.2.cloned.1.call-start = ((), (), s32[]{:S(2)}) async-start(), calls=%async_computation.4 | async-start | bytes 5898240 | tf_op jit(solution)/shard_map/reduce_scatter | solution.py:317
  13.9 8.5 %collective-permute-start.1 = (bf16[2,320,128]{1,2,0:T(8,128)(2,1)S(1)}, bf16[2,320,128]{1,2,0:T(8,128)(2,1)S(1)}, u32[]{:S(2)}, u32[]{:S(2)}) collective-permute-start(bf16[2,320,128]{1,2,0:T(8,128)(2,1)S(1)} %maximum_select_fusion.7), channel_id=1, source_target_pairs={{0,4},{4,8},{8,12},{12,0},{1,5},{5,9},{9,13},{13,1},{2,6},{6,10},{... | collective-permute-start | bytes 491528 | tf_op jit(solution)/shard_map/ppermute | solution.py:28
  15.5 8.7 %collective-permute-start.2 = (bf16[2,320,128]{1,2,0:T(8,128)(2,1)S(1)}, bf16[2,320,128]{1,2,0:T(8,128)(2,1)S(1)}, u32[]{:S(2)}, u32[]{:S(2)}) collective-permute-start(bf16[2,320,128]{1,2,0:T(8,128)(2,1)S(1)} %maximum_select_fusion.7), channel_id=1, source_target_pairs={{0,12},{4,0},{8,4},{12,8},{1,13},{5,1},{9,5},{13,9},{2,14},{6,2},{... | collective-permute-start | bytes 491528 | tf_op jit(solution)/shard_map/ppermute | solution.py:28
  17.2 8.7 %collective-permute-start.3 = (bf16[2,320,128]{1,2,0:T(8,128)(2,1)S(1)}, bf16[2,320,128]{1,2,0:T(8,128)(2,1)S(1)}, u32[]{:S(2)}, u32[]{:S(2)}) collective-permute-start(bf16[2,320,128]{1,2,0:T(8,128)(2,1)S(1)} %maximum_select_fusion.7), channel_id=1, source_target_pairs={{0,8},{4,12},{8,0},{12,4},{1,9},{5,13},{9,1},{13,5},{2,10},{6,14},... | collective-permute-start | bytes 491528 | tf_op jit(solution)/shard_map/ppermute | solution.py:28
  26.3 7.8 %collective-permute-start.5 = (bf16[4,512,128]{2,1,0:T(8,128)(2,1)}, bf16[4,512,128]{2,1,0:T(8,128)(2,1)}, u32[]{:S(2)}, u32[]{:S(2)}) collective-permute-start(bf16[4,512,128]{2,1,0:T(8,128)(2,1)} %param.20), channel_id=1, source_target_pairs={{0,1},{1,0},{2,3},{3,2},{4,5},{5,4},{6,7},{7,6},{8,9},{9,8},{10,11... | collective-permute-start | bytes 1572872 | tf_op jit(solution)/shard_map/ppermute | solution.py:28
  38.4 10.7 %collective-permute-start.8 = (bf16[128,512]{1,0:T(8,128)(2,1)S(1)}, bf16[128,512]{1,0:T(8,128)(2,1)S(1)}, u32[]{:S(2)}, u32[]{:S(2)}) collective-permute-start(bf16[128,512]{1,0:T(8,128)(2,1)S(1)} %bitcast.248), channel_id=1, source_target_pairs={{0,128},{1,144},{16,129},{17,145},{32,160},{33,176},{48,161},{49,1... | collective-permute-start | bytes 393224 | tf_op jit(solution)/shard_map/ppermute | solution.py:72
  49.2 12.2 %collective-permute-start.9 = (bf16[2,128,512]{2,1,0:T(8,128)(2,1)S(1)}, bf16[2,128,512]{2,1,0:T(8,128)(2,1)S(1)}, u32[]{:S(2)}, u32[]{:S(2)}) collective-permute-start(bf16[2,128,512]{2,1,0:T(8,128)(2,1)S(1)} %pad_maximum_fusion), channel_id=1, source_target_pairs={{0,16},{16,32},{32,48},{48,64},{64,80},{80,96},{96,112},{112,0},{1... | collective-permute-start | bytes 786440 | tf_op jit(solution)/shard_map/ppermute | solution.py:28
  49.9 11.5 %collective-permute-start.12 = (bf16[2,128,512]{2,1,0:T(8,128)(2,1)S(1)}, bf16[2,128,512]{2,1,0:T(8,128)(2,1)S(1)}, u32[]{:S(2)}, u32[]{:S(2)}) collective-permute-start(bf16[2,128,512]{2,1,0:T(8,128)(2,1)S(1)} %pad_maximum_fusion), channel_id=1, source_target_pairs={{0,112},{16,0},{32,16},{48,32},{64,48},{80,64},{96,80},{112,96},{1... | collective-permute-start | bytes 786440 | tf_op jit(solution)/shard_map/ppermute | solution.py:28
  61.4 9.4 %collective-permute-start.10 = (bf16[2,128,512]{2,1,0:T(8,128)(2,1)S(1)}, bf16[2,128,512]{2,1,0:T(8,128)(2,1)S(1)}, u32[]{:S(2)}, u32[]{:S(2)}) collective-permute-start(bf16[2,128,512]{2,1,0:T(8,128)(2,1)S(1)} %collective-permute-done.9), channel_id=1, source_target_pairs={{0,16},{16,32},{32,48},{48,64},{64,80},{80,96},{96,112},{112,0},{1... | collective-permute-start | bytes 786440 | tf_op jit(solution)/shard_map/ppermute | solution.py:28
  61.4 9.3 %collective-permute-start.13 = (bf16[2,128,512]{2,1,0:T(8,128)(2,1)S(1)}, bf16[2,128,512]{2,1,0:T(8,128)(2,1)S(1)}, u32[]{:S(2)}, u32[]{:S(2)}) collective-permute-start(bf16[2,128,512]{2,1,0:T(8,128)(2,1)S(1)} %collective-permute-done.12), channel_id=1, source_target_pairs={{0,112},{16,0},{32,16},{48,32},{64,48},{80,64},{96,80},{112,96},{1... | collective-permute-start | bytes 786440 | tf_op jit(solution)/shard_map/ppermute | solution.py:28
  70.7 8.6 %collective-permute-start.11 = (bf16[2,128,512]{2,1,0:T(8,128)(2,1)S(1)}, bf16[2,128,512]{2,1,0:T(8,128)(2,1)}, u32[]{:S(2)}, u32[]{:S(2)}) collective-permute-start(bf16[2,128,512]{2,1,0:T(8,128)(2,1)S(1)} %collective-permute-done.10), channel_id=1, source_target_pairs={{0,16},{16,32},{32,48},{48,64},{64,80},{80,96},{96,112},{112,0},{1... | collective-permute-start | bytes 786440 | tf_op jit(solution)/shard_map/ppermute | solution.py:28
  71.5 7.9 %collective-permute-start.14 = (bf16[2,128,512]{2,1,0:T(8,128)(2,1)S(1)}, bf16[2,128,512]{2,1,0:T(8,128)(2,1)}, u32[]{:S(2)}, u32[]{:S(2)}) collective-permute-start(bf16[2,128,512]{2,1,0:T(8,128)(2,1)S(1)} %collective-permute-done.13), channel_id=1, source_target_pairs={{0,112},{16,0},{32,16},{48,32},{64,48},{80,64},{96,80},{112,96},{1... | collective-permute-start | bytes 786440 | tf_op jit(solution)/shard_map/ppermute | solution.py:28
  91.5 132.7 %all-gather.6.cloned.1.call-start = ((), (), s32[]{:S(2)}) async-start(), calls=%async_computation.5 | async-start | bytes 2949120 | tf_op jit(solution)/shard_map/all_gather | solution.py:327
  91.6 67.8 %collective-permute-start.18 = (bf16[2,128,512]{2,1,0:T(8,128)(2,1)}, bf16[2,128,512]{2,1,0:T(8,128)(2,1)}, u32[]{:S(2)}, u32[]{:S(2)}) collective-permute-start(bf16[2,128,512]{2,1,0:T(8,128)(2,1)} %collective-permute-done.11), channel_id=1, source_target_pairs={{0,16},{16,32},{32,48},{48,64},{64,80},{80,96},{96,112},{112,0},{1... | collective-permute-start | bytes 786440 | tf_op jit(solution)/shard_map/ppermute | solution.py:28
  158.8 11.1 %collective-permute-start.15 = (bf16[320,512]{1,0:T(8,128)(2,1)S(1)}, bf16[320,512]{1,0:T(8,128)(2,1)S(1)}, u32[]{:S(2)}, u32[]{:S(2)}) collective-permute-start(bf16[320,512]{1,0:T(8,128)(2,1)S(1)} %dynamic-slice_bitcast_fusion), channel_id=1, source_target_pairs={{0,128},{128,0},{1,129},{129,1},{2,130},{130,2},{3,131},{131,3},{4... | collective-permute-start | bytes 983048 | tf_op jit(solution)/shard_map/ppermute | solution.py:28
  177.7 14.2 %all-to-all-start = ((bf16[8,320,128]{2,1,0:T(8,128)(2,1)}), bf16[8,320,128]{2,1,0:T(8,128)(2,1)S(1)}, u32[]{:S(2)}, u32[]{:S(2)}) async-start(bf16[8,320,128]{2,1,0:T(8,128)(2,1)} %copy-done.1), calls=%async_computation.1 | async-start | bytes 1310720 | tf_op jit(solution)/shard_map/all_to_all | solution.py:93
  192.7 16.1 %collective-permute-start.20 = (bf16[320,128]{1,0:T(8,128)(2,1)S(1)}, bf16[320,128]{1,0:T(8,128)(2,1)S(1)}, u32[]{:S(2)}, u32[]{:S(2)}) collective-permute-start(bf16[320,128]{1,0:T(8,128)(2,1)S(1)} %reduce_sum.81), channel_id=1, source_target_pairs={{0,2},{1,18},{2,32},{3,48},{4,70},{5,86},{6,100},{7,116},{8,138},{... | collective-permute-start | bytes 245768 | tf_op jit(solution)/shard_map/ppermute | solution.py:336
  209.8 8.3 %collective-permute-start.21 = (bf16[2,320,128]{2,1,0:T(8,128)(2,1)S(1)}, bf16[2,320,128]{2,1,0:T(8,128)(2,1)S(1)}, u32[]{:S(2)}, u32[]{:S(2)}) collective-permute-start(bf16[2,320,128]{2,1,0:T(8,128)(2,1)S(1)} %fusion.28), channel_id=1, source_target_pairs={{0,4},{4,8},{8,12},{12,0},{1,5},{5,9},{9,13},{13,1},{2,6},{6,10},{... | collective-permute-start | bytes 491528 | tf_op jit(solution)/shard_map/ppermute | solution.py:28
  209.9 11.0 %collective-permute-start.22 = (bf16[2,320,128]{2,1,0:T(8,128)(2,1)S(1)}, bf16[2,320,128]{2,1,0:T(8,128)(2,1)S(1)}, u32[]{:S(2)}, u32[]{:S(2)}) collective-permute-start(bf16[2,320,128]{2,1,0:T(8,128)(2,1)S(1)} %fusion.28), channel_id=1, source_target_pairs={{0,12},{4,0},{8,4},{12,8},{1,13},{5,1},{9,5},{13,9},{2,14},{6,2},{... | collective-permute-start | bytes 491528 | tf_op jit(solution)/shard_map/ppermute | solution.py:28
  213.2 8.4 %collective-permute-start.23 = (bf16[2,320,128]{2,1,0:T(8,128)(2,1)S(1)}, bf16[2,320,128]{2,1,0:T(8,128)(2,1)S(1)}, u32[]{:S(2)}, u32[]{:S(2)}) collective-permute-start(bf16[2,320,128]{2,1,0:T(8,128)(2,1)S(1)} %fusion.28), channel_id=1, source_target_pairs={{0,8},{4,12},{8,0},{12,4},{1,9},{5,13},{9,1},{13,5},{2,10},{6,14},... | collective-permute-start | bytes 491528 | tf_op jit(solution)/shard_map/ppermute | solution.py:28
  235.5 7.9 %collective-permute-start.27 = (bf16[128,512]{1,0:T(8,128)(2,1)S(1)}, bf16[128,512]{1,0:T(8,128)(2,1)S(1)}, u32[]{:S(2)}, u32[]{:S(2)}) collective-permute-start(bf16[128,512]{1,0:T(8,128)(2,1)S(1)} %bitcast.245), channel_id=1, source_target_pairs={{0,128},{128,0},{1,129},{129,1},{2,130},{130,2},{3,131},{131,3},{4... | collective-permute-start | bytes 393224 | tf_op jit(solution)/shard_map/ppermute | solution.py:28
  236.0 9.2 %collective-permute-start.28 = (bf16[128,512]{1,0:T(8,128)(2,1)S(1)}, bf16[128,512]{1,0:T(8,128)(2,1)S(1)}, u32[]{:S(2)}, u32[]{:S(2)}) collective-permute-start(bf16[128,512]{1,0:T(8,128)(2,1)S(1)} %bitcast.246), channel_id=1, source_target_pairs={{0,129},{1,128},{128,1},{129,0},{2,131},{3,130},{130,3},{131,2},{4... | collective-permute-start | bytes 393224 | tf_op jit(solution)/shard_map/ppermute | solution.py:347
  272.5 10.2 %collective-permute-start.29 = (bf16[320,128]{1,0:T(8,128)(2,1)S(1)}, bf16[320,128]{1,0:T(8,128)(2,1)S(1)}, u32[]{:S(2)}, u32[]{:S(2)}) collective-permute-start(bf16[320,128]{1,0:T(8,128)(2,1)S(1)} %reduce_sum.85), channel_id=1, source_target_pairs={{0,0},{8,128},{128,8},{136,136},{1,1},{9,129},{129,9},{137,137},{2... | collective-permute-start | bytes 245768 | tf_op jit(solution)/shard_map/ppermute | solution.py:352
  (30 other events, 181.4 us)
Sparse Core Ops, SparseCore 0:
  9.9 69.8 all-gather.3
  91.6 66.1 reduce-scatter.1
  177.8 46.3 all-gather.5

commit v6 on v5

--- a/solution.py
+++ b/solution.py
@@ -48,15 +48,14 @@
 
 
 def gather_rows(rows, shift_x, beside=None):
-    ix, ic = lax.axis_index(X), lax.axis_index("core")
+    ix = lax.axis_index(X)
     ahead, back, across = rotate(rows, X, 1), rotate(rows, X, -1), rotate(rows, X, 2)
     square = jnp.zeros((4,) + rows.shape, rows.dtype)
     square = lax.dynamic_update_index_in_dim(square, rows, ix ^ shift_x, 0)
     square = lax.dynamic_update_index_in_dim(square, ahead, ((ix + 3) % 4) ^ shift_x, 0)
     square = lax.dynamic_update_index_in_dim(square, back, ((ix + 1) % 4) ^ shift_x, 0)
     square = lax.dynamic_update_index_in_dim(square, across, ((ix + 2) % 4) ^ shift_x, 0)
-    square, beside = lax.optimization_barrier((square, beside))
-    return pair_order(square, rotate(square, "core", 1), ic, 2), beside
+    return lax.optimization_barrier((square, beside))
 
 
 def swap_cores(block, flip_role=False):
@@ -94,58 +93,23 @@
     return jnp.sum(blocks.astype(jnp.float32), axis=0)
 
 
-def gradient_kernel(
-    cotangent_ref, inputs_ref, out_ref, cotangents, inputs, outs, inputs_sem, cotangent_sems, out_sems
-):
-    steps, block = cotangents.shape[:2]
-
-    def inputs_copy():
-        return pltpu.make_async_copy(inputs_ref, inputs, inputs_sem)
-
-    def cotangent_copy(i):
-        return pltpu.make_async_copy(
-            cotangent_ref.at[pl.ds(i * block, block)], cotangents.at[i], cotangent_sems.at[i]
-        )
-
-    def out_copy(i):
-        place = out_ref.at[pl.ds(2 * (i % (steps // 2)), 2), i // (steps // 2)]
-        return pltpu.make_async_copy(outs.at[i], place, out_sems.at[i])
-
-    cotangent_copy(0).start()
-    inputs_copy().start()
-    for i in range(1, steps):
-        cotangent_copy(i).start()
-    inputs_copy().wait()
-
-    def step(i, carry):
-        cotangent_copy(i).wait()
-        terms = jnp.dot(cotangents[i], inputs[...], preferred_element_type=jnp.float32)
-        outs[i] = terms.astype(outs.dtype).reshape(outs.shape[1:])
-        out_copy(i).start()
-        return carry
-
-    lax.fori_loop(0, steps, step, 0)
-    for i in range(steps):
-        out_copy(i).wait()
+def gradient_kernel(cotangent_ref, inputs_ref, out_ref):
+    terms = jnp.dot(cotangent_ref[...], inputs_ref[...], preferred_element_type=jnp.float32)
+    out_ref[...] = terms.astype(out_ref.dtype).reshape(out_ref.shape)
 
 
 def gradient_terms(cotangent, inputs):
     tokens, depth = inputs.shape
     part = cotangent.shape[0] // 16
-    steps = 8
     return pl.pallas_call(
         gradient_kernel,
-        in_specs=[pl.BlockSpec(memory_space=pl.ANY)] * 2,
-        out_specs=pl.BlockSpec(memory_space=pl.ANY),
+        grid=(4,),
+        in_specs=[
+            pl.BlockSpec((4 * part, tokens), lambda i: (i, 0)),
+            pl.BlockSpec((tokens, depth), lambda i: (0, 0)),
+        ],
+        out_specs=pl.BlockSpec((4, 1, part, depth), lambda i: (i % 2, i // 2, 0, 0)),
         out_shape=jax.ShapeDtypeStruct((8, 2, part, depth), jnp.bfloat16),
-        scratch_shapes=[
-            pltpu.VMEM((steps, 2 * part, tokens), jnp.bfloat16),
-            pltpu.VMEM((tokens, depth), jnp.bfloat16),
-            pltpu.VMEM((steps, 2, part, depth), jnp.bfloat16),
-            pltpu.SemaphoreType.DMA,
-            pltpu.SemaphoreType.DMA((steps,)),
-            pltpu.SemaphoreType.DMA((steps,)),
-        ],
         compiler_params=pltpu.CompilerParams(vmem_limit_bytes=60 * 1024 * 1024),
         cost_estimate=pl.CostEstimate(
             flops=2 * 16 * part * tokens * depth, bytes_accessed=17_000_000, transcendentals=0
@@ -178,42 +142,38 @@
     )(weight, attended)
 
 
-def project_own_kernel(weight_ref, tokens_ref, out_ref, weights, sems):
-    copies = [
-        pltpu.make_async_copy(weight_ref.at[k], weights.at[k], sems.at[k]) for k in range(4)
-    ]
-    for copy in copies:
-        copy.start()
-    for k in range(4):
-        copies[k].wait()
-        for r in range(2):
-            project_block(weights.at[k], tokens_ref.at[:, r], out_ref, r * 4 + k)
+def project_own_kernel(weight_ref, tokens_ref, out_ref):
+    project_block(weight_ref.at[0], tokens_ref.at[:, 0], out_ref.at[0], 0)
 
 
 def project_own(weight, attended):
     part, depth = weight.shape[2:]
     tokens = attended.shape[2]
-    vmem = pl.BlockSpec(memory_space=pltpu.VMEM)
-    return pl.pallas_call(
+    out = pl.pallas_call(
         project_own_kernel,
-        in_specs=[pl.BlockSpec(memory_space=pl.ANY), vmem],
-        out_specs=vmem,
-        out_shape=jax.ShapeDtypeStruct((8, part, tokens), jnp.bfloat16),
-        scratch_shapes=[
-            pltpu.VMEM(weight.shape, weight.dtype),
-            pltpu.SemaphoreType.DMA((4,)),
+        grid=(2, 4),
+        in_specs=[
+            pl.BlockSpec((1, 2, part, depth), lambda r, k: (k, 0, 0, 0)),
+            pl.BlockSpec((2, 1, tokens, depth), lambda r, k: (0, r, 0, 0)),
         ],
-        compiler_params=pltpu.CompilerParams(vmem_limit_bytes=60 * 1024 * 1024),
+        out_specs=pl.BlockSpec((1, 1, part, tokens), lambda r, k: (r, k, 0, 0)),
+        out_shape=jax.ShapeDtypeStruct((2, 4, part, tokens), jnp.bfloat16),
+        compiler_params=pltpu.CompilerParams(vmem_limit_bytes=32 * 1024 * 1024),
         cost_estimate=pl.CostEstimate(
             flops=32 * part * depth * tokens, bytes_accessed=4_000_000, transcendentals=0
         ),
     )(weight, attended)
-
-
-def normalize(state, norm_gain):
-    values = state.astype(jnp.float32)
-    mean_square = jnp.mean(values * values, axis=0, keepdims=True)
-    return (values * lax.rsqrt(mean_square + NORM_EPS) * norm_gain[:, None]).astype(jnp.bfloat16)
+    return out.reshape(8, part, tokens)
+
+
+def half_products(square, gain, query_weight, keyval_weight):
+    values = square.astype(jnp.float32)
+    squares = jnp.sum(values * values, axis=(0, 1, 2))
+    scaled = (values * gain[..., None]).astype(jnp.bfloat16).reshape(-1, square.shape[-1])
+    dims = (((0,), (0,)), ((), ()))
+    queries = lax.dot_general(scaled, query_weight, dims, preferred_element_type=jnp.float32)
+    keyvals = lax.dot_general(scaled, keyval_weight, dims, preferred_element_type=jnp.float32)
+    return squares, queries, keyvals
 
 
 def revise(current_state, update, pick_codes, mask_values):
@@ -280,21 +240,32 @@
     cache_keys = jnp.where(core == 0, prefix_cache, cache_other)
     cache_values = jnp.where(core == 0, cache_other, prefix_cache)
 
-    masks = mask_vector.reshape(4, 2, 2, part)
     ix, iy = lax.axis_index(X), lax.axis_index("y")
 
-    def rows_of(blocks, index):
-        return lax.dynamic_index_in_dim(pick(blocks, index), core, 1, keepdims=False)
-
-    def attended_of(whole):
-        normed = normalize(whole.reshape(-1, tokens), norm_gain)
-        own_half = lax.dot_general(
-            normed, keyval_weight, (((0,), (0,)), ((), ())), preferred_element_type=f32
-        ).astype(bf16)
+    def half_of(array, which):
+        blocks = array.reshape((4, 2, 2, part) + array.shape[1:])
+        return lax.dynamic_index_in_dim(blocks, which, 2, keepdims=False)
+
+    masks = half_of(mask_vector, core)
+    sides = []
+    for which in (core, 1 - core):
+        sides.append(
+            (
+                half_of(norm_gain, which),
+                half_of(query_weight, which).reshape(-1, query_weight.shape[1]),
+                half_of(keyval_weight, which).reshape(-1, keyval_weight.shape[1]),
+            )
+        )
+    sides = lax.optimization_barrier(sides)
+
+    def attended_of(square):
+        other = rotate(square, "core", 1)
+        halves = [half_products(half, *side) for half, side in zip((square, other), sides)]
+        squares, queries, keyvals = [sum(pair) for pair in zip(*halves)]
+        factor = lax.rsqrt(squares / (16 * part) + NORM_EPS)[:, None]
+        queries = (queries * factor).astype(bf16)
+        own_half = (keyvals * factor).astype(bf16)
         other_half = rotate(own_half, "core", 1)
-        queries = lax.dot_general(
-            normed, query_weight, (((0,), (0,)), ((), ())), preferred_element_type=f32
-        ).astype(bf16)
         block_keys = jnp.where(core == 0, own_half, other_half).reshape(row_count, block_len, HEAD)
         block_values = jnp.where(core == 0, other_half, own_half).reshape(row_count, block_len, HEAD)
         return attend(
@@ -308,13 +279,14 @@
 
     cotangent = lax.all_gather(learner_cotangent, TENSOR, axis=1, tiled=True)
     state = block_states.reshape(tokens, part).T
-    whole, _ = gather_rows(pair_order(state, rotate(state, "y", 1), iy, 0), 0)
-    attended = attended_of(whole)
+    square, _ = gather_rows(pair_order(state, rotate(state, "y", 1), iy, 0), 0)
+    attended = attended_of(square)
     both = jnp.stack([swap_cores(attended), swap_cores(attended, True)])
     attended_all, cotangent = gather_ring(both, cotangent)
 
     terms = gradient_terms(cotangent.T, learner_inputs)
     halves = lax.psum_scatter(terms, "dp", scatter_dimension=0, tiled=False)
+    halves, attended_all = lax.optimization_barrier((halves, attended_all))
     gradient = pick(halves, role).astype(f32) + rotate(pick(halves, 1 - role), "role", 1).astype(f32)
     new_weight, new_first, new_second = adam_update(
         gradient, master_weight.T, first_moment.T, second_moment.T
@@ -338,10 +310,10 @@
     shift_x, shift_y = role * 2 + dp // 4, dp // 2 % 2
     update = pair_order(deal(0), deal(1), iy ^ shift_y, 0).astype(f32) * out_scale
     picks = position_picks.reshape(STEPS, 1, tokens)
-    rows = revise(rows_of(whole, ix ^ shift_x), update, picks[0], rows_of(masks, ix ^ shift_x))
-
-    whole, weight_all = gather_rows(rows, shift_x, weight_all)
-    attended = attended_of(whole)
+    rows = revise(pick(square, ix ^ shift_x), update, picks[0], pick(masks, ix ^ shift_x))
+
+    square, weight_all = gather_rows(rows, shift_x, weight_all)
+    attended = attended_of(square)
     attended_pair = pair_order(attended, rotate(attended, "core", 1), core, 0)
     route = [(r * 2 + c, (1 - r) * 2 + 1 - c) for r in range(2) for c in range(2)]
     far = lax.ppermute(attended, ("role", "core"), route)
@@ -350,8 +322,8 @@
     partial = project_own(weight_all.reshape(4, 2, part, depth), attended_four)
     update = scatter_sum(partial).astype(bf16)
     update = lax.ppermute(update, ("role", "x1"), [(0, 0), (1, 2), (2, 1), (3, 3)])
-    state = pick(rows_of(whole, ix), iy)
-    state = revise(state, update.astype(f32) * out_scale, picks[1], pick(rows_of(masks, ix), iy))
+    state = pick(pick(square, ix), iy)
+    state = revise(state, update.astype(f32) * out_scale, picks[1], pick(pick(masks, ix), iy))
     return (state.T.reshape(row_count, block_len, part), new_weight.T, new_first.T, new_second.T)
 
 

time: 291 us -> 299 us (1.027)
  local copies, waits for them, and re-layouts: 14.4 us -> 32.4 us
  waiting for transfers between devices: 152 us -> 145 us
    reduce_scatter x1, waiting for transfers between devices: 60.3 us -> 53.9 us  [on_device(): halves = lax.psum_scatter(terms, 'dp', scatter_dimension=0, tiled=False)]
    dynamic_slice x0 -> x3, local copies, waits for them, and re-layouts: none -> 5.61 us  [half_of(): return lax.dynamic_index_in_dim(blocks, which, 2, keepdims=False)]
    convert_element_type x2 -> x0, other arithmetic: 4.35 us -> none  [normalize(): (values * lax.rsqrt(mean_square + NORM_EPS) * norm_gain[:, None]).astype(...]
    pallas_call x2, Pallas kernels: 16.7 us -> 12.9 us  [the longest x1 10.1 us: gradient_terms(): pl.pallas_call(gradient_kernel, grid=(4,), in_specs=[pl.BlockSpec((4 * pa...]
  transfers between devices with their start and end apart: 34 -> 34, of which waited for: 23 -> 23; matrix products, arithmetic and copies ran while one was open for 8% -> 14% of each run, Pallas kernels for 1% -> 1%
where the time goes in v6:
time: 299 us; the launch traced here: 298 us
  waiting for transfers between devices  145 us (48%)
  starting transfers between devices  44.1 us (15%)
  local copies, waits for them, and re-layouts  32.4 us (11%)
  blocking collectives  21.4 us (7%)
  other arithmetic  15.4 us (5%)
  Pallas kernels  15.3 us (5%)
  between operations  14.5 us (5%)
  matrix products  9.65 us (3%)
    reduce_scatter x1, waiting for transfers between devices, on_device(): halves = lax.psum_scatter(terms, 'dp', scatter_dimension=0, tiled=False)  53.9 us
    ppermute x23, waiting for transfers between devices, rotate(): lax.ppermute(block, axis, [(low, (low + shift) % count) for low in range(...  49.8 us
    ppermute x23, starting transfers between devices, rotate(): lax.ppermute(block, axis, [(low, (low + shift) % count) for low in range(...  26.8 us
    all_to_all x1, blocking collectives, scatter_sum(): blocks = lax.all_to_all(parts, X + ('y',), 0, 0, tiled=True)  21.4 us
    ppermute x2, waiting for transfers between devices, deal(): return lax.ppermute(update, EVERY, route)  12 us
    pallas_call x1, Pallas kernels, gradient_terms(): pl.pallas_call(gradient_kernel, grid=(4,), in_specs=[pl.BlockSpec((4 * pa...  10.1 us
    all_to_all x1, waiting for transfers between devices, scatter_sum(): blocks = lax.all_to_all(parts, X + ('y',), 0, 0, tiled=True)  8.39 us
    ppermute x3, waiting for transfers between devices, swap_cores(): return lax.ppermute(block, ('role', 'dp', 'core'), route)  8.33 us
  transfers between devices with their start and end apart: 34, of which 23 were waited for; matrix products, arithmetic and copies ran while one was open for 14% of the time, Pallas kernels for 1%

profile of v6, /device:TPU:16, one launch (start us, length us, event | category | flops | bytes accessed | tf_op | source)
XLA Modules:
  0.0 298.0 jit_solution(11751547140742264977)
XLA Ops:
  10.9 4.6 %constant_dynamic-slice_fusion.3 = (bf16[4,2,1,320,512]{4,3,2,1,0:T(8,128)(2,1)}, bf16[4,2,1,320,512]{4,3,2,1,0:T(8,128)(2,1)S(1)}) fusion(bf16[4,2,2,320,512]{4,3,2,1,0:T(8,128)(2,1)} %bitcast.229, s32[]{:T(128)S(6)} %select_n.323, s32[]{:T(128)S(6)} %select_n.322), kind=kLoop, calls=%fused_computation.126 | loop fusion | bytes 10485768 | tf_op jit(solution)/shard_map/jit(dynamic_index_in_dim)/dynamic_slice | solution.py:247
  29.7 5.5 %collective-permute-done.3 = bf16[2,320,128]{1,2,0:T(8,128)(2,1)} collective-permute-done((bf16[2,320,128]{1,2,0:T(8,128)(2,1)}, bf16[2,320,128]{1,2,0:T(8,128)(2,1)}, u32[]{:S(2)}, u32[]{:S(2)}) %collective-permute-start.3) | collective-permute-done | bytes 163872 | tf_op jit(solution)/shard_map/ppermute | solution.py:28
  51.1 8.3 %collective-permute-done.8 = bf16[128,512]{1,0:T(8,128)(2,1)S(1)} collective-permute-done((bf16[128,512]{1,0:T(8,128)(2,1)S(1)}, bf16[128,512]{1,0:T(8,128)(2,1)S(1)}, u32[]{:S(2)}, u32[]{:S(2)}) %collective-permute-start.8) | collective-permute-done | bytes 131104 | tf_op jit(solution)/shard_map/ppermute | solution.py:71
  60.9 6.1 %collective-permute-start.12 = (bf16[2,128,512]{2,1,0:T(8,128)(2,1)S(1)}, bf16[2,128,512]{2,1,0:T(8,128)(2,1)S(1)}, u32[]{:S(2)}, u32[]{:S(2)}) collective-permute-start(bf16[2,128,512]{2,1,0:T(8,128)(2,1)S(1)} %pad_maximum_fusion), channel_id=1, source_target_pairs={{0,112},{16,0},{32,16},{48,32},{64,48},{80,64},{96,80},{112,96},{1... | collective-permute-start | bytes 786440 | tf_op jit(solution)/shard_map/ppermute | solution.py:28
  67.1 6.9 %collective-permute-done.9 = bf16[2,128,512]{2,1,0:T(8,128)(2,1)S(1)} collective-permute-done((bf16[2,128,512]{2,1,0:T(8,128)(2,1)S(1)}, bf16[2,128,512]{2,1,0:T(8,128)(2,1)S(1)}, u32[]{:S(2)}, u32[]{:S(2)}) %collective-permute-start.9) | collective-permute-done | bytes 262176 | tf_op jit(solution)/shard_map/ppermute | solution.py:28
  74.8 3.3 %collective-permute-start.13 = (bf16[2,128,512]{2,1,0:T(8,128)(2,1)S(1)}, bf16[2,128,512]{2,1,0:T(8,128)(2,1)S(1)}, u32[]{:S(2)}, u32[]{:S(2)}) collective-permute-start(bf16[2,128,512]{2,1,0:T(8,128)(2,1)S(1)} %collective-permute-done.12), channel_id=1, source_target_pairs={{0,112},{16,0},{32,16},{48,32},{64,48},{80,64},{96,80},{112,96},{1... | collective-permute-start | bytes 786440 | tf_op jit(solution)/shard_map/ppermute | solution.py:28
  78.0 5.5 %collective-permute-done.10 = bf16[2,128,512]{2,1,0:T(8,128)(2,1)S(1)} collective-permute-done((bf16[2,128,512]{2,1,0:T(8,128)(2,1)S(1)}, bf16[2,128,512]{2,1,0:T(8,128)(2,1)S(1)}, u32[]{:S(2)}, u32[]{:S(2)}) %collective-permute-start.10) | collective-permute-done | bytes 262176 | tf_op jit(solution)/shard_map/ppermute | solution.py:28
  84.4 3.7 %collective-permute-start.14 = (bf16[2,128,512]{2,1,0:T(8,128)(2,1)S(1)}, bf16[2,128,512]{2,1,0:T(8,128)(2,1)}, u32[]{:S(2)}, u32[]{:S(2)}) collective-permute-start(bf16[2,128,512]{2,1,0:T(8,128)(2,1)S(1)} %collective-permute-done.13), channel_id=1, source_target_pairs={{0,112},{16,0},{32,16},{48,32},{64,48},{80,64},{96,80},{112,96},{1... | collective-permute-start | bytes 786440 | tf_op jit(solution)/shard_map/ppermute | solution.py:28
  88.1 4.2 %collective-permute-done.11 = bf16[2,128,512]{2,1,0:T(8,128)(2,1)} collective-permute-done((bf16[2,128,512]{2,1,0:T(8,128)(2,1)S(1)}, bf16[2,128,512]{2,1,0:T(8,128)(2,1)}, u32[]{:S(2)}, u32[]{:S(2)}) %collective-permute-start.11) | collective-permute-done | bytes 262176 | tf_op jit(solution)/shard_map/ppermute | solution.py:28
  93.0 10.1 %shard_map.156 = bf16[8,2,320,512]{3,2,1,0:T(8,128)(2,1)} custom-call(bf16[5120,1024]{1,0:T(8,128)(2,1)} %bitcast.264, bf16[1024,512]{1,0:T(8,128)(2,1)} %inputs_ref.1), custom_call_target="tpu_custom_call" | custom-call | flops 5368709120 | bytes 17000000 | tf_op jit(solution)/shard_map/pallas_call | solution.py:104
  106.7 5.4 %collective-permute-done.15 = bf16[2,128,512]{2,1,0:T(8,128)(2,1)S(1)} collective-permute-done((bf16[2,128,512]{2,1,0:T(8,128)(2,1)}, bf16[2,128,512]{2,1,0:T(8,128)(2,1)S(1)}, u32[]{:S(2)}, u32[]{:S(2)}) %collective-permute-start.15) | collective-permute-done | bytes 262176 | tf_op jit(solution)/shard_map/ppermute | solution.py:28
  113.1 53.9 %reduce-scatter.2.cloned.1.call-done = bf16[1,2,320,512]{3,2,1,0:T(8,128)(2,1)} async-done(((bf16[8,2,320,512]{3,2,1,0:T(8,128)(2,1)}), bf16[1,2,320,512]{3,2,1,0:T(8,128)(2,1)}) %reduce-scatter.2.cloned.1.call-update) | async-done | bytes 655376 | tf_op jit(solution)/shard_map/reduce_scatter | solution.py:288
  169.4 10.8 %collective-permute-done.16 = bf16[320,512]{1,0:T(8,128)(2,1)} collective-permute-done((bf16[320,512]{1,0:T(8,128)(2,1)}, bf16[320,512]{1,0:T(8,128)(2,1)}, u32[]{:S(2)}, u32[]{:S(2)}) %collective-permute-start.16) | collective-permute-done | bytes 327712 | tf_op jit(solution)/shard_map/ppermute | solution.py:28
  180.1 3.1 %fusion.58 = (bf16[320,512]{1,0:T(8,128)(2,1)S(1)}, f32[320,512]{1,0:T(8,128)}, f32[512,320]{0,1:T(8,128)}, f32[512,320]{0,1:T(8,128)}) fusion(f32[512,320]{0,1:T(8,128)S(1)} %copy-done.7, bf16[320,512]{1,0:T(8,128)(2,1)} %collective-permute-done.16, bf16[2,320,512]{2,1,0:T(8,128)(2,1)} %bitcast.234, s32[]{:T(128)S(6)} %select_n.346, f32[512,320]{0,1:T(8,128)} %param.16, ...), kind=kLoop, calls=%fused_computation.145 | loop fusion | flops 3112960 | bytes 4915204 | tf_op jit(solution)/shard_map/convert_element_type | solution.py:294
  188.1 4.9 %all-to-all-start = ((bf16[8,320,128]{2,1,0:T(8,128)(2,1)}), bf16[8,320,128]{2,1,0:T(8,128)(2,1)S(1)}, u32[]{:S(2)}, u32[]{:S(2)}) async-start(bf16[8,320,128]{2,1,0:T(8,128)(2,1)} %shard_map.157), calls=%async_computation.1 | async-start | bytes 1310720 | tf_op jit(solution)/shard_map/all_to_all | solution.py:92
  193.6 8.4 %all-to-all-done = bf16[8,320,128]{2,1,0:T(8,128)(2,1)S(1)} async-done(((bf16[8,320,128]{2,1,0:T(8,128)(2,1)}), bf16[8,320,128]{2,1,0:T(8,128)(2,1)S(1)}, u32[]{:S(2)}, u32[]{:S(2)}) %all-to-all-start) | async-done | bytes 655392 | tf_op jit(solution)/shard_map/all_to_all | solution.py:92
  202.8 3.3 %collective-permute-start.20 = (bf16[320,128]{1,0:T(8,128)(2,1)S(1)}, bf16[320,128]{1,0:T(8,128)(2,1)S(1)}, u32[]{:S(2)}, u32[]{:S(2)}) collective-permute-start(bf16[320,128]{1,0:T(8,128)(2,1)S(1)} %reduce_sum.100), channel_id=1, source_target_pairs={{0,2},{1,18},{2,32},{3,48},{4,70},{5,86},{6,100},{7,116},{8,138},{... | collective-permute-start | bytes 245768 | tf_op jit(solution)/shard_map/ppermute | solution.py:308
  206.3 12.0 %collective-permute-done.20 = bf16[320,128]{1,0:T(8,128)(2,1)S(1)} collective-permute-done((bf16[320,128]{1,0:T(8,128)(2,1)S(1)}, bf16[320,128]{1,0:T(8,128)(2,1)S(1)}, u32[]{:S(2)}, u32[]{:S(2)}) %collective-permute-start.20) | collective-permute-done | bytes 81952 | tf_op jit(solution)/shard_map/ppermute | solution.py:308
  219.5 3.2 %collective-permute-start.22 = (bf16[2,320,128]{2,1,0:T(8,128)(2,1)S(1)}, bf16[2,320,128]{2,1,0:T(8,128)(2,1)S(1)}, u32[]{:S(2)}, u32[]{:S(2)}) collective-permute-start(bf16[2,320,128]{2,1,0:T(8,128)(2,1)S(1)} %fusion.38), channel_id=1, source_target_pairs={{0,12},{4,0},{8,4},{12,8},{1,13},{5,1},{9,5},{13,9},{2,14},{6,2},{... | collective-permute-start | bytes 491528 | tf_op jit(solution)/shard_map/ppermute | solution.py:28
  231.9 3.4 %all-gather.6.cloned.1.call-done = bf16[2560,512]{1,0:T(8,128)(2,1)} async-done(((bf16[320,512]{1,0:T(8,128)(2,1)}), bf16[2560,512]{1,0:T(8,128)(2,1)}) %all-gather.6.cloned.1.call-update) | async-done | bytes 2621456 | tf_op jit(solution)/shard_map/all_gather | solution.py:299
  248.7 4.4 %collective-permute-done.27 = bf16[128,512]{1,0:T(8,128)(2,1)S(1)} collective-permute-done((bf16[128,512]{1,0:T(8,128)(2,1)S(1)}, bf16[128,512]{1,0:T(8,128)(2,1)S(1)}, u32[]{:S(2)}, u32[]{:S(2)}) %collective-permute-start.27) | collective-permute-done | bytes 131104 | tf_op jit(solution)/shard_map/ppermute | solution.py:28
  257.9 21.4 %all_to_all.10 = bf16[8,320,128]{2,1,0:T(8,128)(2,1)S(1)} all-to-all(bf16[8,320,128]{2,1,0:T(8,128)(2,1)S(1)} %bitcast.212), channel_id=1, replica_groups=mesh['role'=2,'dp'=8,'x1'=2,'x0'=2,'y'=2,'core'=2] {'x1','x0','y'}, dimensions={0} | all-to-all | bytes 1310720 | tf_op jit(solution)/shard_map/all_to_all | solution.py:92
  279.4 3.3 %collective-permute-start.29 = (bf16[320,128]{1,0:T(8,128)(2,1)S(1)}, bf16[320,128]{1,0:T(8,128)(2,1)S(1)}, u32[]{:S(2)}, u32[]{:S(2)}) collective-permute-start(bf16[320,128]{1,0:T(8,128)(2,1)S(1)} %reduce_sum.105), channel_id=1, source_target_pairs={{0,0},{8,128},{128,8},{136,136},{1,1},{9,129},{129,9},{137,137},{2... | collective-permute-start | bytes 245768 | tf_op jit(solution)/shard_map/ppermute | solution.py:324
  283.0 6.7 %collective-permute-done.29 = bf16[320,128]{1,0:T(8,128)(2,1)S(1)} collective-permute-done((bf16[320,128]{1,0:T(8,128)(2,1)S(1)}, bf16[320,128]{1,0:T(8,128)(2,1)S(1)}, u32[]{:S(2)}, u32[]{:S(2)}) %collective-permute-start.29) | collective-permute-done | bytes 81952 | tf_op jit(solution)/shard_map/ppermute | solution.py:324
  (186 shorter events, 80.8 us)
Async XLA Ops:
  7.2 85.8 %all-gather.4.cloned.1.call-start = ((), (), s32[]{:S(2)}) async-start(), calls=%async_computation.3 | async-start | bytes 11141120 | tf_op jit(solution)/shard_map/all_gather | solution.py:280
  7.9 159.2 %reduce-scatter.2.cloned.1.call-start = ((), (), s32[]{:S(2)}) async-start(), calls=%async_computation.4 | async-start | bytes 5898240 | tf_op jit(solution)/shard_map/reduce_scatter | solution.py:288
  7.9 8.6 %collective-permute-start = (bf16[320,128]{0,1:T(8,128)(2,1)}, bf16[320,128]{0,1:T(8,128)(2,1)S(1)}, u32[]{:S(2)}, u32[]{:S(2)}) collective-permute-start(bf16[320,128]{0,1:T(8,128)(2,1)} %bitcast.237), channel_id=1, source_target_pairs={{0,2},{2,0},{1,3},{3,1},{4,6},{6,4},{5,7},{7,5},{8,10},{10,8},{9,1... | collective-permute-start | bytes 245768 | tf_op jit(solution)/shard_map/ppermute | solution.py:28
  9.3 36.8 %collective-permute-start.4 = (bf16[4,512,128]{2,1,0:T(8,128)(2,1)}, bf16[4,512,128]{2,1,0:T(8,128)(2,1)}, u32[]{:S(2)}, u32[]{:S(2)}) collective-permute-start(bf16[4,512,128]{2,1,0:T(8,128)(2,1)} %param.20), channel_id=1, source_target_pairs={{0,1},{1,0},{2,3},{3,2},{4,5},{5,4},{6,7},{7,6},{8,9},{9,8},{10,11... | collective-permute-start | bytes 1572872 | tf_op jit(solution)/shard_map/ppermute | solution.py:28
  17.4 9.5 %collective-permute-start.1 = (bf16[2,320,128]{1,2,0:T(8,128)(2,1)}, bf16[2,320,128]{1,2,0:T(8,128)(2,1)}, u32[]{:S(2)}, u32[]{:S(2)}) collective-permute-start(bf16[2,320,128]{1,2,0:T(8,128)(2,1)} %maximum_select_fusion.5), channel_id=1, source_target_pairs={{0,4},{4,8},{8,12},{12,0},{1,5},{5,9},{9,13},{13,1},{2,6},{6,10},{... | collective-permute-start | bytes 491528 | tf_op jit(solution)/shard_map/ppermute | solution.py:28
  18.9 9.1 %collective-permute-start.2 = (bf16[2,320,128]{1,2,0:T(8,128)(2,1)}, bf16[2,320,128]{1,2,0:T(8,128)(2,1)}, u32[]{:S(2)}, u32[]{:S(2)}) collective-permute-start(bf16[2,320,128]{1,2,0:T(8,128)(2,1)} %maximum_select_fusion.5), channel_id=1, source_target_pairs={{0,12},{4,0},{8,4},{12,8},{1,13},{5,1},{9,5},{13,9},{2,14},{6,2},{... | collective-permute-start | bytes 491528 | tf_op jit(solution)/shard_map/ppermute | solution.py:28
  20.6 14.6 %collective-permute-start.3 = (bf16[2,320,128]{1,2,0:T(8,128)(2,1)}, bf16[2,320,128]{1,2,0:T(8,128)(2,1)}, u32[]{:S(2)}, u32[]{:S(2)}) collective-permute-start(bf16[2,320,128]{1,2,0:T(8,128)(2,1)} %maximum_select_fusion.5), channel_id=1, source_target_pairs={{0,8},{4,12},{8,0},{12,4},{1,9},{5,13},{9,1},{13,5},{2,10},{6,14},... | collective-permute-start | bytes 491528 | tf_op jit(solution)/shard_map/ppermute | solution.py:28
  50.3 9.1 %collective-permute-start.8 = (bf16[128,512]{1,0:T(8,128)(2,1)S(1)}, bf16[128,512]{1,0:T(8,128)(2,1)S(1)}, u32[]{:S(2)}, u32[]{:S(2)}) collective-permute-start(bf16[128,512]{1,0:T(8,128)(2,1)S(1)} %bitcast.254), channel_id=1, source_target_pairs={{0,128},{1,144},{16,129},{17,145},{32,160},{33,176},{48,161},{49,1... | collective-permute-start | bytes 393224 | tf_op jit(solution)/shard_map/ppermute | solution.py:71
  59.5 14.6 %collective-permute-start.9 = (bf16[2,128,512]{2,1,0:T(8,128)(2,1)S(1)}, bf16[2,128,512]{2,1,0:T(8,128)(2,1)S(1)}, u32[]{:S(2)}, u32[]{:S(2)}) collective-permute-start(bf16[2,128,512]{2,1,0:T(8,128)(2,1)S(1)} %pad_maximum_fusion), channel_id=1, source_target_pairs={{0,16},{16,32},{32,48},{48,64},{64,80},{80,96},{96,112},{112,0},{1... | collective-permute-start | bytes 786440 | tf_op jit(solution)/shard_map/ppermute | solution.py:28
  60.9 13.1 %collective-permute-start.12 = (bf16[2,128,512]{2,1,0:T(8,128)(2,1)S(1)}, bf16[2,128,512]{2,1,0:T(8,128)(2,1)S(1)}, u32[]{:S(2)}, u32[]{:S(2)}) collective-permute-start(bf16[2,128,512]{2,1,0:T(8,128)(2,1)S(1)} %pad_maximum_fusion), channel_id=1, source_target_pairs={{0,112},{16,0},{32,16},{48,32},{64,48},{80,64},{96,80},{112,96},{1... | collective-permute-start | bytes 786440 | tf_op jit(solution)/shard_map/ppermute | solution.py:28
  74.0 9.5 %collective-permute-start.10 = (bf16[2,128,512]{2,1,0:T(8,128)(2,1)S(1)}, bf16[2,128,512]{2,1,0:T(8,128)(2,1)S(1)}, u32[]{:S(2)}, u32[]{:S(2)}) collective-permute-start(bf16[2,128,512]{2,1,0:T(8,128)(2,1)S(1)} %collective-permute-done.9), channel_id=1, source_target_pairs={{0,16},{16,32},{32,48},{48,64},{64,80},{80,96},{96,112},{112,0},{1... | collective-permute-start | bytes 786440 | tf_op jit(solution)/shard_map/ppermute | solution.py:28
  74.8 9.0 %collective-permute-start.13 = (bf16[2,128,512]{2,1,0:T(8,128)(2,1)S(1)}, bf16[2,128,512]{2,1,0:T(8,128)(2,1)S(1)}, u32[]{:S(2)}, u32[]{:S(2)}) collective-permute-start(bf16[2,128,512]{2,1,0:T(8,128)(2,1)S(1)} %collective-permute-done.12), channel_id=1, source_target_pairs={{0,112},{16,0},{32,16},{48,32},{64,48},{80,64},{96,80},{112,96},{1... | collective-permute-start | bytes 786440 | tf_op jit(solution)/shard_map/ppermute | solution.py:28
  83.6 8.8 %collective-permute-start.11 = (bf16[2,128,512]{2,1,0:T(8,128)(2,1)S(1)}, bf16[2,128,512]{2,1,0:T(8,128)(2,1)}, u32[]{:S(2)}, u32[]{:S(2)}) collective-permute-start(bf16[2,128,512]{2,1,0:T(8,128)(2,1)S(1)} %collective-permute-done.10), channel_id=1, source_target_pairs={{0,16},{16,32},{32,48},{48,64},{64,80},{80,96},{96,112},{112,0},{1... | collective-permute-start | bytes 786440 | tf_op jit(solution)/shard_map/ppermute | solution.py:28
  84.4 8.5 %collective-permute-start.14 = (bf16[2,128,512]{2,1,0:T(8,128)(2,1)S(1)}, bf16[2,128,512]{2,1,0:T(8,128)(2,1)}, u32[]{:S(2)}, u32[]{:S(2)}) collective-permute-start(bf16[2,128,512]{2,1,0:T(8,128)(2,1)S(1)} %collective-permute-done.13), channel_id=1, source_target_pairs={{0,112},{16,0},{32,16},{48,32},{64,48},{80,64},{96,80},{112,96},{1... | collective-permute-start | bytes 786440 | tf_op jit(solution)/shard_map/ppermute | solution.py:28
  103.1 132.2 %all-gather.6.cloned.1.call-start = ((), (), s32[]{:S(2)}) async-start(), calls=%async_computation.5 | async-start | bytes 2949120 | tf_op jit(solution)/shard_map/all_gather | solution.py:299
  103.3 8.7 %collective-permute-start.15 = (bf16[2,128,512]{2,1,0:T(8,128)(2,1)}, bf16[2,128,512]{2,1,0:T(8,128)(2,1)S(1)}, u32[]{:S(2)}, u32[]{:S(2)}) collective-permute-start(bf16[2,128,512]{2,1,0:T(8,128)(2,1)} %collective-permute-done.11), channel_id=1, source_target_pairs={{0,16},{16,32},{32,48},{48,64},{64,80},{80,96},{96,112},{112,0},{1... | collective-permute-start | bytes 786440 | tf_op jit(solution)/shard_map/ppermute | solution.py:28
  168.8 11.3 %collective-permute-start.16 = (bf16[320,512]{1,0:T(8,128)(2,1)}, bf16[320,512]{1,0:T(8,128)(2,1)}, u32[]{:S(2)}, u32[]{:S(2)}) collective-permute-start(bf16[320,512]{1,0:T(8,128)(2,1)} %dynamic-slice_bitcast_fusion), channel_id=1, source_target_pairs={{0,128},{128,0},{1,129},{129,1},{2,130},{130,2},{3,131},{131,3},{4... | collective-permute-start | bytes 983048 | tf_op jit(solution)/shard_map/ppermute | solution.py:28
  188.1 13.9 %all-to-all-start = ((bf16[8,320,128]{2,1,0:T(8,128)(2,1)}), bf16[8,320,128]{2,1,0:T(8,128)(2,1)S(1)}, u32[]{:S(2)}, u32[]{:S(2)}) async-start(bf16[8,320,128]{2,1,0:T(8,128)(2,1)} %shard_map.157), calls=%async_computation.1 | async-start | bytes 1310720 | tf_op jit(solution)/shard_map/all_to_all | solution.py:92
  202.8 15.5 %collective-permute-start.20 = (bf16[320,128]{1,0:T(8,128)(2,1)S(1)}, bf16[320,128]{1,0:T(8,128)(2,1)S(1)}, u32[]{:S(2)}, u32[]{:S(2)}) collective-permute-start(bf16[320,128]{1,0:T(8,128)(2,1)S(1)} %reduce_sum.100), channel_id=1, source_target_pairs={{0,2},{1,18},{2,32},{3,48},{4,70},{5,86},{6,100},{7,116},{8,138},{... | collective-permute-start | bytes 245768 | tf_op jit(solution)/shard_map/ppermute | solution.py:308
  219.5 10.9 %collective-permute-start.22 = (bf16[2,320,128]{2,1,0:T(8,128)(2,1)S(1)}, bf16[2,320,128]{2,1,0:T(8,128)(2,1)S(1)}, u32[]{:S(2)}, u32[]{:S(2)}) collective-permute-start(bf16[2,320,128]{2,1,0:T(8,128)(2,1)S(1)} %fusion.38), channel_id=1, source_target_pairs={{0,12},{4,0},{8,4},{12,8},{1,13},{5,1},{9,5},{13,9},{2,14},{6,2},{... | collective-permute-start | bytes 491528 | tf_op jit(solution)/shard_map/ppermute | solution.py:28
  222.7 8.5 %collective-permute-start.23 = (bf16[2,320,128]{2,1,0:T(8,128)(2,1)S(1)}, bf16[2,320,128]{2,1,0:T(8,128)(2,1)S(1)}, u32[]{:S(2)}, u32[]{:S(2)}) collective-permute-start(bf16[2,320,128]{2,1,0:T(8,128)(2,1)S(1)} %fusion.38), channel_id=1, source_target_pairs={{0,8},{4,12},{8,0},{12,4},{1,9},{5,13},{9,1},{13,5},{2,10},{6,14},... | collective-permute-start | bytes 491528 | tf_op jit(solution)/shard_map/ppermute | solution.py:28
  245.2 7.9 %collective-permute-start.27 = (bf16[128,512]{1,0:T(8,128)(2,1)S(1)}, bf16[128,512]{1,0:T(8,128)(2,1)S(1)}, u32[]{:S(2)}, u32[]{:S(2)}) collective-permute-start(bf16[128,512]{1,0:T(8,128)(2,1)S(1)} %bitcast.251), channel_id=1, source_target_pairs={{0,128},{128,0},{1,129},{129,1},{2,130},{130,2},{3,131},{131,3},{4... | collective-permute-start | bytes 393224 | tf_op jit(solution)/shard_map/ppermute | solution.py:28
  245.8 9.1 %collective-permute-start.28 = (bf16[128,512]{1,0:T(8,128)(2,1)S(1)}, bf16[128,512]{1,0:T(8,128)(2,1)S(1)}, u32[]{:S(2)}, u32[]{:S(2)}) collective-permute-start(bf16[128,512]{1,0:T(8,128)(2,1)S(1)} %bitcast.252), channel_id=1, source_target_pairs={{0,129},{1,128},{128,1},{129,0},{2,131},{3,130},{130,3},{131,2},{4... | collective-permute-start | bytes 393224 | tf_op jit(solution)/shard_map/ppermute | solution.py:319
  279.4 10.2 %collective-permute-start.29 = (bf16[320,128]{1,0:T(8,128)(2,1)S(1)}, bf16[320,128]{1,0:T(8,128)(2,1)S(1)}, u32[]{:S(2)}, u32[]{:S(2)}) collective-permute-start(bf16[320,128]{1,0:T(8,128)(2,1)S(1)} %reduce_sum.105), channel_id=1, source_target_pairs={{0,0},{8,128},{128,8},{136,136},{1,1},{9,129},{129,9},{137,137},{2... | collective-permute-start | bytes 245768 | tf_op jit(solution)/shard_map/ppermute | solution.py:324
  (32 other events, 270.1 us)
Sparse Core Ops, SparseCore 0:
  9.8 71.2 all-gather.3
  103.2 63.8 reduce-scatter.1
  188.2 46.9 all-gather.5

commit v7 on v6

--- a/solution.py
+++ b/solution.py
@@ -47,15 +47,15 @@
     return (weight_new, first_new, second_new)
 
 
-def gather_rows(rows, shift_x, beside=None):
-    ix = lax.axis_index(X)
+def gather_rows(rows):
+    ix, ic = lax.axis_index(X), lax.axis_index("core")
     ahead, back, across = rotate(rows, X, 1), rotate(rows, X, -1), rotate(rows, X, 2)
     square = jnp.zeros((4,) + rows.shape, rows.dtype)
-    square = lax.dynamic_update_index_in_dim(square, rows, ix ^ shift_x, 0)
-    square = lax.dynamic_update_index_in_dim(square, ahead, ((ix + 3) % 4) ^ shift_x, 0)
-    square = lax.dynamic_update_index_in_dim(square, back, ((ix + 1) % 4) ^ shift_x, 0)
-    square = lax.dynamic_update_index_in_dim(square, across, ((ix + 2) % 4) ^ shift_x, 0)
-    return lax.optimization_barrier((square, beside))
+    square = lax.dynamic_update_index_in_dim(square, rows, ix, 0)
+    square = lax.dynamic_update_index_in_dim(square, ahead, (ix + 3) % 4, 0)
+    square = lax.dynamic_update_index_in_dim(square, back, (ix + 1) % 4, 0)
+    square = lax.dynamic_update_index_in_dim(square, across, (ix + 2) % 4, 0)
+    return square, pair_order(square, rotate(square, "core", 1), ic, 2)
 
 
 def swap_cores(block, flip_role=False):
@@ -166,14 +166,18 @@
     return out.reshape(8, part, tokens)
 
 
-def half_products(square, gain, query_weight, keyval_weight):
-    values = square.astype(jnp.float32)
-    squares = jnp.sum(values * values, axis=(0, 1, 2))
-    scaled = (values * gain[..., None]).astype(jnp.bfloat16).reshape(-1, square.shape[-1])
+def normalize(state, norm_gain):
+    values = state.astype(jnp.float32)
+    mean_square = jnp.mean(values * values, axis=0, keepdims=True)
+    return (values * lax.rsqrt(mean_square + NORM_EPS) * norm_gain[:, None]).astype(jnp.bfloat16)
+
+
+def piece_products(piece, gain, weight):
+    values = piece.astype(jnp.float32)
+    squares = jnp.sum(values * values, axis=(0, 1))
+    scaled = (values * gain[..., None]).astype(jnp.bfloat16).reshape(-1, piece.shape[-1])
     dims = (((0,), (0,)), ((), ()))
-    queries = lax.dot_general(scaled, query_weight, dims, preferred_element_type=jnp.float32)
-    keyvals = lax.dot_general(scaled, keyval_weight, dims, preferred_element_type=jnp.float32)
-    return squares, queries, keyvals
+    return squares, lax.dot_general(scaled, weight, dims, preferred_element_type=jnp.float32)
 
 
 def revise(current_state, update, pick_codes, mask_values):
@@ -247,27 +251,13 @@
         return lax.dynamic_index_in_dim(blocks, which, 2, keepdims=False)
 
     masks = half_of(mask_vector, core)
-    sides = []
-    for which in (core, 1 - core):
-        sides.append(
-            (
-                half_of(norm_gain, which),
-                half_of(query_weight, which).reshape(-1, query_weight.shape[1]),
-                half_of(keyval_weight, which).reshape(-1, keyval_weight.shape[1]),
-            )
-        )
-    sides = lax.optimization_barrier(sides)
-
-    def attended_of(square):
-        other = rotate(square, "core", 1)
-        halves = [half_products(half, *side) for half, side in zip((square, other), sides)]
-        squares, queries, keyvals = [sum(pair) for pair in zip(*halves)]
-        factor = lax.rsqrt(squares / (16 * part) + NORM_EPS)[:, None]
-        queries = (queries * factor).astype(bf16)
-        own_half = (keyvals * factor).astype(bf16)
+
+    def attended_from(queries, own_half):
         other_half = rotate(own_half, "core", 1)
         block_keys = jnp.where(core == 0, own_half, other_half).reshape(row_count, block_len, HEAD)
-        block_values = jnp.where(core == 0, other_half, own_half).reshape(row_count, block_len, HEAD)
+        block_values = jnp.where(core == 0, other_half, own_half).reshape(
+            row_count, block_len, HEAD
+        )
         return attend(
             queries.reshape(row_count, block_len, -1, HEAD),
             cache_keys,
@@ -277,16 +267,30 @@
             prefix_lengths,
         )
 
+    def product(normed, weight):
+        return lax.dot_general(
+            normed, weight, (((0,), (0,)), ((), ())), preferred_element_type=f32
+        ).astype(bf16)
+
     cotangent = lax.all_gather(learner_cotangent, TENSOR, axis=1, tiled=True)
     state = block_states.reshape(tokens, part).T
-    square, _ = gather_rows(pair_order(state, rotate(state, "y", 1), iy, 0), 0)
-    attended = attended_of(square)
+    square, whole = gather_rows(pair_order(state, rotate(state, "y", 1), iy, 0))
+    normed = normalize(whole.reshape(-1, tokens), norm_gain)
+    attended = attended_from(product(normed, query_weight), product(normed, keyval_weight))
     both = jnp.stack([swap_cores(attended), swap_cores(attended, True)])
     attended_all, cotangent = gather_ring(both, cotangent)
 
     terms = gradient_terms(cotangent.T, learner_inputs)
     halves = lax.psum_scatter(terms, "dp", scatter_dimension=0, tiled=False)
-    halves, attended_all = lax.optimization_barrier((halves, attended_all))
+    shift_x, shift_y = role * 2 + dp // 4, dp // 2 % 2
+    joined = jnp.concatenate([query_weight, keyval_weight], 1)
+    sides = []
+    for which in (core, 1 - core):
+        gains, weights = half_of(norm_gain, which), half_of(joined, which)
+        for turn in range(4):
+            index = ix ^ shift_x ^ turn
+            sides.append((pick(gains, index), pick(weights, index).reshape(-1, joined.shape[1])))
+    halves, attended_all, sides = lax.optimization_barrier((halves, attended_all, sides))
     gradient = pick(halves, role).astype(f32) + rotate(pick(halves, 1 - role), "role", 1).astype(f32)
     new_weight, new_first, new_second = adam_update(
         gradient, master_weight.T, first_moment.T, second_moment.T
@@ -307,13 +311,22 @@
             route.append((source, sum(bit << 7 - k for k, bit in enumerate(target))))
         return lax.ppermute(update, EVERY, route)
 
-    shift_x, shift_y = role * 2 + dp // 4, dp // 2 % 2
     update = pair_order(deal(0), deal(1), iy ^ shift_y, 0).astype(f32) * out_scale
     picks = position_picks.reshape(STEPS, 1, tokens)
     rows = revise(pick(square, ix ^ shift_x), update, picks[0], pick(masks, ix ^ shift_x))
 
-    square, weight_all = gather_rows(rows, shift_x, weight_all)
-    attended = attended_of(square)
+    pieces = [rows]
+    for turn in range(1, 4):
+        pieces.append(lax.ppermute(rows, X, [(x, x ^ turn) for x in range(4)]))
+    crossed = [rotate(piece, "core", 1) for piece in pieces]
+    squares, products = 0.0, 0.0
+    for piece, side in zip(pieces + crossed, sides):
+        more_squares, more_products = piece_products(piece, *side)
+        squares, products = squares + more_squares, products + more_products
+    factor = lax.rsqrt(squares / (16 * part) + NORM_EPS)[:, None]
+    products = (products * factor).astype(bf16)
+    products, weight_all = lax.optimization_barrier((products, weight_all))
+    attended = attended_from(products[:, :depth], products[:, depth:])
     attended_pair = pair_order(attended, rotate(attended, "core", 1), core, 0)
     route = [(r * 2 + c, (1 - r) * 2 + 1 - c) for r in range(2) for c in range(2)]
     far = lax.ppermute(attended, ("role", "core"), route)
@@ -322,7 +335,7 @@
     partial = project_own(weight_all.reshape(4, 2, part, depth), attended_four)
     update = scatter_sum(partial).astype(bf16)
     update = lax.ppermute(update, ("role", "x1"), [(0, 0), (1, 2), (2, 1), (3, 3)])
-    state = pick(pick(square, ix), iy)
+    state = pick(pick(jnp.stack(pieces), shift_x), iy)
     state = revise(state, update.astype(f32) * out_scale, picks[1], pick(pick(masks, ix), iy))
     return (state.T.reshape(row_count, block_len, part), new_weight.T, new_first.T, new_second.T)
 

time: 299 us -> 292 us (0.977)
  blocking collectives: 21.4 us -> 0 us
  starting transfers between devices: 44.1 us -> 64.9 us
  local copies, waits for them, and re-layouts: 32.4 us -> 13.5 us
  waiting for transfers between devices: 145 us -> 153 us
    all_to_all x1 -> x0, blocking collectives: 21.4 us -> none  [scatter_sum(): blocks = lax.all_to_all(parts, X + ('y',), 0, 0, tiled=True)]
    all_to_all x1 -> x2, waiting for transfers between devices: 8.39 us -> 18.5 us  [scatter_sum(): blocks = lax.all_to_all(parts, X + ('y',), 0, 0, tiled=True)]
    ppermute x0 -> x3, starting transfers between devices: none -> 9.48 us  [on_device(): pieces.append(lax.ppermute(rows, X, [(x, x ^ turn) for x in range(4)]))]
    reduce_scatter x1, waiting for transfers between devices: 53.9 us -> 45.4 us  [on_device(): halves = lax.psum_scatter(terms, 'dp', scatter_dimension=0, tiled=False)]
    ppermute x2, waiting for transfers between devices: 12 us -> 4.22 us  [deal(): return lax.ppermute(update, EVERY, route)]
    dynamic_update_slice x7 -> x4, local copies, waits for them, and re-layouts: 7.47 us -> 0.11 us  [the longest x1 0.03 us: gather_rows(): square = lax.dynamic_update_index_in_dim(square, rows, ix, 0)]
    ppermute x23, starting transfers between devices: 26.8 us -> 33.1 us  [rotate(): lax.ppermute(block, axis, [(low, (low + shift) % count) for low in range(...]
    all_to_all x1 -> x2, starting transfers between devices: 4.89 us -> 10.4 us  [scatter_sum(): blocks = lax.all_to_all(parts, X + ('y',), 0, 0, tiled=True)]
  transfers between devices with their start and end apart: 34 -> 38, of which waited for: 23 -> 26; matrix products, arithmetic and copies ran while one was open for 14% -> 10% of each run, Pallas kernels for 1% -> 1%
where the time goes in v7:
time: 292 us; the launch traced here: 291 us
  waiting for transfers between devices  153 us (52%)
  starting transfers between devices  64.9 us (22%)
  other arithmetic  17.3 us (6%)
  Pallas kernels  16.7 us (6%)
  between operations  15 us (5%)
  local copies, waits for them, and re-layouts  13.5 us (5%)
  matrix products  10.4 us (4%)
    ppermute x23, waiting for transfers between devices, rotate(): lax.ppermute(block, axis, [(low, (low + shift) % count) for low in range(...  52.5 us
    reduce_scatter x1, waiting for transfers between devices, on_device(): halves = lax.psum_scatter(terms, 'dp', scatter_dimension=0, tiled=False)  45.4 us
    ppermute x23, starting transfers between devices, rotate(): lax.ppermute(block, axis, [(low, (low + shift) % count) for low in range(...  33.1 us
    all_to_all x2, waiting for transfers between devices, scatter_sum(): blocks = lax.all_to_all(parts, X + ('y',), 0, 0, tiled=True)  18.5 us
    all_to_all x2, starting transfers between devices, scatter_sum(): blocks = lax.all_to_all(parts, X + ('y',), 0, 0, tiled=True)  10.4 us
    pallas_call x1, Pallas kernels, gradient_terms(): pl.pallas_call(gradient_kernel, grid=(4,), in_specs=[pl.BlockSpec((4 * pa...  10.1 us
    ppermute x3, starting transfers between devices, on_device(): pieces.append(lax.ppermute(rows, X, [(x, x ^ turn) for x in range(4)]))  9.48 us
    ppermute x3, waiting for transfers between devices, swap_cores(): return lax.ppermute(block, ('role', 'dp', 'core'), route)  9.25 us
  transfers between devices with their start and end apart: 38, of which 26 were waited for; matrix products, arithmetic and copies ran while one was open for 10% of the time, Pallas kernels for 1%

profile of v7, /device:TPU:16, one launch (start us, length us, event | category | flops | bytes accessed | tf_op | source)
XLA Modules:
  0.0 291.0 jit_solution(5182671455526834671)
XLA Ops:
  9.3 3.5 %collective-permute-done = bf16[320,128]{0,1:T(8,128)(2,1)S(1)} collective-permute-done((bf16[320,128]{0,1:T(8,128)(2,1)}, bf16[320,128]{0,1:T(8,128)(2,1)S(1)}, u32[]{:S(2)}, u32[]{:S(2)}) %collective-permute-start) | collective-permute-done | bytes 81952 | tf_op jit(solution)/shard_map/ppermute | solution.py:28
  38.9 9.2 %collective-permute-done.8 = bf16[128,512]{1,0:T(8,128)(2,1)S(1)} collective-permute-done((bf16[128,512]{1,0:T(8,128)(2,1)S(1)}, bf16[128,512]{1,0:T(8,128)(2,1)S(1)}, u32[]{:S(2)}, u32[]{:S(2)}) %collective-permute-start.8) | collective-permute-done | bytes 131104 | tf_op jit(solution)/shard_map/ppermute | solution.py:71
  48.3 3.5 %collective-permute-start.12 = (bf16[2,128,512]{2,1,0:T(8,128)(2,1)S(1)}, bf16[2,128,512]{2,1,0:T(8,128)(2,1)S(1)}, u32[]{:S(2)}, u32[]{:S(2)}) collective-permute-start(bf16[2,128,512]{2,1,0:T(8,128)(2,1)S(1)} %pad_maximum_fusion.1), channel_id=1, source_target_pairs={{0,112},{16,0},{32,16},{48,32},{64,48},{80,64},{96,80},{112,96},{1... | collective-permute-start | bytes 786440 | tf_op jit(solution)/shard_map/ppermute | solution.py:28
  51.8 5.6 %collective-permute-done.9 = bf16[2,128,512]{2,1,0:T(8,128)(2,1)S(1)} collective-permute-done((bf16[2,128,512]{2,1,0:T(8,128)(2,1)S(1)}, bf16[2,128,512]{2,1,0:T(8,128)(2,1)S(1)}, u32[]{:S(2)}, u32[]{:S(2)}) %collective-permute-start.9) | collective-permute-done | bytes 262176 | tf_op jit(solution)/shard_map/ppermute | solution.py:28
  57.5 4.3 %collective-permute-start.13 = (bf16[2,128,512]{2,1,0:T(8,128)(2,1)S(1)}, bf16[2,128,512]{2,1,0:T(8,128)(2,1)S(1)}, u32[]{:S(2)}, u32[]{:S(2)}) collective-permute-start(bf16[2,128,512]{2,1,0:T(8,128)(2,1)S(1)} %collective-permute-done.12), channel_id=1, source_target_pairs={{0,112},{16,0},{32,16},{48,32},{64,48},{80,64},{96,80},{112,96},{1... | collective-permute-start | bytes 786440 | tf_op jit(solution)/shard_map/ppermute | solution.py:28
  61.8 6.1 %collective-permute-done.10 = bf16[2,128,512]{2,1,0:T(8,128)(2,1)S(1)} collective-permute-done((bf16[2,128,512]{2,1,0:T(8,128)(2,1)S(1)}, bf16[2,128,512]{2,1,0:T(8,128)(2,1)S(1)}, u32[]{:S(2)}, u32[]{:S(2)}) %collective-permute-start.10) | collective-permute-done | bytes 262176 | tf_op jit(solution)/shard_map/ppermute | solution.py:28
  68.7 3.5 %collective-permute-start.14 = (bf16[2,128,512]{2,1,0:T(8,128)(2,1)S(1)}, bf16[2,128,512]{2,1,0:T(8,128)(2,1)}, u32[]{:S(2)}, u32[]{:S(2)}) collective-permute-start(bf16[2,128,512]{2,1,0:T(8,128)(2,1)S(1)} %collective-permute-done.13), channel_id=1, source_target_pairs={{0,112},{16,0},{32,16},{48,32},{64,48},{80,64},{96,80},{112,96},{1... | collective-permute-start | bytes 786440 | tf_op jit(solution)/shard_map/ppermute | solution.py:28
  72.2 4.5 %collective-permute-done.11 = bf16[2,128,512]{2,1,0:T(8,128)(2,1)} collective-permute-done((bf16[2,128,512]{2,1,0:T(8,128)(2,1)S(1)}, bf16[2,128,512]{2,1,0:T(8,128)(2,1)}, u32[]{:S(2)}, u32[]{:S(2)}) %collective-permute-start.11) | collective-permute-done | bytes 262176 | tf_op jit(solution)/shard_map/ppermute | solution.py:28
  79.7 10.1 %shard_map.156 = bf16[8,2,320,512]{3,2,1,0:T(8,128)(2,1)} custom-call(bf16[5120,1024]{1,0:T(8,128)(2,1)} %bitcast.305, bf16[1024,512]{1,0:T(8,128)(2,1)} %inputs_ref.1), custom_call_target="tpu_custom_call" | custom-call | flops 5368709120 | bytes 17000000 | tf_op jit(solution)/shard_map/pallas_call | solution.py:104
  102.0 11.2 %collective-permute-done.15 = bf16[2,128,512]{2,1,0:T(8,128)(2,1)S(1)} collective-permute-done((bf16[2,128,512]{2,1,0:T(8,128)(2,1)}, bf16[2,128,512]{2,1,0:T(8,128)(2,1)S(1)}, u32[]{:S(2)}, u32[]{:S(2)}) %collective-permute-start.15) | collective-permute-done | bytes 262176 | tf_op jit(solution)/shard_map/ppermute | solution.py:28
  114.3 45.4 %reduce-scatter.2.cloned.1.call-done = bf16[1,2,320,512]{3,2,1,0:T(8,128)(2,1)} async-done(((bf16[8,2,320,512]{3,2,1,0:T(8,128)(2,1)}), bf16[1,2,320,512]{3,2,1,0:T(8,128)(2,1)}) %reduce-scatter.2.cloned.1.call-update) | async-done | bytes 655376 | tf_op jit(solution)/shard_map/reduce_scatter | solution.py:284
  161.6 10.5 %collective-permute-done.16 = bf16[320,512]{1,0:T(8,128)(2,1)} collective-permute-done((bf16[320,512]{1,0:T(8,128)(2,1)S(1)}, bf16[320,512]{1,0:T(8,128)(2,1)}, u32[]{:S(2)}, u32[]{:S(2)}) %collective-permute-start.16) | collective-permute-done | bytes 327712 | tf_op jit(solution)/shard_map/ppermute | solution.py:28
  179.6 4.4 %all-to-all-start = ((bf16[8,320,128]{2,1,0:T(8,128)(2,1)}), bf16[8,320,128]{2,1,0:T(8,128)(2,1)S(1)}, u32[]{:S(2)}, u32[]{:S(2)}) async-start(bf16[8,320,128]{2,1,0:T(8,128)(2,1)} %shard_map.157), calls=%async_computation.1 | async-start | bytes 1310720 | tf_op jit(solution)/shard_map/all_to_all | solution.py:92
  185.4 7.5 %all-to-all-done = bf16[8,320,128]{2,1,0:T(8,128)(2,1)S(1)} async-done(((bf16[8,320,128]{2,1,0:T(8,128)(2,1)}), bf16[8,320,128]{2,1,0:T(8,128)(2,1)S(1)}, u32[]{:S(2)}, u32[]{:S(2)}) %all-to-all-start) | async-done | bytes 655392 | tf_op jit(solution)/shard_map/all_to_all | solution.py:92
  193.9 3.5 %collective-permute-start.20 = (bf16[320,128]{1,0:T(8,128)(2,1)S(1)}, bf16[320,128]{1,0:T(8,128)(2,1)S(1)}, u32[]{:S(2)}, u32[]{:S(2)}) collective-permute-start(bf16[320,128]{1,0:T(8,128)(2,1)S(1)} %reduce_sum.144), channel_id=1, source_target_pairs={{0,2},{1,18},{2,32},{3,48},{4,70},{5,86},{6,100},{7,116},{8,138},{... | collective-permute-start | bytes 245768 | tf_op jit(solution)/shard_map/ppermute | solution.py:312
  197.8 4.2 %collective-permute-done.20 = bf16[320,128]{1,0:T(8,128)(2,1)S(1)} collective-permute-done((bf16[320,128]{1,0:T(8,128)(2,1)S(1)}, bf16[320,128]{1,0:T(8,128)(2,1)S(1)}, u32[]{:S(2)}, u32[]{:S(2)}) %collective-permute-start.20) | collective-permute-done | bytes 81952 | tf_op jit(solution)/shard_map/ppermute | solution.py:312
  202.2 6.5 %collective-permute-start.21 = (bf16[2,320,128]{2,1,0:T(8,128)(2,1)S(1)}, bf16[2,320,128]{2,1,0:T(8,128)(2,1)S(1)}, u32[]{:S(2)}, u32[]{:S(2)}) collective-permute-start(bf16[2,320,128]{2,1,0:T(8,128)(2,1)S(1)} %get-tuple-element.69), channel_id=1, source_target_pairs={{0,4},{4,0},{8,12},{12,8},{1,5},{5,1},{9,13},{13,9},{2,6},{6,2},{1... | collective-permute-start | bytes 491528 | tf_op jit(solution)/shard_map/ppermute | solution.py:320
  225.7 8.8 %all-gather.6.cloned.1.call-done = bf16[2560,512]{1,0:T(8,128)(2,1)} async-done(((bf16[320,512]{1,0:T(8,128)(2,1)}), bf16[2560,512]{1,0:T(8,128)(2,1)}) %all-gather.6.cloned.1.call-update) | async-done | bytes 2621456 | tf_op jit(solution)/shard_map/all_gather | solution.py:303
  242.5 4.2 %collective-permute-done.31 = bf16[128,512]{1,0:T(8,128)(2,1)} collective-permute-done((bf16[128,512]{1,0:T(8,128)(2,1)}, bf16[128,512]{1,0:T(8,128)(2,1)}, u32[]{:S(2)}, u32[]{:S(2)}) %collective-permute-start.31) | collective-permute-done | bytes 131104 | tf_op jit(solution)/shard_map/ppermute | solution.py:332
  251.7 4.3 %shard_map.158 = bf16[2,4,320,128]{3,2,1,0:T(8,128)(2,1)} custom-call(bf16[4,2,320,512]{3,2,1,0:T(8,128)(2,1)S(1)} %bitcast.249, bf16[2,2,128,512]{3,2,1,0:T(8,128)(2,1)S(1)} %maximum_select_fusion.2.tokens_ref), custom_call_target="tpu_custom_call" | custom-call | flops 671088640 | bytes 4000000 | tf_op jit(solution)/shard_map/pallas_call | solution.py:152
  256.0 6.0 %all-to-all-start.1 = ((bf16[8,320,128]{2,1,0:T(8,128)(2,1)}), bf16[8,320,128]{2,1,0:T(8,128)(2,1)S(1)}, u32[]{:S(2)}, u32[]{:S(2)}) async-start(bf16[8,320,128]{2,1,0:T(8,128)(2,1)} %bitcast.91), calls=%async_computation.2 | async-start | bytes 1310720 | tf_op jit(solution)/shard_map/all_to_all | solution.py:92
  262.3 10.9 %all-to-all-done.1 = bf16[8,320,128]{2,1,0:T(8,128)(2,1)S(1)} async-done(((bf16[8,320,128]{2,1,0:T(8,128)(2,1)}), bf16[8,320,128]{2,1,0:T(8,128)(2,1)S(1)}, u32[]{:S(2)}, u32[]{:S(2)}) %all-to-all-start.1) | async-done | bytes 655392 | tf_op jit(solution)/shard_map/all_to_all | solution.py:92
  273.3 4.7 %collective-permute-start.32 = (bf16[320,128]{1,0:T(8,128)(2,1)S(1)}, bf16[320,128]{1,0:T(8,128)(2,1)S(1)}, u32[]{:S(2)}, u32[]{:S(2)}) collective-permute-start(bf16[320,128]{1,0:T(8,128)(2,1)S(1)} %reduce_sum.155), channel_id=1, source_target_pairs={{0,0},{8,128},{128,8},{136,136},{1,1},{9,129},{129,9},{137,137},{2... | collective-permute-start | bytes 245768 | tf_op jit(solution)/shard_map/ppermute | solution.py:337
  278.2 5.3 %collective-permute-done.32 = bf16[320,128]{1,0:T(8,128)(2,1)S(1)} collective-permute-done((bf16[320,128]{1,0:T(8,128)(2,1)S(1)}, bf16[320,128]{1,0:T(8,128)(2,1)S(1)}, u32[]{:S(2)}, u32[]{:S(2)}) %collective-permute-start.32) | collective-permute-done | bytes 81952 | tf_op jit(solution)/shard_map/ppermute | solution.py:337
  (264 shorter events, 88.0 us)
Async XLA Ops:
  7.2 72.6 %all-gather.4.cloned.1.call-start = ((), (), s32[]{:S(2)}) async-start(), calls=%async_computation.3 | async-start | bytes 11141120 | tf_op jit(solution)/shard_map/all_gather | solution.py:275
  7.9 151.8 %reduce-scatter.2.cloned.1.call-start = ((), (), s32[]{:S(2)}) async-start(), calls=%async_computation.4 | async-start | bytes 5898240 | tf_op jit(solution)/shard_map/reduce_scatter | solution.py:284
  13.9 8.5 %collective-permute-start.1 = (bf16[2,320,128]{1,2,0:T(8,128)(2,1)S(1)}, bf16[2,320,128]{1,2,0:T(8,128)(2,1)S(1)}, u32[]{:S(2)}, u32[]{:S(2)}) collective-permute-start(bf16[2,320,128]{1,2,0:T(8,128)(2,1)S(1)} %maximum_select_fusion.6), channel_id=1, source_target_pairs={{0,4},{4,8},{8,12},{12,0},{1,5},{5,9},{9,13},{13,1},{2,6},{6,10},{... | collective-permute-start | bytes 491528 | tf_op jit(solution)/shard_map/ppermute | solution.py:28
  15.5 8.7 %collective-permute-start.2 = (bf16[2,320,128]{1,2,0:T(8,128)(2,1)S(1)}, bf16[2,320,128]{1,2,0:T(8,128)(2,1)S(1)}, u32[]{:S(2)}, u32[]{:S(2)}) collective-permute-start(bf16[2,320,128]{1,2,0:T(8,128)(2,1)S(1)} %maximum_select_fusion.6), channel_id=1, source_target_pairs={{0,12},{4,0},{8,4},{12,8},{1,13},{5,1},{9,5},{13,9},{2,14},{6,2},{... | collective-permute-start | bytes 491528 | tf_op jit(solution)/shard_map/ppermute | solution.py:28
  17.2 8.7 %collective-permute-start.3 = (bf16[2,320,128]{1,2,0:T(8,128)(2,1)S(1)}, bf16[2,320,128]{1,2,0:T(8,128)(2,1)S(1)}, u32[]{:S(2)}, u32[]{:S(2)}) collective-permute-start(bf16[2,320,128]{1,2,0:T(8,128)(2,1)S(1)} %maximum_select_fusion.6), channel_id=1, source_target_pairs={{0,8},{4,12},{8,0},{12,4},{1,9},{5,13},{9,1},{13,5},{2,10},{6,14},... | collective-permute-start | bytes 491528 | tf_op jit(solution)/shard_map/ppermute | solution.py:28
  37.5 10.7 %collective-permute-start.8 = (bf16[128,512]{1,0:T(8,128)(2,1)S(1)}, bf16[128,512]{1,0:T(8,128)(2,1)S(1)}, u32[]{:S(2)}, u32[]{:S(2)}) collective-permute-start(bf16[128,512]{1,0:T(8,128)(2,1)S(1)} %bitcast.294), channel_id=1, source_target_pairs={{0,128},{1,144},{16,129},{17,145},{32,160},{33,176},{48,161},{49,1... | collective-permute-start | bytes 393224 | tf_op jit(solution)/shard_map/ppermute | solution.py:71
  38.2 9.9 %collective-permute-start.7 = (bf16[128,512]{1,0:T(8,128)(2,1)S(1)}, bf16[128,512]{1,0:T(8,128)(2,1)S(1)}, u32[]{:S(2)}, u32[]{:S(2)}) collective-permute-start(bf16[128,512]{1,0:T(8,128)(2,1)S(1)} %bitcast.295), channel_id=1, source_target_pairs={{0,0},{1,16},{16,1},{17,17},{32,32},{33,48},{48,33},{49,49},{64,64... | collective-permute-start | bytes 393224 | tf_op jit(solution)/shard_map/ppermute | solution.py:71
  48.2 9.2 %collective-permute-start.9 = (bf16[2,128,512]{2,1,0:T(8,128)(2,1)S(1)}, bf16[2,128,512]{2,1,0:T(8,128)(2,1)S(1)}, u32[]{:S(2)}, u32[]{:S(2)}) collective-permute-start(bf16[2,128,512]{2,1,0:T(8,128)(2,1)S(1)} %pad_maximum_fusion.1), channel_id=1, source_target_pairs={{0,16},{16,32},{32,48},{48,64},{64,80},{80,96},{96,112},{112,0},{1... | collective-permute-start | bytes 786440 | tf_op jit(solution)/shard_map/ppermute | solution.py:28
  48.3 9.2 %collective-permute-start.12 = (bf16[2,128,512]{2,1,0:T(8,128)(2,1)S(1)}, bf16[2,128,512]{2,1,0:T(8,128)(2,1)S(1)}, u32[]{:S(2)}, u32[]{:S(2)}) collective-permute-start(bf16[2,128,512]{2,1,0:T(8,128)(2,1)S(1)} %pad_maximum_fusion.1), channel_id=1, source_target_pairs={{0,112},{16,0},{32,16},{48,32},{64,48},{80,64},{96,80},{112,96},{1... | collective-permute-start | bytes 786440 | tf_op jit(solution)/shard_map/ppermute | solution.py:28
  57.4 10.6 %collective-permute-start.10 = (bf16[2,128,512]{2,1,0:T(8,128)(2,1)S(1)}, bf16[2,128,512]{2,1,0:T(8,128)(2,1)S(1)}, u32[]{:S(2)}, u32[]{:S(2)}) collective-permute-start(bf16[2,128,512]{2,1,0:T(8,128)(2,1)S(1)} %collective-permute-done.9), channel_id=1, source_target_pairs={{0,16},{16,32},{32,48},{48,64},{64,80},{80,96},{96,112},{112,0},{1... | collective-permute-start | bytes 786440 | tf_op jit(solution)/shard_map/ppermute | solution.py:28
  57.5 10.5 %collective-permute-start.13 = (bf16[2,128,512]{2,1,0:T(8,128)(2,1)S(1)}, bf16[2,128,512]{2,1,0:T(8,128)(2,1)S(1)}, u32[]{:S(2)}, u32[]{:S(2)}) collective-permute-start(bf16[2,128,512]{2,1,0:T(8,128)(2,1)S(1)} %collective-permute-done.12), channel_id=1, source_target_pairs={{0,112},{16,0},{32,16},{48,32},{64,48},{80,64},{96,80},{112,96},{1... | collective-permute-start | bytes 786440 | tf_op jit(solution)/shard_map/ppermute | solution.py:28
  68.0 8.7 %collective-permute-start.11 = (bf16[2,128,512]{2,1,0:T(8,128)(2,1)S(1)}, bf16[2,128,512]{2,1,0:T(8,128)(2,1)}, u32[]{:S(2)}, u32[]{:S(2)}) collective-permute-start(bf16[2,128,512]{2,1,0:T(8,128)(2,1)S(1)} %collective-permute-done.10), channel_id=1, source_target_pairs={{0,16},{16,32},{32,48},{48,64},{64,80},{80,96},{96,112},{112,0},{1... | collective-permute-start | bytes 786440 | tf_op jit(solution)/shard_map/ppermute | solution.py:28
  68.7 8.6 %collective-permute-start.14 = (bf16[2,128,512]{2,1,0:T(8,128)(2,1)S(1)}, bf16[2,128,512]{2,1,0:T(8,128)(2,1)}, u32[]{:S(2)}, u32[]{:S(2)}) collective-permute-start(bf16[2,128,512]{2,1,0:T(8,128)(2,1)S(1)} %collective-permute-done.13), channel_id=1, source_target_pairs={{0,112},{16,0},{32,16},{48,32},{64,48},{80,64},{96,80},{112,96},{1... | collective-permute-start | bytes 786440 | tf_op jit(solution)/shard_map/ppermute | solution.py:28
  99.1 14.1 %collective-permute-start.15 = (bf16[2,128,512]{2,1,0:T(8,128)(2,1)}, bf16[2,128,512]{2,1,0:T(8,128)(2,1)S(1)}, u32[]{:S(2)}, u32[]{:S(2)}) collective-permute-start(bf16[2,128,512]{2,1,0:T(8,128)(2,1)} %collective-permute-done.11), channel_id=1, source_target_pairs={{0,16},{16,32},{32,48},{48,64},{64,80},{80,96},{96,112},{112,0},{1... | collective-permute-start | bytes 786440 | tf_op jit(solution)/shard_map/ppermute | solution.py:28
  160.7 11.4 %collective-permute-start.16 = (bf16[320,512]{1,0:T(8,128)(2,1)S(1)}, bf16[320,512]{1,0:T(8,128)(2,1)}, u32[]{:S(2)}, u32[]{:S(2)}) collective-permute-start(bf16[320,512]{1,0:T(8,128)(2,1)S(1)} %dynamic-slice_bitcast_fusion), channel_id=1, source_target_pairs={{0,128},{128,0},{1,129},{129,1},{2,130},{130,2},{3,131},{131,3},{4... | collective-permute-start | bytes 983048 | tf_op jit(solution)/shard_map/ppermute | solution.py:28
  179.6 13.4 %all-to-all-start = ((bf16[8,320,128]{2,1,0:T(8,128)(2,1)}), bf16[8,320,128]{2,1,0:T(8,128)(2,1)S(1)}, u32[]{:S(2)}, u32[]{:S(2)}) async-start(bf16[8,320,128]{2,1,0:T(8,128)(2,1)} %shard_map.157), calls=%async_computation.1 | async-start | bytes 1310720 | tf_op jit(solution)/shard_map/all_to_all | solution.py:92
  184.0 50.5 %all-gather.6.cloned.1.call-start = ((), (), s32[]{:S(2)}) async-start(), calls=%async_computation.5 | async-start | bytes 2949120 | tf_op jit(solution)/shard_map/all_gather | solution.py:303
  202.2 13.5 %collective-permute-start.21 = (bf16[2,320,128]{2,1,0:T(8,128)(2,1)S(1)}, bf16[2,320,128]{2,1,0:T(8,128)(2,1)S(1)}, u32[]{:S(2)}, u32[]{:S(2)}) collective-permute-start(bf16[2,320,128]{2,1,0:T(8,128)(2,1)S(1)} %get-tuple-element.69), channel_id=1, source_target_pairs={{0,4},{4,0},{8,12},{12,8},{1,5},{5,1},{9,13},{13,9},{2,6},{6,2},{1... | collective-permute-start | bytes 491528 | tf_op jit(solution)/shard_map/ppermute | solution.py:320
  210.9 8.7 %collective-permute-start.23 = (bf16[2,320,128]{2,1,0:T(8,128)(2,1)S(1)}, bf16[2,320,128]{2,1,0:T(8,128)(2,1)S(1)}, u32[]{:S(2)}, u32[]{:S(2)}) collective-permute-start(bf16[2,320,128]{2,1,0:T(8,128)(2,1)S(1)} %get-tuple-element.69), channel_id=1, source_target_pairs={{0,12},{4,8},{8,4},{12,0},{1,13},{5,9},{9,5},{13,1},{2,14},{6,10},... | collective-permute-start | bytes 491528 | tf_op jit(solution)/shard_map/ppermute | solution.py:320
  211.7 10.6 %collective-permute-start.24 = (bf16[2,320,128]{2,1,0:T(8,128)(2,1)S(1)}, bf16[2,320,128]{2,1,0:T(8,128)(2,1)S(1)}, u32[]{:S(2)}, u32[]{:S(2)}) collective-permute-start(bf16[2,320,128]{2,1,0:T(8,128)(2,1)S(1)} %get-tuple-element.69), channel_id=1, source_target_pairs={{0,1},{1,0},{2,3},{3,2},{4,5},{5,4},{6,7},{7,6},{8,9},{9,8},{10,11... | collective-permute-start | bytes 491528 | tf_op jit(solution)/shard_map/ppermute | solution.py:28
  239.1 10.4 %collective-permute-start.30 = (bf16[128,512]{1,0:T(8,128)(2,1)}, bf16[128,512]{1,0:T(8,128)(2,1)}, u32[]{:S(2)}, u32[]{:S(2)}) collective-permute-start(bf16[128,512]{1,0:T(8,128)(2,1)} %bitcast.245), channel_id=1, source_target_pairs={{0,128},{128,0},{1,129},{129,1},{2,130},{130,2},{3,131},{131,3},{4... | collective-permute-start | bytes 393224 | tf_op jit(solution)/shard_map/ppermute | solution.py:28
  242.0 8.6 %collective-permute-start.29 = (bf16[128,512]{1,0:T(8,128)(2,1)}, bf16[128,512]{1,0:T(8,128)(2,1)}, u32[]{:S(2)}, u32[]{:S(2)}) collective-permute-start(bf16[128,512]{1,0:T(8,128)(2,1)} %bitcast.245), channel_id=1, source_target_pairs={{0,1},{1,0},{2,3},{3,2},{4,5},{5,4},{6,7},{7,6},{8,9},{9,8},{10,11... | collective-permute-start | bytes 393224 | tf_op jit(solution)/shard_map/ppermute | solution.py:28
  256.0 17.2 %all-to-all-start.1 = ((bf16[8,320,128]{2,1,0:T(8,128)(2,1)}), bf16[8,320,128]{2,1,0:T(8,128)(2,1)S(1)}, u32[]{:S(2)}, u32[]{:S(2)}) async-start(bf16[8,320,128]{2,1,0:T(8,128)(2,1)} %bitcast.91), calls=%async_computation.2 | async-start | bytes 1310720 | tf_op jit(solution)/shard_map/all_to_all | solution.py:92
  273.3 10.2 %collective-permute-start.32 = (bf16[320,128]{1,0:T(8,128)(2,1)S(1)}, bf16[320,128]{1,0:T(8,128)(2,1)S(1)}, u32[]{:S(2)}, u32[]{:S(2)}) collective-permute-start(bf16[320,128]{1,0:T(8,128)(2,1)S(1)} %reduce_sum.155), channel_id=1, source_target_pairs={{0,0},{8,128},{128,8},{136,136},{1,1},{9,129},{129,9},{137,137},{2... | collective-permute-start | bytes 245768 | tf_op jit(solution)/shard_map/ppermute | solution.py:337
  (65 other events, 745.0 us)
Sparse Core Ops, SparseCore 0:
  9.8 69.8 all-gather.3
  89.9 69.7 reduce-scatter.1
  186.6 47.8 all-gather.5

commit v8 on v6

--- a/solution.py
+++ b/solution.py
@@ -48,14 +48,15 @@
 
 
 def gather_rows(rows, shift_x, beside=None):
-    ix = lax.axis_index(X)
+    ix, ic = lax.axis_index(X), lax.axis_index("core")
     ahead, back, across = rotate(rows, X, 1), rotate(rows, X, -1), rotate(rows, X, 2)
     square = jnp.zeros((4,) + rows.shape, rows.dtype)
     square = lax.dynamic_update_index_in_dim(square, rows, ix ^ shift_x, 0)
     square = lax.dynamic_update_index_in_dim(square, ahead, ((ix + 3) % 4) ^ shift_x, 0)
     square = lax.dynamic_update_index_in_dim(square, back, ((ix + 1) % 4) ^ shift_x, 0)
     square = lax.dynamic_update_index_in_dim(square, across, ((ix + 2) % 4) ^ shift_x, 0)
-    return lax.optimization_barrier((square, beside))
+    other, beside = lax.optimization_barrier((rotate(square, "core", 1), beside))
+    return pair_order(square, other, ic, 2), beside
 
 
 def swap_cores(block, flip_role=False):
@@ -117,63 +118,74 @@
     )(cotangent, inputs)
 
 
-def project_block(weight, attended, out_ref, n):
+def contract(weights, tokens):
     dims = (((1,), (1,)), ((), ()))
-    total = lax.dot_general(weight[0], attended[0], dims, preferred_element_type=jnp.float32)
-    total += lax.dot_general(weight[1], attended[1], dims, preferred_element_type=jnp.float32)
-    out_ref[n] = total.astype(out_ref.dtype)
-
-
-def project_all_kernel(weight_ref, tokens_ref, out_ref):
+    total = 0.0
+    for weight, values in zip(weights, tokens):
+        total += lax.dot_general(weight, values, dims, preferred_element_type=jnp.float32)
+    return total.astype(jnp.bfloat16)
+
+
+def project_all_kernel(place_ref, own_ref, other_ref, tokens_ref, out_ref):
+    core = place_ref[1]
+    weights = own_ref[...], other_ref[...]
     for n in range(8):
-        project_block(weight_ref, tokens_ref.at[n % 4, :, n // 4], out_ref, n)
-
-
-def project_all(weight, attended):
-    part, depth = weight.shape[1:]
+        tokens = [tokens_ref[n % 4, half, n // 4] for half in (core, 1 - core)]
+        out_ref[n] = contract(weights, tokens)
+
+
+def project_all(place, own, other, attended):
+    part, depth = own.shape
     tokens = attended.shape[3]
+    vmem = pl.BlockSpec(memory_space=pltpu.VMEM)
     return pl.pallas_call(
         project_all_kernel,
+        in_specs=[pl.BlockSpec(memory_space=pltpu.SMEM), vmem, vmem, vmem],
+        out_specs=vmem,
         out_shape=jax.ShapeDtypeStruct((8, part, tokens), jnp.bfloat16),
         compiler_params=pltpu.CompilerParams(vmem_limit_bytes=32 * 1024 * 1024),
         cost_estimate=pl.CostEstimate(
             flops=32 * part * depth * tokens, bytes_accessed=3_000_000, transcendentals=0
         ),
-    )(weight, attended)
-
-
-def project_own_kernel(weight_ref, tokens_ref, out_ref):
-    project_block(weight_ref.at[0], tokens_ref.at[:, 0], out_ref.at[0], 0)
-
-
-def project_own(weight, attended):
+    )(place, own, other, attended)
+
+
+def project_own_kernel(place_ref, weight_ref, own_ref, other_ref, far_own_ref, far_other_ref, out_ref):
+    role, core = place_ref[0], place_ref[1]
+    weights = weight_ref[0, core], weight_ref[0, 1 - core]
+    out_ref[role, 0] = contract(weights, (own_ref[...], other_ref[...]))
+    out_ref[1 - role, 0] = contract(weights, (far_own_ref[...], far_other_ref[...]))
+
+
+def project_own(place, weight, *attended):
     part, depth = weight.shape[2:]
-    tokens = attended.shape[2]
+    tokens = attended[0].shape[0]
+    whole = pl.BlockSpec((tokens, depth), lambda k: (0, 0))
     out = pl.pallas_call(
         project_own_kernel,
-        grid=(2, 4),
+        grid=(4,),
         in_specs=[
-            pl.BlockSpec((1, 2, part, depth), lambda r, k: (k, 0, 0, 0)),
-            pl.BlockSpec((2, 1, tokens, depth), lambda r, k: (0, r, 0, 0)),
+            pl.BlockSpec(memory_space=pltpu.SMEM),
+            pl.BlockSpec((1, 2, part, depth), lambda k: (k, 0, 0, 0)),
+            whole,
+            whole,
+            whole,
+            whole,
         ],
-        out_specs=pl.BlockSpec((1, 1, part, tokens), lambda r, k: (r, k, 0, 0)),
+        out_specs=pl.BlockSpec((2, 1, part, tokens), lambda k: (0, k, 0, 0)),
         out_shape=jax.ShapeDtypeStruct((2, 4, part, tokens), jnp.bfloat16),
         compiler_params=pltpu.CompilerParams(vmem_limit_bytes=32 * 1024 * 1024),
         cost_estimate=pl.CostEstimate(
             flops=32 * part * depth * tokens, bytes_accessed=4_000_000, transcendentals=0
         ),
-    )(weight, attended)
+    )(place, weight, *attended)
     return out.reshape(8, part, tokens)
 
 
-def half_products(square, gain, query_weight, keyval_weight):
-    values = square.astype(jnp.float32)
-    squares = jnp.sum(values * values, axis=(0, 1, 2))
-    scaled = (values * gain[..., None]).astype(jnp.bfloat16).reshape(-1, square.shape[-1])
-    dims = (((0,), (0,)), ((), ()))
-    queries = lax.dot_general(scaled, query_weight, dims, preferred_element_type=jnp.float32)
-    keyvals = lax.dot_general(scaled, keyval_weight, dims, preferred_element_type=jnp.float32)
-    return squares, queries, keyvals
+def normalize(state, norm_gain):
+    values = state.astype(jnp.float32)
+    mean_square = jnp.mean(values * values, axis=0, keepdims=True)
+    return (values * lax.rsqrt(mean_square + NORM_EPS) * norm_gain[:, None]).astype(jnp.bfloat16)
 
 
 def revise(current_state, update, pick_codes, mask_values):
@@ -240,32 +252,21 @@
     cache_keys = jnp.where(core == 0, prefix_cache, cache_other)
     cache_values = jnp.where(core == 0, cache_other, prefix_cache)
 
+    masks = mask_vector.reshape(4, 2, 2, part)
     ix, iy = lax.axis_index(X), lax.axis_index("y")
 
-    def half_of(array, which):
-        blocks = array.reshape((4, 2, 2, part) + array.shape[1:])
-        return lax.dynamic_index_in_dim(blocks, which, 2, keepdims=False)
-
-    masks = half_of(mask_vector, core)
-    sides = []
-    for which in (core, 1 - core):
-        sides.append(
-            (
-                half_of(norm_gain, which),
-                half_of(query_weight, which).reshape(-1, query_weight.shape[1]),
-                half_of(keyval_weight, which).reshape(-1, keyval_weight.shape[1]),
-            )
-        )
-    sides = lax.optimization_barrier(sides)
-
-    def attended_of(square):
-        other = rotate(square, "core", 1)
-        halves = [half_products(half, *side) for half, side in zip((square, other), sides)]
-        squares, queries, keyvals = [sum(pair) for pair in zip(*halves)]
-        factor = lax.rsqrt(squares / (16 * part) + NORM_EPS)[:, None]
-        queries = (queries * factor).astype(bf16)
-        own_half = (keyvals * factor).astype(bf16)
+    def rows_of(blocks, index):
+        return lax.dynamic_index_in_dim(pick(blocks, index), core, 1, keepdims=False)
+
+    def attended_of(whole):
+        normed = normalize(whole.reshape(-1, tokens), norm_gain)
+        own_half = lax.dot_general(
+            normed, keyval_weight, (((0,), (0,)), ((), ())), preferred_element_type=f32
+        ).astype(bf16)
         other_half = rotate(own_half, "core", 1)
+        queries = lax.dot_general(
+            normed, query_weight, (((0,), (0,)), ((), ())), preferred_element_type=f32
+        ).astype(bf16)
         block_keys = jnp.where(core == 0, own_half, other_half).reshape(row_count, block_len, HEAD)
         block_values = jnp.where(core == 0, other_half, own_half).reshape(row_count, block_len, HEAD)
         return attend(
@@ -279,8 +280,8 @@
 
     cotangent = lax.all_gather(learner_cotangent, TENSOR, axis=1, tiled=True)
     state = block_states.reshape(tokens, part).T
-    square, _ = gather_rows(pair_order(state, rotate(state, "y", 1), iy, 0), 0)
-    attended = attended_of(square)
+    whole, _ = gather_rows(pair_order(state, rotate(state, "y", 1), iy, 0), 0)
+    attended = attended_of(whole)
     both = jnp.stack([swap_cores(attended), swap_cores(attended, True)])
     attended_all, cotangent = gather_ring(both, cotangent)
 
@@ -292,9 +293,14 @@
         gradient, master_weight.T, first_moment.T, second_moment.T
     )
     weight_part = new_weight.astype(bf16)
-    weight_pair = pair_order(weight_part, rotate(weight_part, "core", 1), core, 0)
-
-    partial = project_all(weight_pair, attended_all.reshape(4, 2, 2, tokens, depth))
+
+    place = jnp.stack([role, core]).astype(jnp.int32)
+    partial = project_all(
+        place,
+        weight_part,
+        rotate(weight_part, "core", 1),
+        attended_all.reshape(4, 2, 2, tokens, depth),
+    )
     weight_half, partial = lax.optimization_barrier((swap_cores(weight_part), partial))
     weight_all = lax.all_gather(weight_half, "dp", axis=0)
     update = scatter_sum(partial).astype(bf16)
@@ -310,20 +316,23 @@
     shift_x, shift_y = role * 2 + dp // 4, dp // 2 % 2
     update = pair_order(deal(0), deal(1), iy ^ shift_y, 0).astype(f32) * out_scale
     picks = position_picks.reshape(STEPS, 1, tokens)
-    rows = revise(pick(square, ix ^ shift_x), update, picks[0], pick(masks, ix ^ shift_x))
-
-    square, weight_all = gather_rows(rows, shift_x, weight_all)
-    attended = attended_of(square)
-    attended_pair = pair_order(attended, rotate(attended, "core", 1), core, 0)
+    rows = revise(rows_of(whole, ix ^ shift_x), update, picks[0], rows_of(masks, ix ^ shift_x))
+
+    whole, weight_all = gather_rows(rows, shift_x, weight_all)
+    attended = attended_of(whole)
     route = [(r * 2 + c, (1 - r) * 2 + 1 - c) for r in range(2) for c in range(2)]
-    far = lax.ppermute(attended, ("role", "core"), route)
-    far_pair = pair_order(rotate(attended, "role", 1), far, core, 0)
-    attended_four = pair_order(attended_pair, far_pair, role, 1)
-    partial = project_own(weight_all.reshape(4, 2, part, depth), attended_four)
+    partial = project_own(
+        place,
+        weight_all.reshape(4, 2, part, depth),
+        attended,
+        rotate(attended, "core", 1),
+        rotate(attended, "role", 1),
+        lax.ppermute(attended, ("role", "core"), route),
+    )
     update = scatter_sum(partial).astype(bf16)
     update = lax.ppermute(update, ("role", "x1"), [(0, 0), (1, 2), (2, 1), (3, 3)])
-    state = pick(pick(square, ix), iy)
-    state = revise(state, update.astype(f32) * out_scale, picks[1], pick(pick(masks, ix), iy))
+    state = pick(rows_of(whole, ix), iy)
+    state = revise(state, update.astype(f32) * out_scale, picks[1], pick(rows_of(masks, ix), iy))
     return (state.T.reshape(row_count, block_len, part), new_weight.T, new_first.T, new_second.T)
 
 

time: 299 us -> 287 us (0.960)
  local copies, waits for them, and re-layouts: 32.4 us -> 14 us
  waiting for transfers between devices: 145 us -> 150 us
    dynamic_slice x3 -> x0, local copies, waits for them, and re-layouts: 5.61 us -> none  [half_of(): return lax.dynamic_index_in_dim(blocks, which, 2, keepdims=False)]
    convert_element_type x0 -> x2, other arithmetic: none -> 4.35 us  [normalize(): (values * lax.rsqrt(mean_square + NORM_EPS) * norm_gain[:, None]).astype(...]
    ppermute x23, waiting for transfers between devices: 49.8 us -> 54.2 us  [rotate(): lax.ppermute(block, axis, [(low, (low + shift) % count) for low in range(...]
  transfers between devices with their start and end apart: 34 -> 34, of which waited for: 23 -> 26; matrix products, arithmetic and copies ran while one was open for 14% -> 7% of each run, Pallas kernels for 1% -> 1%
where the time goes in v8:
time: 287 us; the launch traced here: 286 us
  waiting for transfers between devices  150 us (52%)
  starting transfers between devices  46.2 us (16%)
  blocking collectives  21.2 us (7%)
  other arithmetic  16.1 us (6%)
  Pallas kernels  14.9 us (5%)
  between operations  14.5 us (5%)
  local copies, waits for them, and re-layouts  14 us (5%)
  matrix products  8.98 us (3%)
    reduce_scatter x1, waiting for transfers between devices, on_device(): halves = lax.psum_scatter(terms, 'dp', scatter_dimension=0, tiled=False)  54.7 us
    ppermute x23, waiting for transfers between devices, rotate(): lax.ppermute(block, axis, [(low, (low + shift) % count) for low in range(...  54.2 us
    ppermute x23, starting transfers between devices, rotate(): lax.ppermute(block, axis, [(low, (low + shift) % count) for low in range(...  29.6 us
    all_to_all x1, blocking collectives, scatter_sum(): blocks = lax.all_to_all(parts, X + ('y',), 0, 0, tiled=True)  21.2 us
    ppermute x2, waiting for transfers between devices, deal(): return lax.ppermute(update, EVERY, route)  12.4 us
    pallas_call x1, Pallas kernels, gradient_terms(): pl.pallas_call(gradient_kernel, grid=(4,), in_specs=[pl.BlockSpec((4 * pa...  10.1 us
    ppermute x3, waiting for transfers between devices, swap_cores(): return lax.ppermute(block, ('role', 'dp', 'core'), route)  9.97 us
    all_to_all x1, waiting for transfers between devices, scatter_sum(): blocks = lax.all_to_all(parts, X + ('y',), 0, 0, tiled=True)  8.92 us
  transfers between devices with their start and end apart: 34, of which 26 were waited for; matrix products, arithmetic and copies ran while one was open for 7% of the time, Pallas kernels for 1%

profile of v8, /device:TPU:16, one launch (start us, length us, event | category | flops | bytes accessed | tf_op | source)
XLA Modules:
  0.0 286.2 jit_solution(11381898721306624559)
XLA Ops:
  9.3 3.5 %collective-permute-done = bf16[320,128]{0,1:T(8,128)(2,1)S(1)} collective-permute-done((bf16[320,128]{0,1:T(8,128)(2,1)}, bf16[320,128]{0,1:T(8,128)(2,1)S(1)}, u32[]{:S(2)}, u32[]{:S(2)}) %collective-permute-start) | collective-permute-done | bytes 81952 | tf_op jit(solution)/shard_map/ppermute | solution.py:28
  39.2 10.0 %collective-permute-done.8 = bf16[128,512]{1,0:T(8,128)(2,1)S(1)} collective-permute-done((bf16[128,512]{1,0:T(8,128)(2,1)S(1)}, bf16[128,512]{1,0:T(8,128)(2,1)S(1)}, u32[]{:S(2)}, u32[]{:S(2)}) %collective-permute-start.8) | collective-permute-done | bytes 131104 | tf_op jit(solution)/shard_map/ppermute | solution.py:72
  49.9 5.1 %collective-permute-start.12 = (bf16[2,128,512]{2,1,0:T(8,128)(2,1)S(1)}, bf16[2,128,512]{2,1,0:T(8,128)(2,1)S(1)}, u32[]{:S(2)}, u32[]{:S(2)}) collective-permute-start(bf16[2,128,512]{2,1,0:T(8,128)(2,1)S(1)} %pad_maximum_fusion), channel_id=1, source_target_pairs={{0,112},{16,0},{32,16},{48,32},{64,48},{80,64},{96,80},{112,96},{1... | collective-permute-start | bytes 786440 | tf_op jit(solution)/shard_map/ppermute | solution.py:28
  55.0 6.3 %collective-permute-done.9 = bf16[2,128,512]{2,1,0:T(8,128)(2,1)S(1)} collective-permute-done((bf16[2,128,512]{2,1,0:T(8,128)(2,1)S(1)}, bf16[2,128,512]{2,1,0:T(8,128)(2,1)S(1)}, u32[]{:S(2)}, u32[]{:S(2)}) %collective-permute-start.9) | collective-permute-done | bytes 262176 | tf_op jit(solution)/shard_map/ppermute | solution.py:28
  62.1 3.5 %collective-permute-start.13 = (bf16[2,128,512]{2,1,0:T(8,128)(2,1)S(1)}, bf16[2,128,512]{2,1,0:T(8,128)(2,1)S(1)}, u32[]{:S(2)}, u32[]{:S(2)}) collective-permute-start(bf16[2,128,512]{2,1,0:T(8,128)(2,1)S(1)} %collective-permute-done.12), channel_id=1, source_target_pairs={{0,112},{16,0},{32,16},{48,32},{64,48},{80,64},{96,80},{112,96},{1... | collective-permute-start | bytes 786440 | tf_op jit(solution)/shard_map/ppermute | solution.py:28
  65.6 5.0 %collective-permute-done.10 = bf16[2,128,512]{2,1,0:T(8,128)(2,1)S(1)} collective-permute-done((bf16[2,128,512]{2,1,0:T(8,128)(2,1)S(1)}, bf16[2,128,512]{2,1,0:T(8,128)(2,1)S(1)}, u32[]{:S(2)}, u32[]{:S(2)}) %collective-permute-start.10) | collective-permute-done | bytes 262176 | tf_op jit(solution)/shard_map/ppermute | solution.py:28
  71.8 3.7 %collective-permute-start.14 = (bf16[2,128,512]{2,1,0:T(8,128)(2,1)S(1)}, bf16[2,128,512]{2,1,0:T(8,128)(2,1)}, u32[]{:S(2)}, u32[]{:S(2)}) collective-permute-start(bf16[2,128,512]{2,1,0:T(8,128)(2,1)S(1)} %collective-permute-done.13), channel_id=1, source_target_pairs={{0,112},{16,0},{32,16},{48,32},{64,48},{80,64},{96,80},{112,96},{1... | collective-permute-start | bytes 786440 | tf_op jit(solution)/shard_map/ppermute | solution.py:28
  75.5 3.8 %collective-permute-done.11 = bf16[2,128,512]{2,1,0:T(8,128)(2,1)} collective-permute-done((bf16[2,128,512]{2,1,0:T(8,128)(2,1)S(1)}, bf16[2,128,512]{2,1,0:T(8,128)(2,1)}, u32[]{:S(2)}, u32[]{:S(2)}) %collective-permute-start.11) | collective-permute-done | bytes 262176 | tf_op jit(solution)/shard_map/ppermute | solution.py:28
  80.1 10.1 %shard_map.156 = bf16[8,2,320,512]{3,2,1,0:T(8,128)(2,1)} custom-call(bf16[5120,1024]{1,0:T(8,128)(2,1)} %bitcast.256, bf16[1024,512]{1,0:T(8,128)(2,1)} %inputs_ref.1), custom_call_target="tpu_custom_call" | custom-call | flops 5368709120 | bytes 17000000 | tf_op jit(solution)/shard_map/pallas_call | solution.py:105
  95.9 4.5 %collective-permute-done.15 = bf16[2,128,512]{2,1,0:T(8,128)(2,1)S(1)} collective-permute-done((bf16[2,128,512]{2,1,0:T(8,128)(2,1)}, bf16[2,128,512]{2,1,0:T(8,128)(2,1)S(1)}, u32[]{:S(2)}, u32[]{:S(2)}) %collective-permute-start.15) | collective-permute-done | bytes 262176 | tf_op jit(solution)/shard_map/ppermute | solution.py:28
  101.5 54.7 %reduce-scatter.2.cloned.1.call-done = bf16[1,2,320,512]{3,2,1,0:T(8,128)(2,1)} async-done(((bf16[8,2,320,512]{3,2,1,0:T(8,128)(2,1)}), bf16[1,2,320,512]{3,2,1,0:T(8,128)(2,1)}) %reduce-scatter.2.cloned.1.call-update) | async-done | bytes 655376 | tf_op jit(solution)/shard_map/reduce_scatter | solution.py:289
  158.5 10.8 %collective-permute-done.16 = bf16[320,512]{1,0:T(8,128)(2,1)} collective-permute-done((bf16[320,512]{1,0:T(8,128)(2,1)}, bf16[320,512]{1,0:T(8,128)(2,1)}, u32[]{:S(2)}, u32[]{:S(2)}) %collective-permute-start.16) | collective-permute-done | bytes 327712 | tf_op jit(solution)/shard_map/ppermute | solution.py:28
  169.3 3.3 %fusion.48 = (bf16[320,512]{1,0:T(8,128)(2,1)S(1)}, f32[320,512]{1,0:T(8,128)}, f32[512,320]{0,1:T(8,128)}, f32[512,320]{0,1:T(8,128)}) fusion(f32[512,320]{0,1:T(8,128)} %param.17, bf16[320,512]{1,0:T(8,128)(2,1)} %collective-permute-done.16, bf16[2,320,512]{2,1,0:T(8,128)(2,1)} %bitcast.227, s32[]{:T(128)S(6)} %select_n.330, f32[512,320]{0,1:T(8,128)} %param.16, ...), kind=kLoop, calls=%fused_computation.121 | loop fusion | flops 3112960 | bytes 4915204 | tf_op jit(solution)/shard_map/convert_element_type | solution.py:295
  177.2 4.9 %all-to-all-start = ((bf16[8,320,128]{2,1,0:T(8,128)(2,1)}), bf16[8,320,128]{2,1,0:T(8,128)(2,1)S(1)}, u32[]{:S(2)}, u32[]{:S(2)}) async-start(bf16[8,320,128]{2,1,0:T(8,128)(2,1)} %copy-done.2), calls=%async_computation.1 | async-start | bytes 1310720 | tf_op jit(solution)/shard_map/all_to_all | solution.py:93
  182.2 8.9 %all-to-all-done = bf16[8,320,128]{2,1,0:T(8,128)(2,1)S(1)} async-done(((bf16[8,320,128]{2,1,0:T(8,128)(2,1)}), bf16[8,320,128]{2,1,0:T(8,128)(2,1)S(1)}, u32[]{:S(2)}, u32[]{:S(2)}) %all-to-all-start) | async-done | bytes 655392 | tf_op jit(solution)/shard_map/all_to_all | solution.py:93
  191.9 3.3 %collective-permute-start.20 = (bf16[320,128]{1,0:T(8,128)(2,1)S(1)}, bf16[320,128]{1,0:T(8,128)(2,1)S(1)}, u32[]{:S(2)}, u32[]{:S(2)}) collective-permute-start(bf16[320,128]{1,0:T(8,128)(2,1)S(1)} %reduce_sum.81), channel_id=1, source_target_pairs={{0,2},{1,18},{2,32},{3,48},{4,70},{5,86},{6,100},{7,116},{8,138},{... | collective-permute-start | bytes 245768 | tf_op jit(solution)/shard_map/ppermute | solution.py:314
  195.4 12.4 %collective-permute-done.20 = bf16[320,128]{1,0:T(8,128)(2,1)S(1)} collective-permute-done((bf16[320,128]{1,0:T(8,128)(2,1)S(1)}, bf16[320,128]{1,0:T(8,128)(2,1)S(1)}, u32[]{:S(2)}, u32[]{:S(2)}) %collective-permute-start.20) | collective-permute-done | bytes 81952 | tf_op jit(solution)/shard_map/ppermute | solution.py:314
  209.0 3.2 %collective-permute-start.22 = (bf16[2,320,128]{2,1,0:T(8,128)(2,1)S(1)}, bf16[2,320,128]{2,1,0:T(8,128)(2,1)S(1)}, u32[]{:S(2)}, u32[]{:S(2)}) collective-permute-start(bf16[2,320,128]{2,1,0:T(8,128)(2,1)S(1)} %fusion.28), channel_id=1, source_target_pairs={{0,12},{4,0},{8,4},{12,8},{1,13},{5,1},{9,5},{13,9},{2,14},{6,2},{... | collective-permute-start | bytes 491528 | tf_op jit(solution)/shard_map/ppermute | solution.py:28
  217.1 3.7 %collective-permute-done.23 = bf16[2,320,128]{2,1,0:T(8,128)(2,1)S(1)} collective-permute-done((bf16[2,320,128]{2,1,0:T(8,128)(2,1)S(1)}, bf16[2,320,128]{2,1,0:T(8,128)(2,1)S(1)}, u32[]{:S(2)}, u32[]{:S(2)}) %collective-permute-start.23) | collective-permute-done | bytes 163872 | tf_op jit(solution)/shard_map/ppermute | solution.py:28
  238.2 4.5 %collective-permute-done.27.far_own_ref = bf16[128,512]{1,0:T(8,128)(2,1)S(1)} collective-permute-done((bf16[128,512]{1,0:T(8,128)(2,1)S(1)}, bf16[128,512]{1,0:T(8,128)(2,1)S(1)}, u32[]{:S(2)}, u32[]{:S(2)}) %collective-permute-start.27) | collective-permute-done | bytes 131104 | tf_op jit(solution)/shard_map/ppermute | solution.py:28
  244.6 2.7 shard_map.158
  247.3 21.2 %all_to_all.10 = bf16[8,320,128]{2,1,0:T(8,128)(2,1)S(1)} all-to-all(bf16[8,320,128]{2,1,0:T(8,128)(2,1)S(1)} %bitcast.217), channel_id=1, replica_groups=mesh['role'=2,'dp'=8,'x1'=2,'x0'=2,'y'=2,'core'=2] {'x1','x0','y'}, dimensions={0} | all-to-all | bytes 1310720 | tf_op jit(solution)/shard_map/all_to_all | solution.py:93
  268.6 3.2 %collective-permute-start.29 = (bf16[320,128]{1,0:T(8,128)(2,1)S(1)}, bf16[320,128]{1,0:T(8,128)(2,1)S(1)}, u32[]{:S(2)}, u32[]{:S(2)}) collective-permute-start(bf16[320,128]{1,0:T(8,128)(2,1)S(1)} %reduce_sum.85), channel_id=1, source_target_pairs={{0,0},{8,128},{128,8},{136,136},{1,1},{9,129},{129,9},{137,137},{2... | collective-permute-start | bytes 245768 | tf_op jit(solution)/shard_map/ppermute | solution.py:333
  272.0 6.8 %collective-permute-done.29 = bf16[320,128]{1,0:T(8,128)(2,1)S(1)} collective-permute-done((bf16[320,128]{1,0:T(8,128)(2,1)S(1)}, bf16[320,128]{1,0:T(8,128)(2,1)S(1)}, u32[]{:S(2)}, u32[]{:S(2)}) %collective-permute-start.29) | collective-permute-done | bytes 81952 | tf_op jit(solution)/shard_map/ppermute | solution.py:333
  (173 shorter events, 72.3 us)
Async XLA Ops:
  7.2 72.9 %all-gather.4.cloned.1.call-start = ((), (), s32[]{:S(2)}) async-start(), calls=%async_computation.3 | async-start | bytes 11141120 | tf_op jit(solution)/shard_map/all_gather | solution.py:281
  7.9 148.3 %reduce-scatter.2.cloned.1.call-start = ((), (), s32[]{:S(2)}) async-start(), calls=%async_computation.4 | async-start | bytes 5898240 | tf_op jit(solution)/shard_map/reduce_scatter | solution.py:289
  13.9 8.5 %collective-permute-start.1 = (bf16[2,320,128]{1,2,0:T(8,128)(2,1)S(1)}, bf16[2,320,128]{1,2,0:T(8,128)(2,1)S(1)}, u32[]{:S(2)}, u32[]{:S(2)}) collective-permute-start(bf16[2,320,128]{1,2,0:T(8,128)(2,1)S(1)} %maximum_select_fusion.3), channel_id=1, source_target_pairs={{0,4},{4,8},{8,12},{12,0},{1,5},{5,9},{9,13},{13,1},{2,6},{6,10},{... | collective-permute-start | bytes 491528 | tf_op jit(solution)/shard_map/ppermute | solution.py:28
  15.5 8.7 %collective-permute-start.2 = (bf16[2,320,128]{1,2,0:T(8,128)(2,1)S(1)}, bf16[2,320,128]{1,2,0:T(8,128)(2,1)S(1)}, u32[]{:S(2)}, u32[]{:S(2)}) collective-permute-start(bf16[2,320,128]{1,2,0:T(8,128)(2,1)S(1)} %maximum_select_fusion.3), channel_id=1, source_target_pairs={{0,12},{4,0},{8,4},{12,8},{1,13},{5,1},{9,5},{13,9},{2,14},{6,2},{... | collective-permute-start | bytes 491528 | tf_op jit(solution)/shard_map/ppermute | solution.py:28
  17.2 8.7 %collective-permute-start.3 = (bf16[2,320,128]{1,2,0:T(8,128)(2,1)S(1)}, bf16[2,320,128]{1,2,0:T(8,128)(2,1)S(1)}, u32[]{:S(2)}, u32[]{:S(2)}) collective-permute-start(bf16[2,320,128]{1,2,0:T(8,128)(2,1)S(1)} %maximum_select_fusion.3), channel_id=1, source_target_pairs={{0,8},{4,12},{8,0},{12,4},{1,9},{5,13},{9,1},{13,5},{2,10},{6,14},... | collective-permute-start | bytes 491528 | tf_op jit(solution)/shard_map/ppermute | solution.py:28
  26.3 7.8 %collective-permute-start.5 = (bf16[4,512,128]{2,1,0:T(8,128)(2,1)}, bf16[4,512,128]{2,1,0:T(8,128)(2,1)}, u32[]{:S(2)}, u32[]{:S(2)}) collective-permute-start(bf16[4,512,128]{2,1,0:T(8,128)(2,1)} %param.20), channel_id=1, source_target_pairs={{0,1},{1,0},{2,3},{3,2},{4,5},{5,4},{6,7},{7,6},{8,9},{9,8},{10,11... | collective-permute-start | bytes 1572872 | tf_op jit(solution)/shard_map/ppermute | solution.py:28
  38.4 10.7 %collective-permute-start.8 = (bf16[128,512]{1,0:T(8,128)(2,1)S(1)}, bf16[128,512]{1,0:T(8,128)(2,1)S(1)}, u32[]{:S(2)}, u32[]{:S(2)}) collective-permute-start(bf16[128,512]{1,0:T(8,128)(2,1)S(1)} %bitcast.246), channel_id=1, source_target_pairs={{0,128},{1,144},{16,129},{17,145},{32,160},{33,176},{48,161},{49,1... | collective-permute-start | bytes 393224 | tf_op jit(solution)/shard_map/ppermute | solution.py:72
  49.2 12.1 %collective-permute-start.9 = (bf16[2,128,512]{2,1,0:T(8,128)(2,1)S(1)}, bf16[2,128,512]{2,1,0:T(8,128)(2,1)S(1)}, u32[]{:S(2)}, u32[]{:S(2)}) collective-permute-start(bf16[2,128,512]{2,1,0:T(8,128)(2,1)S(1)} %pad_maximum_fusion), channel_id=1, source_target_pairs={{0,16},{16,32},{32,48},{48,64},{64,80},{80,96},{96,112},{112,0},{1... | collective-permute-start | bytes 786440 | tf_op jit(solution)/shard_map/ppermute | solution.py:28
  49.9 11.5 %collective-permute-start.12 = (bf16[2,128,512]{2,1,0:T(8,128)(2,1)S(1)}, bf16[2,128,512]{2,1,0:T(8,128)(2,1)S(1)}, u32[]{:S(2)}, u32[]{:S(2)}) collective-permute-start(bf16[2,128,512]{2,1,0:T(8,128)(2,1)S(1)} %pad_maximum_fusion), channel_id=1, source_target_pairs={{0,112},{16,0},{32,16},{48,32},{64,48},{80,64},{96,80},{112,96},{1... | collective-permute-start | bytes 786440 | tf_op jit(solution)/shard_map/ppermute | solution.py:28
  61.3 9.3 %collective-permute-start.10 = (bf16[2,128,512]{2,1,0:T(8,128)(2,1)S(1)}, bf16[2,128,512]{2,1,0:T(8,128)(2,1)S(1)}, u32[]{:S(2)}, u32[]{:S(2)}) collective-permute-start(bf16[2,128,512]{2,1,0:T(8,128)(2,1)S(1)} %collective-permute-done.9), channel_id=1, source_target_pairs={{0,16},{16,32},{32,48},{48,64},{64,80},{80,96},{96,112},{112,0},{1... | collective-permute-start | bytes 786440 | tf_op jit(solution)/shard_map/ppermute | solution.py:28
  62.1 9.0 %collective-permute-start.13 = (bf16[2,128,512]{2,1,0:T(8,128)(2,1)S(1)}, bf16[2,128,512]{2,1,0:T(8,128)(2,1)S(1)}, u32[]{:S(2)}, u32[]{:S(2)}) collective-permute-start(bf16[2,128,512]{2,1,0:T(8,128)(2,1)S(1)} %collective-permute-done.12), channel_id=1, source_target_pairs={{0,112},{16,0},{32,16},{48,32},{64,48},{80,64},{96,80},{112,96},{1... | collective-permute-start | bytes 786440 | tf_op jit(solution)/shard_map/ppermute | solution.py:28
  70.7 8.6 %collective-permute-start.11 = (bf16[2,128,512]{2,1,0:T(8,128)(2,1)S(1)}, bf16[2,128,512]{2,1,0:T(8,128)(2,1)}, u32[]{:S(2)}, u32[]{:S(2)}) collective-permute-start(bf16[2,128,512]{2,1,0:T(8,128)(2,1)S(1)} %collective-permute-done.10), channel_id=1, source_target_pairs={{0,16},{16,32},{32,48},{48,64},{64,80},{80,96},{96,112},{112,0},{1... | collective-permute-start | bytes 786440 | tf_op jit(solution)/shard_map/ppermute | solution.py:28
  71.8 8.2 %collective-permute-start.14 = (bf16[2,128,512]{2,1,0:T(8,128)(2,1)S(1)}, bf16[2,128,512]{2,1,0:T(8,128)(2,1)}, u32[]{:S(2)}, u32[]{:S(2)}) collective-permute-start(bf16[2,128,512]{2,1,0:T(8,128)(2,1)S(1)} %collective-permute-done.13), channel_id=1, source_target_pairs={{0,112},{16,0},{32,16},{48,32},{64,48},{80,64},{96,80},{112,96},{1... | collective-permute-start | bytes 786440 | tf_op jit(solution)/shard_map/ppermute | solution.py:28
  90.2 133.8 %all-gather.6.cloned.1.call-start = ((), (), s32[]{:S(2)}) async-start(), calls=%async_computation.5 | async-start | bytes 2949120 | tf_op jit(solution)/shard_map/all_gather | solution.py:305
  90.4 10.0 %collective-permute-start.15 = (bf16[2,128,512]{2,1,0:T(8,128)(2,1)}, bf16[2,128,512]{2,1,0:T(8,128)(2,1)S(1)}, u32[]{:S(2)}, u32[]{:S(2)}) collective-permute-start(bf16[2,128,512]{2,1,0:T(8,128)(2,1)} %collective-permute-done.11), channel_id=1, source_target_pairs={{0,16},{16,32},{32,48},{48,64},{64,80},{80,96},{96,112},{112,0},{1... | collective-permute-start | bytes 786440 | tf_op jit(solution)/shard_map/ppermute | solution.py:28
  157.9 11.3 %collective-permute-start.16 = (bf16[320,512]{1,0:T(8,128)(2,1)}, bf16[320,512]{1,0:T(8,128)(2,1)}, u32[]{:S(2)}, u32[]{:S(2)}) collective-permute-start(bf16[320,512]{1,0:T(8,128)(2,1)} %dynamic-slice_bitcast_fusion), channel_id=1, source_target_pairs={{0,128},{128,0},{1,129},{129,1},{2,130},{130,2},{3,131},{131,3},{4... | collective-permute-start | bytes 983048 | tf_op jit(solution)/shard_map/ppermute | solution.py:28
  177.2 13.9 %all-to-all-start = ((bf16[8,320,128]{2,1,0:T(8,128)(2,1)}), bf16[8,320,128]{2,1,0:T(8,128)(2,1)S(1)}, u32[]{:S(2)}, u32[]{:S(2)}) async-start(bf16[8,320,128]{2,1,0:T(8,128)(2,1)} %copy-done.2), calls=%async_computation.1 | async-start | bytes 1310720 | tf_op jit(solution)/shard_map/all_to_all | solution.py:93
  191.9 15.9 %collective-permute-start.20 = (bf16[320,128]{1,0:T(8,128)(2,1)S(1)}, bf16[320,128]{1,0:T(8,128)(2,1)S(1)}, u32[]{:S(2)}, u32[]{:S(2)}) collective-permute-start(bf16[320,128]{1,0:T(8,128)(2,1)S(1)} %reduce_sum.81), channel_id=1, source_target_pairs={{0,2},{1,18},{2,32},{3,48},{4,70},{5,86},{6,100},{7,116},{8,138},{... | collective-permute-start | bytes 245768 | tf_op jit(solution)/shard_map/ppermute | solution.py:314
  208.9 8.1 %collective-permute-start.21 = (bf16[2,320,128]{2,1,0:T(8,128)(2,1)S(1)}, bf16[2,320,128]{2,1,0:T(8,128)(2,1)S(1)}, u32[]{:S(2)}, u32[]{:S(2)}) collective-permute-start(bf16[2,320,128]{2,1,0:T(8,128)(2,1)S(1)} %fusion.28), channel_id=1, source_target_pairs={{0,4},{4,8},{8,12},{12,0},{1,5},{5,9},{9,13},{13,1},{2,6},{6,10},{... | collective-permute-start | bytes 491528 | tf_op jit(solution)/shard_map/ppermute | solution.py:28
  209.0 8.1 %collective-permute-start.22 = (bf16[2,320,128]{2,1,0:T(8,128)(2,1)S(1)}, bf16[2,320,128]{2,1,0:T(8,128)(2,1)S(1)}, u32[]{:S(2)}, u32[]{:S(2)}) collective-permute-start(bf16[2,320,128]{2,1,0:T(8,128)(2,1)S(1)} %fusion.28), channel_id=1, source_target_pairs={{0,12},{4,0},{8,4},{12,8},{1,13},{5,1},{9,5},{13,9},{2,14},{6,2},{... | collective-permute-start | bytes 491528 | tf_op jit(solution)/shard_map/ppermute | solution.py:28
  212.2 8.6 %collective-permute-start.23 = (bf16[2,320,128]{2,1,0:T(8,128)(2,1)S(1)}, bf16[2,320,128]{2,1,0:T(8,128)(2,1)S(1)}, u32[]{:S(2)}, u32[]{:S(2)}) collective-permute-start(bf16[2,320,128]{2,1,0:T(8,128)(2,1)S(1)} %fusion.28), channel_id=1, source_target_pairs={{0,8},{4,12},{8,0},{12,4},{1,9},{5,13},{9,1},{13,5},{2,10},{6,14},... | collective-permute-start | bytes 491528 | tf_op jit(solution)/shard_map/ppermute | solution.py:28
  234.8 7.9 %collective-permute-start.27 = (bf16[128,512]{1,0:T(8,128)(2,1)S(1)}, bf16[128,512]{1,0:T(8,128)(2,1)S(1)}, u32[]{:S(2)}, u32[]{:S(2)}) collective-permute-start(bf16[128,512]{1,0:T(8,128)(2,1)S(1)} %bitcast.219), channel_id=1, source_target_pairs={{0,128},{128,0},{1,129},{129,1},{2,130},{130,2},{3,131},{131,3},{4... | collective-permute-start | bytes 393224 | tf_op jit(solution)/shard_map/ppermute | solution.py:28
  236.6 8.0 %collective-permute-start.28 = (bf16[128,512]{1,0:T(8,128)(2,1)S(1)}, bf16[128,512]{1,0:T(8,128)(2,1)S(1)}, u32[]{:S(2)}, u32[]{:S(2)}) collective-permute-start(bf16[128,512]{1,0:T(8,128)(2,1)S(1)} %bitcast.220), channel_id=1, source_target_pairs={{0,129},{1,128},{128,1},{129,0},{2,131},{3,130},{130,3},{131,2},{4... | collective-permute-start | bytes 393224 | tf_op jit(solution)/shard_map/ppermute | solution.py:330
  268.6 10.2 %collective-permute-start.29 = (bf16[320,128]{1,0:T(8,128)(2,1)S(1)}, bf16[320,128]{1,0:T(8,128)(2,1)S(1)}, u32[]{:S(2)}, u32[]{:S(2)}) collective-permute-start(bf16[320,128]{1,0:T(8,128)(2,1)S(1)} %reduce_sum.85), channel_id=1, source_target_pairs={{0,0},{8,128},{128,8},{136,136},{1,1},{9,129},{129,9},{137,137},{2... | collective-permute-start | bytes 245768 | tf_op jit(solution)/shard_map/ppermute | solution.py:333
  (31 other events, 162.1 us)
Sparse Core Ops, SparseCore 0:
  9.9 69.8 all-gather.3
  90.3 65.8 reduce-scatter.1
  177.3 46.6 all-gather.5

commit v9 on v8

--- a/solution.py
+++ b/solution.py
@@ -150,36 +150,41 @@
     )(place, own, other, attended)
 
 
-def project_own_kernel(place_ref, weight_ref, own_ref, other_ref, far_own_ref, far_other_ref, out_ref):
+def project_own_kernel(place_ref, weight_ref, own_ref, far_ref, near_ref, away_ref):
     role, core = place_ref[0], place_ref[1]
-    weights = weight_ref[0, core], weight_ref[0, 1 - core]
-    out_ref[role, 0] = contract(weights, (own_ref[...], other_ref[...]))
-    out_ref[1 - role, 0] = contract(weights, (far_own_ref[...], far_other_ref[...]))
-
-
-def project_own(place, weight, *attended):
-    part, depth = weight.shape[2:]
-    tokens = attended[0].shape[0]
+    dims = (((1,), (1,)), ((), ()))
+    for tokens_ref, index in ((own_ref, role), (far_ref, 1 - role)):
+        tokens = tokens_ref[...]
+        near_ref[index, 0] = lax.dot_general(
+            weight_ref[core], tokens, dims, preferred_element_type=jnp.float32
+        )
+        away_ref[index, 0] = contract((weight_ref[1 - core],), (tokens,))
+
+
+def project_own(place, weight, own, far):
+    part, depth = weight.shape[1:]
+    tokens = own.shape[0]
     whole = pl.BlockSpec((tokens, depth), lambda k: (0, 0))
-    out = pl.pallas_call(
+    block = pl.BlockSpec((2, 1, part, tokens), lambda k: (0, k, 0, 0))
+    return pl.pallas_call(
         project_own_kernel,
         grid=(4,),
         in_specs=[
             pl.BlockSpec(memory_space=pltpu.SMEM),
-            pl.BlockSpec((1, 2, part, depth), lambda k: (k, 0, 0, 0)),
-            whole,
-            whole,
+            pl.BlockSpec((2, part, depth), lambda k: (k, 0, 0)),
             whole,
             whole,
         ],
-        out_specs=pl.BlockSpec((2, 1, part, tokens), lambda k: (0, k, 0, 0)),
-        out_shape=jax.ShapeDtypeStruct((2, 4, part, tokens), jnp.bfloat16),
+        out_specs=[block, block],
+        out_shape=[
+            jax.ShapeDtypeStruct((2, 4, part, tokens), jnp.float32),
+            jax.ShapeDtypeStruct((2, 4, part, tokens), jnp.bfloat16),
+        ],
         compiler_params=pltpu.CompilerParams(vmem_limit_bytes=32 * 1024 * 1024),
         cost_estimate=pl.CostEstimate(
-            flops=32 * part * depth * tokens, bytes_accessed=4_000_000, transcendentals=0
+            flops=32 * part * depth * tokens, bytes_accessed=5_000_000, transcendentals=0
         ),
-    )(place, weight, *attended)
-    return out.reshape(8, part, tokens)
+    )(place, weight, own, far)
 
 
 def normalize(state, norm_gain):
@@ -293,6 +298,7 @@
         gradient, master_weight.T, first_moment.T, second_moment.T
     )
     weight_part = new_weight.astype(bf16)
+    weight_all = lax.all_gather(weight_part, "dp", axis=0)
 
     place = jnp.stack([role, core]).astype(jnp.int32)
     partial = project_all(
@@ -301,8 +307,6 @@
         rotate(weight_part, "core", 1),
         attended_all.reshape(4, 2, 2, tokens, depth),
     )
-    weight_half, partial = lax.optimization_barrier((swap_cores(weight_part), partial))
-    weight_all = lax.all_gather(weight_half, "dp", axis=0)
     update = scatter_sum(partial).astype(bf16)
 
     def deal(flip):
@@ -320,15 +324,9 @@
 
     whole, weight_all = gather_rows(rows, shift_x, weight_all)
     attended = attended_of(whole)
-    route = [(r * 2 + c, (1 - r) * 2 + 1 - c) for r in range(2) for c in range(2)]
-    partial = project_own(
-        place,
-        weight_all.reshape(4, 2, part, depth),
-        attended,
-        rotate(attended, "core", 1),
-        rotate(attended, "role", 1),
-        lax.ppermute(attended, ("role", "core"), route),
-    )
+    near, away = project_own(place, weight_all, attended, rotate(attended, "role", 1))
+    partial = (near + rotate(away, "core", 1).astype(f32)).astype(bf16)
+    partial = partial.reshape(8, part, tokens)
     update = scatter_sum(partial).astype(bf16)
     update = lax.ppermute(update, ("role", "x1"), [(0, 0), (1, 2), (2, 1), (3, 3)])
     state = pick(rows_of(whole, ix), iy)

time: 287 us -> 285 us (level)
  starting transfers between devices: 46.2 us -> 41.6 us
  waiting for transfers between devices: 150 us -> 154 us
  blocking collectives: 21.2 us -> 17.6 us
    ppermute x23, waiting for transfers between devices: 54.2 us -> 58 us  [rotate(): lax.ppermute(block, axis, [(low, (low + shift) % count) for low in range(...]
    all_to_all x1, blocking collectives: 21.2 us -> 17.6 us  [scatter_sum(): blocks = lax.all_to_all(parts, X + ('y',), 0, 0, tiled=True)]
    unnamed x45 -> x47, local copies, waits for them, and re-layouts: 4.4 us -> 6.08 us
    ppermute x3 -> x2, waiting for transfers between devices: 9.97 us -> 9.97 us  [swap_cores(): return lax.ppermute(block, ('role', 'dp', 'core'), route)]
  transfers between devices with their start and end apart: 34 -> 32, of which waited for: 26 -> 25; matrix products, arithmetic and copies ran while one was open for 7% -> 7% of each run, Pallas kernels for 1% -> 1%
where the time goes in v9:
time: 285 us; the launch traced here: 284 us
  waiting for transfers between devices  154 us (54%)
  starting transfers between devices  41.6 us (15%)
  blocking collectives  17.6 us (6%)
  other arithmetic  16.6 us (6%)
  local copies, waits for them, and re-layouts  15.7 us (6%)
  Pallas kernels  14.9 us (5%)
  between operations  14.5 us (5%)
  matrix products  8.98 us (3%)
    ppermute x23, waiting for transfers between devices, rotate(): lax.ppermute(block, axis, [(low, (low + shift) % count) for low in range(...  58 us
    reduce_scatter x1, waiting for transfers between devices, on_device(): halves = lax.psum_scatter(terms, 'dp', scatter_dimension=0, tiled=False)  54.7 us
    ppermute x23, starting transfers between devices, rotate(): lax.ppermute(block, axis, [(low, (low + shift) % count) for low in range(...  28.2 us
    all_to_all x1, blocking collectives, scatter_sum(): blocks = lax.all_to_all(parts, X + ('y',), 0, 0, tiled=True)  17.6 us
    ppermute x2, waiting for transfers between devices, deal(): return lax.ppermute(update, EVERY, route)  12.2 us
    all_to_all x1, waiting for transfers between devices, scatter_sum(): blocks = lax.all_to_all(parts, X + ('y',), 0, 0, tiled=True)  11.1 us
    pallas_call x1, Pallas kernels, gradient_terms(): pl.pallas_call(gradient_kernel, grid=(4,), in_specs=[pl.BlockSpec((4 * pa...  10.1 us
    ppermute x2, waiting for transfers between devices, swap_cores(): return lax.ppermute(block, ('role', 'dp', 'core'), route)  9.97 us
  transfers between devices with their start and end apart: 32, of which 25 were waited for; matrix products, arithmetic and copies ran while one was open for 7% of the time, Pallas kernels for 1%

profile of v9, /device:TPU:16, one launch (start us, length us, event | category | flops | bytes accessed | tf_op | source)
XLA Modules:
  0.0 283.9 jit_solution(1097354643564807217)
XLA Ops:
  9.3 3.5 %collective-permute-done = bf16[320,128]{0,1:T(8,128)(2,1)S(1)} collective-permute-done((bf16[320,128]{0,1:T(8,128)(2,1)}, bf16[320,128]{0,1:T(8,128)(2,1)S(1)}, u32[]{:S(2)}, u32[]{:S(2)}) %collective-permute-start) | collective-permute-done | bytes 81952 | tf_op jit(solution)/shard_map/ppermute | solution.py:28
  39.2 10.0 %collective-permute-done.8 = bf16[128,512]{1,0:T(8,128)(2,1)S(1)} collective-permute-done((bf16[128,512]{1,0:T(8,128)(2,1)S(1)}, bf16[128,512]{1,0:T(8,128)(2,1)S(1)}, u32[]{:S(2)}, u32[]{:S(2)}) %collective-permute-start.8) | collective-permute-done | bytes 131104 | tf_op jit(solution)/shard_map/ppermute | solution.py:72
  49.9 5.1 %collective-permute-start.12 = (bf16[2,128,512]{2,1,0:T(8,128)(2,1)S(1)}, bf16[2,128,512]{2,1,0:T(8,128)(2,1)S(1)}, u32[]{:S(2)}, u32[]{:S(2)}) collective-permute-start(bf16[2,128,512]{2,1,0:T(8,128)(2,1)S(1)} %pad_maximum_fusion), channel_id=1, source_target_pairs={{0,112},{16,0},{32,16},{48,32},{64,48},{80,64},{96,80},{112,96},{1... | collective-permute-start | bytes 786440 | tf_op jit(solution)/shard_map/ppermute | solution.py:28
  55.0 6.3 %collective-permute-done.9 = bf16[2,128,512]{2,1,0:T(8,128)(2,1)S(1)} collective-permute-done((bf16[2,128,512]{2,1,0:T(8,128)(2,1)S(1)}, bf16[2,128,512]{2,1,0:T(8,128)(2,1)S(1)}, u32[]{:S(2)}, u32[]{:S(2)}) %collective-permute-start.9) | collective-permute-done | bytes 262176 | tf_op jit(solution)/shard_map/ppermute | solution.py:28
  62.1 3.5 %collective-permute-start.13 = (bf16[2,128,512]{2,1,0:T(8,128)(2,1)S(1)}, bf16[2,128,512]{2,1,0:T(8,128)(2,1)S(1)}, u32[]{:S(2)}, u32[]{:S(2)}) collective-permute-start(bf16[2,128,512]{2,1,0:T(8,128)(2,1)S(1)} %collective-permute-done.12), channel_id=1, source_target_pairs={{0,112},{16,0},{32,16},{48,32},{64,48},{80,64},{96,80},{112,96},{1... | collective-permute-start | bytes 786440 | tf_op jit(solution)/shard_map/ppermute | solution.py:28
  65.6 5.0 %collective-permute-done.10 = bf16[2,128,512]{2,1,0:T(8,128)(2,1)S(1)} collective-permute-done((bf16[2,128,512]{2,1,0:T(8,128)(2,1)S(1)}, bf16[2,128,512]{2,1,0:T(8,128)(2,1)S(1)}, u32[]{:S(2)}, u32[]{:S(2)}) %collective-permute-start.10) | collective-permute-done | bytes 262176 | tf_op jit(solution)/shard_map/ppermute | solution.py:28
  71.8 3.7 %collective-permute-start.14 = (bf16[2,128,512]{2,1,0:T(8,128)(2,1)S(1)}, bf16[2,128,512]{2,1,0:T(8,128)(2,1)}, u32[]{:S(2)}, u32[]{:S(2)}) collective-permute-start(bf16[2,128,512]{2,1,0:T(8,128)(2,1)S(1)} %collective-permute-done.13), channel_id=1, source_target_pairs={{0,112},{16,0},{32,16},{48,32},{64,48},{80,64},{96,80},{112,96},{1... | collective-permute-start | bytes 786440 | tf_op jit(solution)/shard_map/ppermute | solution.py:28
  75.5 3.8 %collective-permute-done.11 = bf16[2,128,512]{2,1,0:T(8,128)(2,1)} collective-permute-done((bf16[2,128,512]{2,1,0:T(8,128)(2,1)S(1)}, bf16[2,128,512]{2,1,0:T(8,128)(2,1)}, u32[]{:S(2)}, u32[]{:S(2)}) %collective-permute-start.11) | collective-permute-done | bytes 262176 | tf_op jit(solution)/shard_map/ppermute | solution.py:28
  80.1 10.1 %shard_map.156 = bf16[8,2,320,512]{3,2,1,0:T(8,128)(2,1)} custom-call(bf16[5120,1024]{1,0:T(8,128)(2,1)} %bitcast.253, bf16[1024,512]{1,0:T(8,128)(2,1)} %inputs_ref.1), custom_call_target="tpu_custom_call" | custom-call | flops 5368709120 | bytes 17000000 | tf_op jit(solution)/shard_map/pallas_call | solution.py:105
  95.9 4.5 %collective-permute-done.15 = bf16[2,128,512]{2,1,0:T(8,128)(2,1)S(1)} collective-permute-done((bf16[2,128,512]{2,1,0:T(8,128)(2,1)}, bf16[2,128,512]{2,1,0:T(8,128)(2,1)S(1)}, u32[]{:S(2)}, u32[]{:S(2)}) %collective-permute-start.15) | collective-permute-done | bytes 262176 | tf_op jit(solution)/shard_map/ppermute | solution.py:28
  101.5 54.7 %reduce-scatter.2.cloned.1.call-done = bf16[1,2,320,512]{3,2,1,0:T(8,128)(2,1)} async-done(((bf16[8,2,320,512]{3,2,1,0:T(8,128)(2,1)}), bf16[1,2,320,512]{3,2,1,0:T(8,128)(2,1)}) %reduce-scatter.2.cloned.1.call-update) | async-done | bytes 655376 | tf_op jit(solution)/shard_map/reduce_scatter | solution.py:294
  158.5 10.8 %collective-permute-done.16 = bf16[320,512]{1,0:T(8,128)(2,1)} collective-permute-done((bf16[320,512]{1,0:T(8,128)(2,1)}, bf16[320,512]{1,0:T(8,128)(2,1)}, u32[]{:S(2)}, u32[]{:S(2)}) %collective-permute-start.16) | collective-permute-done | bytes 327712 | tf_op jit(solution)/shard_map/ppermute | solution.py:28
  169.3 3.6 %fusion.48 = (bf16[320,512]{1,0:T(8,128)(2,1)}, f32[320,512]{1,0:T(8,128)}, f32[512,320]{0,1:T(8,128)}, f32[512,320]{0,1:T(8,128)}) fusion(f32[512,320]{0,1:T(8,128)} %param.17, bf16[320,512]{1,0:T(8,128)(2,1)} %collective-permute-done.16, bf16[2,320,512]{2,1,0:T(8,128)(2,1)} %bitcast.224, s32[]{:T(128)S(6)} %select_n.330, f32[512,320]{0,1:T(8,128)} %param.16, ...), kind=kLoop, calls=%fused_computation.122 | loop fusion | flops 3112960 | bytes 4915204 | tf_op jit(solution)/shard_map/convert_element_type | solution.py:300
  178.7 4.9 %all-to-all-start = ((bf16[8,320,128]{2,1,0:T(8,128)(2,1)}), bf16[8,320,128]{2,1,0:T(8,128)(2,1)S(1)}, u32[]{:S(2)}, u32[]{:S(2)}) async-start(bf16[8,320,128]{2,1,0:T(8,128)(2,1)} %copy-done.3), calls=%async_computation.1 | async-start | bytes 1310720 | tf_op jit(solution)/shard_map/all_to_all | solution.py:93
  183.7 11.1 %all-to-all-done = bf16[8,320,128]{2,1,0:T(8,128)(2,1)S(1)} async-done(((bf16[8,320,128]{2,1,0:T(8,128)(2,1)}), bf16[8,320,128]{2,1,0:T(8,128)(2,1)S(1)}, u32[]{:S(2)}, u32[]{:S(2)}) %all-to-all-start) | async-done | bytes 655392 | tf_op jit(solution)/shard_map/all_to_all | solution.py:93
  195.6 3.6 %collective-permute-start.19 = (bf16[320,128]{1,0:T(8,128)(2,1)S(1)}, bf16[320,128]{1,0:T(8,128)(2,1)S(1)}, u32[]{:S(2)}, u32[]{:S(2)}) collective-permute-start(bf16[320,128]{1,0:T(8,128)(2,1)S(1)} %reduce_sum.81), channel_id=1, source_target_pairs={{0,2},{1,18},{2,32},{3,48},{4,70},{5,86},{6,100},{7,116},{8,138},{... | collective-permute-start | bytes 245768 | tf_op jit(solution)/shard_map/ppermute | solution.py:318
  199.3 12.2 %collective-permute-done.19 = bf16[320,128]{1,0:T(8,128)(2,1)S(1)} collective-permute-done((bf16[320,128]{1,0:T(8,128)(2,1)S(1)}, bf16[320,128]{1,0:T(8,128)(2,1)S(1)}, u32[]{:S(2)}, u32[]{:S(2)}) %collective-permute-start.19) | collective-permute-done | bytes 81952 | tf_op jit(solution)/shard_map/ppermute | solution.py:318
  212.7 3.2 %collective-permute-start.21 = (bf16[2,320,128]{2,1,0:T(8,128)(2,1)S(1)}, bf16[2,320,128]{2,1,0:T(8,128)(2,1)S(1)}, u32[]{:S(2)}, u32[]{:S(2)}) collective-permute-start(bf16[2,320,128]{2,1,0:T(8,128)(2,1)S(1)} %fusion.28), channel_id=1, source_target_pairs={{0,12},{4,0},{8,4},{12,8},{1,13},{5,1},{9,5},{13,9},{2,14},{6,2},{... | collective-permute-start | bytes 491528 | tf_op jit(solution)/shard_map/ppermute | solution.py:28
  219.2 2.5 collective-permute-done.21
  239.3 4.1 %collective-permute-done.25.far_ref = bf16[128,512]{1,0:T(8,128)(2,1)S(1)} collective-permute-done((bf16[128,512]{1,0:T(8,128)(2,1)S(1)}, bf16[128,512]{1,0:T(8,128)(2,1)S(1)}, u32[]{:S(2)}, u32[]{:S(2)}) %collective-permute-start.25) | collective-permute-done | bytes 131104 | tf_op jit(solution)/shard_map/ppermute | solution.py:28
  243.5 2.8 shard_map.158
  248.6 17.6 %all_to_all.10 = bf16[8,320,128]{2,1,0:T(8,128)(2,1)S(1)} all-to-all(bf16[8,320,128]{2,1,0:T(8,128)(2,1)S(1)} %bitcast.220), channel_id=1, replica_groups=mesh['role'=2,'dp'=8,'x1'=2,'x0'=2,'y'=2,'core'=2] {'x1','x0','y'}, dimensions={0} | all-to-all | bytes 1310720 | tf_op jit(solution)/shard_map/all_to_all | solution.py:93
  266.3 2.7 collective-permute-start.27
  269.2 7.3 %collective-permute-done.27 = bf16[320,128]{1,0:T(8,128)(2,1)S(1)} collective-permute-done((bf16[320,128]{1,0:T(8,128)(2,1)S(1)}, bf16[320,128]{1,0:T(8,128)(2,1)S(1)}, u32[]{:S(2)}, u32[]{:S(2)}) %collective-permute-start.27) | collective-permute-done | bytes 81952 | tf_op jit(solution)/shard_map/ppermute | solution.py:331
  (172 shorter events, 72.7 us)
Async XLA Ops:
  7.2 72.9 %all-gather.4.cloned.1.call-start = ((), (), s32[]{:S(2)}) async-start(), calls=%async_computation.3 | async-start | bytes 11141120 | tf_op jit(solution)/shard_map/all_gather | solution.py:286
  7.9 148.3 %reduce-scatter.2.cloned.1.call-start = ((), (), s32[]{:S(2)}) async-start(), calls=%async_computation.4 | async-start | bytes 5898240 | tf_op jit(solution)/shard_map/reduce_scatter | solution.py:294
  8.0 4.9 %collective-permute-start = (bf16[320,128]{0,1:T(8,128)(2,1)}, bf16[320,128]{0,1:T(8,128)(2,1)S(1)}, u32[]{:S(2)}, u32[]{:S(2)}) collective-permute-start(bf16[320,128]{0,1:T(8,128)(2,1)} %bitcast.230), channel_id=1, source_target_pairs={{0,2},{2,0},{1,3},{3,1},{4,6},{6,4},{5,7},{7,5},{8,10},{10,8},{9,1... | collective-permute-start | bytes 245768 | tf_op jit(solution)/shard_map/ppermute | solution.py:28
  13.9 8.5 %collective-permute-start.1 = (bf16[2,320,128]{1,2,0:T(8,128)(2,1)S(1)}, bf16[2,320,128]{1,2,0:T(8,128)(2,1)S(1)}, u32[]{:S(2)}, u32[]{:S(2)}) collective-permute-start(bf16[2,320,128]{1,2,0:T(8,128)(2,1)S(1)} %maximum_select_fusion.3), channel_id=1, source_target_pairs={{0,4},{4,8},{8,12},{12,0},{1,5},{5,9},{9,13},{13,1},{2,6},{6,10},{... | collective-permute-start | bytes 491528 | tf_op jit(solution)/shard_map/ppermute | solution.py:28
  15.5 8.7 %collective-permute-start.2 = (bf16[2,320,128]{1,2,0:T(8,128)(2,1)S(1)}, bf16[2,320,128]{1,2,0:T(8,128)(2,1)S(1)}, u32[]{:S(2)}, u32[]{:S(2)}) collective-permute-start(bf16[2,320,128]{1,2,0:T(8,128)(2,1)S(1)} %maximum_select_fusion.3), channel_id=1, source_target_pairs={{0,12},{4,0},{8,4},{12,8},{1,13},{5,1},{9,5},{13,9},{2,14},{6,2},{... | collective-permute-start | bytes 491528 | tf_op jit(solution)/shard_map/ppermute | solution.py:28
  17.2 8.7 %collective-permute-start.3 = (bf16[2,320,128]{1,2,0:T(8,128)(2,1)S(1)}, bf16[2,320,128]{1,2,0:T(8,128)(2,1)S(1)}, u32[]{:S(2)}, u32[]{:S(2)}) collective-permute-start(bf16[2,320,128]{1,2,0:T(8,128)(2,1)S(1)} %maximum_select_fusion.3), channel_id=1, source_target_pairs={{0,8},{4,12},{8,0},{12,4},{1,9},{5,13},{9,1},{13,5},{2,10},{6,14},... | collective-permute-start | bytes 491528 | tf_op jit(solution)/shard_map/ppermute | solution.py:28
  26.3 7.8 %collective-permute-start.5 = (bf16[4,512,128]{2,1,0:T(8,128)(2,1)}, bf16[4,512,128]{2,1,0:T(8,128)(2,1)}, u32[]{:S(2)}, u32[]{:S(2)}) collective-permute-start(bf16[4,512,128]{2,1,0:T(8,128)(2,1)} %param.20), channel_id=1, source_target_pairs={{0,1},{1,0},{2,3},{3,2},{4,5},{5,4},{6,7},{7,6},{8,9},{9,8},{10,11... | collective-permute-start | bytes 1572872 | tf_op jit(solution)/shard_map/ppermute | solution.py:28
  38.4 10.7 %collective-permute-start.8 = (bf16[128,512]{1,0:T(8,128)(2,1)S(1)}, bf16[128,512]{1,0:T(8,128)(2,1)S(1)}, u32[]{:S(2)}, u32[]{:S(2)}) collective-permute-start(bf16[128,512]{1,0:T(8,128)(2,1)S(1)} %bitcast.243), channel_id=1, source_target_pairs={{0,128},{1,144},{16,129},{17,145},{32,160},{33,176},{48,161},{49,1... | collective-permute-start | bytes 393224 | tf_op jit(solution)/shard_map/ppermute | solution.py:72
  49.2 12.1 %collective-permute-start.9 = (bf16[2,128,512]{2,1,0:T(8,128)(2,1)S(1)}, bf16[2,128,512]{2,1,0:T(8,128)(2,1)S(1)}, u32[]{:S(2)}, u32[]{:S(2)}) collective-permute-start(bf16[2,128,512]{2,1,0:T(8,128)(2,1)S(1)} %pad_maximum_fusion), channel_id=1, source_target_pairs={{0,16},{16,32},{32,48},{48,64},{64,80},{80,96},{96,112},{112,0},{1... | collective-permute-start | bytes 786440 | tf_op jit(solution)/shard_map/ppermute | solution.py:28
  49.9 11.5 %collective-permute-start.12 = (bf16[2,128,512]{2,1,0:T(8,128)(2,1)S(1)}, bf16[2,128,512]{2,1,0:T(8,128)(2,1)S(1)}, u32[]{:S(2)}, u32[]{:S(2)}) collective-permute-start(bf16[2,128,512]{2,1,0:T(8,128)(2,1)S(1)} %pad_maximum_fusion), channel_id=1, source_target_pairs={{0,112},{16,0},{32,16},{48,32},{64,48},{80,64},{96,80},{112,96},{1... | collective-permute-start | bytes 786440 | tf_op jit(solution)/shard_map/ppermute | solution.py:28
  61.3 9.3 %collective-permute-start.10 = (bf16[2,128,512]{2,1,0:T(8,128)(2,1)S(1)}, bf16[2,128,512]{2,1,0:T(8,128)(2,1)S(1)}, u32[]{:S(2)}, u32[]{:S(2)}) collective-permute-start(bf16[2,128,512]{2,1,0:T(8,128)(2,1)S(1)} %collective-permute-done.9), channel_id=1, source_target_pairs={{0,16},{16,32},{32,48},{48,64},{64,80},{80,96},{96,112},{112,0},{1... | collective-permute-start | bytes 786440 | tf_op jit(solution)/shard_map/ppermute | solution.py:28
  62.1 9.0 %collective-permute-start.13 = (bf16[2,128,512]{2,1,0:T(8,128)(2,1)S(1)}, bf16[2,128,512]{2,1,0:T(8,128)(2,1)S(1)}, u32[]{:S(2)}, u32[]{:S(2)}) collective-permute-start(bf16[2,128,512]{2,1,0:T(8,128)(2,1)S(1)} %collective-permute-done.12), channel_id=1, source_target_pairs={{0,112},{16,0},{32,16},{48,32},{64,48},{80,64},{96,80},{112,96},{1... | collective-permute-start | bytes 786440 | tf_op jit(solution)/shard_map/ppermute | solution.py:28
  70.7 8.6 %collective-permute-start.11 = (bf16[2,128,512]{2,1,0:T(8,128)(2,1)S(1)}, bf16[2,128,512]{2,1,0:T(8,128)(2,1)}, u32[]{:S(2)}, u32[]{:S(2)}) collective-permute-start(bf16[2,128,512]{2,1,0:T(8,128)(2,1)S(1)} %collective-permute-done.10), channel_id=1, source_target_pairs={{0,16},{16,32},{32,48},{48,64},{64,80},{80,96},{96,112},{112,0},{1... | collective-permute-start | bytes 786440 | tf_op jit(solution)/shard_map/ppermute | solution.py:28
  71.8 8.2 %collective-permute-start.14 = (bf16[2,128,512]{2,1,0:T(8,128)(2,1)S(1)}, bf16[2,128,512]{2,1,0:T(8,128)(2,1)}, u32[]{:S(2)}, u32[]{:S(2)}) collective-permute-start(bf16[2,128,512]{2,1,0:T(8,128)(2,1)S(1)} %collective-permute-done.13), channel_id=1, source_target_pairs={{0,112},{16,0},{32,16},{48,32},{64,48},{80,64},{96,80},{112,96},{1... | collective-permute-start | bytes 786440 | tf_op jit(solution)/shard_map/ppermute | solution.py:28
  90.2 135.2 %all-gather.6.cloned.1.call-start = ((), (), s32[]{:S(2)}) async-start(), calls=%async_computation.5 | async-start | bytes 2949120 | tf_op jit(solution)/shard_map/all_gather | solution.py:301
  90.4 10.0 %collective-permute-start.15 = (bf16[2,128,512]{2,1,0:T(8,128)(2,1)}, bf16[2,128,512]{2,1,0:T(8,128)(2,1)S(1)}, u32[]{:S(2)}, u32[]{:S(2)}) collective-permute-start(bf16[2,128,512]{2,1,0:T(8,128)(2,1)} %collective-permute-done.11), channel_id=1, source_target_pairs={{0,16},{16,32},{32,48},{48,64},{64,80},{80,96},{96,112},{112,0},{1... | collective-permute-start | bytes 786440 | tf_op jit(solution)/shard_map/ppermute | solution.py:28
  157.9 11.3 %collective-permute-start.16 = (bf16[320,512]{1,0:T(8,128)(2,1)}, bf16[320,512]{1,0:T(8,128)(2,1)}, u32[]{:S(2)}, u32[]{:S(2)}) collective-permute-start(bf16[320,512]{1,0:T(8,128)(2,1)} %dynamic-slice_bitcast_fusion), channel_id=1, source_target_pairs={{0,128},{128,0},{1,129},{129,1},{2,130},{130,2},{3,131},{131,3},{4... | collective-permute-start | bytes 983048 | tf_op jit(solution)/shard_map/ppermute | solution.py:28
  178.7 16.1 %all-to-all-start = ((bf16[8,320,128]{2,1,0:T(8,128)(2,1)}), bf16[8,320,128]{2,1,0:T(8,128)(2,1)S(1)}, u32[]{:S(2)}, u32[]{:S(2)}) async-start(bf16[8,320,128]{2,1,0:T(8,128)(2,1)} %copy-done.3), calls=%async_computation.1 | async-start | bytes 1310720 | tf_op jit(solution)/shard_map/all_to_all | solution.py:93
  195.6 15.9 %collective-permute-start.19 = (bf16[320,128]{1,0:T(8,128)(2,1)S(1)}, bf16[320,128]{1,0:T(8,128)(2,1)S(1)}, u32[]{:S(2)}, u32[]{:S(2)}) collective-permute-start(bf16[320,128]{1,0:T(8,128)(2,1)S(1)} %reduce_sum.81), channel_id=1, source_target_pairs={{0,2},{1,18},{2,32},{3,48},{4,70},{5,86},{6,100},{7,116},{8,138},{... | collective-permute-start | bytes 245768 | tf_op jit(solution)/shard_map/ppermute | solution.py:318
  212.6 6.6 %collective-permute-start.20 = (bf16[2,320,128]{2,1,0:T(8,128)(2,1)S(1)}, bf16[2,320,128]{2,1,0:T(8,128)(2,1)S(1)}, u32[]{:S(2)}, u32[]{:S(2)}) collective-permute-start(bf16[2,320,128]{2,1,0:T(8,128)(2,1)S(1)} %fusion.28), channel_id=1, source_target_pairs={{0,4},{4,8},{8,12},{12,0},{1,5},{5,9},{9,13},{13,1},{2,6},{6,10},{... | collective-permute-start | bytes 491528 | tf_op jit(solution)/shard_map/ppermute | solution.py:28
  212.7 9.0 %collective-permute-start.21 = (bf16[2,320,128]{2,1,0:T(8,128)(2,1)S(1)}, bf16[2,320,128]{2,1,0:T(8,128)(2,1)S(1)}, u32[]{:S(2)}, u32[]{:S(2)}) collective-permute-start(bf16[2,320,128]{2,1,0:T(8,128)(2,1)S(1)} %fusion.28), channel_id=1, source_target_pairs={{0,12},{4,0},{8,4},{12,8},{1,13},{5,1},{9,5},{13,9},{2,14},{6,2},{... | collective-permute-start | bytes 491528 | tf_op jit(solution)/shard_map/ppermute | solution.py:28
  215.9 7.1 %collective-permute-start.22 = (bf16[2,320,128]{2,1,0:T(8,128)(2,1)S(1)}, bf16[2,320,128]{2,1,0:T(8,128)(2,1)S(1)}, u32[]{:S(2)}, u32[]{:S(2)}) collective-permute-start(bf16[2,320,128]{2,1,0:T(8,128)(2,1)S(1)} %fusion.28), channel_id=1, source_target_pairs={{0,8},{4,12},{8,0},{12,4},{1,9},{5,13},{9,1},{13,5},{2,10},{6,14},... | collective-permute-start | bytes 491528 | tf_op jit(solution)/shard_map/ppermute | solution.py:28
  236.9 6.6 %collective-permute-start.25 = (bf16[128,512]{1,0:T(8,128)(2,1)S(1)}, bf16[128,512]{1,0:T(8,128)(2,1)S(1)}, u32[]{:S(2)}, u32[]{:S(2)}) collective-permute-start(bf16[128,512]{1,0:T(8,128)(2,1)S(1)} %bitcast.216), channel_id=1, source_target_pairs={{0,128},{128,0},{1,129},{129,1},{2,130},{130,2},{3,131},{131,3},{4... | collective-permute-start | bytes 393224 | tf_op jit(solution)/shard_map/ppermute | solution.py:28
  266.3 10.2 %collective-permute-start.27 = (bf16[320,128]{1,0:T(8,128)(2,1)S(1)}, bf16[320,128]{1,0:T(8,128)(2,1)S(1)}, u32[]{:S(2)}, u32[]{:S(2)}) collective-permute-start(bf16[320,128]{1,0:T(8,128)(2,1)S(1)} %reduce_sum.85), channel_id=1, source_target_pairs={{0,0},{8,128},{128,8},{136,136},{1,1},{9,129},{129,9},{137,137},{2... | collective-permute-start | bytes 245768 | tf_op jit(solution)/shard_map/ppermute | solution.py:331
  (30 other events, 149.5 us)
Sparse Core Ops, SparseCore 0:
  9.9 69.8 all-gather.3
  90.3 65.8 reduce-scatter.1
  173.0 42.6 all-gather.5

commit v10 on v9

--- a/solution.py
+++ b/solution.py
@@ -55,8 +55,8 @@
     square = lax.dynamic_update_index_in_dim(square, ahead, ((ix + 3) % 4) ^ shift_x, 0)
     square = lax.dynamic_update_index_in_dim(square, back, ((ix + 1) % 4) ^ shift_x, 0)
     square = lax.dynamic_update_index_in_dim(square, across, ((ix + 2) % 4) ^ shift_x, 0)
-    other, beside = lax.optimization_barrier((rotate(square, "core", 1), beside))
-    return pair_order(square, other, ic, 2), beside
+    square, beside = lax.optimization_barrier((square, beside))
+    return pair_order(square, rotate(square, "core", 1), ic, 2), beside
 
 
 def swap_cores(block, flip_role=False):
@@ -94,28 +94,33 @@
     return jnp.sum(blocks.astype(jnp.float32), axis=0)
 
 
-def gradient_kernel(cotangent_ref, inputs_ref, out_ref):
+def gradient_kernel(role_ref, cotangent_ref, inputs_ref, out_ref):
     terms = jnp.dot(cotangent_ref[...], inputs_ref[...], preferred_element_type=jnp.float32)
     out_ref[...] = terms.astype(out_ref.dtype).reshape(out_ref.shape)
 
 
-def gradient_terms(cotangent, inputs):
+def gradient_terms(role, cotangent, inputs):
     tokens, depth = inputs.shape
     part = cotangent.shape[0] // 16
     return pl.pallas_call(
         gradient_kernel,
-        grid=(4,),
-        in_specs=[
-            pl.BlockSpec((4 * part, tokens), lambda i: (i, 0)),
-            pl.BlockSpec((tokens, depth), lambda i: (0, 0)),
-        ],
-        out_specs=pl.BlockSpec((4, 1, part, depth), lambda i: (i % 2, i // 2, 0, 0)),
+        grid_spec=pltpu.PrefetchScalarGridSpec(
+            num_scalar_prefetch=1,
+            grid=(4,),
+            in_specs=[
+                pl.BlockSpec((4 * part, tokens), lambda i, role: (i, 0)),
+                pl.BlockSpec((tokens, depth), lambda i, role: (0, 0)),
+            ],
+            out_specs=pl.BlockSpec(
+                (4, 1, part, depth), lambda i, role: (i % 2, (i // 2) ^ role[0], 0, 0)
+            ),
+        ),
         out_shape=jax.ShapeDtypeStruct((8, 2, part, depth), jnp.bfloat16),
         compiler_params=pltpu.CompilerParams(vmem_limit_bytes=60 * 1024 * 1024),
         cost_estimate=pl.CostEstimate(
             flops=2 * 16 * part * tokens * depth, bytes_accessed=17_000_000, transcendentals=0
         ),
-    )(cotangent, inputs)
+    )(role, cotangent, inputs)
 
 
 def contract(weights, tokens):
@@ -290,15 +295,17 @@
     both = jnp.stack([swap_cores(attended), swap_cores(attended, True)])
     attended_all, cotangent = gather_ring(both, cotangent)
 
-    terms = gradient_terms(cotangent.T, learner_inputs)
+    terms = gradient_terms(role.astype(jnp.int32).reshape(1), cotangent.T, learner_inputs)
     halves = lax.psum_scatter(terms, "dp", scatter_dimension=0, tiled=False)
     halves, attended_all = lax.optimization_barrier((halves, attended_all))
-    gradient = pick(halves, role).astype(f32) + rotate(pick(halves, 1 - role), "role", 1).astype(f32)
+    halves = halves.reshape(2, part, depth)
+    gradient = halves[0].astype(f32) + rotate(halves[1], "role", 1).astype(f32)
     new_weight, new_first, new_second = adam_update(
         gradient, master_weight.T, first_moment.T, second_moment.T
     )
     weight_part = new_weight.astype(bf16)
-    weight_all = lax.all_gather(weight_part, "dp", axis=0)
+    weight_sent = lax.optimization_barrier(new_weight).astype(bf16)
+    weight_all = lax.all_gather(weight_sent, "dp", axis=0)
 
     place = jnp.stack([role, core]).astype(jnp.int32)
     partial = project_all(

time: 285 us -> 283 us (level)
    unnamed x47 -> x51, local copies, waits for them, and re-layouts: 6.08 us -> 5.38 us
where the time goes in v10:
time: 283 us; the launch traced here: 282 us
  waiting for transfers between devices  155 us (55%)
  starting transfers between devices  41.9 us (15%)
  blocking collectives  17.6 us (6%)
  other arithmetic  15.5 us (5%)
  Pallas kernels  14.9 us (5%)
  between operations  14.5 us (5%)
  local copies, waits for them, and re-layouts  13.3 us (5%)
  matrix products  8.97 us (3%)
    ppermute x23, waiting for transfers between devices, rotate(): lax.ppermute(block, axis, [(low, (low + shift) % count) for low in range(...  57.8 us
    reduce_scatter x1, waiting for transfers between devices, on_device(): halves = lax.psum_scatter(terms, 'dp', scatter_dimension=0, tiled=False)  55.6 us
    ppermute x23, starting transfers between devices, rotate(): lax.ppermute(block, axis, [(low, (low + shift) % count) for low in range(...  28.6 us
    all_to_all x1, blocking collectives, scatter_sum(): blocks = lax.all_to_all(parts, X + ('y',), 0, 0, tiled=True)  17.6 us
    ppermute x2, waiting for transfers between devices, deal(): return lax.ppermute(update, EVERY, route)  12.2 us
    all_to_all x1, waiting for transfers between devices, scatter_sum(): blocks = lax.all_to_all(parts, X + ('y',), 0, 0, tiled=True)  11.1 us
    pallas_call x1, Pallas kernels, gradient_terms(): pl.pallas_call(gradient_kernel, grid_spec=pltpu.PrefetchScalarGridSpec(nu...  10.1 us
    ppermute x2, waiting for transfers between devices, swap_cores(): return lax.ppermute(block, ('role', 'dp', 'core'), route)  9.97 us
  transfers between devices with their start and end apart: 32, of which 25 were waited for; matrix products, arithmetic and copies ran while one was open for 7% of the time, Pallas kernels for 1%

profile of v10, /device:TPU:16, one launch (start us, length us, event | category | flops | bytes accessed | tf_op | source)
XLA Modules:
  0.0 281.8 jit_solution(5985184176820476385)
XLA Ops:
  9.3 3.5 %collective-permute-done = bf16[320,128]{0,1:T(8,128)(2,1)S(1)} collective-permute-done((bf16[320,128]{0,1:T(8,128)(2,1)}, bf16[320,128]{0,1:T(8,128)(2,1)S(1)}, u32[]{:S(2)}, u32[]{:S(2)}) %collective-permute-start) | collective-permute-done | bytes 81952 | tf_op jit(solution)/shard_map/ppermute | solution.py:28
  39.2 10.0 %collective-permute-done.8 = bf16[128,512]{1,0:T(8,128)(2,1)S(1)} collective-permute-done((bf16[128,512]{1,0:T(8,128)(2,1)S(1)}, bf16[128,512]{1,0:T(8,128)(2,1)S(1)}, u32[]{:S(2)}, u32[]{:S(2)}) %collective-permute-start.8) | collective-permute-done | bytes 131104 | tf_op jit(solution)/shard_map/ppermute | solution.py:72
  49.9 5.1 %collective-permute-start.12 = (bf16[2,128,512]{2,1,0:T(8,128)(2,1)S(1)}, bf16[2,128,512]{2,1,0:T(8,128)(2,1)S(1)}, u32[]{:S(2)}, u32[]{:S(2)}) collective-permute-start(bf16[2,128,512]{2,1,0:T(8,128)(2,1)S(1)} %pad_maximum_fusion), channel_id=1, source_target_pairs={{0,112},{16,0},{32,16},{48,32},{64,48},{80,64},{96,80},{112,96},{1... | collective-permute-start | bytes 786440 | tf_op jit(solution)/shard_map/ppermute | solution.py:28
  55.0 6.4 %collective-permute-done.9 = bf16[2,128,512]{2,1,0:T(8,128)(2,1)S(1)} collective-permute-done((bf16[2,128,512]{2,1,0:T(8,128)(2,1)S(1)}, bf16[2,128,512]{2,1,0:T(8,128)(2,1)S(1)}, u32[]{:S(2)}, u32[]{:S(2)}) %collective-permute-start.9) | collective-permute-done | bytes 262176 | tf_op jit(solution)/shard_map/ppermute | solution.py:28
  62.1 3.5 %collective-permute-start.13 = (bf16[2,128,512]{2,1,0:T(8,128)(2,1)S(1)}, bf16[2,128,512]{2,1,0:T(8,128)(2,1)S(1)}, u32[]{:S(2)}, u32[]{:S(2)}) collective-permute-start(bf16[2,128,512]{2,1,0:T(8,128)(2,1)S(1)} %collective-permute-done.12), channel_id=1, source_target_pairs={{0,112},{16,0},{32,16},{48,32},{64,48},{80,64},{96,80},{112,96},{1... | collective-permute-start | bytes 786440 | tf_op jit(solution)/shard_map/ppermute | solution.py:28
  65.6 5.1 %collective-permute-done.10 = bf16[2,128,512]{2,1,0:T(8,128)(2,1)S(1)} collective-permute-done((bf16[2,128,512]{2,1,0:T(8,128)(2,1)S(1)}, bf16[2,128,512]{2,1,0:T(8,128)(2,1)S(1)}, u32[]{:S(2)}, u32[]{:S(2)}) %collective-permute-start.10) | collective-permute-done | bytes 262176 | tf_op jit(solution)/shard_map/ppermute | solution.py:28
  71.1 3.7 %collective-permute-start.14 = (bf16[2,128,512]{2,1,0:T(8,128)(2,1)S(1)}, bf16[2,128,512]{2,1,0:T(8,128)(2,1)S(1)}, u32[]{:S(2)}, u32[]{:S(2)}) collective-permute-start(bf16[2,128,512]{2,1,0:T(8,128)(2,1)S(1)} %collective-permute-done.13), channel_id=1, source_target_pairs={{0,112},{16,0},{32,16},{48,32},{64,48},{80,64},{96,80},{112,96},{1... | collective-permute-start | bytes 786440 | tf_op jit(solution)/shard_map/ppermute | solution.py:28
  74.8 4.5 %collective-permute-done.11 = bf16[2,128,512]{2,1,0:T(8,128)(2,1)} collective-permute-done((bf16[2,128,512]{2,1,0:T(8,128)(2,1)S(1)}, bf16[2,128,512]{2,1,0:T(8,128)(2,1)}, u32[]{:S(2)}, u32[]{:S(2)}) %collective-permute-start.11) | collective-permute-done | bytes 262176 | tf_op jit(solution)/shard_map/ppermute | solution.py:28
  79.7 10.1 %shard_map.156 = bf16[8,2,320,512]{3,2,1,0:T(8,128)(2,1)} custom-call(s32[1]{0:T(128)} %bitcast.15.role_ref, bf16[5120,1024]{1,0:T(8,128)(2,1)} %bitcast.253, bf16[1024,512]{1,0:T(8,128)(2,1)} %inputs_ref.1), custom_call_target="tpu_custom_call" | custom-call | flops 5368709120 | bytes 17000000 | tf_op jit(solution)/shard_map/pallas_call | solution.py:105
  95.8 4.5 %collective-permute-done.15 = bf16[2,128,512]{2,1,0:T(8,128)(2,1)S(1)} collective-permute-done((bf16[2,128,512]{2,1,0:T(8,128)(2,1)}, bf16[2,128,512]{2,1,0:T(8,128)(2,1)S(1)}, u32[]{:S(2)}, u32[]{:S(2)}) %collective-permute-start.15) | collective-permute-done | bytes 262176 | tf_op jit(solution)/shard_map/ppermute | solution.py:28
  100.5 55.6 %reduce-scatter.2.cloned.1.call-done = bf16[1,2,320,512]{3,2,1,0:T(8,128)(2,1)} async-done(((bf16[8,2,320,512]{3,2,1,0:T(8,128)(2,1)}), bf16[1,2,320,512]{3,2,1,0:T(8,128)(2,1)}) %reduce-scatter.2.cloned.1.call-update) | async-done | bytes 655376 | tf_op jit(solution)/shard_map/reduce_scatter | solution.py:299
  157.7 10.5 %collective-permute-done.16 = bf16[320,512]{1,0:T(8,128)(2,1)S(1)} collective-permute-done((bf16[320,512]{1,0:T(8,128)(2,1)S(1)}, bf16[320,512]{1,0:T(8,128)(2,1)S(1)}, u32[]{:S(2)}, u32[]{:S(2)}) %collective-permute-start.16) | collective-permute-done | bytes 327712 | tf_op jit(solution)/shard_map/ppermute | solution.py:28
  168.2 3.1 %fusion.48 = (bf16[320,512]{1,0:T(8,128)(2,1)}, f32[320,512]{1,0:T(8,128)S(1)}, f32[512,320]{0,1:T(8,128)}, f32[512,320]{0,1:T(8,128)}) fusion(f32[512,320]{0,1:T(8,128)} %param.17, bf16[320,512]{1,0:T(8,128)(2,1)S(1)} %collective-permute-done.16, bf16[2,320,512]{2,1,0:T(8,128)(2,1)} %bitcast.225, f32[512,320]{0,1:T(8,128)} %param.16, f32[512,320]{0,1:T(8,128)} %param.15), kind=kLoop, calls=%fused_computation.122 | loop fusion | flops 3112960 | bytes 4915200 | tf_op jit(solution)/shard_map/convert_element_type | solution.py:306
  178.8 4.9 %all-to-all-start = ((bf16[8,320,128]{2,1,0:T(8,128)(2,1)}), bf16[8,320,128]{2,1,0:T(8,128)(2,1)S(1)}, u32[]{:S(2)}, u32[]{:S(2)}) async-start(bf16[8,320,128]{2,1,0:T(8,128)(2,1)} %copy-done.2), calls=%async_computation.1 | async-start | bytes 1310720 | tf_op jit(solution)/shard_map/all_to_all | solution.py:93
  183.8 11.1 %all-to-all-done = bf16[8,320,128]{2,1,0:T(8,128)(2,1)S(1)} async-done(((bf16[8,320,128]{2,1,0:T(8,128)(2,1)}), bf16[8,320,128]{2,1,0:T(8,128)(2,1)S(1)}, u32[]{:S(2)}, u32[]{:S(2)}) %all-to-all-start) | async-done | bytes 655392 | tf_op jit(solution)/shard_map/all_to_all | solution.py:93
  195.6 3.6 %collective-permute-start.19 = (bf16[320,128]{1,0:T(8,128)(2,1)S(1)}, bf16[320,128]{1,0:T(8,128)(2,1)S(1)}, u32[]{:S(2)}, u32[]{:S(2)}) collective-permute-start(bf16[320,128]{1,0:T(8,128)(2,1)S(1)} %reduce_sum.81), channel_id=1, source_target_pairs={{0,2},{1,18},{2,32},{3,48},{4,70},{5,86},{6,100},{7,116},{8,138},{... | collective-permute-start | bytes 245768 | tf_op jit(solution)/shard_map/ppermute | solution.py:325
  199.4 12.2 %collective-permute-done.19 = bf16[320,128]{1,0:T(8,128)(2,1)S(1)} collective-permute-done((bf16[320,128]{1,0:T(8,128)(2,1)S(1)}, bf16[320,128]{1,0:T(8,128)(2,1)S(1)}, u32[]{:S(2)}, u32[]{:S(2)}) %collective-permute-start.19) | collective-permute-done | bytes 81952 | tf_op jit(solution)/shard_map/ppermute | solution.py:325
  212.7 3.2 %collective-permute-start.21 = (bf16[2,320,128]{2,1,0:T(8,128)(2,1)S(1)}, bf16[2,320,128]{2,1,0:T(8,128)(2,1)S(1)}, u32[]{:S(2)}, u32[]{:S(2)}) collective-permute-start(bf16[2,320,128]{2,1,0:T(8,128)(2,1)S(1)} %fusion.28), channel_id=1, source_target_pairs={{0,12},{4,0},{8,4},{12,8},{1,13},{5,1},{9,5},{13,9},{2,14},{6,2},{... | collective-permute-start | bytes 491528 | tf_op jit(solution)/shard_map/ppermute | solution.py:28
  219.3 2.5 collective-permute-done.21
  237.2 4.1 %collective-permute-done.25.far_ref = bf16[128,512]{1,0:T(8,128)(2,1)S(1)} collective-permute-done((bf16[128,512]{1,0:T(8,128)(2,1)S(1)}, bf16[128,512]{1,0:T(8,128)(2,1)S(1)}, u32[]{:S(2)}, u32[]{:S(2)}) %collective-permute-start.25) | collective-permute-done | bytes 131104 | tf_op jit(solution)/shard_map/ppermute | solution.py:28
  241.3 2.8 shard_map.158
  246.4 17.6 %all_to_all.10 = bf16[8,320,128]{2,1,0:T(8,128)(2,1)S(1)} all-to-all(bf16[8,320,128]{2,1,0:T(8,128)(2,1)S(1)} %bitcast.220), channel_id=1, replica_groups=mesh['role'=2,'dp'=8,'x1'=2,'x0'=2,'y'=2,'core'=2] {'x1','x0','y'}, dimensions={0} | all-to-all | bytes 1310720 | tf_op jit(solution)/shard_map/all_to_all | solution.py:93
  264.1 2.7 collective-permute-start.27
  267.0 7.3 %collective-permute-done.27 = bf16[320,128]{1,0:T(8,128)(2,1)S(1)} collective-permute-done((bf16[320,128]{1,0:T(8,128)(2,1)S(1)}, bf16[320,128]{1,0:T(8,128)(2,1)S(1)}, u32[]{:S(2)}, u32[]{:S(2)}) %collective-permute-start.27) | collective-permute-done | bytes 81952 | tf_op jit(solution)/shard_map/ppermute | solution.py:338
  (177 shorter events, 69.7 us)
Async XLA Ops:
  7.2 72.6 %all-gather.4.cloned.1.call-start = ((), (), s32[]{:S(2)}) async-start(), calls=%async_computation.3 | async-start | bytes 11141120 | tf_op jit(solution)/shard_map/all_gather | solution.py:291
  7.9 148.2 %reduce-scatter.2.cloned.1.call-start = ((), (), s32[]{:S(2)}) async-start(), calls=%async_computation.4 | async-start | bytes 5898240 | tf_op jit(solution)/shard_map/reduce_scatter | solution.py:299
  8.0 4.9 %collective-permute-start = (bf16[320,128]{0,1:T(8,128)(2,1)}, bf16[320,128]{0,1:T(8,128)(2,1)S(1)}, u32[]{:S(2)}, u32[]{:S(2)}) collective-permute-start(bf16[320,128]{0,1:T(8,128)(2,1)} %bitcast.230), channel_id=1, source_target_pairs={{0,2},{2,0},{1,3},{3,1},{4,6},{6,4},{5,7},{7,5},{8,10},{10,8},{9,1... | collective-permute-start | bytes 245768 | tf_op jit(solution)/shard_map/ppermute | solution.py:28
  13.9 8.5 %collective-permute-start.1 = (bf16[2,320,128]{1,2,0:T(8,128)(2,1)S(1)}, bf16[2,320,128]{1,2,0:T(8,128)(2,1)S(1)}, u32[]{:S(2)}, u32[]{:S(2)}) collective-permute-start(bf16[2,320,128]{1,2,0:T(8,128)(2,1)S(1)} %maximum_select_fusion.3), channel_id=1, source_target_pairs={{0,4},{4,8},{8,12},{12,0},{1,5},{5,9},{9,13},{13,1},{2,6},{6,10},{... | collective-permute-start | bytes 491528 | tf_op jit(solution)/shard_map/ppermute | solution.py:28
  15.5 8.7 %collective-permute-start.2 = (bf16[2,320,128]{1,2,0:T(8,128)(2,1)S(1)}, bf16[2,320,128]{1,2,0:T(8,128)(2,1)S(1)}, u32[]{:S(2)}, u32[]{:S(2)}) collective-permute-start(bf16[2,320,128]{1,2,0:T(8,128)(2,1)S(1)} %maximum_select_fusion.3), channel_id=1, source_target_pairs={{0,12},{4,0},{8,4},{12,8},{1,13},{5,1},{9,5},{13,9},{2,14},{6,2},{... | collective-permute-start | bytes 491528 | tf_op jit(solution)/shard_map/ppermute | solution.py:28
  17.2 8.7 %collective-permute-start.3 = (bf16[2,320,128]{1,2,0:T(8,128)(2,1)S(1)}, bf16[2,320,128]{1,2,0:T(8,128)(2,1)S(1)}, u32[]{:S(2)}, u32[]{:S(2)}) collective-permute-start(bf16[2,320,128]{1,2,0:T(8,128)(2,1)S(1)} %maximum_select_fusion.3), channel_id=1, source_target_pairs={{0,8},{4,12},{8,0},{12,4},{1,9},{5,13},{9,1},{13,5},{2,10},{6,14},... | collective-permute-start | bytes 491528 | tf_op jit(solution)/shard_map/ppermute | solution.py:28
  26.3 7.8 %collective-permute-start.5 = (bf16[4,512,128]{2,1,0:T(8,128)(2,1)}, bf16[4,512,128]{2,1,0:T(8,128)(2,1)}, u32[]{:S(2)}, u32[]{:S(2)}) collective-permute-start(bf16[4,512,128]{2,1,0:T(8,128)(2,1)} %param.20), channel_id=1, source_target_pairs={{0,1},{1,0},{2,3},{3,2},{4,5},{5,4},{6,7},{7,6},{8,9},{9,8},{10,11... | collective-permute-start | bytes 1572872 | tf_op jit(solution)/shard_map/ppermute | solution.py:28
  38.4 10.7 %collective-permute-start.8 = (bf16[128,512]{1,0:T(8,128)(2,1)S(1)}, bf16[128,512]{1,0:T(8,128)(2,1)S(1)}, u32[]{:S(2)}, u32[]{:S(2)}) collective-permute-start(bf16[128,512]{1,0:T(8,128)(2,1)S(1)} %bitcast.243), channel_id=1, source_target_pairs={{0,128},{1,144},{16,129},{17,145},{32,160},{33,176},{48,161},{49,1... | collective-permute-start | bytes 393224 | tf_op jit(solution)/shard_map/ppermute | solution.py:72
  49.2 12.2 %collective-permute-start.9 = (bf16[2,128,512]{2,1,0:T(8,128)(2,1)S(1)}, bf16[2,128,512]{2,1,0:T(8,128)(2,1)S(1)}, u32[]{:S(2)}, u32[]{:S(2)}) collective-permute-start(bf16[2,128,512]{2,1,0:T(8,128)(2,1)S(1)} %pad_maximum_fusion), channel_id=1, source_target_pairs={{0,16},{16,32},{32,48},{48,64},{64,80},{80,96},{96,112},{112,0},{1... | collective-permute-start | bytes 786440 | tf_op jit(solution)/shard_map/ppermute | solution.py:28
  49.9 11.5 %collective-permute-start.12 = (bf16[2,128,512]{2,1,0:T(8,128)(2,1)S(1)}, bf16[2,128,512]{2,1,0:T(8,128)(2,1)S(1)}, u32[]{:S(2)}, u32[]{:S(2)}) collective-permute-start(bf16[2,128,512]{2,1,0:T(8,128)(2,1)S(1)} %pad_maximum_fusion), channel_id=1, source_target_pairs={{0,112},{16,0},{32,16},{48,32},{64,48},{80,64},{96,80},{112,96},{1... | collective-permute-start | bytes 786440 | tf_op jit(solution)/shard_map/ppermute | solution.py:28
  61.4 9.4 %collective-permute-start.10 = (bf16[2,128,512]{2,1,0:T(8,128)(2,1)S(1)}, bf16[2,128,512]{2,1,0:T(8,128)(2,1)S(1)}, u32[]{:S(2)}, u32[]{:S(2)}) collective-permute-start(bf16[2,128,512]{2,1,0:T(8,128)(2,1)S(1)} %collective-permute-done.9), channel_id=1, source_target_pairs={{0,16},{16,32},{32,48},{48,64},{64,80},{80,96},{96,112},{112,0},{1... | collective-permute-start | bytes 786440 | tf_op jit(solution)/shard_map/ppermute | solution.py:28
  62.1 9.0 %collective-permute-start.13 = (bf16[2,128,512]{2,1,0:T(8,128)(2,1)S(1)}, bf16[2,128,512]{2,1,0:T(8,128)(2,1)S(1)}, u32[]{:S(2)}, u32[]{:S(2)}) collective-permute-start(bf16[2,128,512]{2,1,0:T(8,128)(2,1)S(1)} %collective-permute-done.12), channel_id=1, source_target_pairs={{0,112},{16,0},{32,16},{48,32},{64,48},{80,64},{96,80},{112,96},{1... | collective-permute-start | bytes 786440 | tf_op jit(solution)/shard_map/ppermute | solution.py:28
  70.7 8.6 %collective-permute-start.11 = (bf16[2,128,512]{2,1,0:T(8,128)(2,1)S(1)}, bf16[2,128,512]{2,1,0:T(8,128)(2,1)}, u32[]{:S(2)}, u32[]{:S(2)}) collective-permute-start(bf16[2,128,512]{2,1,0:T(8,128)(2,1)S(1)} %collective-permute-done.10), channel_id=1, source_target_pairs={{0,16},{16,32},{32,48},{48,64},{64,80},{80,96},{96,112},{112,0},{1... | collective-permute-start | bytes 786440 | tf_op jit(solution)/shard_map/ppermute | solution.py:28
  71.1 8.3 %collective-permute-start.14 = (bf16[2,128,512]{2,1,0:T(8,128)(2,1)S(1)}, bf16[2,128,512]{2,1,0:T(8,128)(2,1)S(1)}, u32[]{:S(2)}, u32[]{:S(2)}) collective-permute-start(bf16[2,128,512]{2,1,0:T(8,128)(2,1)S(1)} %collective-permute-done.13), channel_id=1, source_target_pairs={{0,112},{16,0},{32,16},{48,32},{64,48},{80,64},{96,80},{112,96},{1... | collective-permute-start | bytes 786440 | tf_op jit(solution)/shard_map/ppermute | solution.py:28
  89.8 133.3 %all-gather.6.cloned.1.call-start = ((), (), s32[]{:S(2)}) async-start(), calls=%async_computation.5 | async-start | bytes 2949120 | tf_op jit(solution)/shard_map/all_gather | solution.py:308
  90.0 10.3 %collective-permute-start.15 = (bf16[2,128,512]{2,1,0:T(8,128)(2,1)}, bf16[2,128,512]{2,1,0:T(8,128)(2,1)S(1)}, u32[]{:S(2)}, u32[]{:S(2)}) collective-permute-start(bf16[2,128,512]{2,1,0:T(8,128)(2,1)} %collective-permute-done.11), channel_id=1, source_target_pairs={{0,16},{16,32},{32,48},{48,64},{64,80},{80,96},{96,112},{112,0},{1... | collective-permute-start | bytes 786440 | tf_op jit(solution)/shard_map/ppermute | solution.py:28
  157.1 11.1 %collective-permute-start.16 = (bf16[320,512]{1,0:T(8,128)(2,1)S(1)}, bf16[320,512]{1,0:T(8,128)(2,1)S(1)}, u32[]{:S(2)}, u32[]{:S(2)}) collective-permute-start(bf16[320,512]{1,0:T(8,128)(2,1)S(1)} %slice_bitcast_fusion), channel_id=1, source_target_pairs={{0,128},{128,0},{1,129},{129,1},{2,130},{130,2},{3,131},{131,3},{4... | collective-permute-start | bytes 983048 | tf_op jit(solution)/shard_map/ppermute | solution.py:28
  178.8 16.1 %all-to-all-start = ((bf16[8,320,128]{2,1,0:T(8,128)(2,1)}), bf16[8,320,128]{2,1,0:T(8,128)(2,1)S(1)}, u32[]{:S(2)}, u32[]{:S(2)}) async-start(bf16[8,320,128]{2,1,0:T(8,128)(2,1)} %copy-done.2), calls=%async_computation.1 | async-start | bytes 1310720 | tf_op jit(solution)/shard_map/all_to_all | solution.py:93
  195.6 15.9 %collective-permute-start.19 = (bf16[320,128]{1,0:T(8,128)(2,1)S(1)}, bf16[320,128]{1,0:T(8,128)(2,1)S(1)}, u32[]{:S(2)}, u32[]{:S(2)}) collective-permute-start(bf16[320,128]{1,0:T(8,128)(2,1)S(1)} %reduce_sum.81), channel_id=1, source_target_pairs={{0,2},{1,18},{2,32},{3,48},{4,70},{5,86},{6,100},{7,116},{8,138},{... | collective-permute-start | bytes 245768 | tf_op jit(solution)/shard_map/ppermute | solution.py:325
  212.6 6.6 %collective-permute-start.20 = (bf16[2,320,128]{2,1,0:T(8,128)(2,1)S(1)}, bf16[2,320,128]{2,1,0:T(8,128)(2,1)S(1)}, u32[]{:S(2)}, u32[]{:S(2)}) collective-permute-start(bf16[2,320,128]{2,1,0:T(8,128)(2,1)S(1)} %fusion.28), channel_id=1, source_target_pairs={{0,4},{4,8},{8,12},{12,0},{1,5},{5,9},{9,13},{13,1},{2,6},{6,10},{... | collective-permute-start | bytes 491528 | tf_op jit(solution)/shard_map/ppermute | solution.py:28
  212.7 9.1 %collective-permute-start.21 = (bf16[2,320,128]{2,1,0:T(8,128)(2,1)S(1)}, bf16[2,320,128]{2,1,0:T(8,128)(2,1)S(1)}, u32[]{:S(2)}, u32[]{:S(2)}) collective-permute-start(bf16[2,320,128]{2,1,0:T(8,128)(2,1)S(1)} %fusion.28), channel_id=1, source_target_pairs={{0,12},{4,0},{8,4},{12,8},{1,13},{5,1},{9,5},{13,9},{2,14},{6,2},{... | collective-permute-start | bytes 491528 | tf_op jit(solution)/shard_map/ppermute | solution.py:28
  215.9 7.1 %collective-permute-start.22 = (bf16[2,320,128]{2,1,0:T(8,128)(2,1)S(1)}, bf16[2,320,128]{2,1,0:T(8,128)(2,1)S(1)}, u32[]{:S(2)}, u32[]{:S(2)}) collective-permute-start(bf16[2,320,128]{2,1,0:T(8,128)(2,1)S(1)} %fusion.28), channel_id=1, source_target_pairs={{0,8},{4,12},{8,0},{12,4},{1,9},{5,13},{9,1},{13,5},{2,10},{6,14},... | collective-permute-start | bytes 491528 | tf_op jit(solution)/shard_map/ppermute | solution.py:28
  234.7 6.6 %collective-permute-start.25 = (bf16[128,512]{1,0:T(8,128)(2,1)S(1)}, bf16[128,512]{1,0:T(8,128)(2,1)S(1)}, u32[]{:S(2)}, u32[]{:S(2)}) collective-permute-start(bf16[128,512]{1,0:T(8,128)(2,1)S(1)} %bitcast.216), channel_id=1, source_target_pairs={{0,128},{128,0},{1,129},{129,1},{2,130},{130,2},{3,131},{131,3},{4... | collective-permute-start | bytes 393224 | tf_op jit(solution)/shard_map/ppermute | solution.py:28
  264.1 10.2 %collective-permute-start.27 = (bf16[320,128]{1,0:T(8,128)(2,1)S(1)}, bf16[320,128]{1,0:T(8,128)(2,1)S(1)}, u32[]{:S(2)}, u32[]{:S(2)}) collective-permute-start(bf16[320,128]{1,0:T(8,128)(2,1)S(1)} %reduce_sum.85), channel_id=1, source_target_pairs={{0,0},{8,128},{128,8},{136,136},{1,1},{9,129},{129,9},{137,137},{2... | collective-permute-start | bytes 245768 | tf_op jit(solution)/shard_map/ppermute | solution.py:338
  (32 other events, 191.6 us)
Sparse Core Ops, SparseCore 0:
  9.9 69.8 all-gather.3
  90.0 66.1 reduce-scatter.1
  173.1 42.6 all-gather.5

commit v11 on v10

--- a/solution.py
+++ b/solution.py
@@ -304,8 +304,7 @@
         gradient, master_weight.T, first_moment.T, second_moment.T
     )
     weight_part = new_weight.astype(bf16)
-    weight_sent = lax.optimization_barrier(new_weight).astype(bf16)
-    weight_all = lax.all_gather(weight_sent, "dp", axis=0)
+    weight_all = lax.all_gather(weight_part, "dp", axis=0)
 
     place = jnp.stack([role, core]).astype(jnp.int32)
     partial = project_all(

time: 283 us -> 281 us (level)
  transfers between devices with their start and end apart: 32 -> 32, of which waited for: 25 -> 26; matrix products, arithmetic and copies ran while one was open for 7% -> 7% of each run, Pallas kernels for 1% -> 1%
where the time goes in v11:
time: 281 us
  waiting for transfers between devices  155 us (55%)
  starting transfers between devices  41.9 us (15%)
  blocking collectives  17.7 us (6%)
  other arithmetic  15.1 us (5%)
  Pallas kernels  14.9 us (5%)
  between operations  14.5 us (5%)
  local copies, waits for them, and re-layouts  12.4 us (4%)
  matrix products  8.98 us (3%)
    ppermute x23, waiting for transfers between devices, rotate(): lax.ppermute(block, axis, [(low, (low + shift) % count) for low in range(...  57.8 us
    reduce_scatter x1, waiting for transfers between devices, on_device(): halves = lax.psum_scatter(terms, 'dp', scatter_dimension=0, tiled=False)  55.6 us
    ppermute x23, starting transfers between devices, rotate(): lax.ppermute(block, axis, [(low, (low + shift) % count) for low in range(...  28.6 us
    all_to_all x1, blocking collectives, scatter_sum(): blocks = lax.all_to_all(parts, X + ('y',), 0, 0, tiled=True)  17.7 us
    ppermute x2, waiting for transfers between devices, deal(): return lax.ppermute(update, EVERY, route)  12.2 us
    all_to_all x1, waiting for transfers between devices, scatter_sum(): blocks = lax.all_to_all(parts, X + ('y',), 0, 0, tiled=True)  11.1 us
    pallas_call x1, Pallas kernels, gradient_terms(): pl.pallas_call(gradient_kernel, grid_spec=pltpu.PrefetchScalarGridSpec(nu...  10.1 us
    ppermute x2, waiting for transfers between devices, swap_cores(): return lax.ppermute(block, ('role', 'dp', 'core'), route)  9.98 us
  transfers between devices with their start and end apart: 32, of which 26 were waited for; matrix products, arithmetic and copies ran while one was open for 7% of the time, Pallas kernels for 1%

profile of v11, /device:TPU:16, one launch (start us, length us, event | category | flops | bytes accessed | tf_op | source)
XLA Modules:
  0.0 280.6 jit_solution(6303097043859360379)
XLA Ops:
  9.3 3.5 %collective-permute-done = bf16[320,128]{0,1:T(8,128)(2,1)S(1)} collective-permute-done((bf16[320,128]{0,1:T(8,128)(2,1)}, bf16[320,128]{0,1:T(8,128)(2,1)S(1)}, u32[]{:S(2)}, u32[]{:S(2)}) %collective-permute-start) | collective-permute-done | bytes 81952 | tf_op jit(solution)/shard_map/ppermute | solution.py:28
  39.2 10.0 %collective-permute-done.8 = bf16[128,512]{1,0:T(8,128)(2,1)S(1)} collective-permute-done((bf16[128,512]{1,0:T(8,128)(2,1)S(1)}, bf16[128,512]{1,0:T(8,128)(2,1)S(1)}, u32[]{:S(2)}, u32[]{:S(2)}) %collective-permute-start.8) | collective-permute-done | bytes 131104 | tf_op jit(solution)/shard_map/ppermute | solution.py:72
  49.9 5.1 %collective-permute-start.12 = (bf16[2,128,512]{2,1,0:T(8,128)(2,1)S(1)}, bf16[2,128,512]{2,1,0:T(8,128)(2,1)S(1)}, u32[]{:S(2)}, u32[]{:S(2)}) collective-permute-start(bf16[2,128,512]{2,1,0:T(8,128)(2,1)S(1)} %pad_maximum_fusion), channel_id=1, source_target_pairs={{0,112},{16,0},{32,16},{48,32},{64,48},{80,64},{96,80},{112,96},{1... | collective-permute-start | bytes 786440 | tf_op jit(solution)/shard_map/ppermute | solution.py:28
  55.0 6.4 %collective-permute-done.9 = bf16[2,128,512]{2,1,0:T(8,128)(2,1)S(1)} collective-permute-done((bf16[2,128,512]{2,1,0:T(8,128)(2,1)S(1)}, bf16[2,128,512]{2,1,0:T(8,128)(2,1)S(1)}, u32[]{:S(2)}, u32[]{:S(2)}) %collective-permute-start.9) | collective-permute-done | bytes 262176 | tf_op jit(solution)/shard_map/ppermute | solution.py:28
  62.1 3.5 %collective-permute-start.13 = (bf16[2,128,512]{2,1,0:T(8,128)(2,1)S(1)}, bf16[2,128,512]{2,1,0:T(8,128)(2,1)S(1)}, u32[]{:S(2)}, u32[]{:S(2)}) collective-permute-start(bf16[2,128,512]{2,1,0:T(8,128)(2,1)S(1)} %collective-permute-done.12), channel_id=1, source_target_pairs={{0,112},{16,0},{32,16},{48,32},{64,48},{80,64},{96,80},{112,96},{1... | collective-permute-start | bytes 786440 | tf_op jit(solution)/shard_map/ppermute | solution.py:28
  65.6 5.1 %collective-permute-done.10 = bf16[2,128,512]{2,1,0:T(8,128)(2,1)S(1)} collective-permute-done((bf16[2,128,512]{2,1,0:T(8,128)(2,1)S(1)}, bf16[2,128,512]{2,1,0:T(8,128)(2,1)S(1)}, u32[]{:S(2)}, u32[]{:S(2)}) %collective-permute-start.10) | collective-permute-done | bytes 262176 | tf_op jit(solution)/shard_map/ppermute | solution.py:28
  71.1 3.7 %collective-permute-start.14 = (bf16[2,128,512]{2,1,0:T(8,128)(2,1)S(1)}, bf16[2,128,512]{2,1,0:T(8,128)(2,1)S(1)}, u32[]{:S(2)}, u32[]{:S(2)}) collective-permute-start(bf16[2,128,512]{2,1,0:T(8,128)(2,1)S(1)} %collective-permute-done.13), channel_id=1, source_target_pairs={{0,112},{16,0},{32,16},{48,32},{64,48},{80,64},{96,80},{112,96},{1... | collective-permute-start | bytes 786440 | tf_op jit(solution)/shard_map/ppermute | solution.py:28
  74.8 4.5 %collective-permute-done.11 = bf16[2,128,512]{2,1,0:T(8,128)(2,1)} collective-permute-done((bf16[2,128,512]{2,1,0:T(8,128)(2,1)S(1)}, bf16[2,128,512]{2,1,0:T(8,128)(2,1)}, u32[]{:S(2)}, u32[]{:S(2)}) %collective-permute-start.11) | collective-permute-done | bytes 262176 | tf_op jit(solution)/shard_map/ppermute | solution.py:28
  79.7 10.1 %shard_map.156 = bf16[8,2,320,512]{3,2,1,0:T(8,128)(2,1)} custom-call(s32[1]{0:T(128)} %bitcast.15.role_ref, bf16[5120,1024]{1,0:T(8,128)(2,1)} %bitcast.253, bf16[1024,512]{1,0:T(8,128)(2,1)} %inputs_ref.1), custom_call_target="tpu_custom_call" | custom-call | flops 5368709120 | bytes 17000000 | tf_op jit(solution)/shard_map/pallas_call | solution.py:105
  95.9 4.5 %collective-permute-done.15 = bf16[2,128,512]{2,1,0:T(8,128)(2,1)S(1)} collective-permute-done((bf16[2,128,512]{2,1,0:T(8,128)(2,1)}, bf16[2,128,512]{2,1,0:T(8,128)(2,1)S(1)}, u32[]{:S(2)}, u32[]{:S(2)}) %collective-permute-start.15) | collective-permute-done | bytes 262176 | tf_op jit(solution)/shard_map/ppermute | solution.py:28
  100.5 55.6 %reduce-scatter.2.cloned.1.call-done = bf16[1,2,320,512]{3,2,1,0:T(8,128)(2,1)} async-done(((bf16[8,2,320,512]{3,2,1,0:T(8,128)(2,1)}), bf16[1,2,320,512]{3,2,1,0:T(8,128)(2,1)}) %reduce-scatter.2.cloned.1.call-update) | async-done | bytes 655376 | tf_op jit(solution)/shard_map/reduce_scatter | solution.py:299
  157.7 10.5 %collective-permute-done.16 = bf16[320,512]{1,0:T(8,128)(2,1)S(1)} collective-permute-done((bf16[320,512]{1,0:T(8,128)(2,1)S(1)}, bf16[320,512]{1,0:T(8,128)(2,1)S(1)}, u32[]{:S(2)}, u32[]{:S(2)}) %collective-permute-start.16) | collective-permute-done | bytes 327712 | tf_op jit(solution)/shard_map/ppermute | solution.py:28
  168.2 3.5 %fusion.48 = (bf16[320,512]{1,0:T(8,128)(2,1)}, f32[320,512]{1,0:T(8,128)}, f32[512,320]{0,1:T(8,128)}, f32[512,320]{0,1:T(8,128)}) fusion(f32[512,320]{0,1:T(8,128)} %param.17, bf16[320,512]{1,0:T(8,128)(2,1)S(1)} %collective-permute-done.16, bf16[2,320,512]{2,1,0:T(8,128)(2,1)} %bitcast.224, f32[512,320]{0,1:T(8,128)} %param.16, f32[512,320]{0,1:T(8,128)} %param.15), kind=kLoop, calls=%fused_computation.122 | loop fusion | flops 3112960 | bytes 4915200 | tf_op jit(solution)/shard_map/convert_element_type | solution.py:306
  177.6 4.9 %all-to-all-start = ((bf16[8,320,128]{2,1,0:T(8,128)(2,1)}), bf16[8,320,128]{2,1,0:T(8,128)(2,1)S(1)}, u32[]{:S(2)}, u32[]{:S(2)}) async-start(bf16[8,320,128]{2,1,0:T(8,128)(2,1)} %copy-done.3), calls=%async_computation.1 | async-start | bytes 1310720 | tf_op jit(solution)/shard_map/all_to_all | solution.py:93
  182.6 11.1 %all-to-all-done = bf16[8,320,128]{2,1,0:T(8,128)(2,1)S(1)} async-done(((bf16[8,320,128]{2,1,0:T(8,128)(2,1)}), bf16[8,320,128]{2,1,0:T(8,128)(2,1)S(1)}, u32[]{:S(2)}, u32[]{:S(2)}) %all-to-all-start) | async-done | bytes 655392 | tf_op jit(solution)/shard_map/all_to_all | solution.py:93
  194.4 3.6 %collective-permute-start.19 = (bf16[320,128]{1,0:T(8,128)(2,1)S(1)}, bf16[320,128]{1,0:T(8,128)(2,1)S(1)}, u32[]{:S(2)}, u32[]{:S(2)}) collective-permute-start(bf16[320,128]{1,0:T(8,128)(2,1)S(1)} %reduce_sum.81), channel_id=1, source_target_pairs={{0,2},{1,18},{2,32},{3,48},{4,70},{5,86},{6,100},{7,116},{8,138},{... | collective-permute-start | bytes 245768 | tf_op jit(solution)/shard_map/ppermute | solution.py:324
  198.2 12.2 %collective-permute-done.19 = bf16[320,128]{1,0:T(8,128)(2,1)S(1)} collective-permute-done((bf16[320,128]{1,0:T(8,128)(2,1)S(1)}, bf16[320,128]{1,0:T(8,128)(2,1)S(1)}, u32[]{:S(2)}, u32[]{:S(2)}) %collective-permute-start.19) | collective-permute-done | bytes 81952 | tf_op jit(solution)/shard_map/ppermute | solution.py:324
  211.5 3.2 %collective-permute-start.21 = (bf16[2,320,128]{2,1,0:T(8,128)(2,1)S(1)}, bf16[2,320,128]{2,1,0:T(8,128)(2,1)S(1)}, u32[]{:S(2)}, u32[]{:S(2)}) collective-permute-start(bf16[2,320,128]{2,1,0:T(8,128)(2,1)S(1)} %fusion.28), channel_id=1, source_target_pairs={{0,12},{4,0},{8,4},{12,8},{1,13},{5,1},{9,5},{13,9},{2,14},{6,2},{... | collective-permute-start | bytes 491528 | tf_op jit(solution)/shard_map/ppermute | solution.py:28
  218.1 2.5 collective-permute-done.21
  235.9 4.1 %collective-permute-done.25.far_ref = bf16[128,512]{1,0:T(8,128)(2,1)S(1)} collective-permute-done((bf16[128,512]{1,0:T(8,128)(2,1)S(1)}, bf16[128,512]{1,0:T(8,128)(2,1)S(1)}, u32[]{:S(2)}, u32[]{:S(2)}) %collective-permute-start.25) | collective-permute-done | bytes 131104 | tf_op jit(solution)/shard_map/ppermute | solution.py:28
  240.1 2.8 shard_map.158
  245.2 17.7 %all_to_all.10 = bf16[8,320,128]{2,1,0:T(8,128)(2,1)S(1)} all-to-all(bf16[8,320,128]{2,1,0:T(8,128)(2,1)S(1)} %bitcast.220), channel_id=1, replica_groups=mesh['role'=2,'dp'=8,'x1'=2,'x0'=2,'y'=2,'core'=2] {'x1','x0','y'}, dimensions={0} | all-to-all | bytes 1310720 | tf_op jit(solution)/shard_map/all_to_all | solution.py:93
  263.0 2.7 collective-permute-start.27
  265.8 7.4 %collective-permute-done.27 = bf16[320,128]{1,0:T(8,128)(2,1)S(1)} collective-permute-done((bf16[320,128]{1,0:T(8,128)(2,1)S(1)}, bf16[320,128]{1,0:T(8,128)(2,1)S(1)}, u32[]{:S(2)}, u32[]{:S(2)}) %collective-permute-start.27) | collective-permute-done | bytes 81952 | tf_op jit(solution)/shard_map/ppermute | solution.py:337
  (174 shorter events, 68.1 us)
Async XLA Ops:
  7.2 72.6 %all-gather.4.cloned.1.call-start = ((), (), s32[]{:S(2)}) async-start(), calls=%async_computation.3 | async-start | bytes 11141120 | tf_op jit(solution)/shard_map/all_gather | solution.py:291
  7.9 148.2 %reduce-scatter.2.cloned.1.call-start = ((), (), s32[]{:S(2)}) async-start(), calls=%async_computation.4 | async-start | bytes 5898240 | tf_op jit(solution)/shard_map/reduce_scatter | solution.py:299
  8.0 4.9 %collective-permute-start = (bf16[320,128]{0,1:T(8,128)(2,1)}, bf16[320,128]{0,1:T(8,128)(2,1)S(1)}, u32[]{:S(2)}, u32[]{:S(2)}) collective-permute-start(bf16[320,128]{0,1:T(8,128)(2,1)} %bitcast.230), channel_id=1, source_target_pairs={{0,2},{2,0},{1,3},{3,1},{4,6},{6,4},{5,7},{7,5},{8,10},{10,8},{9,1... | collective-permute-start | bytes 245768 | tf_op jit(solution)/shard_map/ppermute | solution.py:28
  13.9 8.5 %collective-permute-start.1 = (bf16[2,320,128]{1,2,0:T(8,128)(2,1)S(1)}, bf16[2,320,128]{1,2,0:T(8,128)(2,1)S(1)}, u32[]{:S(2)}, u32[]{:S(2)}) collective-permute-start(bf16[2,320,128]{1,2,0:T(8,128)(2,1)S(1)} %maximum_select_fusion.3), channel_id=1, source_target_pairs={{0,4},{4,8},{8,12},{12,0},{1,5},{5,9},{9,13},{13,1},{2,6},{6,10},{... | collective-permute-start | bytes 491528 | tf_op jit(solution)/shard_map/ppermute | solution.py:28
  15.5 8.7 %collective-permute-start.2 = (bf16[2,320,128]{1,2,0:T(8,128)(2,1)S(1)}, bf16[2,320,128]{1,2,0:T(8,128)(2,1)S(1)}, u32[]{:S(2)}, u32[]{:S(2)}) collective-permute-start(bf16[2,320,128]{1,2,0:T(8,128)(2,1)S(1)} %maximum_select_fusion.3), channel_id=1, source_target_pairs={{0,12},{4,0},{8,4},{12,8},{1,13},{5,1},{9,5},{13,9},{2,14},{6,2},{... | collective-permute-start | bytes 491528 | tf_op jit(solution)/shard_map/ppermute | solution.py:28
  17.2 8.7 %collective-permute-start.3 = (bf16[2,320,128]{1,2,0:T(8,128)(2,1)S(1)}, bf16[2,320,128]{1,2,0:T(8,128)(2,1)S(1)}, u32[]{:S(2)}, u32[]{:S(2)}) collective-permute-start(bf16[2,320,128]{1,2,0:T(8,128)(2,1)S(1)} %maximum_select_fusion.3), channel_id=1, source_target_pairs={{0,8},{4,12},{8,0},{12,4},{1,9},{5,13},{9,1},{13,5},{2,10},{6,14},... | collective-permute-start | bytes 491528 | tf_op jit(solution)/shard_map/ppermute | solution.py:28
  26.3 7.8 %collective-permute-start.5 = (bf16[4,512,128]{2,1,0:T(8,128)(2,1)}, bf16[4,512,128]{2,1,0:T(8,128)(2,1)}, u32[]{:S(2)}, u32[]{:S(2)}) collective-permute-start(bf16[4,512,128]{2,1,0:T(8,128)(2,1)} %param.20), channel_id=1, source_target_pairs={{0,1},{1,0},{2,3},{3,2},{4,5},{5,4},{6,7},{7,6},{8,9},{9,8},{10,11... | collective-permute-start | bytes 1572872 | tf_op jit(solution)/shard_map/ppermute | solution.py:28
  38.4 10.7 %collective-permute-start.8 = (bf16[128,512]{1,0:T(8,128)(2,1)S(1)}, bf16[128,512]{1,0:T(8,128)(2,1)S(1)}, u32[]{:S(2)}, u32[]{:S(2)}) collective-permute-start(bf16[128,512]{1,0:T(8,128)(2,1)S(1)} %bitcast.243), channel_id=1, source_target_pairs={{0,128},{1,144},{16,129},{17,145},{32,160},{33,176},{48,161},{49,1... | collective-permute-start | bytes 393224 | tf_op jit(solution)/shard_map/ppermute | solution.py:72
  49.2 12.1 %collective-permute-start.9 = (bf16[2,128,512]{2,1,0:T(8,128)(2,1)S(1)}, bf16[2,128,512]{2,1,0:T(8,128)(2,1)S(1)}, u32[]{:S(2)}, u32[]{:S(2)}) collective-permute-start(bf16[2,128,512]{2,1,0:T(8,128)(2,1)S(1)} %pad_maximum_fusion), channel_id=1, source_target_pairs={{0,16},{16,32},{32,48},{48,64},{64,80},{80,96},{96,112},{112,0},{1... | collective-permute-start | bytes 786440 | tf_op jit(solution)/shard_map/ppermute | solution.py:28
  49.9 11.5 %collective-permute-start.12 = (bf16[2,128,512]{2,1,0:T(8,128)(2,1)S(1)}, bf16[2,128,512]{2,1,0:T(8,128)(2,1)S(1)}, u32[]{:S(2)}, u32[]{:S(2)}) collective-permute-start(bf16[2,128,512]{2,1,0:T(8,128)(2,1)S(1)} %pad_maximum_fusion), channel_id=1, source_target_pairs={{0,112},{16,0},{32,16},{48,32},{64,48},{80,64},{96,80},{112,96},{1... | collective-permute-start | bytes 786440 | tf_op jit(solution)/shard_map/ppermute | solution.py:28
  61.3 9.4 %collective-permute-start.10 = (bf16[2,128,512]{2,1,0:T(8,128)(2,1)S(1)}, bf16[2,128,512]{2,1,0:T(8,128)(2,1)S(1)}, u32[]{:S(2)}, u32[]{:S(2)}) collective-permute-start(bf16[2,128,512]{2,1,0:T(8,128)(2,1)S(1)} %collective-permute-done.9), channel_id=1, source_target_pairs={{0,16},{16,32},{32,48},{48,64},{64,80},{80,96},{96,112},{112,0},{1... | collective-permute-start | bytes 786440 | tf_op jit(solution)/shard_map/ppermute | solution.py:28
  62.1 9.0 %collective-permute-start.13 = (bf16[2,128,512]{2,1,0:T(8,128)(2,1)S(1)}, bf16[2,128,512]{2,1,0:T(8,128)(2,1)S(1)}, u32[]{:S(2)}, u32[]{:S(2)}) collective-permute-start(bf16[2,128,512]{2,1,0:T(8,128)(2,1)S(1)} %collective-permute-done.12), channel_id=1, source_target_pairs={{0,112},{16,0},{32,16},{48,32},{64,48},{80,64},{96,80},{112,96},{1... | collective-permute-start | bytes 786440 | tf_op jit(solution)/shard_map/ppermute | solution.py:28
  70.7 8.6 %collective-permute-start.11 = (bf16[2,128,512]{2,1,0:T(8,128)(2,1)S(1)}, bf16[2,128,512]{2,1,0:T(8,128)(2,1)}, u32[]{:S(2)}, u32[]{:S(2)}) collective-permute-start(bf16[2,128,512]{2,1,0:T(8,128)(2,1)S(1)} %collective-permute-done.10), channel_id=1, source_target_pairs={{0,16},{16,32},{32,48},{48,64},{64,80},{80,96},{96,112},{112,0},{1... | collective-permute-start | bytes 786440 | tf_op jit(solution)/shard_map/ppermute | solution.py:28
  71.1 8.3 %collective-permute-start.14 = (bf16[2,128,512]{2,1,0:T(8,128)(2,1)S(1)}, bf16[2,128,512]{2,1,0:T(8,128)(2,1)S(1)}, u32[]{:S(2)}, u32[]{:S(2)}) collective-permute-start(bf16[2,128,512]{2,1,0:T(8,128)(2,1)S(1)} %collective-permute-done.13), channel_id=1, source_target_pairs={{0,112},{16,0},{32,16},{48,32},{64,48},{80,64},{96,80},{112,96},{1... | collective-permute-start | bytes 786440 | tf_op jit(solution)/shard_map/ppermute | solution.py:28
  89.8 132.0 %all-gather.6.cloned.1.call-start = ((), (), s32[]{:S(2)}) async-start(), calls=%async_computation.5 | async-start | bytes 2949120 | tf_op jit(solution)/shard_map/all_gather | solution.py:307
  90.0 10.3 %collective-permute-start.15 = (bf16[2,128,512]{2,1,0:T(8,128)(2,1)}, bf16[2,128,512]{2,1,0:T(8,128)(2,1)S(1)}, u32[]{:S(2)}, u32[]{:S(2)}) collective-permute-start(bf16[2,128,512]{2,1,0:T(8,128)(2,1)} %collective-permute-done.11), channel_id=1, source_target_pairs={{0,16},{16,32},{32,48},{48,64},{64,80},{80,96},{96,112},{112,0},{1... | collective-permute-start | bytes 786440 | tf_op jit(solution)/shard_map/ppermute | solution.py:28
  157.1 11.1 %collective-permute-start.16 = (bf16[320,512]{1,0:T(8,128)(2,1)S(1)}, bf16[320,512]{1,0:T(8,128)(2,1)S(1)}, u32[]{:S(2)}, u32[]{:S(2)}) collective-permute-start(bf16[320,512]{1,0:T(8,128)(2,1)S(1)} %slice_bitcast_fusion), channel_id=1, source_target_pairs={{0,128},{128,0},{1,129},{129,1},{2,130},{130,2},{3,131},{131,3},{4... | collective-permute-start | bytes 983048 | tf_op jit(solution)/shard_map/ppermute | solution.py:28
  177.6 16.1 %all-to-all-start = ((bf16[8,320,128]{2,1,0:T(8,128)(2,1)}), bf16[8,320,128]{2,1,0:T(8,128)(2,1)S(1)}, u32[]{:S(2)}, u32[]{:S(2)}) async-start(bf16[8,320,128]{2,1,0:T(8,128)(2,1)} %copy-done.3), calls=%async_computation.1 | async-start | bytes 1310720 | tf_op jit(solution)/shard_map/all_to_all | solution.py:93
  194.4 15.9 %collective-permute-start.19 = (bf16[320,128]{1,0:T(8,128)(2,1)S(1)}, bf16[320,128]{1,0:T(8,128)(2,1)S(1)}, u32[]{:S(2)}, u32[]{:S(2)}) collective-permute-start(bf16[320,128]{1,0:T(8,128)(2,1)S(1)} %reduce_sum.81), channel_id=1, source_target_pairs={{0,2},{1,18},{2,32},{3,48},{4,70},{5,86},{6,100},{7,116},{8,138},{... | collective-permute-start | bytes 245768 | tf_op jit(solution)/shard_map/ppermute | solution.py:324
  211.4 6.6 %collective-permute-start.20 = (bf16[2,320,128]{2,1,0:T(8,128)(2,1)S(1)}, bf16[2,320,128]{2,1,0:T(8,128)(2,1)S(1)}, u32[]{:S(2)}, u32[]{:S(2)}) collective-permute-start(bf16[2,320,128]{2,1,0:T(8,128)(2,1)S(1)} %fusion.28), channel_id=1, source_target_pairs={{0,4},{4,8},{8,12},{12,0},{1,5},{5,9},{9,13},{13,1},{2,6},{6,10},{... | collective-permute-start | bytes 491528 | tf_op jit(solution)/shard_map/ppermute | solution.py:28
  211.5 9.0 %collective-permute-start.21 = (bf16[2,320,128]{2,1,0:T(8,128)(2,1)S(1)}, bf16[2,320,128]{2,1,0:T(8,128)(2,1)S(1)}, u32[]{:S(2)}, u32[]{:S(2)}) collective-permute-start(bf16[2,320,128]{2,1,0:T(8,128)(2,1)S(1)} %fusion.28), channel_id=1, source_target_pairs={{0,12},{4,0},{8,4},{12,8},{1,13},{5,1},{9,5},{13,9},{2,14},{6,2},{... | collective-permute-start | bytes 491528 | tf_op jit(solution)/shard_map/ppermute | solution.py:28
  214.7 7.1 %collective-permute-start.22 = (bf16[2,320,128]{2,1,0:T(8,128)(2,1)S(1)}, bf16[2,320,128]{2,1,0:T(8,128)(2,1)S(1)}, u32[]{:S(2)}, u32[]{:S(2)}) collective-permute-start(bf16[2,320,128]{2,1,0:T(8,128)(2,1)S(1)} %fusion.28), channel_id=1, source_target_pairs={{0,8},{4,12},{8,0},{12,4},{1,9},{5,13},{9,1},{13,5},{2,10},{6,14},... | collective-permute-start | bytes 491528 | tf_op jit(solution)/shard_map/ppermute | solution.py:28
  233.5 6.6 %collective-permute-start.25 = (bf16[128,512]{1,0:T(8,128)(2,1)S(1)}, bf16[128,512]{1,0:T(8,128)(2,1)S(1)}, u32[]{:S(2)}, u32[]{:S(2)}) collective-permute-start(bf16[128,512]{1,0:T(8,128)(2,1)S(1)} %bitcast.216), channel_id=1, source_target_pairs={{0,128},{128,0},{1,129},{129,1},{2,130},{130,2},{3,131},{131,3},{4... | collective-permute-start | bytes 393224 | tf_op jit(solution)/shard_map/ppermute | solution.py:28
  263.0 10.2 %collective-permute-start.27 = (bf16[320,128]{1,0:T(8,128)(2,1)S(1)}, bf16[320,128]{1,0:T(8,128)(2,1)S(1)}, u32[]{:S(2)}, u32[]{:S(2)}) collective-permute-start(bf16[320,128]{1,0:T(8,128)(2,1)S(1)} %reduce_sum.85), channel_id=1, source_target_pairs={{0,0},{8,128},{128,8},{136,136},{1,1},{9,129},{129,9},{137,137},{2... | collective-permute-start | bytes 245768 | tf_op jit(solution)/shard_map/ppermute | solution.py:337
  (31 other events, 190.8 us)
Sparse Core Ops, SparseCore 0:
  9.9 69.8 all-gather.3
  90.0 66.1 reduce-scatter.1
  171.9 42.6 all-gather.5

commit v12 on v11

--- a/solution.py
+++ b/solution.py
@@ -131,24 +131,50 @@
     return total.astype(jnp.bfloat16)
 
 
-def project_all_kernel(place_ref, own_ref, other_ref, tokens_ref, out_ref):
+def project_all_kernel(
+    place_ref, own_ref, other_ref, tokens_ref, out_ref, weights, tokens, outs, in_sems, out_sems
+):
     core = place_ref[1]
-    weights = own_ref[...], other_ref[...]
-    for n in range(8):
-        tokens = [tokens_ref[n % 4, half, n // 4] for half in (core, 1 - core)]
-        out_ref[n] = contract(weights, tokens)
+    reads = [
+        pltpu.make_async_copy(own_ref, weights.at[0], in_sems.at[0]),
+        pltpu.make_async_copy(other_ref, weights.at[1], in_sems.at[1]),
+    ]
+    for k in range(4):
+        reads.append(pltpu.make_async_copy(tokens_ref.at[k], tokens.at[k], in_sems.at[2 + k]))
+    for copy in reads:
+        copy.start()
+    reads[0].wait()
+    reads[1].wait()
+    copies = []
+    for k in range(4):
+        reads[2 + k].wait()
+        for r in range(2):
+            n = r * 4 + k
+            values = [tokens[k, half, r] for half in (core, 1 - core)]
+            outs[n] = contract((weights[0], weights[1]), values)
+            copies.append(pltpu.make_async_copy(outs.at[n], out_ref.at[n], out_sems.at[n]))
+            copies[-1].start()
+    for copy in copies:
+        copy.wait()
 
 
 def project_all(place, own, other, attended):
     part, depth = own.shape
     tokens = attended.shape[3]
-    vmem = pl.BlockSpec(memory_space=pltpu.VMEM)
+    anywhere = pl.BlockSpec(memory_space=pl.ANY)
     return pl.pallas_call(
         project_all_kernel,
-        in_specs=[pl.BlockSpec(memory_space=pltpu.SMEM), vmem, vmem, vmem],
-        out_specs=vmem,
+        in_specs=[pl.BlockSpec(memory_space=pltpu.SMEM), anywhere, anywhere, anywhere],
+        out_specs=anywhere,
         out_shape=jax.ShapeDtypeStruct((8, part, tokens), jnp.bfloat16),
-        compiler_params=pltpu.CompilerParams(vmem_limit_bytes=32 * 1024 * 1024),
+        scratch_shapes=[
+            pltpu.VMEM((2, part, depth), jnp.bfloat16),
+            pltpu.VMEM(attended.shape, jnp.bfloat16),
+            pltpu.VMEM((8, part, tokens), jnp.bfloat16),
+            pltpu.SemaphoreType.DMA((6,)),
+            pltpu.SemaphoreType.DMA((8,)),
+        ],
+        compiler_params=pltpu.CompilerParams(vmem_limit_bytes=60 * 1024 * 1024),
         cost_estimate=pl.CostEstimate(
             flops=32 * part * depth * tokens, bytes_accessed=3_000_000, transcendentals=0
         ),

time: 281 us -> 283 us (level)
  transfers between devices with their start and end apart: 32 -> 32, of which waited for: 26 -> 25; matrix products, arithmetic and copies ran while one was open for 7% -> 7% of each run, Pallas kernels for 1% -> 2%
where the time goes in v12:
time: 283 us; the launch traced here: 282 us
  waiting for transfers between devices  154 us (54%)
  starting transfers between devices  42.3 us (15%)
  Pallas kernels  17.7 us (6%)
  blocking collectives  17.7 us (6%)
  other arithmetic  15.7 us (6%)
  between operations  14.6 us (5%)
  local copies, waits for them, and re-layouts  11.4 us (4%)
  matrix products  8.99 us (3%)
    ppermute x23, waiting for transfers between devices, rotate(): lax.ppermute(block, axis, [(low, (low + shift) % count) for low in range(...  56.8 us
    reduce_scatter x1, waiting for transfers between devices, on_device(): halves = lax.psum_scatter(terms, 'dp', scatter_dimension=0, tiled=False)  55.6 us
    ppermute x23, starting transfers between devices, rotate(): lax.ppermute(block, axis, [(low, (low + shift) % count) for low in range(...  28.8 us
    all_to_all x1, blocking collectives, scatter_sum(): blocks = lax.all_to_all(parts, X + ('y',), 0, 0, tiled=True)  17.7 us
    ppermute x2, waiting for transfers between devices, deal(): return lax.ppermute(update, EVERY, route)  12.1 us
    all_to_all x1, waiting for transfers between devices, scatter_sum(): blocks = lax.all_to_all(parts, X + ('y',), 0, 0, tiled=True)  11.1 us
    pallas_call x1, Pallas kernels, gradient_terms(): pl.pallas_call(gradient_kernel, grid_spec=pltpu.PrefetchScalarGridSpec(nu...  10.1 us
    ppermute x2, waiting for transfers between devices, swap_cores(): return lax.ppermute(block, ('role', 'dp', 'core'), route)  9.97 us
  transfers between devices with their start and end apart: 32, of which 25 were waited for; matrix products, arithmetic and copies ran while one was open for 7% of the time, Pallas kernels for 2%

profile of v12, /device:TPU:16, one launch (start us, length us, event | category | flops | bytes accessed | tf_op | source)
XLA Modules:
  0.0 282.3 jit_solution(14970049492429989964)
XLA Ops:
  9.3 3.5 %collective-permute-done = bf16[320,128]{0,1:T(8,128)(2,1)S(1)} collective-permute-done((bf16[320,128]{0,1:T(8,128)(2,1)}, bf16[320,128]{0,1:T(8,128)(2,1)S(1)}, u32[]{:S(2)}, u32[]{:S(2)}) %collective-permute-start) | collective-permute-done | bytes 81952 | tf_op jit(solution)/shard_map/ppermute | solution.py:28
  39.2 10.0 %collective-permute-done.8 = bf16[128,512]{1,0:T(8,128)(2,1)S(1)} collective-permute-done((bf16[128,512]{1,0:T(8,128)(2,1)S(1)}, bf16[128,512]{1,0:T(8,128)(2,1)S(1)}, u32[]{:S(2)}, u32[]{:S(2)}) %collective-permute-start.8) | collective-permute-done | bytes 131104 | tf_op jit(solution)/shard_map/ppermute | solution.py:72
  49.9 5.1 %collective-permute-start.12 = (bf16[2,128,512]{2,1,0:T(8,128)(2,1)S(1)}, bf16[2,128,512]{2,1,0:T(8,128)(2,1)S(1)}, u32[]{:S(2)}, u32[]{:S(2)}) collective-permute-start(bf16[2,128,512]{2,1,0:T(8,128)(2,1)S(1)} %pad_maximum_fusion), channel_id=1, source_target_pairs={{0,112},{16,0},{32,16},{48,32},{64,48},{80,64},{96,80},{112,96},{1... | collective-permute-start | bytes 786440 | tf_op jit(solution)/shard_map/ppermute | solution.py:28
  55.0 6.4 %collective-permute-done.9 = bf16[2,128,512]{2,1,0:T(8,128)(2,1)S(1)} collective-permute-done((bf16[2,128,512]{2,1,0:T(8,128)(2,1)S(1)}, bf16[2,128,512]{2,1,0:T(8,128)(2,1)S(1)}, u32[]{:S(2)}, u32[]{:S(2)}) %collective-permute-start.9) | collective-permute-done | bytes 262176 | tf_op jit(solution)/shard_map/ppermute | solution.py:28
  62.1 3.5 %collective-permute-start.13 = (bf16[2,128,512]{2,1,0:T(8,128)(2,1)S(1)}, bf16[2,128,512]{2,1,0:T(8,128)(2,1)S(1)}, u32[]{:S(2)}, u32[]{:S(2)}) collective-permute-start(bf16[2,128,512]{2,1,0:T(8,128)(2,1)S(1)} %collective-permute-done.12), channel_id=1, source_target_pairs={{0,112},{16,0},{32,16},{48,32},{64,48},{80,64},{96,80},{112,96},{1... | collective-permute-start | bytes 786440 | tf_op jit(solution)/shard_map/ppermute | solution.py:28
  65.6 5.1 %collective-permute-done.10 = bf16[2,128,512]{2,1,0:T(8,128)(2,1)S(1)} collective-permute-done((bf16[2,128,512]{2,1,0:T(8,128)(2,1)S(1)}, bf16[2,128,512]{2,1,0:T(8,128)(2,1)S(1)}, u32[]{:S(2)}, u32[]{:S(2)}) %collective-permute-start.10) | collective-permute-done | bytes 262176 | tf_op jit(solution)/shard_map/ppermute | solution.py:28
  71.1 3.7 %collective-permute-start.14 = (bf16[2,128,512]{2,1,0:T(8,128)(2,1)S(1)}, bf16[2,128,512]{2,1,0:T(8,128)(2,1)S(1)}, u32[]{:S(2)}, u32[]{:S(2)}) collective-permute-start(bf16[2,128,512]{2,1,0:T(8,128)(2,1)S(1)} %collective-permute-done.13), channel_id=1, source_target_pairs={{0,112},{16,0},{32,16},{48,32},{64,48},{80,64},{96,80},{112,96},{1... | collective-permute-start | bytes 786440 | tf_op jit(solution)/shard_map/ppermute | solution.py:28
  74.8 4.5 %collective-permute-done.11 = bf16[2,128,512]{2,1,0:T(8,128)(2,1)} collective-permute-done((bf16[2,128,512]{2,1,0:T(8,128)(2,1)S(1)}, bf16[2,128,512]{2,1,0:T(8,128)(2,1)}, u32[]{:S(2)}, u32[]{:S(2)}) %collective-permute-start.11) | collective-permute-done | bytes 262176 | tf_op jit(solution)/shard_map/ppermute | solution.py:28
  79.7 10.1 %shard_map.156 = bf16[8,2,320,512]{3,2,1,0:T(8,128)(2,1)} custom-call(s32[1]{0:T(128)} %bitcast.15.role_ref, bf16[5120,1024]{1,0:T(8,128)(2,1)} %bitcast.253, bf16[1024,512]{1,0:T(8,128)(2,1)} %inputs_ref.1), custom_call_target="tpu_custom_call" | custom-call | flops 5368709120 | bytes 17000000 | tf_op jit(solution)/shard_map/pallas_call | solution.py:105
  95.9 4.5 %collective-permute-done.15 = bf16[2,128,512]{2,1,0:T(8,128)(2,1)S(1)} collective-permute-done((bf16[2,128,512]{2,1,0:T(8,128)(2,1)}, bf16[2,128,512]{2,1,0:T(8,128)(2,1)S(1)}, u32[]{:S(2)}, u32[]{:S(2)}) %collective-permute-start.15) | collective-permute-done | bytes 262176 | tf_op jit(solution)/shard_map/ppermute | solution.py:28
  100.5 55.6 %reduce-scatter.2.cloned.1.call-done = bf16[1,2,320,512]{3,2,1,0:T(8,128)(2,1)} async-done(((bf16[8,2,320,512]{3,2,1,0:T(8,128)(2,1)}), bf16[1,2,320,512]{3,2,1,0:T(8,128)(2,1)}) %reduce-scatter.2.cloned.1.call-update) | async-done | bytes 655376 | tf_op jit(solution)/shard_map/reduce_scatter | solution.py:325
  157.7 10.5 %collective-permute-done.16 = bf16[320,512]{1,0:T(8,128)(2,1)S(1)} collective-permute-done((bf16[320,512]{1,0:T(8,128)(2,1)S(1)}, bf16[320,512]{1,0:T(8,128)(2,1)S(1)}, u32[]{:S(2)}, u32[]{:S(2)}) %collective-permute-start.16) | collective-permute-done | bytes 327712 | tf_op jit(solution)/shard_map/ppermute | solution.py:28
  168.2 3.5 %fusion.48 = (bf16[320,512]{1,0:T(8,128)(2,1)}, f32[320,512]{1,0:T(8,128)}, f32[512,320]{0,1:T(8,128)}, f32[512,320]{0,1:T(8,128)}) fusion(f32[512,320]{0,1:T(8,128)} %param.17, bf16[320,512]{1,0:T(8,128)(2,1)S(1)} %collective-permute-done.16, bf16[2,320,512]{2,1,0:T(8,128)(2,1)} %bitcast.224, f32[512,320]{0,1:T(8,128)} %param.16, f32[512,320]{0,1:T(8,128)} %param.15), kind=kLoop, calls=%fused_computation.122 | loop fusion | flops 3112960 | bytes 4915200 | tf_op jit(solution)/shard_map/convert_element_type | solution.py:332
  174.4 4.9 %shard_map.157 = bf16[8,320,128]{2,1,0:T(8,128)(2,1)} custom-call(s32[2]{0:T(128)} %pad_add_fusion.place_ref, bf16[320,512]{1,0:T(8,128)(2,1)} %get-tuple-element.38.own_ref, bf16[320,512]{1,0:T(8,128)(2,1)} %copy-done.7, bf16[4,2,2,128,512]{4,3,2,1,0:T(8,128)(2,1)} %bitcast.219), custom_call_target="tpu_custom_call" | custom-call | flops 671088640 | bytes 3000000 | tf_op jit(solution)/shard_map/pallas_call | solution.py:165
  179.3 4.9 %all-to-all-start = ((bf16[8,320,128]{2,1,0:T(8,128)(2,1)}), bf16[8,320,128]{2,1,0:T(8,128)(2,1)S(1)}, u32[]{:S(2)}, u32[]{:S(2)}) async-start(bf16[8,320,128]{2,1,0:T(8,128)(2,1)} %shard_map.157), calls=%async_computation.1 | async-start | bytes 1310720 | tf_op jit(solution)/shard_map/all_to_all | solution.py:93
  184.3 11.1 %all-to-all-done = bf16[8,320,128]{2,1,0:T(8,128)(2,1)S(1)} async-done(((bf16[8,320,128]{2,1,0:T(8,128)(2,1)}), bf16[8,320,128]{2,1,0:T(8,128)(2,1)S(1)}, u32[]{:S(2)}, u32[]{:S(2)}) %all-to-all-start) | async-done | bytes 655392 | tf_op jit(solution)/shard_map/all_to_all | solution.py:93
  196.2 3.6 %collective-permute-start.19 = (bf16[320,128]{1,0:T(8,128)(2,1)S(1)}, bf16[320,128]{1,0:T(8,128)(2,1)S(1)}, u32[]{:S(2)}, u32[]{:S(2)}) collective-permute-start(bf16[320,128]{1,0:T(8,128)(2,1)S(1)} %reduce_sum.81), channel_id=1, source_target_pairs={{0,2},{1,18},{2,32},{3,48},{4,70},{5,86},{6,100},{7,116},{8,138},{... | collective-permute-start | bytes 245768 | tf_op jit(solution)/shard_map/ppermute | solution.py:350
  199.9 12.1 %collective-permute-done.19 = bf16[320,128]{1,0:T(8,128)(2,1)S(1)} collective-permute-done((bf16[320,128]{1,0:T(8,128)(2,1)S(1)}, bf16[320,128]{1,0:T(8,128)(2,1)S(1)}, u32[]{:S(2)}, u32[]{:S(2)}) %collective-permute-start.19) | collective-permute-done | bytes 81952 | tf_op jit(solution)/shard_map/ppermute | solution.py:350
  213.2 3.2 %collective-permute-start.21 = (bf16[2,320,128]{2,1,0:T(8,128)(2,1)S(1)}, bf16[2,320,128]{2,1,0:T(8,128)(2,1)S(1)}, u32[]{:S(2)}, u32[]{:S(2)}) collective-permute-start(bf16[2,320,128]{2,1,0:T(8,128)(2,1)S(1)} %fusion.28), channel_id=1, source_target_pairs={{0,12},{4,0},{8,4},{12,8},{1,13},{5,1},{9,5},{13,9},{2,14},{6,2},{... | collective-permute-start | bytes 491528 | tf_op jit(solution)/shard_map/ppermute | solution.py:28
  237.7 4.0 %collective-permute-done.25.far_ref = bf16[128,512]{1,0:T(8,128)(2,1)S(1)} collective-permute-done((bf16[128,512]{1,0:T(8,128)(2,1)S(1)}, bf16[128,512]{1,0:T(8,128)(2,1)S(1)}, u32[]{:S(2)}, u32[]{:S(2)}) %collective-permute-start.25) | collective-permute-done | bytes 131104 | tf_op jit(solution)/shard_map/ppermute | solution.py:28
  241.7 2.8 shard_map.158
  246.8 17.7 %all_to_all.10 = bf16[8,320,128]{2,1,0:T(8,128)(2,1)S(1)} all-to-all(bf16[8,320,128]{2,1,0:T(8,128)(2,1)S(1)} %bitcast.220), channel_id=1, replica_groups=mesh['role'=2,'dp'=8,'x1'=2,'x0'=2,'y'=2,'core'=2] {'x1','x0','y'}, dimensions={0} | all-to-all | bytes 1310720 | tf_op jit(solution)/shard_map/all_to_all | solution.py:93
  264.7 2.8 collective-permute-start.27
  267.7 7.2 %collective-permute-done.27 = bf16[320,128]{1,0:T(8,128)(2,1)S(1)} collective-permute-done((bf16[320,128]{1,0:T(8,128)(2,1)S(1)}, bf16[320,128]{1,0:T(8,128)(2,1)S(1)}, u32[]{:S(2)}, u32[]{:S(2)}) %collective-permute-start.27) | collective-permute-done | bytes 81952 | tf_op jit(solution)/shard_map/ppermute | solution.py:363
  (176 shorter events, 67.5 us)
Async XLA Ops:
  7.2 72.6 %all-gather.4.cloned.1.call-start = ((), (), s32[]{:S(2)}) async-start(), calls=%async_computation.3 | async-start | bytes 11141120 | tf_op jit(solution)/shard_map/all_gather | solution.py:317
  7.9 148.2 %reduce-scatter.2.cloned.1.call-start = ((), (), s32[]{:S(2)}) async-start(), calls=%async_computation.4 | async-start | bytes 5898240 | tf_op jit(solution)/shard_map/reduce_scatter | solution.py:325
  8.0 4.9 %collective-permute-start = (bf16[320,128]{0,1:T(8,128)(2,1)}, bf16[320,128]{0,1:T(8,128)(2,1)S(1)}, u32[]{:S(2)}, u32[]{:S(2)}) collective-permute-start(bf16[320,128]{0,1:T(8,128)(2,1)} %bitcast.230), channel_id=1, source_target_pairs={{0,2},{2,0},{1,3},{3,1},{4,6},{6,4},{5,7},{7,5},{8,10},{10,8},{9,1... | collective-permute-start | bytes 245768 | tf_op jit(solution)/shard_map/ppermute | solution.py:28
  13.9 8.5 %collective-permute-start.1 = (bf16[2,320,128]{1,2,0:T(8,128)(2,1)S(1)}, bf16[2,320,128]{1,2,0:T(8,128)(2,1)S(1)}, u32[]{:S(2)}, u32[]{:S(2)}) collective-permute-start(bf16[2,320,128]{1,2,0:T(8,128)(2,1)S(1)} %maximum_select_fusion.3), channel_id=1, source_target_pairs={{0,4},{4,8},{8,12},{12,0},{1,5},{5,9},{9,13},{13,1},{2,6},{6,10},{... | collective-permute-start | bytes 491528 | tf_op jit(solution)/shard_map/ppermute | solution.py:28
  15.5 8.7 %collective-permute-start.2 = (bf16[2,320,128]{1,2,0:T(8,128)(2,1)S(1)}, bf16[2,320,128]{1,2,0:T(8,128)(2,1)S(1)}, u32[]{:S(2)}, u32[]{:S(2)}) collective-permute-start(bf16[2,320,128]{1,2,0:T(8,128)(2,1)S(1)} %maximum_select_fusion.3), channel_id=1, source_target_pairs={{0,12},{4,0},{8,4},{12,8},{1,13},{5,1},{9,5},{13,9},{2,14},{6,2},{... | collective-permute-start | bytes 491528 | tf_op jit(solution)/shard_map/ppermute | solution.py:28
  17.2 8.7 %collective-permute-start.3 = (bf16[2,320,128]{1,2,0:T(8,128)(2,1)S(1)}, bf16[2,320,128]{1,2,0:T(8,128)(2,1)S(1)}, u32[]{:S(2)}, u32[]{:S(2)}) collective-permute-start(bf16[2,320,128]{1,2,0:T(8,128)(2,1)S(1)} %maximum_select_fusion.3), channel_id=1, source_target_pairs={{0,8},{4,12},{8,0},{12,4},{1,9},{5,13},{9,1},{13,5},{2,10},{6,14},... | collective-permute-start | bytes 491528 | tf_op jit(solution)/shard_map/ppermute | solution.py:28
  26.3 7.8 %collective-permute-start.5 = (bf16[4,512,128]{2,1,0:T(8,128)(2,1)}, bf16[4,512,128]{2,1,0:T(8,128)(2,1)}, u32[]{:S(2)}, u32[]{:S(2)}) collective-permute-start(bf16[4,512,128]{2,1,0:T(8,128)(2,1)} %param.20), channel_id=1, source_target_pairs={{0,1},{1,0},{2,3},{3,2},{4,5},{5,4},{6,7},{7,6},{8,9},{9,8},{10,11... | collective-permute-start | bytes 1572872 | tf_op jit(solution)/shard_map/ppermute | solution.py:28
  38.4 10.7 %collective-permute-start.8 = (bf16[128,512]{1,0:T(8,128)(2,1)S(1)}, bf16[128,512]{1,0:T(8,128)(2,1)S(1)}, u32[]{:S(2)}, u32[]{:S(2)}) collective-permute-start(bf16[128,512]{1,0:T(8,128)(2,1)S(1)} %bitcast.243), channel_id=1, source_target_pairs={{0,128},{1,144},{16,129},{17,145},{32,160},{33,176},{48,161},{49,1... | collective-permute-start | bytes 393224 | tf_op jit(solution)/shard_map/ppermute | solution.py:72
  49.2 12.2 %collective-permute-start.9 = (bf16[2,128,512]{2,1,0:T(8,128)(2,1)S(1)}, bf16[2,128,512]{2,1,0:T(8,128)(2,1)S(1)}, u32[]{:S(2)}, u32[]{:S(2)}) collective-permute-start(bf16[2,128,512]{2,1,0:T(8,128)(2,1)S(1)} %pad_maximum_fusion), channel_id=1, source_target_pairs={{0,16},{16,32},{32,48},{48,64},{64,80},{80,96},{96,112},{112,0},{1... | collective-permute-start | bytes 786440 | tf_op jit(solution)/shard_map/ppermute | solution.py:28
  49.9 11.5 %collective-permute-start.12 = (bf16[2,128,512]{2,1,0:T(8,128)(2,1)S(1)}, bf16[2,128,512]{2,1,0:T(8,128)(2,1)S(1)}, u32[]{:S(2)}, u32[]{:S(2)}) collective-permute-start(bf16[2,128,512]{2,1,0:T(8,128)(2,1)S(1)} %pad_maximum_fusion), channel_id=1, source_target_pairs={{0,112},{16,0},{32,16},{48,32},{64,48},{80,64},{96,80},{112,96},{1... | collective-permute-start | bytes 786440 | tf_op jit(solution)/shard_map/ppermute | solution.py:28
  61.4 9.4 %collective-permute-start.10 = (bf16[2,128,512]{2,1,0:T(8,128)(2,1)S(1)}, bf16[2,128,512]{2,1,0:T(8,128)(2,1)S(1)}, u32[]{:S(2)}, u32[]{:S(2)}) collective-permute-start(bf16[2,128,512]{2,1,0:T(8,128)(2,1)S(1)} %collective-permute-done.9), channel_id=1, source_target_pairs={{0,16},{16,32},{32,48},{48,64},{64,80},{80,96},{96,112},{112,0},{1... | collective-permute-start | bytes 786440 | tf_op jit(solution)/shard_map/ppermute | solution.py:28
  62.1 9.0 %collective-permute-start.13 = (bf16[2,128,512]{2,1,0:T(8,128)(2,1)S(1)}, bf16[2,128,512]{2,1,0:T(8,128)(2,1)S(1)}, u32[]{:S(2)}, u32[]{:S(2)}) collective-permute-start(bf16[2,128,512]{2,1,0:T(8,128)(2,1)S(1)} %collective-permute-done.12), channel_id=1, source_target_pairs={{0,112},{16,0},{32,16},{48,32},{64,48},{80,64},{96,80},{112,96},{1... | collective-permute-start | bytes 786440 | tf_op jit(solution)/shard_map/ppermute | solution.py:28
  70.7 8.6 %collective-permute-start.11 = (bf16[2,128,512]{2,1,0:T(8,128)(2,1)S(1)}, bf16[2,128,512]{2,1,0:T(8,128)(2,1)}, u32[]{:S(2)}, u32[]{:S(2)}) collective-permute-start(bf16[2,128,512]{2,1,0:T(8,128)(2,1)S(1)} %collective-permute-done.10), channel_id=1, source_target_pairs={{0,16},{16,32},{32,48},{48,64},{64,80},{80,96},{96,112},{112,0},{1... | collective-permute-start | bytes 786440 | tf_op jit(solution)/shard_map/ppermute | solution.py:28
  71.1 8.3 %collective-permute-start.14 = (bf16[2,128,512]{2,1,0:T(8,128)(2,1)S(1)}, bf16[2,128,512]{2,1,0:T(8,128)(2,1)S(1)}, u32[]{:S(2)}, u32[]{:S(2)}) collective-permute-start(bf16[2,128,512]{2,1,0:T(8,128)(2,1)S(1)} %collective-permute-done.13), channel_id=1, source_target_pairs={{0,112},{16,0},{32,16},{48,32},{64,48},{80,64},{96,80},{112,96},{1... | collective-permute-start | bytes 786440 | tf_op jit(solution)/shard_map/ppermute | solution.py:28
  89.8 133.6 %all-gather.6.cloned.1.call-start = ((), (), s32[]{:S(2)}) async-start(), calls=%async_computation.5 | async-start | bytes 2949120 | tf_op jit(solution)/shard_map/all_gather | solution.py:333
  90.0 10.3 %collective-permute-start.15 = (bf16[2,128,512]{2,1,0:T(8,128)(2,1)}, bf16[2,128,512]{2,1,0:T(8,128)(2,1)S(1)}, u32[]{:S(2)}, u32[]{:S(2)}) collective-permute-start(bf16[2,128,512]{2,1,0:T(8,128)(2,1)} %collective-permute-done.11), channel_id=1, source_target_pairs={{0,16},{16,32},{32,48},{48,64},{64,80},{80,96},{96,112},{112,0},{1... | collective-permute-start | bytes 786440 | tf_op jit(solution)/shard_map/ppermute | solution.py:28
  157.1 11.1 %collective-permute-start.16 = (bf16[320,512]{1,0:T(8,128)(2,1)S(1)}, bf16[320,512]{1,0:T(8,128)(2,1)S(1)}, u32[]{:S(2)}, u32[]{:S(2)}) collective-permute-start(bf16[320,512]{1,0:T(8,128)(2,1)S(1)} %slice_bitcast_fusion), channel_id=1, source_target_pairs={{0,128},{128,0},{1,129},{129,1},{2,130},{130,2},{3,131},{131,3},{4... | collective-permute-start | bytes 983048 | tf_op jit(solution)/shard_map/ppermute | solution.py:28
  179.3 16.1 %all-to-all-start = ((bf16[8,320,128]{2,1,0:T(8,128)(2,1)}), bf16[8,320,128]{2,1,0:T(8,128)(2,1)S(1)}, u32[]{:S(2)}, u32[]{:S(2)}) async-start(bf16[8,320,128]{2,1,0:T(8,128)(2,1)} %shard_map.157), calls=%async_computation.1 | async-start | bytes 1310720 | tf_op jit(solution)/shard_map/all_to_all | solution.py:93
  196.2 15.9 %collective-permute-start.19 = (bf16[320,128]{1,0:T(8,128)(2,1)S(1)}, bf16[320,128]{1,0:T(8,128)(2,1)S(1)}, u32[]{:S(2)}, u32[]{:S(2)}) collective-permute-start(bf16[320,128]{1,0:T(8,128)(2,1)S(1)} %reduce_sum.81), channel_id=1, source_target_pairs={{0,2},{1,18},{2,32},{3,48},{4,70},{5,86},{6,100},{7,116},{8,138},{... | collective-permute-start | bytes 245768 | tf_op jit(solution)/shard_map/ppermute | solution.py:350
  213.1 6.6 %collective-permute-start.20 = (bf16[2,320,128]{2,1,0:T(8,128)(2,1)S(1)}, bf16[2,320,128]{2,1,0:T(8,128)(2,1)S(1)}, u32[]{:S(2)}, u32[]{:S(2)}) collective-permute-start(bf16[2,320,128]{2,1,0:T(8,128)(2,1)S(1)} %fusion.28), channel_id=1, source_target_pairs={{0,4},{4,8},{8,12},{12,0},{1,5},{5,9},{9,13},{13,1},{2,6},{6,10},{... | collective-permute-start | bytes 491528 | tf_op jit(solution)/shard_map/ppermute | solution.py:28
  213.2 9.1 %collective-permute-start.21 = (bf16[2,320,128]{2,1,0:T(8,128)(2,1)S(1)}, bf16[2,320,128]{2,1,0:T(8,128)(2,1)S(1)}, u32[]{:S(2)}, u32[]{:S(2)}) collective-permute-start(bf16[2,320,128]{2,1,0:T(8,128)(2,1)S(1)} %fusion.28), channel_id=1, source_target_pairs={{0,12},{4,0},{8,4},{12,8},{1,13},{5,1},{9,5},{13,9},{2,14},{6,2},{... | collective-permute-start | bytes 491528 | tf_op jit(solution)/shard_map/ppermute | solution.py:28
  216.5 7.0 %collective-permute-start.22 = (bf16[2,320,128]{2,1,0:T(8,128)(2,1)S(1)}, bf16[2,320,128]{2,1,0:T(8,128)(2,1)S(1)}, u32[]{:S(2)}, u32[]{:S(2)}) collective-permute-start(bf16[2,320,128]{2,1,0:T(8,128)(2,1)S(1)} %fusion.28), channel_id=1, source_target_pairs={{0,8},{4,12},{8,0},{12,4},{1,9},{5,13},{9,1},{13,5},{2,10},{6,14},... | collective-permute-start | bytes 491528 | tf_op jit(solution)/shard_map/ppermute | solution.py:28
  235.1 6.6 %collective-permute-start.25 = (bf16[128,512]{1,0:T(8,128)(2,1)S(1)}, bf16[128,512]{1,0:T(8,128)(2,1)S(1)}, u32[]{:S(2)}, u32[]{:S(2)}) collective-permute-start(bf16[128,512]{1,0:T(8,128)(2,1)S(1)} %bitcast.215), channel_id=1, source_target_pairs={{0,128},{128,0},{1,129},{129,1},{2,130},{130,2},{3,131},{131,3},{4... | collective-permute-start | bytes 393224 | tf_op jit(solution)/shard_map/ppermute | solution.py:28
  264.7 10.2 %collective-permute-start.27 = (bf16[320,128]{1,0:T(8,128)(2,1)S(1)}, bf16[320,128]{1,0:T(8,128)(2,1)S(1)}, u32[]{:S(2)}, u32[]{:S(2)}) collective-permute-start(bf16[320,128]{1,0:T(8,128)(2,1)S(1)} %reduce_sum.85), channel_id=1, source_target_pairs={{0,0},{8,128},{128,8},{136,136},{1,1},{9,129},{129,9},{137,137},{2... | collective-permute-start | bytes 245768 | tf_op jit(solution)/shard_map/ppermute | solution.py:363
  (32 other events, 273.2 us)
Sparse Core Ops, SparseCore 0:
  9.9 69.8 all-gather.3
  90.0 66.1 reduce-scatter.1
  171.9 42.5 all-gather.5
